TPU v7x, 32 devices: a whole 2x2x4 slice. The times are simulated.
32 devices in a mesh: batch: 2 (over x), lat: 4 (over z), lon: 4 (over y, core).
Axes of the slice: x: 2, y: 2, z: 4, core: 2. Of those that a mesh axis runs over, the one named last changes fastest.
Arguments:
- inputs: bfloat16 [8, 64, 128, 128], P('batch', 'lat', 'lon'), may hold values from -22 to 22
- kernels: bfloat16 [4, 3, 3, 128, 128], replicated, may hold values from -0.1875 to 0.1875
- biases: float32 [4, 128], replicated, may hold values from -3 to 3
- gains: float32 [4, 128], replicated, may hold values from 0.1 to 1.9
- offsets: float32 [4, 128], replicated, may hold values from -2 to 2
- keep_masks: int32 [4, 8, 64, 128, 128], P(None, 'batch', 'lat', 'lon'), may hold values 0 or 1
- cotangent: bfloat16 [8, 64, 128, 128], P('batch', 'lat', 'lon'), may hold values from -6 to 6
Outputs:
- output: bfloat16 [8, 64, 128, 128], P('batch', 'lat', 'lon')
- input_grad: float32 [8, 64, 128, 128], P('batch', 'lat', 'lon')
- kernel_grad: float32 [4, 3, 3, 128, 128], replicated
- bias_grad: float32 [4, 128], replicated
- gain_grad: float32 [4, 128], replicated
- offset_grad: float32 [4, 128], replicated
All inputs are finite; a program needn't handle non-finite values. No bound on the sum of `keep_masks` on one device may be relied on, other than what follows from the above.
Results may differ from a plain program's by a relative error of at most 0.0065.
Values may be sent and summed in bfloat16 or wider, within the bound.
No kernel may reach another device: no remote copies, remote signals or barrier semaphores. Data moves between devices by JAX's collectives and lax.ppermute only.
A program may use at most 128 MiB of HBM per device.

v0:
```python
import jax
import jax.numpy as jnp
from jax import lax
from jax.sharding import PartitionSpec as P

eps = 1e-05
keep_rate = 0.9


def extended(block, sides, width, periodic):
    for axis, dim in sides:
        count = lax.axis_size(axis)
        forward = [(i, i + 1) for i in range(count - 1)]
        if periodic:
            forward.append((count - 1, 0))
        backward = [(target, source) for source, target in forward]
        low = lax.ppermute(
            lax.slice_in_dim(block, block.shape[dim] - width, None, axis=dim), axis, forward
        )
        high = lax.ppermute(lax.slice_in_dim(block, 0, width, axis=dim), axis, backward)
        block = jnp.concatenate([low, block, high], axis=dim)
    return block


def act_padded(field_low):
    widened = extended(field_low, (("lon", 2),), 1, True)
    return extended(widened, (("lat", 1),), 1, False)


def grad_padded(grad_low):
    widened = extended(grad_low, (("lon", 2),), 1, True)
    return extended(widened, (("lat", 1),), 1, False)


def apply_kernel(padded, kernel):
    return lax.conv_general_dilated(
        padded,
        kernel,
        (1, 1),
        "VALID",
        dimension_numbers=("NHWC", "HWIO", "NHWC"),
        preferred_element_type=jnp.float32,
    )


def count_all(act):
    return (
        act.shape[0]
        * act.shape[1]
        * act.shape[2]
        * lax.axis_size("batch")
        * lax.axis_size("lat")
        * lax.axis_size("lon")
    )


def moments(act):
    number = count_all(act)
    total = lax.psum(jnp.sum(act, axis=(0, 1, 2)), ("batch", "lat", "lon"))
    center = total / number
    spread = (
        lax.psum(jnp.sum(jnp.square(act - center), axis=(0, 1, 2)), ("batch", "lat", "lon"))
        / number
    )
    return (center, lax.rsqrt(spread + eps))


def layer_forward(field, kernel, shift_bias, gain_row, offset_row, keeper):
    padded = act_padded(field.astype(jnp.bfloat16))
    pre = apply_kernel(padded, kernel) + shift_bias
    act = jax.nn.silu(pre)
    center, inv_spread = moments(act)
    normed = (act - center) * inv_spread
    return ((normed * gain_row + offset_row) * keeper * (1.0 / keep_rate), (center, inv_spread))


def layer_again(field, kernel, shift_bias, gain_row, offset_row, keeper, stats):
    padded = act_padded(field.astype(jnp.bfloat16))
    pre = apply_kernel(padded, kernel) + shift_bias
    normed = (jax.nn.silu(pre) - stats[0]) * stats[1]
    result = (normed * gain_row + offset_row) * keeper * (1.0 / keep_rate)
    return (result, (padded, pre, normed))


def finish(kernel_term, bias_term):
    return lax.psum((kernel_term, bias_term), ("batch", "lat", "lon"))


def layer_backward(grad, kept, kernel, gain_row, keeper, stats):
    padded, pre, normed = kept
    number = count_all(pre)
    dnorm = grad * keeper * (1.0 / keep_rate)
    offset_term, gain_term = lax.psum(
        (jnp.sum(dnorm, axis=(0, 1, 2)), jnp.sum(dnorm * normed, axis=(0, 1, 2))),
        ("batch", "lat", "lon"),
    )
    dact = gain_row * stats[1] * (dnorm - offset_term / number - normed * gain_term / number)
    sigma = jax.nn.sigmoid(pre)
    dpre = (dact * sigma * (1.0 + pre * (1.0 - sigma))).astype(jnp.bfloat16)
    rows = pre.shape[1]
    cols = pre.shape[2]
    kernel_rows = []
    for row_off in range(3):
        kernel_cols = []
        for col_off in range(3):
            window = padded[:, row_off : row_off + rows, col_off : col_off + cols, :]
            kernel_cols.append(
                jnp.einsum("bhwc,bhwd->cd", window, dpre, preferred_element_type=jnp.float32)
            )
        kernel_rows.append(jnp.stack(kernel_cols))
    kernel_term = jnp.stack(kernel_rows)
    bias_term = jnp.sum(dpre, axis=(0, 1, 2), dtype=jnp.float32)
    kernel_term, bias_term = finish(kernel_term, bias_term)
    flipped = jnp.transpose(jnp.flip(kernel, (0, 1)), (0, 1, 3, 2))
    dfield = apply_kernel(grad_padded(dpre), flipped)
    return (dfield, kernel_term, bias_term, gain_term, offset_term)


def local(inputs, kernels, biases, gains, offsets, keep_masks, cotangent):
    field = inputs.astype(jnp.float32)
    block_inputs = []
    stats_all = []
    for section in range(2):
        block_inputs.append(field)
        hidden = field
        for inner in range(2):
            layer_idx = 2 * section + inner
            hidden, stats = layer_forward(
                hidden,
                kernels[layer_idx],
                biases[layer_idx],
                gains[layer_idx],
                offsets[layer_idx],
                keep_masks[layer_idx].astype(jnp.float32),
            )
            stats_all.append(stats)
        field = field + hidden
    output = field.astype(jnp.bfloat16)
    grad = cotangent.astype(jnp.float32)
    kernel_parts = [None] * 4
    bias_parts = [None] * 4
    gain_parts = [None] * 4
    offset_parts = [None] * 4
    for section in (1, 0):
        first_idx = 2 * section
        second_idx = first_idx + 1
        first_keep = keep_masks[first_idx].astype(jnp.float32)
        second_keep = keep_masks[second_idx].astype(jnp.float32)
        first_out, kept_first = layer_again(
            block_inputs[section],
            kernels[first_idx],
            biases[first_idx],
            gains[first_idx],
            offsets[first_idx],
            first_keep,
            stats_all[first_idx],
        )
        unused, kept_second = layer_again(
            first_out,
            kernels[second_idx],
            biases[second_idx],
            gains[second_idx],
            offsets[second_idx],
            second_keep,
            stats_all[second_idx],
        )
        back_second = layer_backward(
            grad,
            kept_second,
            kernels[second_idx],
            gains[second_idx],
            second_keep,
            stats_all[second_idx],
        )
        back_first = layer_backward(
            back_second[0],
            kept_first,
            kernels[first_idx],
            gains[first_idx],
            first_keep,
            stats_all[first_idx],
        )
        for layer_idx, result in ((second_idx, back_second), (first_idx, back_first)):
            kernel_parts[layer_idx] = result[1]
            bias_parts[layer_idx] = result[2]
            gain_parts[layer_idx] = result[3]
            offset_parts[layer_idx] = result[4]
        grad = grad + back_first[0]
    kernel_grad = jnp.stack(kernel_parts)
    bias_grad = jnp.stack(bias_parts)
    return (output, grad, kernel_grad, bias_grad, jnp.stack(gain_parts), jnp.stack(offset_parts))


def solution(mesh):
    in_specs = (
        P("batch", "lat", "lon", None),
        P(),
        P(),
        P(),
        P(),
        P(None, "batch", "lat", "lon", None),
        P("batch", "lat", "lon", None),
    )
    out_specs = (P("batch", "lat", "lon", None), P("batch", "lat", "lon", None), P(), P(), P(), P())
    return jax.shard_map(local, mesh=mesh, in_specs=in_specs, out_specs=out_specs, check_vma=False)
```

profile of v0, /device:TPU:1, one launch (start us, length us, event | category | flops | bytes accessed | tf_op | source)
XLA Modules:
  0.0 854.1 jit_solution(12307175888265759842)
XLA Ops:
  8.4 2.6 collective-permute-start
  14.6 4.0 collective-permute-start.2
  22.6 2.9 select_reduce_fusion.7
  25.5 41.7 %psum.168 = f32[128]{0:T(128)S(1)} all-reduce(f32[128]{0:T(128)S(1)} %get-tuple-element.117), channel_id=1, replica_groups=mesh['batch'=2,'lat'=4,'lon'=4] {'batch','lat','lon'}, use_global_device_ids=true, to_apply=%region_1.2 | all-reduce | flops 128 | bytes 1024 | tf_op jit(solution)/shard_map/psum | solution.py:59
  67.1 2.2 add_divide_fusion.3
  69.3 40.5 %psum.169 = f32[128]{0:T(128)S(1)} all-reduce(f32[128]{0:T(128)S(1)} %get-tuple-element.58), channel_id=1, replica_groups=mesh['batch'=2,'lat'=4,'lon'=4] {'batch','lat','lon'}, use_global_device_ids=true, to_apply=%region_3.4 | all-reduce | flops 128 | bytes 1024 | tf_op jit(solution)/shard_map/psum | solution.py:62
  111.2 1.7 fusion.58
  113.0 1.5 collective-permute-start.5
  114.5 1.9 collective-permute-start.4
  116.5 1.8 collective-permute-done.5
  119.6 4.0 collective-permute-start.6
  126.1 2.9 select_reduce_fusion.5
  129.0 40.7 %psum.170 = f32[128]{0:T(128)S(1)} all-reduce(f32[128]{0:T(128)S(1)} %get-tuple-element.119), channel_id=1, replica_groups=mesh['batch'=2,'lat'=4,'lon'=4] {'batch','lat','lon'}, use_global_device_ids=true, to_apply=%region_5.6 | all-reduce | flops 128 | bytes 1024 | tf_op jit(solution)/shard_map/psum | solution.py:59
  169.7 2.1 add_divide_fusion.2
  171.9 39.5 %psum.171 = f32[128]{0:T(128)S(1)} all-reduce(f32[128]{0:T(128)S(1)} %get-tuple-element.55), channel_id=1, replica_groups=mesh['batch'=2,'lat'=4,'lon'=4] {'batch','lat','lon'}, use_global_device_ids=true, to_apply=%region_7.8 | all-reduce | flops 128 | bytes 1024 | tf_op jit(solution)/shard_map/psum | solution.py:62
  211.4 1.8 multiply_add_fusion.4
  215.0 2.2 fusion.145
  217.2 1.5 collective-permute-start.9
  218.8 1.9 collective-permute-start.8
  220.7 1.8 collective-permute-done.9
  223.9 4.0 collective-permute-start.10
  237.1 3.9 select_reduce_fusion.3
  241.0 39.6 %psum.172 = f32[128]{0:T(128)S(1)} all-reduce(f32[128]{0:T(128)S(1)} %get-tuple-element.121), channel_id=1, replica_groups=mesh['batch'=2,'lat'=4,'lon'=4] {'batch','lat','lon'}, use_global_device_ids=true, to_apply=%region_9.10 | all-reduce | flops 128 | bytes 1024 | tf_op jit(solution)/shard_map/psum | solution.py:59
  280.5 3.5 add_divide_fusion.1
  284.1 39.5 %psum.173 = f32[128]{0:T(128)S(1)} all-reduce(f32[128]{0:T(128)S(1)} %get-tuple-element.52), channel_id=1, replica_groups=mesh['batch'=2,'lat'=4,'lon'=4] {'batch','lat','lon'}, use_global_device_ids=true, to_apply=%region_11.12 | all-reduce | flops 128 | bytes 1024 | tf_op jit(solution)/shard_map/psum | solution.py:62
  323.5 1.9 multiply_add_fusion.2
  326.3 1.8 fusion.52
  328.2 1.5 collective-permute-start.13
  329.7 1.9 collective-permute-start.12
  340.8 4.2 collective-permute-start.14
  354.2 3.9 select_reduce_fusion.1
  358.1 38.1 %psum.174 = f32[128]{0:T(128)S(1)} all-reduce(f32[128]{0:T(128)S(1)} %get-tuple-element.123), channel_id=1, replica_groups=mesh['batch'=2,'lat'=4,'lon'=4] {'batch','lat','lon'}, use_global_device_ids=true, to_apply=%region_13.14 | all-reduce | flops 128 | bytes 1024 | tf_op jit(solution)/shard_map/psum | solution.py:59
  396.2 2.0 add_divide_fusion
  401.9 39.6 %psum.175 = f32[128]{0:T(128)S(1)} all-reduce(f32[128]{0:T(128)S(1)} %get-tuple-element.49), channel_id=1, replica_groups=mesh['batch'=2,'lat'=4,'lon'=4] {'batch','lat','lon'}, use_global_device_ids=true, to_apply=%region_15.16 | all-reduce | flops 128 | bytes 1024 | tf_op jit(solution)/shard_map/psum | solution.py:62
  441.5 2.9 multiply_add_fusion
  446.5 1.7 fusion.132
  448.2 40.5 %all-reduce.4 = (f32[128]{0:T(128)S(1)}, f32[128]{0:T(128)S(1)}) all-reduce(f32[128]{0:T(128)S(1)} %get-tuple-element.11, f32[128]{0:T(128)S(1)} %get-tuple-element.10), channel_id=1, replica_groups=mesh['batch'=2,'lat'=4,'lon'=4] {'batch','lat','lon'}, use_global_device_ids=true, to_apply=%region_19.20 | all-reduce | flops 256 | bytes 2048 | tf_op jit(solution)/shard_map/psum | solution.py:93
  488.7 1.6 multiply_multiply_fusion
  496.9 1.5 collective-permute-start.17
  498.4 1.9 collective-permute-start.16
  503.5 4.4 collective-permute-start.18
  512.0 2.7 convolution_select_fusion.3
  517.7 38.6 %all-reduce.3 = (f32[128]{0:T(128)S(1)}, f32[128]{0:T(128)S(1)}) all-reduce(f32[128]{0:T(128)S(1)} %get-tuple-element.9, f32[128]{0:T(128)S(1)} %get-tuple-element.8), channel_id=1, replica_groups=mesh['batch'=2,'lat'=4,'lon'=4] {'batch','lat','lon'}, use_global_device_ids=true, to_apply=%region_23.24 | all-reduce | flops 256 | bytes 2048 | tf_op jit(solution)/shard_map/psum | solution.py:93
  556.3 1.6 multiply_multiply_fusion.1
  565.8 1.5 collective-permute-start.21
  567.3 2.1 collective-permute-start.20
  572.7 4.0 collective-permute-start.22
  579.2 2.7 convolution_select_fusion.2
  584.0 1.8 fusion.152
  585.8 40.3 %all-reduce.2 = (f32[128]{0:T(128)S(1)}, f32[128]{0:T(128)S(1)}) all-reduce(f32[128]{0:T(128)S(1)} %get-tuple-element.13, f32[128]{0:T(128)S(1)} %get-tuple-element.12), channel_id=1, replica_groups=mesh['batch'=2,'lat'=4,'lon'=4] {'batch','lat','lon'}, use_global_device_ids=true, to_apply=%region_27.28 | all-reduce | flops 256 | bytes 2048 | tf_op jit(solution)/shard_map/psum | solution.py:93
  635.2 1.9 collective-permute-start.24
  640.6 3.8 collective-permute-start.26
  646.8 2.7 convolution_select_fusion.1
  651.5 2.3 fusion.147
  653.8 40.7 %all-reduce.1 = (f32[128]{0:T(128)S(1)}, f32[128]{0:T(128)S(1)}) all-reduce(f32[128]{0:T(128)S(1)} %get-tuple-element.7, f32[128]{0:T(128)S(1)} %get-tuple-element.6), channel_id=1, replica_groups=mesh['batch'=2,'lat'=4,'lon'=4] {'batch','lat','lon'}, use_global_device_ids=true, to_apply=%region_31.32 | all-reduce | flops 256 | bytes 2048 | tf_op jit(solution)/shard_map/psum | solution.py:93
  697.8 4.5 convert_reduce_fusion.3
  705.2 1.5 collective-permute-start.29
  706.7 2.2 collective-permute-start.28
  710.6 37.2 %all-reduce = (f32[1,128]{1,0:T(1,128)S(1)}, f32[1,128]{1,0:T(1,128)S(1)}, f32[1,128]{1,0:T(1,128)S(1)}, f32[1,128]{1,0:T(1,128)S(1)}) all-reduce(f32[1,128]{1,0:T(1,128)S(1)} %bitcast.713, f32[1,128]{1,0:T(1,128)S(1)} %bitcast.714, f32[1,128]{1,0:T(1,128)S(1)} %bitcast.720, ...), channel_id=1, replica_groups=mesh['batch'=2,'lat'=4,'lon'=4] {'batch','lat','lon'}, use_global_device_ids=true, to_apply=%region_43.44 | all-reduce | flops 512 | bytes 4096 | tf_op jit(solution)/shard_map/psum | solution.py:86
  750.3 4.0 collective-permute-start.30
  756.8 2.7 convolution_select_fusion
  761.6 1.6 fusion.13
  763.2 80.4 %all-reduce.8.cloned.1.call-done = (f32[1,3,3,128,128]{4,3,2,1,0:T(8,128)}, f32[1,3,3,128,128]{4,3,2,1,0:T(8,128)}, f32[1,3,3,128,128]{4,3,2,1,0:T(8,128)}, f32[1,3,3,128,128]{4,3,2,1,0:T(8,128)}) async-done(((f32[1,3,3,128,128]{4,3,2,1,0:T(8,128)}, f32[1,3,3,128,128]{4,3,2,1,0:T(8,128)}, f32[1,3,3,128,128]{4,3,2,1,0:T(8,128)}, f32[1,3,3,128,128]{4,3,2,1,0:T(8,128)}), (f32[1,3,3,128,128]{4,3,2,1,0:T(8,128)}, ...) | async-done | bytes 2359312 | tf_op jit(solution)/shard_map/psum | solution.py:86
  843.6 3.3 pad_maximum_fusion
  (362 shorter events, 114.7 us)
Async XLA Ops:
  7.2 836.4 %all-reduce.8.cloned.1.call-start = ((), (), s32[]{:S(2)}) async-start(), calls=%async_computation | async-start | bytes 4718592 | tf_op jit(solution)/shard_map/psum | solution.py:86
  8.2 4.3 collective-permute-start.1
  8.4 4.2 collective-permute-start
  13.3 6.6 collective-permute-start.3
  14.6 5.4 collective-permute-start.2
  112.9 12.4 %copy-start.14 = (bf16[4,16,32,128]{3,2,1,0:T(8,128)(2,1)}, bf16[4,16,32,128]{3,2,1,0:T(8,128)(2,1)S(1)}, u32[]{:S(2)}) copy-start(bf16[4,16,32,128]{3,2,1,0:T(8,128)(2,1)S(1)} %fusion.58) | copy-start | bytes 1572868
  113.0 5.3 collective-permute-start.5
  114.5 3.8 collective-permute-start.4
  118.3 5.3 collective-permute-start.7
  119.6 5.1 collective-permute-start.6
  129.0 42.9 %copy-start.26 = (f32[16,32,5,128]{3,1,2,0:T(8,128)}, f32[16,32,5,128]{3,1,2,0:T(8,128)S(1)}, u32[]{:S(2)}) copy-start(f32[16,32,5,128]{3,1,2,0:T(8,128)S(1)} %get-tuple-element.120) | copy-start | bytes 3932164
  215.0 2.2 copy-start.6
  217.2 18.4 %copy-start.19 = (bf16[4,16,32,128]{3,2,1,0:T(8,128)(2,1)}, bf16[4,16,32,128]{3,2,1,0:T(8,128)(2,1)S(1)}, u32[]{:S(2)}) copy-start(bf16[4,16,32,128]{3,2,1,0:T(8,128)(2,1)S(1)} %fusion.145) | copy-start | bytes 1572868
  217.2 5.3 collective-permute-start.9
  218.8 10.6 %copy-start.29 = (f32[16,32,5,128]{3,1,2,0:T(8,128)S(1)}, f32[16,32,5,128]{3,1,2,0:T(8,128)}, u32[]{:S(2)}) copy-start(f32[16,32,5,128]{3,1,2,0:T(8,128)} %get-tuple-element.59) | copy-start | bytes 3932164
  218.8 3.8 collective-permute-start.8
  222.6 13.0 %collective-permute-start.11 = (bf16[4,1,34,128]{3,2,1,0:T(8,128)(2,1)S(1)}, bf16[4,1,34,128]{3,2,1,0:T(8,128)(2,1)S(1)}, u32[]{:S(2)}, u32[]{:S(2)}) collective-permute-start(bf16[4,1,34,128]{3,2,1,0:T(8,128)(2,1)S(1)} %get-tuple-element.79), channel_id=1, source_target_pairs={{4,0},{8,4},{12,8},{5,1},{9,5},{13,9},{6,2},{10,6},{14,10},{7,3},{... | collective-permute-start | bytes 104456 | tf_op jit(solution)/shard_map/ppermute | solution.py:20
  223.9 11.7 %collective-permute-start.10 = (bf16[4,1,34,128]{3,2,1,0:T(8,128)(2,1)S(1)}, bf16[4,1,34,128]{3,2,1,0:T(8,128)(2,1)S(1)}, u32[]{:S(2)}, u32[]{:S(2)}) collective-permute-start(bf16[4,1,34,128]{3,2,1,0:T(8,128)(2,1)S(1)} %get-tuple-element.78), channel_id=1, source_target_pairs={{0,4},{4,8},{8,12},{1,5},{5,9},{9,13},{2,6},{6,10},{10,14},{3,7},{... | collective-permute-start | bytes 104456 | tf_op jit(solution)/shard_map/ppermute | solution.py:17
  280.5 43.0 %copy-start.58 = (f32[128]{0:T(128)S(1)}, f32[128]{0:T(128)}, u32[]{:S(2)}) copy-start(f32[128]{0:T(128)} %get-tuple-element.115) | copy-start | bytes 1540
  280.5 43.0 %copy-start.59 = (f32[128]{0:T(128)S(1)}, f32[128]{0:T(128)}, u32[]{:S(2)}) copy-start(f32[128]{0:T(128)} %get-tuple-element.125) | copy-start | bytes 1540
  323.5 1.9 copy-start.66
  325.4 25.3 %copy-start.4 = (f32[16,32,5,128]{3,1,2,0:T(8,128)}, f32[16,32,5,128]{3,1,2,0:T(8,128)S(1)}, u32[]{:S(2)}) copy-start(f32[16,32,5,128]{3,1,2,0:T(8,128)S(1)} %get-tuple-element.42) | copy-start | bytes 3932164
  326.3 5.4 copy-start.15
  328.1 24.5 %copy-start.17 = (bf16[4,16,32,128]{3,2,1,0:T(8,128)(2,1)}, bf16[4,16,32,128]{3,2,1,0:T(8,128)(2,1)S(1)}, u32[]{:S(2)}) copy-start(bf16[4,16,32,128]{3,2,1,0:T(8,128)(2,1)S(1)} %fusion.52) | copy-start | bytes 1572868
  328.1 5.1 copy-start.30
  328.2 11.1 %collective-permute-start.13 = (bf16[4,16,1,128]{3,2,1,0:T(2,128)(2,1)S(1)}, bf16[4,16,1,128]{3,2,1,0:T(2,128)(2,1)S(1)}, u32[]{:S(2)}, u32[]{:S(2)}) collective-permute-start(bf16[4,16,1,128]{3,2,1,0:T(2,128)(2,1)S(1)} %get-tuple-element.93), channel_id=1, source_target_pairs={{1,0},{2,1},{3,2},{0,3},{5,4},{6,5},{7,6},{4,7},{9,8},{10,9},{11,1... | collective-permute-start | bytes 49160 | tf_op jit(solution)/shard_map/ppermute | solution.py:20
  329.7 9.6 %collective-permute-start.12 = (bf16[4,16,1,128]{3,2,1,0:T(2,128)(2,1)S(1)}, bf16[4,16,1,128]{3,2,1,0:T(2,128)(2,1)S(1)}, u32[]{:S(2)}, u32[]{:S(2)}) collective-permute-start(bf16[4,16,1,128]{3,2,1,0:T(2,128)(2,1)S(1)} %get-tuple-element.92), channel_id=1, source_target_pairs={{0,1},{1,2},{2,3},{3,0},{4,5},{5,6},{6,7},{7,4},{8,9},{9,10},{10,1... | collective-permute-start | bytes 49160 | tf_op jit(solution)/shard_map/ppermute | solution.py:17
  338.2 6.7 copy-start.20
  338.2 6.7 copy-start.52
  339.3 7.2 copy-start.33
  339.3 13.3 %collective-permute-start.15 = (bf16[4,1,34,128]{3,2,1,0:T(8,128)(2,1)S(1)}, bf16[4,1,34,128]{3,2,1,0:T(8,128)(2,1)S(1)}, u32[]{:S(2)}, u32[]{:S(2)}) collective-permute-start(bf16[4,1,34,128]{3,2,1,0:T(8,128)(2,1)S(1)} %get-tuple-element.77), channel_id=1, source_target_pairs={{4,0},{8,4},{12,8},{5,1},{9,5},{13,9},{6,2},{10,6},{14,10},{7,3},{... | collective-permute-start | bytes 104456 | tf_op jit(solution)/shard_map/ppermute | solution.py:20
  340.8 11.9 %collective-permute-start.14 = (bf16[4,1,34,128]{3,2,1,0:T(8,128)(2,1)S(1)}, bf16[4,1,34,128]{3,2,1,0:T(8,128)(2,1)S(1)}, u32[]{:S(2)}, u32[]{:S(2)}) collective-permute-start(bf16[4,1,34,128]{3,2,1,0:T(8,128)(2,1)S(1)} %get-tuple-element.76), channel_id=1, source_target_pairs={{0,4},{4,8},{8,12},{1,5},{5,9},{9,13},{2,6},{6,10},{10,14},{3,7},{... | collective-permute-start | bytes 104456 | tf_op jit(solution)/shard_map/ppermute | solution.py:17
  400.8 40.7 %copy-start.56 = (f32[4,128]{1,0:T(4,128)S(1)}, f32[4,128]{1,0:T(4,128)}, u32[]{:S(2)}) copy-start(f32[4,128]{1,0:T(4,128)} %param.10) | copy-start | bytes 6148
  400.8 40.7 %copy-start.62 = (f32[128]{0:T(128)S(1)}, f32[128]{0:T(128)}, u32[]{:S(2)}) copy-start(f32[128]{0:T(128)} %copy-done.61) | copy-start | bytes 1540
  400.8 40.7 %copy-start.64 = (f32[128]{0:T(128)S(1)}, f32[128]{0:T(128)}, u32[]{:S(2)}) copy-start(f32[128]{0:T(128)} %copy-done.63) | copy-start | bytes 1540
  400.8 40.7 %copy-start.67 = (f32[128]{0:T(128)S(1)}, f32[128]{0:T(128)}, u32[]{:S(2)}) copy-start(f32[128]{0:T(128)} %copy-done.66) | copy-start | bytes 1540
  400.8 40.7 %copy-start.57 = (f32[128]{0:T(128)S(1)}, f32[128]{0:T(128)}, u32[]{:S(2)}) copy-start(f32[128]{0:T(128)} %get-tuple-element.126) | copy-start | bytes 1540
  488.7 2.5 copy-start.43
  488.7 2.5 copy-start.44
  490.4 2.3 copy-start
  496.9 5.3 collective-permute-start.17
  498.4 3.8 collective-permute-start.16
  501.1 7.7 copy-start.31
  502.2 8.4 collective-permute-start.19
  503.5 7.1 collective-permute-start.18
  556.3 2.5 copy-start.13
  556.3 2.5 copy-start.36
  556.3 2.5 copy-start.37
  558.0 2.3 copy-start.1
  565.8 5.6 collective-permute-start.21
  567.3 4.1 collective-permute-start.20
  571.4 6.2 collective-permute-start.23
  572.7 5.1 collective-permute-start.22
  633.7 5.3 collective-permute-start.25
  635.2 3.8 collective-permute-start.24
  639.0 6.2 collective-permute-start.27
  640.6 4.9 collective-permute-start.26
  651.5 2.3 copy-start.10
  694.7 3.0 copy-start.2
  697.8 4.6 copy-start.46
  705.2 43.8 %collective-permute-start.29 = (bf16[4,16,1,128]{3,2,1,0:T(2,128)(2,1)S(1)}, bf16[4,16,1,128]{3,2,1,0:T(2,128)(2,1)S(1)}, u32[]{:S(2)}, u32[]{:S(2)}) collective-permute-start(bf16[4,16,1,128]{3,2,1,0:T(2,128)(2,1)S(1)} %get-tuple-element.85), channel_id=1, source_target_pairs={{1,0},{2,1},{3,2},{0,3},{5,4},{6,5},{7,6},{4,7},{9,8},{10,9},{11,1... | collective-permute-start | bytes 49160 | tf_op jit(solution)/shard_map/ppermute | solution.py:20
  706.7 42.2 %collective-permute-start.28 = (bf16[4,16,1,128]{3,2,1,0:T(2,128)(2,1)S(1)}, bf16[4,16,1,128]{3,2,1,0:T(2,128)(2,1)S(1)}, u32[]{:S(2)}, u32[]{:S(2)}) collective-permute-start(bf16[4,16,1,128]{3,2,1,0:T(2,128)(2,1)S(1)} %get-tuple-element.84), channel_id=1, source_target_pairs={{0,1},{1,2},{2,3},{3,0},{4,5},{5,6},{6,7},{7,4},{8,9},{9,10},{10,1... | collective-permute-start | bytes 49160 | tf_op jit(solution)/shard_map/ppermute | solution.py:17
  749.0 5.9 collective-permute-start.31
  750.3 5.1 collective-permute-start.30
  (37 other events, 44.9 us)
Sparse Core Ops, SparseCore 0:
  710.7 132.8 all-reduce.7
where the time goes:
time: 867 us; the launch traced here: 854 us
  blocking collectives  517 us (60%)
  waiting for transfers between devices  89.4 us (10%)
  starting transfers between devices  70.5 us (8%)
  other arithmetic  64.6 us (7%)
  local copies, waits for them, and re-layouts  60.4 us (7%)
  matrix products  36.6 us (4%)
  between operations  16.1 us (2%)
    psum x4, blocking collectives, layer_backward(): lax.psum((jnp.sum(dnorm, axis=(0, 1, 2)), jnp.sum(dnorm * normed, axis=(0...  160 us
    psum x4, blocking collectives, moments(): total = lax.psum(jnp.sum(act, axis=(0, 1, 2)), ('batch', 'lat', 'lon'))  160 us
    psum x4, blocking collectives, moments(): lax.psum(jnp.sum(jnp.square(act - center), axis=(0, 1, 2)), ('batch', 'la...  159 us
    psum x1, waiting for transfers between devices, finish(): return lax.psum((kernel_term, bias_term), ('batch', 'lat', 'lon'))  80.4 us
    ppermute x16, starting transfers between devices, extended(): lax.ppermute(lax.slice_in_dim(block, block.shape[dim] - width, None, axis...  48.9 us
    psum x1, blocking collectives, finish(): return lax.psum((kernel_term, bias_term), ('batch', 'lat', 'lon'))  37.2 us
    conv_general_dilated x8, matrix products, apply_kernel(): lax.conv_general_dilated(padded, kernel, (1, 1), 'VALID', dimension_numbe...  24.2 us
    unnamed x144, local copies, waits for them, and re-layouts  21.6 us
  transfers between devices with their start and end apart: 33, of which 11 were waited for; matrix products, arithmetic and copies ran while one was open for 5% of the time, Pallas kernels for 0%

commit v1 on v0

v1 whole, which is shorter than its diff:
```python
import functools

import jax
import jax.numpy as jnp
from jax import lax
from jax.experimental import pallas as pl
from jax.experimental.pallas import tpu as pltpu
from jax.sharding import PartitionSpec as P

eps = 1e-05
keep_rate = 0.9
EVERY = ("batch", "lat", "lon")
EXT = 8
LANES = 128
F32 = jnp.float32
LOW = jnp.bfloat16


def partners(axis, periodic):
    count = lax.axis_size(axis)
    first = [(i, i ^ 1) for i in range(count)]
    second = []
    for i in range(count):
        j = i + 1 if i % 2 else i - 1
        if periodic:
            second.append((i, j % count))
        elif 0 <= j < count:
            second.append((i, j))
    return first, second


def trade(pair, axis, periodic):
    first, second = partners(axis, periodic)
    return lax.ppermute(pair[0], axis, first), lax.ppermute(pair[1], axis, second)


def to_all(rows):
    return lax.all_to_all(rows, EVERY, 0, 0)


def to_half(rows, devices):
    groups = [[i for i in range(devices) if i % 2 == side] for side in range(2)]
    return lax.all_to_all(rows, EVERY, 0, 0, axis_index_groups=groups)


def to_pair(block):
    return lax.ppermute(block, "lon", partners("lon", True)[0])


def sigmoid(v):
    return 0.5 * jnp.tanh(0.5 * v) + 0.5


def norm_consts(stats_ref, devices):
    stats = stats_ref[...]
    total = jnp.sum(stats, axis=0)
    center = total[0:1] * (1.0 / devices)
    apart = jnp.sum(jnp.square(stats - center[None]), axis=0)
    spread = (total[1:2] + apart[0:1]) * (1.0 / devices)
    return center, lax.rsqrt(spread + eps)


def top_sums(stats_ref, center, inv):
    stats = stats_ref[...]
    total = jnp.sum(stats, axis=0)
    apart = stats[:, 0:1, :] - center[None]
    return total[2:3], (total[3:4] + jnp.sum(apart * stats[:, 2:3, :], axis=0)) * inv


def shifted(value, width):
    return pltpu.roll(value, 1, 1), value, pltpu.roll(value, width - 1, 1)


def store_shifted(taps, row, count, value, width):
    for s, part in enumerate(shifted(value, width)):
        taps[s, pl.ds(row, count)] = part.astype(LOW)


def lay_weights(kernel_ref, layer, back, out):
    blank = jnp.zeros((3 * LANES, LANES), LOW)
    out[9 * LANES : 12 * LANES, 0:LANES] = blank
    out[0 : 3 * LANES, LANES : 2 * LANES] = blank
    for r in range(3):
        for s in range(3):
            if back:
                block = kernel_ref[layer, (2 - r) * 3 + 2 - s].astype(F32).T.astype(LOW)
            else:
                block = kernel_ref[layer, r * 3 + s]
            at = (r * 3 + s) * LANES
            out[at : at + LANES, 0:LANES] = block
            out[at + 3 * LANES : at + 4 * LANES, LANES : 2 * LANES] = block


def conv_pairs(taps, weight_ref, row, pairs, cols):
    parts = []
    for t in range(4):
        for s in range(3):
            parts.append(jnp.stack([taps[s, row - 1 + t + 2 * k, 0:cols, :] for k in range(pairs)]))
    left = jnp.concatenate(parts, axis=-1).reshape(pairs * cols, 12 * LANES)
    both = jnp.dot(left, weight_ref[...], preferred_element_type=F32)
    out = []
    for k in range(pairs):
        for h in range(2):
            out.append(both[k * cols : (k + 1) * cols, h * LANES : (h + 1) * LANES])
    return out


def chunks(lo, hi, pairs):
    at = lo
    while at < hi:
        count = min(pairs, (hi - at) // 2)
        yield at, count
        at += 2 * count


def loop_rows(lo, hi, body):
    def step(i, carry):
        body(lo + 2 * i)
        return carry

    lax.fori_loop(0, (hi - lo) // 2, step, 0, unroll=2)


def loop_grids(grids, body):
    def step(g, carry):
        body(g)
        return carry

    lax.fori_loop(0, grids, step, 0)


def fold(value):
    return jnp.sum(value.reshape(-1, 8, LANES), axis=0)


def to_row(value):
    return jnp.sum(value, axis=0, keepdims=True)


def both_ways(even, give_first, give_second):
    @pl.when(even == 1)
    def _():
        give_first(False)
        give_second(True)

    @pl.when(even == 0)
    def _():
        give_first(True)
        give_second(False)


def whichever(even, place, got_first, got_second):
    @pl.when(even == 1)
    def _():
        place(got_second, got_first)

    @pl.when(even == 0)
    def _():
        place(got_first, got_second)


def row_edges(geo, info, sources, heights, first, second):
    grids, rows = geo["G"], geo["R"]

    def give(out):
        def act(low):
            at = 0
            for src, h in zip(sources, heights):
                for g in range(grids):
                    out[g, at : at + h] = src[g, 0:h] if low else src[g, rows - h : rows]
                at += h
        return act

    both_ways(info[0], give(first), give(second))


def field_edge_kernel(geo, info, x, first, second):
    row_edges(geo, info, [x], [EXT], first, second)


def mask_edge_kernel(geo, info, masks, cot, *outs):
    grids = geo["G"]
    lows = outs[0:4]
    for k in range(4):
        for g in range(grids):
            lows[k][g] = masks[k, g].astype(F32).astype(LOW)
    row_edges(geo, info, [lows[0]], geo["heights"][1:2], outs[4], outs[5])
    row_edges(geo, info, list(lows[1:]) + [cot], geo["heights"][2:], outs[6], outs[7])


def stack_kernel(geo, heights, info, *refs):
    grids, rows, cols = geo["G"], geo["R"], geo["C"]
    count = len(heights)
    sources, got_first, got_second = refs[:count], refs[count], refs[count + 1]
    talls = refs[count + 2 : 2 * count + 2]
    first, second = refs[2 * count + 2 :]

    def place(low, high):
        at = 0
        for k, h in enumerate(heights):
            for g in range(grids):
                talls[k][g, 0:h] = low[g, at : at + h]
                talls[k][g, h + rows : 2 * h + rows] = high[g, at : at + h]
            at += h

    whichever(info[0], place, got_first, got_second)
    for k, h in enumerate(heights):
        for g in range(grids):
            talls[k][g, h : h + rows] = sources[k][g]

    def give(out):
        def act(low):
            at = 0
            for k, h in enumerate(heights):
                for g in range(grids):
                    part = talls[k][g, :, 0:EXT, :] if low else talls[k][g, :, cols - EXT : cols, :]
                    out[g, at : at + rows + 2 * h] = part
                at += rows + 2 * h
        return act

    both_ways(info[1], give(first), give(second))


def widen(geo, info, height, at, tall, got_first, got_second, out):
    cols, total = geo["C"], geo["R"] + 2 * height

    def place(low, high):
        for g in range(geo["G"]):
            right = high[g, at : at + total].astype(F32)
            left = low[g, at : at + total].astype(F32)
            out[g, :, cols:, :] = jnp.concatenate([right, left], axis=1).astype(LOW)

    whichever(info[1], place, got_first, got_second)
    for g in range(geo["G"]):
        out[g, :, 0:cols, :] = tall[g]


def forward_kernel(layer, geo, *refs):
    grids, rows, devices, width, cols = geo["G"], geo["R"], geo["D"], geo["CE"], geo["C"]
    heights = geo["heights"]
    refs = list(refs)
    info, gains, offsets, biases, kernels = (refs.pop(0) for _ in range(5))
    if layer:
        stats, pre_in = refs.pop(0), refs.pop(0)
    field = refs.pop(0) if layer == 2 else None
    members = geo["members"][layer]
    pieces = [[refs.pop(0) for _ in range(3)] for _ in members]
    sums_out = refs.pop(0)
    exts = [refs.pop(0) for _ in members]
    pre_out = refs.pop(0)
    low_out = refs.pop(0) if layer else None
    field_out = refs.pop(0) if layer == 2 else None
    taps, weight, acts, acc = refs
    lo, hi = layer + 1, geo["RE"] - 1 - layer

    lay_weights(kernels, layer, False, weight)
    for k, parts, ext in zip(members, pieces, exts):
        widen(geo, info, heights[k], geo["starts"][k], *parts, ext)
    ext = exts[0]
    if layer == 3:
        keep3, cot = exts[1], exts[2]
    if layer:
        center, inv = norm_consts(stats, devices)
        scale = inv * gains[layer - 1 : layer, :]
        shift = offsets[layer - 1 : layer, :]
    bias = biases[layer : layer + 1, :]

    def one_grid(g):
        def prepare(r):
            if layer == 0:
                value = ext[g, pl.ds(r, 2)].astype(F32)
            else:
                p = pre_in[g, pl.ds(r, 2)]
                act = p * sigmoid(p)
                kept = ext[g, pl.ds(r - layer, 2)].astype(F32) * (1.0 / keep_rate)
                value = ((act - center) * scale + shift) * kept
                if layer == 2:
                    value = value + field[g, pl.ds(r, 2)].astype(F32)
            store_shifted(taps, r, 2, value, width)
            if layer == 2:
                @pl.when((r >= EXT - 1) & (r < EXT + rows))
                def _():
                    field_out[g, pl.ds(r - (EXT - 1), 2)] = value[:, 0:cols, :]

        loop_rows(lo - 1, hi + 1, prepare)
        if layer:
            low_out[g] = taps[1, EXT - 1 : EXT + 1 + rows]
        number = rows * cols
        total = jnp.zeros((8, LANES), F32)
        for at, count in chunks(lo, hi, 5):
            for k, part in enumerate(conv_pairs(taps, weight, at, count, width)):
                part = part + bias
                pre_out[g, at + k] = part
                if EXT <= at + k < EXT + rows:
                    inner = part[0:cols]
                    act = inner * sigmoid(inner)
                    acts[at + k - EXT] = act
                    total = total + fold(act)
        mean = to_row(total) * (1.0 / number)
        square = jnp.zeros((8, LANES), F32)
        first = jnp.zeros((8, LANES), F32)
        second = jnp.zeros((8, LANES), F32)
        for k in range(rows):
            act = acts[k]
            apart = act - mean
            square = square + fold(jnp.square(apart))
            if layer == 3:
                z = cot[g, heights[5] + k, 0:cols, :].astype(F32) * keep3[g, heights[4] + k, 0:cols, :].astype(F32)
                first = first + fold(z)
                second = second + fold(z * apart)
            if layer == 0:
                p = pre_out[g, EXT + k, 0:cols, :]
                s = sigmoid(p)
                slope = s * (1.0 + p * (1.0 - s))
                first = first + fold(slope)
                second = second + fold(slope * act)
        acc[pl.ds(g, 1)] = mean
        acc[pl.ds(grids + g, 1)] = to_row(square) * (1.0 / number)
        if layer in (0, 3):
            acc[pl.ds(2 * grids + g, 1)] = to_row(first)
            acc[pl.ds(3 * grids + g, 1)] = to_row(second)

    loop_grids(grids, one_grid)
    means = acc[0:grids]
    middle = jnp.mean(means, axis=0, keepdims=True)
    away = means - middle
    spread = jnp.mean(acc[grids : 2 * grids] + jnp.square(away), axis=0, keepdims=True)
    out = [middle, spread]
    if layer == 3:
        ones = acc[2 * grids : 3 * grids]
        out.append(to_row(ones) * (1.0 / keep_rate))
        out.append(to_row(acc[3 * grids : 4 * grids] + away * ones) * (1.0 / keep_rate))
    if layer == 0:
        out += [to_row(acc[2 * grids : 3 * grids]), to_row(acc[3 * grids : 4 * grids])]
    for k, row in enumerate(out):
        sums_out[:, k : k + 1, :] = jnp.broadcast_to(row[None], (devices, 1, LANES))


def back_consts(layer, geo, stats, sums, gains):
    center, inv = norm_consts(stats, geo["D"])
    if layer == 3:
        one, two = top_sums(stats, center, inv)
    else:
        total = jnp.sum(sums[...], axis=0)
        one, two = total[0:1], total[1:2]
    pixels = float(geo["D"] * geo["G"] * geo["R"] * geo["C"])
    return center, inv, inv * gains[layer : layer + 1, :], one * (1.0 / pixels), two * (1.0 / pixels)


def backward_kernel(layer, geo, *refs):
    grids, rows, devices, width, cols = geo["G"], geo["R"], geo["D"], geo["CE"], geo["C"]
    heights = geo["heights"]
    refs = list(refs)
    info, gains, offsets, kernels, stats, sums, pre = (refs.pop(0) for _ in range(7))
    cot = refs.pop(0) if layer >= 2 else None
    if layer == 3:
        keep_top, field = refs.pop(0), refs.pop(0)
    else:
        z_in = refs.pop(0)
    if layer:
        keep, stats_below, pre_below = refs.pop(0), refs.pop(0), refs.pop(0)
        sums_out, low_out, z_out = refs.pop(0), refs.pop(0), refs.pop(0)
    else:
        grad_in = refs.pop(0)
    grad_out = refs.pop(0) if layer in (0, 2) else None
    result = refs.pop(0) if layer == 3 else None
    taps, weight = refs
    lo, hi = EXT - layer, EXT + rows + layer
    wide = width if layer else cols
    keep_off = EXT - heights[layer] if layer else 0
    cot_off = EXT - heights[5]
    top_off = EXT - heights[4]

    lay_weights(kernels, layer, True, weight)
    center, inv, scale, one, two = back_consts(layer, geo, stats, sums, gains)
    first_row, last_row = info[2], info[3]
    if layer:
        center_b, inv_b = norm_consts(stats_below, devices)

    def one_grid(g, carry):
        def prepare(r):
            p = pre[g, pl.ds(r, 2)]
            s = sigmoid(p)
            act = p * s
            normed = (act - center) * inv
            if layer == 3:
                kept = keep_top[g, pl.ds(r - top_off, 2)].astype(F32) * (1.0 / keep_rate)
                z = cot[g, pl.ds(r - cot_off, 2)].astype(F32) * kept
            else:
                z = z_in[g, pl.ds(r, 2)]
            value = scale * (z - one - normed * two) * (s * (1.0 + p * (1.0 - s)))
            real = [
                jnp.where((r + k >= first_row) & (r + k < last_row), 1.0, 0.0).astype(F32) for k in range(2)
            ]
            value = jnp.stack([value[0] * real[0], value[1] * real[1]])
            store_shifted(taps, r, 2, value, width)

        loop_rows(lo - 1, hi + 1, prepare)
        if layer == 3:
            def finish(k):
                p = pre[g, pl.ds(EXT + k, 2), 0:cols, :]
                normed = (p * sigmoid(p) - center) * inv
                kept = keep_top[g, pl.ds(EXT - top_off + k, 2), 0:cols, :].astype(F32) * (1.0 / keep_rate)
                y = (normed * gains[layer : layer + 1, :] + offsets[layer : layer + 1, :]) * kept
                result[g, pl.ds(k, 2)] = (field[g, pl.ds(k + 1, 2)] + y).astype(LOW)

            loop_rows(0, rows, finish)
        if layer == 0:
            for at, count in chunks(lo, hi, 4):
                for k, part in enumerate(conv_pairs(taps, weight, at, count, cols)):
                    grad_out[g, at + k - EXT] = grad_in[g, at + k - EXT] + part
            return carry
        first, second, third, fourth = carry
        for k in range(rows):
            row = taps[1, EXT + k, 0:cols, :]
            low_out[g, k] = row
            third = third + fold(row.astype(F32))
        for at, count in chunks(lo, hi, 5):
            for k, part in enumerate(conv_pairs(taps, weight, at, count, width)):
                r = at + k
                inner = EXT <= r < EXT + rows
                if layer == 2:
                    part = part + cot[g, r - cot_off].astype(F32)
                    if inner:
                        grad_out[g, r - EXT] = part[0:cols]
                z = part * (keep[g, r - keep_off].astype(F32) * (1.0 / keep_rate))
                z_out[g, r] = z
                if inner:
                    z = z[0:cols]
                    p = pre_below[g, r, 0:cols, :]
                    s = sigmoid(p)
                    first = first + fold(z)
                    second = second + fold(z * (p * s - center_b))
                    if layer == 1:
                        fourth = fourth + fold(z * (s * (1.0 + p * (1.0 - s))))
        return first, second, third, fourth

    zero = jnp.zeros((8, LANES), F32)
    found = lax.fori_loop(0, grids, one_grid, (zero,) * 4)
    if layer:
        out = [to_row(v) for v in found]
        out[1] = out[1] * inv_b
        for k in range(4 if layer == 1 else 3):
            sums_out[:, k : k + 1, :] = jnp.broadcast_to(out[k][None], (devices, 1, LANES))


def weight_kernel(layer, geo, *refs):
    grids, rows, cols, width = geo["G"], geo["R"], geo["C"], geo["CE"]
    refs = list(refs)
    info, low = refs.pop(0), refs.pop(0)
    if layer:
        dpre = refs.pop(0)
    else:
        gains, stats, sums, pre, z_in = (refs.pop(0) for _ in range(5))
        center, inv, scale, one, two = back_consts(layer, geo, stats, sums, gains)
    keep_half, send_half, taps, acc = refs
    low_off = 0 if layer else EXT - 1
    acc[...] = jnp.zeros(acc.shape, F32)

    def one_grid(g):
        def prepare(r):
            value = low[g, pl.ds(r + low_off, 2)].astype(F32)
            for s, part in enumerate(shifted(value, width)):
                taps[s, pl.ds(r, 2)] = part[:, 0:cols, :].astype(LOW)

        loop_rows(0, rows + 2, prepare)
        parts = [taps[s, r : r + rows] for r in range(3) for s in range(3)]
        spread = jnp.concatenate(parts, axis=-1).reshape(rows * cols, 9 * LANES)
        if layer:
            right = dpre[g].reshape(rows * cols, LANES)
        else:
            p = pre[g, EXT : EXT + rows, 0:cols, :]
            s = sigmoid(p)
            normed = (p * s - center) * inv
            z = z_in[g, EXT : EXT + rows, 0:cols, :]
            value = scale * (z - one - normed * two) * (s * (1.0 + p * (1.0 - s)))
            right = value.astype(LOW).reshape(rows * cols, LANES)
        acc[...] += lax.dot_general(right, spread, (((0,), (0,)), ((), ())), preferred_element_type=F32)

    loop_grids(grids, one_grid)
    half = 9 * LANES // 2

    def give(upper, out):
        for t in range(9):
            lo, hi = max(t * LANES, half * upper), min((t + 1) * LANES, half * (upper + 1))
            if lo < hi:
                block = acc[:, t * LANES : (t + 1) * LANES].T
                out[lo - half * upper : hi - half * upper] = block[lo - t * LANES : hi - t * LANES]

    both_ways(info[1], lambda odd: give(int(odd), keep_half), lambda odd: give(int(odd), send_half))


def share_kernel(count, kept, got, out):
    del count
    out[...] = (kept[...] + got[...]).astype(LOW)


def total_kernel(devices, got, out):
    total = jnp.sum(got[...].astype(F32), axis=0)
    out[...] = jnp.broadcast_to(total.astype(LOW)[None], out.shape)


def join_kernel(geo, info, mine, other, out):
    half = 9 * LANES // 2

    def place(low, high):
        for k in range(4):
            out[k, 0:half] = low[k].astype(F32)
            out[k, half:] = high[k].astype(F32)

    @pl.when(info[1] == 1)
    def _():
        place(mine, other)

    @pl.when(info[1] == 0)
    def _():
        place(other, mine)


def rows_kernel(geo, gains, *refs):
    stats, sums = refs[0:4], refs[4:7]
    bias_out, gain_out, offset_out = refs[7:]
    for layer in range(4):
        center, inv = norm_consts(stats[layer], geo["D"])
        if layer == 3:
            one, two = top_sums(stats[3], center, inv)
        else:
            total = jnp.sum(sums[layer][...], axis=0)
            one, two = total[0:1], total[1:2]
        offset_out[layer : layer + 1] = one
        gain_out[layer : layer + 1] = two
        if layer:
            bias_out[layer : layer + 1] = jnp.sum(sums[layer - 1][...], axis=0)[2:3]
        else:
            pixels = float(geo["D"] * geo["G"] * geo["R"] * geo["C"])
            slopes = jnp.sum(stats[0][...], axis=0)
            flat, lifted = slopes[2:3], (slopes[3:4] - center * slopes[2:3]) * inv
            bias_out[0:1] = inv * gains[0:1, :] * (total[3:4] - flat * one / pixels - lifted * two / pixels)


def call(kernel, operands, outs, scratch, flops=10**6, moved=10**6, scalars=1, final=False):
    space = pl.BlockSpec(memory_space=pltpu.VMEM)
    specs = [pl.BlockSpec(memory_space=pltpu.SMEM)] * scalars + [space] * (len(operands) - scalars)
    operands = list(operands[:scalars]) + [pltpu.with_memory_space_constraint(v, pltpu.VMEM) for v in operands[scalars:]]
    shapes = [jax.ShapeDtypeStruct(s, d) if final else pltpu.VMEM(s, d) for s, d in outs]
    return pl.pallas_call(
        kernel,
        in_specs=specs,
        out_specs=[space] * len(outs),
        out_shape=shapes,
        scratch_shapes=[pltpu.VMEM(s, d) for s, d in scratch],
        compiler_params=pltpu.CompilerParams(vmem_limit_bytes=(12 if final else 8) * 2**20),
        cost_estimate=pl.CostEstimate(flops=flops, bytes_accessed=moved, transcendentals=0),
    )(*operands)


def forward_call(layer, geo, operands):
    grids, rows, rows_ext, width, devices = geo["G"], geo["R"], geo["RE"], geo["CE"], geo["D"]
    kinds = 4 if layer in (0, 3) else 2
    outs = [((devices, kinds, LANES), F32)]
    for k in geo["members"][layer]:
        outs.append(((grids, rows + 2 * geo["heights"][k], width, LANES), LOW))
    outs.append(((grids, rows_ext, width, LANES), F32))
    if layer:
        outs.append(((grids, rows + 2, width, LANES), LOW))
    if layer == 2:
        outs.append(((grids, rows + 2, geo["C"], LANES), F32))
    scratch = [
        ((3, rows_ext, width, LANES), LOW),
        ((12 * LANES, 2 * LANES), LOW),
        ((rows, geo["C"], LANES), F32),
        ((kinds * grids, LANES), F32),
    ]
    return call(functools.partial(forward_kernel, layer, geo), operands, outs, scratch, 2 * 10**9, 8 * 10**6)


def backward_call(layer, geo, operands):
    grids, rows, rows_ext, width, devices, cols = geo["G"], geo["R"], geo["RE"], geo["CE"], geo["D"], geo["C"]
    outs = []
    if layer:
        outs.append(((devices, 4 if layer == 1 else 3, LANES), F32))
        outs.append(((grids, rows, cols, LANES), LOW))
        outs.append(((grids, rows_ext, width, LANES), F32))
    if layer in (0, 2):
        outs.append(((grids, rows, cols, LANES), F32))
    if layer == 3:
        outs.append(((grids, rows, cols, LANES), LOW))
    scratch = [((3, rows_ext, width, LANES), LOW), ((12 * LANES, 2 * LANES), LOW)]
    return call(functools.partial(backward_kernel, layer, geo), operands, outs, scratch, 2 * 10**9, 8 * 10**6)


def weight_call(layer, geo, operands):
    half = ((9 * LANES // 2, LANES), F32)
    scratch = [((3, geo["R"] + 2, geo["C"], LANES), LOW), ((LANES, 9 * LANES), F32)]
    return call(functools.partial(weight_kernel, layer, geo), operands, [half, half], scratch, 10**9, 3 * 10**6)


def local(inputs, kernels, biases, gains, offsets, keep_masks, cotangent):
    grids, rows, cols, _ = inputs.shape
    devices = lax.axis_size("batch") * lax.axis_size("lat") * lax.axis_size("lon")
    heights = [EXT, 7, 6, 5, 4, 4]
    starts = [0, 0]
    at = 0
    for k in range(2, 6):
        starts.append(at)
        at += rows + 2 * heights[k]
    geo = dict(
        G=grids, R=rows, C=cols, D=devices, RE=rows + 2 * EXT, CE=cols + 2 * EXT, heights=heights, starts=starts,
        members=[[0], [1], [2], [3, 4, 5]],
    )
    lat, lon = lax.axis_index("lat"), lax.axis_index("lon")
    info = jnp.stack(
        [
            1 - lax.rem(lat, 2),
            1 - lax.rem(lon, 2),
            jnp.where(lat == 0, EXT, 0),
            jnp.where(lat == lax.axis_size("lat") - 1, EXT + rows, rows + 2 * EXT),
        ]
    ).astype(jnp.int32)
    kernels = kernels.reshape(4, 9, LANES, LANES)

    def edges(count):
        return [((grids, count, cols, LANES), LOW)] * 2

    def stacked(sources, got, group):
        tall = [((grids, rows + 2 * heights[k], cols, LANES), LOW) for k in group]
        strip = ((grids, sum(rows + 2 * heights[k] for k in group), EXT, LANES), LOW)
        kernel = functools.partial(stack_kernel, geo, [heights[k] for k in group])
        outs = call(kernel, [info] + sources + list(got), tall + [strip, strip], [])
        return outs[:-2], outs[-2:]

    x_edges = call(functools.partial(field_edge_kernel, geo), [info, inputs], edges(EXT), [])
    x_got = trade(x_edges, "lat", False)
    whole = ((grids, rows, cols, LANES), LOW)
    outs = call(
        functools.partial(mask_edge_kernel, geo), [info, keep_masks, cotangent],
        [whole] * 4 + edges(heights[1]) + edges(sum(heights[2:])), [],
    )
    rest = list(outs[:4]) + [cotangent]
    first_got = trade(outs[4:6], "lat", False)
    later_got = trade(outs[6:8], "lat", False)
    (x_tall,), strips = stacked([inputs], x_got, [0])
    pieces = [(x_tall, *trade(strips, "lon", True))]
    (k_tall,), strips = stacked(rest[:1], first_got, [1])
    pieces.append((k_tall, *trade(strips, "lon", True)))
    talls, strips = stacked(rest[1:], later_got, [2, 3, 4, 5])
    later = trade(strips, "lon", True)
    pieces += [(tall, *later) for tall in talls]

    pres, lows, stats, exts = [None] * 4, [None] * 4, [None] * 4, [None] * 6
    field = None
    for layer in range(4):
        operands = [info, gains, offsets, biases, kernels]
        if layer:
            operands += [stats[layer - 1], pres[layer - 1]]
        if layer == 2:
            operands.append(exts[0])
        members = geo["members"][layer]
        outs = list(forward_call(layer, geo, operands + [v for k in members for v in pieces[k]]))
        stats[layer] = to_all(outs.pop(0))
        for k in members:
            exts[k] = outs.pop(0)
        pres[layer] = outs.pop(0)
        lows[layer] = outs.pop(0) if layer else exts[0]
        if layer == 2:
            field = outs.pop(0)
    keeps, keep_top, cot = exts[1:5], exts[4], exts[5]

    sums = [None] * 4
    sums[3] = stats[3]
    halves = [None] * 4
    z = grad = output = None
    for layer in (3, 2, 1):
        operands = [info, gains, offsets, kernels, stats[layer], sums[layer], pres[layer]]
        if layer >= 2:
            operands.append(cot)
        operands += [keep_top, field] if layer == 3 else [z]
        operands += [keeps[layer - 1], stats[layer - 1], pres[layer - 1]]
        outs = backward_call(layer, geo, operands)
        sums[layer - 1] = to_all(outs[0])
        z = outs[2]
        if layer == 2:
            grad = outs[3]
        if layer == 3:
            output = outs[3]
        halves[layer] = weight_call(layer, geo, [info, lows[layer], outs[1]])
    halves[0] = weight_call(0, geo, [info, lows[0], gains, stats[0], sums[0], pres[0], z])
    operands = [info, gains, offsets, kernels, stats[0], sums[0], pres[0], z, grad]
    (input_grad,) = backward_call(0, geo, operands)

    half = 9 * LANES // 2
    shares = []
    for kept, sent in halves:
        shares += call(functools.partial(share_kernel, 1), [kept, to_pair(sent)], [((half, LANES), LOW)], [], scalars=0)
    share = 4 * half // (devices // 2)
    slots = (devices // 2, share, LANES)
    got = to_half(jnp.stack(shares).reshape(slots), devices)
    (mine,) = call(functools.partial(total_kernel, devices), [got], [(slots, LOW)], [], scalars=0)
    mine = to_half(mine, devices).reshape(4, half, LANES)
    (kernel_grad,) = call(
        functools.partial(join_kernel, geo), [info, mine, to_pair(mine)], [((4, 9 * LANES, LANES), F32)], [], final=True
    )
    small = ((4, LANES), F32)
    bias_grad, gain_grad, offset_grad = call(
        functools.partial(rows_kernel, geo), [gains] + stats + sums[:3], [small] * 3, [], scalars=0, final=True
    )
    return (output, input_grad, kernel_grad.reshape(4, 3, 3, LANES, LANES), bias_grad, gain_grad, offset_grad)


def solution(mesh):
    in_specs = (
        P("batch", "lat", "lon", None),
        P(),
        P(),
        P(),
        P(),
        P(None, "batch", "lat", "lon", None),
        P("batch", "lat", "lon", None),
    )
    out_specs = (P("batch", "lat", "lon", None), P("batch", "lat", "lon", None), P(), P(), P(), P())
    return jax.shard_map(local, mesh=mesh, in_specs=in_specs, out_specs=out_specs, check_vma=False)
```

time: 867 us -> 259 us (0.30); the launches traced: 854 us -> 258 us
  blocking collectives: 517 us -> 79.3 us
  Pallas kernels: 0 us -> 69.4 us
  other arithmetic: 64.6 us -> 0.15 us
  waiting for transfers between devices: 89.4 us -> 32.8 us
  matrix products: 36.6 us -> 0 us
  starting transfers between devices: 70.5 us -> 36.9 us
  local copies, waits for them, and re-layouts: 60.4 us -> 38.6 us
  between operations: 16.1 us -> 1.13 us
    psum x13 -> x0, blocking collectives: 517 us -> none  [the longest x4 160 us: layer_backward(): lax.psum((jnp.sum(dnorm, axis=(0, 1, 2)), jnp.sum(dnorm * normed, axis=(0...]
    psum x1 -> x0, waiting for transfers between devices: 80.4 us -> none  [finish(): return lax.psum((kernel_term, bias_term), ('batch', 'lat', 'lon'))]
    all_to_all x0 -> x6, blocking collectives: none -> 79.3 us  [the longest x2 43.3 us: to_half(): return lax.all_to_all(rows, EVERY, 0, 0, axis_index_groups=groups)]
    pallas_call x0 -> x24, Pallas kernels: none -> 69.4 us  [call(): pl.pallas_call(kernel, in_specs=specs, out_specs=[space] * len(outs), out...]
    ppermute x32 -> x17, starting transfers between devices: 70.5 us -> 20.4 us  [the longest x6 11.3 us: trade(): lax.ppermute(pair[0], axis, first)]
    conv_general_dilated x8 -> x0, matrix products: 24.2 us -> none  [apply_kernel(): lax.conv_general_dilated(padded, kernel, (1, 1), 'VALID', dimension_numbe...]
    unnamed x144 -> x124, local copies, waits for them, and re-layouts: 21.6 us -> 38.6 us
    all_to_all x0 -> x3, starting transfers between devices: none -> 16.4 us  [to_all(): return lax.all_to_all(rows, EVERY, 0, 0)]
  transfers between devices with their start and end apart: 33 -> 20, of which waited for: 11 -> 5; matrix products, arithmetic and copies ran while one was open for 5% -> 1% of each run, Pallas kernels for 0% -> 17%
where the time goes in v1:
time: 259 us; the launch traced here: 258 us
  blocking collectives  79.3 us (31%)
  Pallas kernels  69.4 us (27%)
  local copies, waits for them, and re-layouts  38.6 us (15%)
  starting transfers between devices  36.9 us (14%)
  waiting for transfers between devices  32.8 us (13%)
    pallas_call x24, Pallas kernels, call(): pl.pallas_call(kernel, in_specs=specs, out_specs=[space] * len(outs), out...  69.4 us
    all_to_all x2, blocking collectives, to_half(): return lax.all_to_all(rows, EVERY, 0, 0, axis_index_groups=groups)  43.3 us
    unnamed x124, local copies, waits for them, and re-layouts  38.6 us
    all_to_all x4, blocking collectives, to_all(): return lax.all_to_all(rows, EVERY, 0, 0)  36 us
    ppermute x6, waiting for transfers between devices, trade(): lax.ppermute(pair[1], axis, second)  18 us
    all_to_all x3, starting transfers between devices, to_all(): return lax.all_to_all(rows, EVERY, 0, 0)  16.4 us
    ppermute x6, starting transfers between devices, trade(): lax.ppermute(pair[0], axis, first)  11.3 us
    all_to_all x3, waiting for transfers between devices, to_all(): return lax.all_to_all(rows, EVERY, 0, 0)  7.85 us
  transfers between devices with their start and end apart: 20, of which 5 were waited for; matrix products, arithmetic and copies ran while one was open for 1% of the time, Pallas kernels for 17%

profile of v1, /device:TPU:1, one launch (start us, length us, event | category | flops | bytes accessed | tf_op | source)
XLA Modules:
  0.0 258.2 jit_solution(16313662136602835163)
XLA Ops:
  0.7 2.2 copy-done.14
  2.9 1.0 copy-done.17
  4.0 0.9 shard_map.121
  4.8 2.2 collective-permute-start.8
  8.3 3.9 %collective-permute-start = (bf16[4,8,32,128]{3,2,1,0:T(8,128)(2,1)S(1)}, bf16[4,8,32,128]{3,2,1,0:T(8,128)(2,1)S(1)}, u32[]{:S(2)}, u32[]{:S(2)}) collective-permute-start(bf16[4,8,32,128]{3,2,1,0:T(8,128)(2,1)S(1)} %get-tuple-element.68), channel_id=1, source_target_pairs={{0,4},{4,0},{8,12},{12,8},{1,5},{5,1},{9,13},{13,9},{2,6},{6,2},{1... | collective-permute-start | bytes 786440 | tf_op jit(solution)/shard_map/ppermute | solution.py:34
  12.9 1.3 collective-permute-start.4
  14.2 6.6 %collective-permute-done.8.refs_4_ = bf16[4,19,32,128]{3,2,1,0:T(8,128)(2,1)S(1)} collective-permute-done((bf16[4,19,32,128]{3,2,1,0:T(8,128)(2,1)S(1)}, bf16[4,19,32,128]{3,2,1,0:T(8,128)(2,1)S(1)}, u32[]{:S(2)}, u32[]{:S(2)}) %collective-permute-start.8) | collective-permute-done | bytes 622624 | tf_op jit(solution)/shard_map/ppermute | solution.py:34
  20.8 2.2 shard_map.124
  23.1 0.9 copy-done.30
  23.9 0.9 copy-done.32
  24.8 2.1 collective-permute-start.10
  26.9 1.6 collective-permute-start.11
  29.8 1.1 collective-permute-start.3
  32.0 1.5 shard_map.122
  33.5 1.2 collective-permute-start.6
  34.7 1.4 collective-permute-start.7
  36.1 17.9 %collective-permute-done.3.refs_7_ = bf16[4,32,8,128]{3,2,1,0:T(8,128)(2,1)S(1)} collective-permute-done((bf16[4,32,8,128]{3,2,1,0:T(8,128)(2,1)S(1)}, bf16[4,32,8,128]{3,2,1,0:T(8,128)(2,1)S(1)}, u32[]{:S(2)}, u32[]{:S(2)}) %collective-permute-start.3) | collective-permute-done | bytes 262176 | tf_op jit(solution)/shard_map/ppermute | solution.py:34
  54.1 5.7 %shard_map.120 = (f32[32,4,128]{2,1,0:T(4,128)}, bf16[4,32,48,128]{3,2,1,0:T(8,128)(2,1)S(1)}, f32[4,32,48,128]{3,2,1,0:T(8,128)S(1)}) custom-call(s32[4]{0:T(128)S(1)} %pad_add_fusion.info.refs_0_, f32[4,128]{1,0:T(4,128)S(1)} %copy-done.44, f32[4,128]{1,0:T(4,128)S(1)} %copy-done.45, f32[4,128]{1,0:T(4,128)S(1)} %copy-done.46, ...), custom_call_target="tpu_custom_call" | custom-call | flops 2000000000 | bytes 8000000 | tf_op jit(solution)/shard_map/pallas_call | solution.py:546
  59.7 1.6 copy-done.1
  61.4 1.1 copy-done.11
  62.5 8.6 %all-to-all-start = ((f32[32,4,128]{2,1,0:T(4,128)}), f32[32,4,128]{2,1,0:T(4,128)S(1)}, u32[]{:S(2)}, u32[]{:S(2)}) async-start(f32[32,4,128]{2,1,0:T(4,128)} %get-tuple-element.73), calls=%async_computation | async-start | bytes 131072 | tf_op jit(solution)/shard_map/all_to_all | solution.py:38
  71.2 7.3 %all-to-all-done.refs_5_.refs_9_.refs_4_.refs_3_.refs_0_ = f32[32,4,128]{2,1,0:T(4,128)S(1)} async-done(((f32[32,4,128]{2,1,0:T(4,128)}), f32[32,4,128]{2,1,0:T(4,128)S(1)}, u32[]{:S(2)}, u32[]{:S(2)}) %all-to-all-start) | async-done | bytes 65568 | tf_op jit(solution)/shard_map/all_to_all | solution.py:38
  78.4 1.9 copy-done.2
  80.3 1.2 copy-done.48
  81.5 6.2 %shard_map.123 = (f32[32,2,128]{2,1,0:T(2,128)S(1)}, bf16[4,30,48,128]{3,2,1,0:T(8,128)(2,1)S(1)}, f32[4,32,48,128]{3,2,1,0:T(8,128)S(1)}, bf16[4,18,48,128]{3,2,1,0:T(8,128)(2,1)S(1)}) custom-call(s32[4]{0:T(128)S(1)} %pad_add_fusion.info.refs_0_, f32[4,128]{1,0:T(4,128)S(1)} %copy-done.44, f32[4,128]{1,0:T(4,128)S(1)} %copy-done.45, ...), custom_call_target="tpu_custom_call" | custom-call | flops 2000000000 | bytes 8000000 | tf_op jit(solution)/shard_map/pallas_call | solution.py:546
  87.7 1.1 copy-done.20
  88.9 8.9 %all_to_all.45.refs_5_.refs_10_.refs_4_.refs_1_ = f32[32,2,128]{2,1,0:T(2,128)S(1)} all-to-all(f32[32,2,128]{2,1,0:T(2,128)S(1)} %get-tuple-element.81), channel_id=1, replica_groups=mesh['batch'=2,'lat'=4,'lon'=4] {'batch','lat','lon'}, dimensions={0} | all-to-all | bytes 65536 | tf_op jit(solution)/shard_map/all_to_all | solution.py:38
  97.8 6.0 %shard_map.125 = (f32[32,2,128]{2,1,0:T(2,128)S(1)}, bf16[4,28,48,128]{3,2,1,0:T(8,128)(2,1)S(1)}, f32[4,32,48,128]{3,2,1,0:T(8,128)S(1)}, bf16[4,18,48,128]{3,2,1,0:T(8,128)(2,1)S(1)}, f32[4,18,32,128]{3,2,1,0:T(8,128)S(1)}) custom-call(s32[4]{0:T(128)S(1)} %pad_add_fusion.info.refs_0_, f32[4,128]{1,0:T(4,128)S(1)} %copy-done.44, f32[4,128]{1,0:T(4,128)S(1)} %copy-done.45, ...), custom_call_target="tpu_custom_call" | custom-call | flops 2000000000 | bytes 8000000 | tf_op jit(solution)/shard_map/pallas_call | solution.py:546
  103.8 8.9 %all_to_all.46.refs_5_.refs_11_.refs_4_.refs_2_ = f32[32,2,128]{2,1,0:T(2,128)S(1)} all-to-all(f32[32,2,128]{2,1,0:T(2,128)S(1)} %get-tuple-element.92), channel_id=1, replica_groups=mesh['batch'=2,'lat'=4,'lon'=4] {'batch','lat','lon'}, dimensions={0} | all-to-all | bytes 65536 | tf_op jit(solution)/shard_map/all_to_all | solution.py:38
  112.8 5.4 %shard_map.126 = (f32[32,4,128]{2,1,0:T(4,128)S(1)}, bf16[4,26,48,128]{3,2,1,0:T(8,128)(2,1)S(1)}, bf16[4,24,48,128]{3,2,1,0:T(8,128)(2,1)S(1)}, bf16[4,24,48,12...) custom-call(s32[4]{0:T(128)S(1)} %pad_add_fusion.info.refs_0_, ...), custom_call_target="tpu_custom_call" | custom-call | flops 2000000000 | bytes 8000000 | tf_op jit(solution)/shard_map/pallas_call | solution.py:546
  118.3 9.1 %all_to_all.47.refs_4_.refs_5_.refs_3_ = f32[32,4,128]{2,1,0:T(4,128)S(1)} all-to-all(f32[32,4,128]{2,1,0:T(4,128)S(1)} %get-tuple-element.97), channel_id=1, replica_groups=mesh['batch'=2,'lat'=4,'lon'=4] {'batch','lat','lon'}, dimensions={0} | all-to-all | bytes 131072 | tf_op jit(solution)/shard_map/all_to_all | solution.py:38
  127.4 6.4 %shard_map.127 = (f32[32,3,128]{2,1,0:T(4,128)S(1)}, bf16[4,16,32,128]{3,2,1,0:T(8,128)(2,1)S(1)}, f32[4,32,48,128]{3,2,1,0:T(8,128)S(1)}, bf16[4,16,32,128]{3,2,1,0:T(8,128)(2,1)S(1)}) custom-call(s32[4]{0:T(128)S(1)} %pad_add_fusion.info.refs_0_, f32[4,128]{1,0:T(4,128)S(1)} %copy-done.44, f32[4,128]{1,0:T(4,128)S(1)} %copy-done.45, ...), custom_call_target="tpu_custom_call" | custom-call | flops 2000000000 | bytes 8000000 | tf_op jit(solution)/shard_map/pallas_call | solution.py:546
  134.6 9.1 %all_to_all.48.refs_5_.refs_6_ = f32[32,3,128]{2,1,0:T(4,128)S(1)} all-to-all(f32[32,3,128]{2,1,0:T(4,128)S(1)} %get-tuple-element.104), channel_id=1, replica_groups=mesh['batch'=2,'lat'=4,'lon'=4] {'batch','lat','lon'}, dimensions={0} | all-to-all | bytes 98304 | tf_op jit(solution)/shard_map/all_to_all | solution.py:38
  143.7 5.5 %shard_map.128 = (f32[32,3,128]{2,1,0:T(4,128)}, bf16[4,16,32,128]{3,2,1,0:T(8,128)(2,1)S(1)}, f32[4,32,48,128]{3,2,1,0:T(8,128)S(1)}, f32[4,16,32,128]{3,2,1,0:T(8,128)S(1)}) custom-call(s32[4]{0:T(128)S(1)} %pad_add_fusion.info.refs_0_, f32[4,128]{1,0:T(4,128)S(1)} %copy-done.44, f32[4,128]{1,0:T(4,128)S(1)} %copy-done.45, ...), custom_call_target="tpu_custom_call" | custom-call | flops 2000000000 | bytes 8000000 | tf_op jit(solution)/shard_map/pallas_call | solution.py:546
  149.2 1.6 copy-done.15
  150.8 1.0 copy-done.22
  152.4 0.8 copy-done.53
  153.2 2.7 %all-to-all-start.5 = ((f32[32,3,128]{2,1,0:T(4,128)}), f32[32,3,128]{2,1,0:T(4,128)S(1)}, u32[]{:S(2)}, u32[]{:S(2)}) async-start(f32[32,3,128]{2,1,0:T(4,128)} %get-tuple-element.107), calls=%async_computation.5 | async-start | bytes 131072 | tf_op jit(solution)/shard_map/all_to_all | solution.py:38
  155.9 1.2 copy-done.52
  157.1 1.0 copy-done.56
  158.1 3.5 %shard_map.137 = (f32[576,128]{1,0:T(8,128)S(1)}, f32[576,128]{1,0:T(8,128)}) custom-call(s32[4]{0:T(128)S(1)} %pad_add_fusion.info.refs_0_, bf16[4,18,48,128]{3,2,1,0:T(8,128)(2,1)S(1)} %copy-done.52, bf16[4,16,32,128]{3,2,1,0:T(8,128)(2,1)S(1)} %copy-done.56), custom_call_target="tpu_custom_call" | custom-call | flops 1000000000 | bytes 3000000 | tf_op jit(solution)/shard_map/pallas_call | solution.py:546
  163.3 1.9 copy-done.3
  165.2 1.9 copy-done.7
  167.1 1.9 copy-done.16
  169.0 5.4 %shard_map.129 = (f32[32,4,128]{2,1,0:T(4,128)}, bf16[4,16,32,128]{3,2,1,0:T(8,128)(2,1)S(1)}, f32[4,32,48,128]{3,2,1,0:T(8,128)S(1)}) custom-call(s32[4]{0:T(128)S(1)} %pad_add_fusion.info.refs_0_, f32[4,128]{1,0:T(4,128)S(1)} %copy-done.44, f32[4,128]{1,0:T(4,128)S(1)} %copy-done.45, bf16[4,9,128,128]{3,2,1,0:T(8,128)(2,1)S(1)} %bitcast.18, ...), custom_call_target="tpu_custom_call" | custom-call | flops 2000000000 | bytes 8000000 | tf_op jit(solution)/shard_map/pallas_call | solution.py:546
  174.4 1.7 copy-done.8
  177.0 5.1 %all-to-all-start.6 = ((f32[32,4,128]{2,1,0:T(4,128)}), f32[32,4,128]{2,1,0:T(4,128)S(1)}, u32[]{:S(2)}, u32[]{:S(2)}) async-start(f32[32,4,128]{2,1,0:T(4,128)} %get-tuple-element.110), calls=%async_computation.6 | async-start | bytes 131072 | tf_op jit(solution)/shard_map/all_to_all | solution.py:38
  182.1 1.2 copy-done.50
  183.3 1.0 copy-done.54
  184.3 3.3 %shard_map.135 = (f32[576,128]{1,0:T(8,128)S(1)}, f32[576,128]{1,0:T(8,128)}) custom-call(s32[4]{0:T(128)S(1)} %pad_add_fusion.info.refs_0_, bf16[4,18,48,128]{3,2,1,0:T(8,128)(2,1)S(1)} %copy-done.50, bf16[4,16,32,128]{3,2,1,0:T(8,128)(2,1)S(1)} %copy-done.54), custom_call_target="tpu_custom_call" | custom-call | flops 1000000000 | bytes 3000000 | tf_op jit(solution)/shard_map/pallas_call | solution.py:546
  188.7 1.3 copy-done.60
  190.0 3.3 %shard_map.133 = (f32[576,128]{1,0:T(8,128)S(1)}, f32[576,128]{1,0:T(8,128)}) custom-call(s32[4]{0:T(128)S(1)} %pad_add_fusion.info.refs_0_, bf16[4,18,48,128]{3,2,1,0:T(8,128)(2,1)S(1)} %copy-done.60, bf16[4,16,32,128]{3,2,1,0:T(8,128)(2,1)S(1)} %copy-done.58), custom_call_target="tpu_custom_call" | custom-call | flops 1000000000 | bytes 3000000 | tf_op jit(solution)/shard_map/pallas_call | solution.py:546
  194.3 1.9 copy-done.4
  196.2 1.9 copy-done.9
  198.1 3.1 %shard_map.131 = (f32[576,128]{1,0:T(8,128)S(1)}, f32[576,128]{1,0:T(8,128)S(1)}) custom-call(s32[4]{0:T(128)S(1)} %pad_add_fusion.info.refs_0_, bf16[4,32,48,128]{3,2,1,0:T(8,128)(2,1)S(1)} %copy-done.13, f32[4,128]{1,0:T(4,128)S(1)} %copy-done.44, f32[32,4,128]{2,1,0:T(4,128)S(1)} %all-to-all-done.refs_5_.refs_9_.refs_4_.refs_3_.refs_0_, ...), custom_call_target="tpu_custom_call" | custom-call | flops 1000000000 | bytes 3000000 | tf_op jit(solution)/shard_map/pallas_call | solution.py:546
  201.6 1.0 shard_map.138
  202.6 1.1 shard_map.136
  203.7 1.0 shard_map.134
  204.9 23.3 %all_to_all.49.got = bf16[16,144,128]{2,1,0:T(8,128)(2,1)S(1)} all-to-all(bf16[16,144,128]{2,1,0:T(8,128)(2,1)S(1)} %bitcast.26), channel_id=1, replica_groups={{0,2,4,6,8,10,12,14,16,18,20,22,24,26,28,30},{1,3,5,7,9,11,13,15,17,19,..., dimensions={0} | all-to-all | bytes 1179648 | tf_op jit(solution)/shard_map/all_to_all | solution.py:43
  228.3 19.9 %all_to_all.50 = bf16[16,144,128]{2,1,0:T(8,128)(2,1)S(1)} all-to-all(bf16[16,144,128]{2,1,0:T(8,128)(2,1)S(1)} %shard_map.139), channel_id=1, replica_groups={{0,2,4,6,8,10,12,14,16,18,20,22,24,26,28,30},{1,3,5,7,9,11,13,15,17,19,..., dimensions={0} | all-to-all | bytes 1179648 | tf_op jit(solution)/shard_map/all_to_all | solution.py:43
  248.2 1.8 collective-permute-start.16
  250.9 3.5 %shard_map.130 = f32[4,16,32,128]{3,2,1,0:T(8,128)S(1)} custom-call(s32[4]{0:T(128)S(1)} %pad_add_fusion.info.refs_0_, f32[4,128]{1,0:T(4,128)S(1)} %copy-done.44, f32[4,128]{1,0:T(4,128)S(1)} %copy-done.45, bf16[4,9,128,128]{3,2,1,0:T(8,128)(2,1)S(1)} %bitcast.19, f32[32,4,128]{2,1,0:T(4,128)S(1)} %all-to-all-done.refs_5_.refs_9_.refs_4_.refs_3_.refs_0_, ...), custom_call_target="tpu_custom_call" | custom-call | flops 2000000000 | bytes 8000000 | tf_op jit(solution)/shard_map/pallas_call | solution.py:546
  254.4 1.0 copy.14
  256.1 2.1 shard_map.140
  (132 shorter events, 12.5 us)
Async XLA Ops:
  0.7 2.2 copy-start.14
  4.0 3.8 %copy-start.19 = (bf16[4,16,32,128]{3,2,1,0:T(8,128)(2,1)S(1)}, bf16[4,16,32,128]{3,2,1,0:T(8,128)(2,1)}, u32[]{:S(2)}) copy-start(bf16[4,16,32,128]{3,2,1,0:T(8,128)(2,1)} %refs_0_.1) | copy-start | bytes 1572868
  4.0 16.8 %copy-start.18 = (bf16[4,16,32,128]{3,2,1,0:T(8,128)(2,1)S(1)}, bf16[4,16,32,128]{3,2,1,0:T(8,128)(2,1)}, u32[]{:S(2)}) copy-start(bf16[4,16,32,128]{3,2,1,0:T(8,128)(2,1)} %refs_3_.7) | copy-start | bytes 1572868
  4.8 15.9 %collective-permute-start.8 = (bf16[4,19,32,128]{3,2,1,0:T(8,128)(2,1)S(1)}, bf16[4,19,32,128]{3,2,1,0:T(8,128)(2,1)S(1)}, u32[]{:S(2)}, u32[]{:S(2)}) collective-permute-start(bf16[4,19,32,128]{3,2,1,0:T(8,128)(2,1)S(1)} %get-tuple-element.87), channel_id=1, source_target_pairs={{0,4},{4,0},{8,12},{12,8},{1,5},{5,1},{9,13},{13,9},{2,6},{6,2},{1... | collective-permute-start | bytes 1867784 | tf_op jit(solution)/shard_map/ppermute | solution.py:34
  7.0 13.8 %collective-permute-start.9 = (bf16[4,19,32,128]{3,2,1,0:T(8,128)(2,1)S(1)}, bf16[4,19,32,128]{3,2,1,0:T(8,128)(2,1)S(1)}, u32[]{:S(2)}, u32[]{:S(2)}) collective-permute-start(bf16[4,19,32,128]{3,2,1,0:T(8,128)(2,1)S(1)} %get-tuple-element.88), channel_id=1, source_target_pairs={{4,8},{8,4},{5,9},{9,5},{6,10},{10,6},{7,11},{11,7},{20,24},{24,20... | collective-permute-start | bytes 1867784 | tf_op jit(solution)/shard_map/ppermute | solution.py:34
  8.3 20.2 %collective-permute-start = (bf16[4,8,32,128]{3,2,1,0:T(8,128)(2,1)S(1)}, bf16[4,8,32,128]{3,2,1,0:T(8,128)(2,1)S(1)}, u32[]{:S(2)}, u32[]{:S(2)}) collective-permute-start(bf16[4,8,32,128]{3,2,1,0:T(8,128)(2,1)S(1)} %get-tuple-element.68), channel_id=1, source_target_pairs={{0,4},{4,0},{8,12},{12,8},{1,5},{5,1},{9,13},{13,9},{2,6},{6,2},{1... | collective-permute-start | bytes 786440 | tf_op jit(solution)/shard_map/ppermute | solution.py:34
  12.2 16.3 %collective-permute-start.1 = (bf16[4,8,32,128]{3,2,1,0:T(8,128)(2,1)S(1)}, bf16[4,8,32,128]{3,2,1,0:T(8,128)(2,1)S(1)}, u32[]{:S(2)}, u32[]{:S(2)}) collective-permute-start(bf16[4,8,32,128]{3,2,1,0:T(8,128)(2,1)S(1)} %get-tuple-element.69), channel_id=1, source_target_pairs={{4,8},{8,4},{5,9},{9,5},{6,10},{10,6},{7,11},{11,7},{20,24},{24,20... | collective-permute-start | bytes 786440 | tf_op jit(solution)/shard_map/ppermute | solution.py:34
  12.9 18.5 %collective-permute-start.4 = (bf16[4,7,32,128]{3,2,1,0:T(8,128)(2,1)S(1)}, bf16[4,7,32,128]{3,2,1,0:T(8,128)(2,1)S(1)}, u32[]{:S(2)}, u32[]{:S(2)}) collective-permute-start(bf16[4,7,32,128]{3,2,1,0:T(8,128)(2,1)S(1)} %get-tuple-element.76), channel_id=1, source_target_pairs={{0,4},{4,0},{8,12},{12,8},{1,5},{5,1},{9,13},{13,9},{2,6},{6,2},{1... | collective-permute-start | bytes 688136 | tf_op jit(solution)/shard_map/ppermute | solution.py:34
  20.8 33.2 %copy-start = (bf16[4,3,3,128,128]{4,3,2,1,0:T(8,128)(2,1)S(1)}, bf16[4,3,3,128,128]{4,3,2,1,0:T(8,128)(2,1)}, u32[]{:S(2)}) copy-start(bf16[4,3,3,128,128]{4,3,2,1,0:T(8,128)(2,1)} %param.8) | copy-start | bytes 3538948
  20.8 33.2 %copy-start.44 = (f32[4,128]{1,0:T(4,128)S(1)}, f32[4,128]{1,0:T(4,128)}, u32[]{:S(2)}) copy-start(f32[4,128]{1,0:T(4,128)} %gains.1) | copy-start | bytes 6148
  20.8 33.2 %copy-start.45 = (f32[4,128]{1,0:T(4,128)S(1)}, f32[4,128]{1,0:T(4,128)}, u32[]{:S(2)}) copy-start(f32[4,128]{1,0:T(4,128)} %refs_2_.16) | copy-start | bytes 6148
  20.8 33.2 %copy-start.46 = (f32[4,128]{1,0:T(4,128)S(1)}, f32[4,128]{1,0:T(4,128)}, u32[]{:S(2)}) copy-start(f32[4,128]{1,0:T(4,128)} %refs_3_.9) | copy-start | bytes 6148
  24.8 29.2 %copy-start.24 = (bf16[4,28,32,128]{3,2,1,0:T(8,128)(2,1)}, bf16[4,28,32,128]{3,2,1,0:T(8,128)(2,1)S(1)}, u32[]{:S(2)}) copy-start(bf16[4,28,32,128]{3,2,1,0:T(8,128)(2,1)S(1)} %get-tuple-element.89.refs_8_) | copy-start | bytes 2752516
  24.8 29.2 %copy-start.26 = (bf16[4,26,32,128]{3,2,1,0:T(8,128)(2,1)}, bf16[4,26,32,128]{3,2,1,0:T(8,128)(2,1)S(1)}, u32[]{:S(2)}) copy-start(bf16[4,26,32,128]{3,2,1,0:T(8,128)(2,1)S(1)} %get-tuple-element.94.refs_7_) | copy-start | bytes 2555908
  24.8 73.0 %collective-permute-start.10 = (bf16[4,102,8,128]{3,2,1,0:T(8,128)(2,1)}, bf16[4,102,8,128]{3,2,1,0:T(8,128)(2,1)S(1)}, u32[]{:S(2)}, u32[]{:S(2)}) collective-permute-start(bf16[4,102,8,128]{3,2,1,0:T(8,128)(2,1)} %get-tuple-element.90), channel_id=1, source_target_pairs={{0,1},{1,0},{2,3},{3,2},{4,5},{5,4},{6,7},{7,6},{8,9},{9,8},{10,11... | collective-permute-start | bytes 2506760 | tf_op jit(solution)/shard_map/ppermute | solution.py:34
  26.9 70.9 %collective-permute-start.11 = (bf16[4,102,8,128]{3,2,1,0:T(8,128)(2,1)}, bf16[4,102,8,128]{3,2,1,0:T(8,128)(2,1)S(1)}, u32[]{:S(2)}, u32[]{:S(2)}) collective-permute-start(bf16[4,102,8,128]{3,2,1,0:T(8,128)(2,1)} %get-tuple-element.91), channel_id=1, source_target_pairs={{0,3},{1,2},{2,1},{3,0},{4,7},{5,6},{6,5},{7,4},{8,11},{9,10},{10,... | collective-permute-start | bytes 2506760 | tf_op jit(solution)/shard_map/ppermute | solution.py:34
  29.2 5.5 %collective-permute-start.2 = (bf16[4,32,8,128]{3,2,1,0:T(8,128)(2,1)S(1)}, bf16[4,32,8,128]{3,2,1,0:T(8,128)(2,1)S(1)}, u32[]{:S(2)}, u32[]{:S(2)}) collective-permute-start(bf16[4,32,8,128]{3,2,1,0:T(8,128)(2,1)S(1)} %get-tuple-element.71), channel_id=1, source_target_pairs={{0,1},{1,0},{2,3},{3,2},{4,5},{5,4},{6,7},{7,6},{8,9},{9,8},{10,11... | collective-permute-start | bytes 786440 | tf_op jit(solution)/shard_map/ppermute | solution.py:34
  29.8 24.2 %collective-permute-start.3 = (bf16[4,32,8,128]{3,2,1,0:T(8,128)(2,1)S(1)}, bf16[4,32,8,128]{3,2,1,0:T(8,128)(2,1)S(1)}, u32[]{:S(2)}, u32[]{:S(2)}) collective-permute-start(bf16[4,32,8,128]{3,2,1,0:T(8,128)(2,1)S(1)} %get-tuple-element.72), channel_id=1, source_target_pairs={{0,3},{1,2},{2,1},{3,0},{4,7},{5,6},{6,5},{7,4},{8,11},{9,10},{10,... | collective-permute-start | bytes 786440 | tf_op jit(solution)/shard_map/ppermute | solution.py:34
  31.3 0.7 collective-permute-start.5
  33.5 26.3 %copy-start.47 = (bf16[4,30,32,128]{3,2,1,0:T(8,128)(2,1)}, bf16[4,30,32,128]{3,2,1,0:T(8,128)(2,1)S(1)}, u32[]{:S(2)}) copy-start(bf16[4,30,32,128]{3,2,1,0:T(8,128)(2,1)S(1)} %get-tuple-element.78.refs_7_) | copy-start | bytes 2949124
  33.5 37.7 %collective-permute-start.6 = (bf16[4,30,8,128]{3,2,1,0:T(8,128)(2,1)}, bf16[4,30,8,128]{3,2,1,0:T(8,128)(2,1)S(1)}, u32[]{:S(2)}, u32[]{:S(2)}) collective-permute-start(bf16[4,30,8,128]{3,2,1,0:T(8,128)(2,1)} %get-tuple-element.79), channel_id=1, source_target_pairs={{0,1},{1,0},{2,3},{3,2},{4,5},{5,4},{6,7},{7,6},{8,9},{9,8},{10,11... | collective-permute-start | bytes 737288 | tf_op jit(solution)/shard_map/ppermute | solution.py:34
  34.7 36.4 %collective-permute-start.7 = (bf16[4,30,8,128]{3,2,1,0:T(8,128)(2,1)}, bf16[4,30,8,128]{3,2,1,0:T(8,128)(2,1)}, u32[]{:S(2)}, u32[]{:S(2)}) collective-permute-start(bf16[4,30,8,128]{3,2,1,0:T(8,128)(2,1)} %get-tuple-element.80), channel_id=1, source_target_pairs={{0,3},{1,2},{2,1},{3,0},{4,7},{5,6},{6,5},{7,4},{8,11},{9,10},{10,... | collective-permute-start | bytes 737288 | tf_op jit(solution)/shard_map/ppermute | solution.py:34
  59.7 1.6 copy-start.1
  62.5 15.9 %all-to-all-start = ((f32[32,4,128]{2,1,0:T(4,128)}), f32[32,4,128]{2,1,0:T(4,128)S(1)}, u32[]{:S(2)}, u32[]{:S(2)}) async-start(f32[32,4,128]{2,1,0:T(4,128)} %get-tuple-element.73), calls=%async_computation | async-start | bytes 131072 | tf_op jit(solution)/shard_map/all_to_all | solution.py:38
  78.4 1.9 copy-start.2
  80.3 1.2 copy-start.48
  81.5 16.3 %copy-start.12 = (bf16[4,32,48,128]{3,2,1,0:T(8,128)(2,1)S(1)}, bf16[4,32,48,128]{3,2,1,0:T(8,128)(2,1)}, u32[]{:S(2)}) copy-start(bf16[4,32,48,128]{3,2,1,0:T(8,128)(2,1)} %copy-done.11) | copy-start | bytes 4718596
  81.5 16.3 %copy-start.25 = (bf16[4,28,32,128]{3,2,1,0:T(8,128)(2,1)S(1)}, bf16[4,28,32,128]{3,2,1,0:T(8,128)(2,1)}, u32[]{:S(2)}) copy-start(bf16[4,28,32,128]{3,2,1,0:T(8,128)(2,1)} %copy-done.24) | copy-start | bytes 2752516
  88.9 14.9 %copy-start.59 = (bf16[4,18,48,128]{3,2,1,0:T(8,128)(2,1)}, bf16[4,18,48,128]{3,2,1,0:T(8,128)(2,1)S(1)}, u32[]{:S(2)}) copy-start(bf16[4,18,48,128]{3,2,1,0:T(8,128)(2,1)S(1)} %get-tuple-element.115.refs_1_) | copy-start | bytes 2654212
  88.9 54.8 %copy-start.6 = (f32[4,32,48,128]{3,2,1,0:T(8,128)}, f32[4,32,48,128]{3,2,1,0:T(8,128)S(1)}, u32[]{:S(2)}) copy-start(f32[4,32,48,128]{3,2,1,0:T(8,128)S(1)} %get-tuple-element.82.refs_6_.refs_11_) | copy-start | bytes 9437188
  97.8 15.0 %copy-start.27 = (bf16[4,26,32,128]{3,2,1,0:T(8,128)(2,1)S(1)}, bf16[4,26,32,128]{3,2,1,0:T(8,128)(2,1)}, u32[]{:S(2)}) copy-start(bf16[4,26,32,128]{3,2,1,0:T(8,128)(2,1)} %copy-done.26) | copy-start | bytes 2555908
  97.8 15.0 %copy-start.31 = (bf16[4,24,32,128]{3,2,1,0:T(8,128)(2,1)S(1)}, bf16[4,24,32,128]{3,2,1,0:T(8,128)(2,1)}, u32[]{:S(2)}) copy-start(bf16[4,24,32,128]{3,2,1,0:T(8,128)(2,1)} %copy-done.30) | copy-start | bytes 2359300
  97.8 14.9 %copy-start.33 = (bf16[4,24,32,128]{3,2,1,0:T(8,128)(2,1)S(1)}, bf16[4,24,32,128]{3,2,1,0:T(8,128)(2,1)}, u32[]{:S(2)}) copy-start(bf16[4,24,32,128]{3,2,1,0:T(8,128)(2,1)} %copy-done.32) | copy-start | bytes 2359300
  103.8 14.4 %copy-start.49 = (bf16[4,18,48,128]{3,2,1,0:T(8,128)(2,1)}, bf16[4,18,48,128]{3,2,1,0:T(8,128)(2,1)S(1)}, u32[]{:S(2)}) copy-start(bf16[4,18,48,128]{3,2,1,0:T(8,128)(2,1)S(1)} %get-tuple-element.119.refs_1_) | copy-start | bytes 2654212
  112.8 30.9 %copy-start.28 = (f32[32,2,128]{2,1,0:T(2,128)}, f32[32,2,128]{2,1,0:T(2,128)S(1)}, u32[]{:S(2)}) copy-start(f32[32,2,128]{2,1,0:T(2,128)S(1)} %all_to_all.46.refs_5_.refs_11_.refs_4_.refs_2_) | copy-start | bytes 98308
  118.2 15.5 %copy-start.51 = (bf16[4,18,48,128]{3,2,1,0:T(8,128)(2,1)}, bf16[4,18,48,128]{3,2,1,0:T(8,128)(2,1)S(1)}, u32[]{:S(2)}) copy-start(bf16[4,18,48,128]{3,2,1,0:T(8,128)(2,1)S(1)} %get-tuple-element.123.refs_1_) | copy-start | bytes 2654212
  149.2 1.6 copy-start.15
  153.2 10.1 %copy-start.21 = (bf16[4,30,48,128]{3,2,1,0:T(8,128)(2,1)S(1)}, bf16[4,30,48,128]{3,2,1,0:T(8,128)(2,1)}, u32[]{:S(2)}) copy-start(bf16[4,30,48,128]{3,2,1,0:T(8,128)(2,1)} %copy-done.20) | copy-start | bytes 4423684
  153.2 10.1 %all-to-all-start.5 = ((f32[32,3,128]{2,1,0:T(4,128)}), f32[32,3,128]{2,1,0:T(4,128)S(1)}, u32[]{:S(2)}, u32[]{:S(2)}) async-start(f32[32,3,128]{2,1,0:T(4,128)} %get-tuple-element.107), calls=%async_computation.5 | async-start | bytes 131072 | tf_op jit(solution)/shard_map/all_to_all | solution.py:38
  162.3 39.2 %collective-permute-start.15 = (f32[576,128]{1,0:T(8,128)}, f32[576,128]{1,0:T(8,128)}, u32[]{:S(2)}, u32[]{:S(2)}) collective-permute-start(f32[576,128]{1,0:T(8,128)} %get-tuple-element.126), channel_id=1, source_target_pairs={{0,1},{1,0},{2,3},{3,2},{4,5},{5,4},{6,7},{7,6},{8,9},{9,8},{10,11... | collective-permute-start | bytes 884744 | tf_op jit(solution)/shard_map/ppermute | solution.py:47
  163.3 11.1 %copy-start.36 = (f32[32,3,128]{2,1,0:T(4,128)}, f32[32,3,128]{2,1,0:T(4,128)S(1)}, u32[]{:S(2)}) copy-start(f32[32,3,128]{2,1,0:T(4,128)S(1)} %all-to-all-done.5.refs_5_) | copy-start | bytes 147460
  163.3 1.9 copy-start.3
  165.2 1.9 copy-start.7
  167.1 1.9 copy-start.16
  174.4 1.7 copy-start.8
  177.0 17.3 %all-to-all-start.6 = ((f32[32,4,128]{2,1,0:T(4,128)}), f32[32,4,128]{2,1,0:T(4,128)S(1)}, u32[]{:S(2)}, u32[]{:S(2)}) async-start(f32[32,4,128]{2,1,0:T(4,128)} %get-tuple-element.110), calls=%async_computation.6 | async-start | bytes 131072 | tf_op jit(solution)/shard_map/all_to_all | solution.py:38
  184.3 4.4 %copy-start.58 = (bf16[4,16,32,128]{3,2,1,0:T(8,128)(2,1)S(1)}, bf16[4,16,32,128]{3,2,1,0:T(8,128)(2,1)}, u32[]{:S(2)}) copy-start(bf16[4,16,32,128]{3,2,1,0:T(8,128)(2,1)} %copy-done.57) | copy-start | bytes 1572868
  188.4 5.9 %copy-start.13 = (bf16[4,32,48,128]{3,2,1,0:T(8,128)(2,1)S(1)}, bf16[4,32,48,128]{3,2,1,0:T(8,128)(2,1)}, u32[]{:S(2)}) copy-start(bf16[4,32,48,128]{3,2,1,0:T(8,128)(2,1)} %copy-done.11) | copy-start | bytes 4718596
  188.4 14.2 %collective-permute-start.14 = (f32[576,128]{1,0:T(8,128)}, f32[576,128]{1,0:T(8,128)}, u32[]{:S(2)}, u32[]{:S(2)}) collective-permute-start(f32[576,128]{1,0:T(8,128)} %get-tuple-element.122), channel_id=1, source_target_pairs={{0,1},{1,0},{2,3},{3,2},{4,5},{5,4},{6,7},{7,6},{8,9},{9,8},{10,11... | collective-permute-start | bytes 884744 | tf_op jit(solution)/shard_map/ppermute | solution.py:47
  188.7 1.3 copy-start.60
  194.1 9.6 %collective-permute-start.13 = (f32[576,128]{1,0:T(8,128)}, f32[576,128]{1,0:T(8,128)}, u32[]{:S(2)}, u32[]{:S(2)}) collective-permute-start(f32[576,128]{1,0:T(8,128)} %get-tuple-element.118), channel_id=1, source_target_pairs={{0,1},{1,0},{2,3},{3,2},{4,5},{5,4},{6,7},{7,6},{8,9},{9,8},{10,11... | collective-permute-start | bytes 884744 | tf_op jit(solution)/shard_map/ppermute | solution.py:47
  194.3 1.9 copy-start.4
  196.2 1.9 copy-start.9
  198.1 3.5 %copy-start.39 = (f32[576,128]{1,0:T(8,128)S(1)}, f32[576,128]{1,0:T(8,128)}, u32[]{:S(2)}) copy-start(f32[576,128]{1,0:T(8,128)} %copy-done.38) | copy-start | bytes 884740
  198.1 4.5 %copy-start.41 = (f32[576,128]{1,0:T(8,128)S(1)}, f32[576,128]{1,0:T(8,128)}, u32[]{:S(2)}) copy-start(f32[576,128]{1,0:T(8,128)} %copy-done.40) | copy-start | bytes 884740
  198.1 5.6 %copy-start.43 = (f32[576,128]{1,0:T(8,128)S(1)}, f32[576,128]{1,0:T(8,128)}, u32[]{:S(2)}) copy-start(f32[576,128]{1,0:T(8,128)} %copy-done.42) | copy-start | bytes 884740
  201.2 3.5 %collective-permute-start.12 = (f32[576,128]{1,0:T(8,128)S(1)}, f32[576,128]{1,0:T(8,128)S(1)}, u32[]{:S(2)}, u32[]{:S(2)}) collective-permute-start(f32[576,128]{1,0:T(8,128)S(1)} %get-tuple-element.114), channel_id=1, source_target_pairs={{0,1},{1,0},{2,3},{3,2},{4,5},{5,4},{6,7},{7,6},{8,9},{9,8},{10,11... | collective-permute-start | bytes 884744 | tf_op jit(solution)/shard_map/ppermute | solution.py:47
  202.6 48.3 %copy-start.23 = (f32[4,16,32,128]{3,2,1,0:T(8,128)S(1)}, f32[4,16,32,128]{3,2,1,0:T(8,128)}, u32[]{:S(2)}) copy-start(f32[4,16,32,128]{3,2,1,0:T(8,128)} %copy-done.22) | copy-start | bytes 3145732
  204.7 46.1 %copy-start.10 = (f32[4,32,48,128]{3,2,1,0:T(8,128)S(1)}, f32[4,32,48,128]{3,2,1,0:T(8,128)}, u32[]{:S(2)}) copy-start(f32[4,32,48,128]{3,2,1,0:T(8,128)} %copy-done.8) | copy-start | bytes 9437188
  204.8 46.0 %copy-start.5 = (f32[4,32,48,128]{3,2,1,0:T(8,128)S(1)}, f32[4,32,48,128]{3,2,1,0:T(8,128)}, u32[]{:S(2)}) copy-start(f32[4,32,48,128]{3,2,1,0:T(8,128)} %copy-done.1) | copy-start | bytes 9437188
  248.2 7.9 %collective-permute-start.16 = (bf16[4,576,128]{2,1,0:T(8,128)(2,1)S(1)}, bf16[4,576,128]{2,1,0:T(8,128)(2,1)S(1)}, u32[]{:S(2)}, u32[]{:S(2)}) collective-permute-start(bf16[4,576,128]{2,1,0:T(8,128)(2,1)S(1)} %bitcast.20), channel_id=1, source_target_pairs={{0,1},{1,0},{2,3},{3,2},{4,5},{5,4},{6,7},{7,6},{8,9},{9,8},{10,11... | collective-permute-start | bytes 1769480 | tf_op jit(solution)/shard_map/ppermute | solution.py:47
  250.8 4.5 %copy-start.29 = (f32[32,2,128]{2,1,0:T(2,128)S(1)}, f32[32,2,128]{2,1,0:T(2,128)}, u32[]{:S(2)}) copy-start(f32[32,2,128]{2,1,0:T(2,128)} %copy-done.28) | copy-start | bytes 98308
  250.8 4.5 %copy-start.35 = (f32[32,3,128]{2,1,0:T(4,128)S(1)}, f32[32,3,128]{2,1,0:T(4,128)}, u32[]{:S(2)}) copy-start(f32[32,3,128]{2,1,0:T(4,128)} %copy-done.34) | copy-start | bytes 147460
  250.9 4.5 %copy-start.37 = (f32[32,3,128]{2,1,0:T(4,128)S(1)}, f32[32,3,128]{2,1,0:T(4,128)}, u32[]{:S(2)}) copy-start(f32[32,3,128]{2,1,0:T(4,128)} %copy-done.36) | copy-start | bytes 147460
  (17 other events, 15.7 us)

commit v2 on v1

v2 whole, which is shorter than its diff:
```python
import functools

import jax
import jax.numpy as jnp
from jax import lax
from jax.experimental import pallas as pl
from jax.experimental.pallas import tpu as pltpu
from jax.sharding import PartitionSpec as P

eps = 1e-05
keep_rate = 0.9
EVERY = ("batch", "lat", "lon")
EXT = 8
LANES = 128
F32 = jnp.float32
LOW = jnp.bfloat16


def partners(axis, periodic):
    count = lax.axis_size(axis)
    first = [(i, i ^ 1) for i in range(count)]
    second = []
    for i in range(count):
        j = i + 1 if i % 2 else i - 1
        if periodic:
            second.append((i, j % count))
        elif 0 <= j < count:
            second.append((i, j))
    return first, second


def trade(pair, axis, periodic):
    first, second = partners(axis, periodic)
    return lax.ppermute(pair[0], axis, first), lax.ppermute(pair[1], axis, second)


def to_all(rows):
    return lax.all_to_all(rows, EVERY, 0, 0)


def to_half(rows, devices):
    groups = [[i for i in range(devices) if i % 2 == side] for side in range(2)]
    return lax.all_to_all(rows, EVERY, 0, 0, axis_index_groups=groups)


def to_pair(block):
    return lax.ppermute(block, "lon", partners("lon", True)[0])


def sigmoid(v):
    return 0.5 * jnp.tanh(0.5 * v) + 0.5


def norm_consts(stats_ref, devices):
    stats = stats_ref[...]
    total = jnp.sum(stats, axis=0)
    center = total[0:1] * (1.0 / devices)
    apart = jnp.sum(jnp.square(stats - center[None]), axis=0)
    spread = (total[1:2] + apart[0:1]) * (1.0 / devices)
    return center, lax.rsqrt(spread + eps)


def top_sums(stats_ref, center, inv):
    stats = stats_ref[...]
    total = jnp.sum(stats, axis=0)
    apart = stats[:, 0:1, :] - center[None]
    return total[2:3], (total[3:4] + jnp.sum(apart * stats[:, 2:3, :], axis=0)) * inv


def shifted(value, width):
    return pltpu.roll(value, 1, 1), value, pltpu.roll(value, width - 1, 1)


def store_shifted(taps, slot, row, value, width):
    for s, part in enumerate(shifted(value, width)):
        taps[slot, s, pl.ds(row, 2)] = part.astype(LOW)


def lay_weights(kernel_ref, layer, back, out):
    blank = jnp.zeros((3 * LANES, LANES), LOW)
    out[9 * LANES : 12 * LANES, 0:LANES] = blank
    out[0 : 3 * LANES, LANES : 2 * LANES] = blank
    for r in range(3):
        for s in range(3):
            if back:
                block = kernel_ref[layer, (2 - r) * 3 + 2 - s].astype(F32).T.astype(LOW)
            else:
                block = kernel_ref[layer, r * 3 + s]
            at = (r * 3 + s) * LANES
            out[at : at + LANES, 0:LANES] = block
            out[at + 3 * LANES : at + 4 * LANES, LANES : 2 * LANES] = block


def conv_pairs(taps, slot, weight_ref, row, pairs, cols):
    parts = []
    for t in range(4):
        for s in range(3):
            parts.append(jnp.stack([taps[slot, s, row - 1 + t + 2 * k, 0:cols, :] for k in range(pairs)]))
    left = jnp.concatenate(parts, axis=-1).reshape(pairs * cols, 12 * LANES)
    both = jnp.dot(left, weight_ref[...], preferred_element_type=F32)
    out = []
    for k in range(pairs):
        for h in range(2):
            out.append(both[k * cols : (k + 1) * cols, h * LANES : (h + 1) * LANES])
    return out


def chunks(lo, hi, pairs):
    at = lo
    while at < hi:
        count = min(pairs, (hi - at) // 2)
        yield at, count
        at += 2 * count


def pipeline(grids, lo, hi, pairs, prepare, convolve, after):
    def step(i, carry):
        prepare(0, lo - 1 + 2 * i, 0)
        return carry

    count = (hi - lo) // 2 + 1
    lax.fori_loop(0, count, step, 0, unroll=4)
    parts = list(chunks(lo, hi, pairs))
    for g in range(grids):
        for j, (at, size) in enumerate(parts):
            if g + 1 < grids:
                for i in range(count * j // len(parts), count * (j + 1) // len(parts)):
                    prepare(g + 1, lo - 1 + 2 * i, (g + 1) % 2)
            convolve(g, at, size, g % 2)
        after(g, g % 2)


def guard(condition, act):
    if isinstance(condition, bool):
        if condition:
            act()
    else:
        pl.when(condition)(act)


def fold(value):
    return jnp.sum(value.reshape(-1, 8, LANES), axis=0)


def to_row(value):
    return jnp.sum(value, axis=0, keepdims=True)


def both_ways(even, give_first, give_second):
    @pl.when(even == 1)
    def _():
        give_first(False)
        give_second(True)

    @pl.when(even == 0)
    def _():
        give_first(True)
        give_second(False)


def whichever(even, place, got_first, got_second):
    @pl.when(even == 1)
    def _():
        place(got_second, got_first)

    @pl.when(even == 0)
    def _():
        place(got_first, got_second)


def cut_rows(geo, info, sources, heights, first, second):
    grids, rows = geo["G"], geo["R"]

    def give(out):
        def act(low):
            at = 0
            for src, h in zip(sources, heights):
                for g in range(grids):
                    out[g, at : at + h] = src[g, 0:h] if low else src[g, src.shape[1] - h :]
                at += h
        return act

    both_ways(info[0], give(first), give(second))


def cut_cols(geo, info, sources, first, second):
    grids, cols = geo["G"], geo["C"]

    def give(out):
        def act(low):
            at = 0
            for src in sources:
                for g in range(grids):
                    part = src[g, :, 0:EXT, :] if low else src[g, :, cols - EXT : cols, :]
                    out[g, at : at + src.shape[1]] = part
                at += src.shape[1]
        return act

    both_ways(info[1], give(first), give(second))


def add_rows(geo, info, sources, heights, got_first, got_second, outs):
    grids, rows = geo["G"], geo["R"]

    def place(low, high):
        at = 0
        for out, h in zip(outs, heights):
            for g in range(grids):
                out[g, 0:h] = low[g, at : at + h]
                out[g, h + rows : 2 * h + rows] = high[g, at : at + h]
            at += h

    whichever(info[0], place, got_first, got_second)
    for src, out, h in zip(sources, outs, heights):
        for g in range(grids):
            out[g, h : h + rows] = src[g]


def add_cols(geo, info, sources, starts, got_first, got_second, outs):
    cols = geo["C"]

    def place(low, high):
        for src, out, at in zip(sources, outs, starts):
            total = src.shape[1]
            for g in range(geo["G"]):
                right = high[g, at : at + total].astype(F32)
                left = low[g, at : at + total].astype(F32)
                out[g, :, cols:, :] = jnp.concatenate([right, left], axis=1).astype(LOW)

    whichever(info[1], place, got_first, got_second)
    for src, out in zip(sources, outs):
        for g in range(geo["G"]):
            out[g, :, 0:cols, :] = src[g]


def field_edge_kernel(geo, info, x, first, second, sem):
    rows = geo["R"]

    def fetch(high_out, low_out):
        copies = [
            pltpu.make_async_copy(x.at[:, rows - EXT : rows], high_out, sem.at[0]),
            pltpu.make_async_copy(x.at[:, 0:EXT], low_out, sem.at[1]),
        ]
        for c in copies:
            c.start()
        for c in copies:
            c.wait()

    @pl.when(info[0] == 1)
    def _():
        fetch(first, second)

    @pl.when(info[0] == 0)
    def _():
        fetch(second, first)


def mask_edge_kernel(geo, info, masks, cot, *outs):
    grids = geo["G"]
    lows, masked = outs[0:4], outs[4]
    for g in range(grids):
        for k in range(4):
            lows[k][g] = masks[k, g].astype(F32).astype(LOW)
        masked[g] = (cot[g].astype(F32) * masks[3, g].astype(F32)).astype(LOW)
    cut_cols(geo, info, lows[0:2], outs[5], outs[6])
    cut_rows(geo, info, [lows[2], masked, cot], geo["heights"][3:], outs[7], outs[8])


def middle_kernel(geo, info, x, x_first, x_second, mask0, mask1, m_first, m_second, *outs):
    x_tall, x_out, wides, m_out = outs[0], outs[1:3], outs[3:5], outs[5:7]
    add_rows(geo, info, [x], [EXT], x_first, x_second, [x_tall])
    cut_cols(geo, info, [x_tall], *x_out)
    add_cols(geo, info, [mask0, mask1], [0, geo["R"]], m_first, m_second, wides)
    cut_rows(geo, info, wides, geo["heights"][1:3], *m_out)


def late_kernel(geo, info, mask2, masked, cot, first, second, before, *outs):
    del before
    add_rows(geo, info, [mask2, masked, cot], geo["heights"][3:], first, second, outs[0:3])
    cut_cols(geo, info, outs[0:3], *outs[3:5])


def gate_kernel(sums, *refs):
    refs[-1][...] = sums[...]


def forward_kernel(layer, geo, *refs):
    grids, rows, devices, width, cols = geo["G"], geo["R"], geo["D"], geo["CE"], geo["C"]
    heights = geo["heights"]
    refs = list(refs)
    info, gains, offsets, biases, kernels = (refs.pop(0) for _ in range(5))
    if layer:
        stats, pre_in = refs.pop(0), refs.pop(0)
    field = refs.pop(0) if layer == 2 else None
    members = geo["members"][layer]
    sources = [refs.pop(0) for _ in members]
    got = [refs.pop(0), refs.pop(0)]
    sums_out = refs.pop(0)
    exts = [refs.pop(0) for _ in members]
    pre_out, low_out = refs.pop(0), refs.pop(0)
    field_out = refs.pop(0) if layer == 2 else None
    taps, weight, acts, acc = refs
    lo, hi = layer + 1, geo["RE"] - 1 - layer

    lay_weights(kernels, layer, False, weight)
    if layer in (0, 3):
        add_cols(geo, info, sources, geo["starts"][layer], *got, exts)
    else:
        skip = 0 if layer == 1 else heights[1]
        place = [r.at[:, skip : skip + heights[layer]] for r in got]
        add_rows(geo, info, sources, [heights[layer]], *place, exts)
    ext = exts[0]
    if layer:
        center, inv = norm_consts(stats, devices)
        scale = inv * gains[layer - 1 : layer, :]
        shift = offsets[layer - 1 : layer, :]
    bias = biases[layer : layer + 1, :]
    number = rows * cols
    totals = [jnp.zeros((8, LANES), F32)] * grids

    def prepare(g, r, slot):
        if layer == 0:
            value = ext[g, pl.ds(r, 2)].astype(F32)
        else:
            p = pre_in[g, pl.ds(r, 2)]
            act = p * sigmoid(p)
            kept = ext[g, pl.ds(r - layer, 2)].astype(F32) * (1.0 / keep_rate)
            value = ((act - center) * scale + shift) * kept
            if layer == 2:
                value = value + field[g, pl.ds(r, 2)].astype(F32)

                def save():
                    field_out[g, pl.ds(r - (EXT - 1), 2)] = value[:, 0:cols, :]

                guard((r >= EXT - 1) & (r < EXT + rows), save)
        store_shifted(taps, slot, r, value, width)

    def convolve(g, at, count, slot):
        for k, part in enumerate(conv_pairs(taps, slot, weight, at, count, width)):
            part = part + bias
            pre_out[g, at + k] = part
            if EXT <= at + k < EXT + rows:
                inner = part[0:cols]
                act = inner * sigmoid(inner)
                acts[slot, at + k - EXT] = act
                totals[g] = totals[g] + fold(act)

    def after(g, slot):
        for s in range(3):
            low_out[s, g] = taps[slot, s, EXT - 1 : EXT + 1 + rows, 0:cols, :]
        mean = to_row(totals[g]) * (1.0 / number)
        square = jnp.zeros((8, LANES), F32)
        first = jnp.zeros((8, LANES), F32)
        second = jnp.zeros((8, LANES), F32)
        for k in range(rows):
            act = acts[slot, k]
            apart = act - mean
            square = square + fold(jnp.square(apart))
            if layer == 3:
                z = exts[1][g, heights[4] + k, 0:cols, :].astype(F32)
                first = first + fold(z)
                second = second + fold(z * apart)
            if layer == 0:
                p = pre_out[g, EXT + k, 0:cols, :]
                s = sigmoid(p)
                slope = s * (1.0 + p * (1.0 - s))
                first = first + fold(slope)
                second = second + fold(slope * act)
        acc[g : g + 1] = mean
        acc[grids + g : grids + g + 1] = to_row(square) * (1.0 / number)
        if layer in (0, 3):
            acc[2 * grids + g : 2 * grids + g + 1] = to_row(first)
            acc[3 * grids + g : 3 * grids + g + 1] = to_row(second)

    pipeline(grids, lo, hi, 5, prepare, convolve, after)
    means = acc[0:grids]
    middle = jnp.mean(means, axis=0, keepdims=True)
    away = means - middle
    spread = jnp.mean(acc[grids : 2 * grids] + jnp.square(away), axis=0, keepdims=True)
    out = [middle, spread]
    if layer == 3:
        ones = acc[2 * grids : 3 * grids]
        out.append(to_row(ones) * (1.0 / keep_rate))
        out.append(to_row(acc[3 * grids : 4 * grids] + away * ones) * (1.0 / keep_rate))
    if layer == 0:
        out += [to_row(acc[2 * grids : 3 * grids]), to_row(acc[3 * grids : 4 * grids])]
    for k, row in enumerate(out):
        sums_out[:, k : k + 1, :] = jnp.broadcast_to(row[None], (devices, 1, LANES))


def back_consts(layer, geo, stats, sums, gains):
    center, inv = norm_consts(stats, geo["D"])
    if layer == 3:
        one, two = top_sums(stats, center, inv)
    else:
        total = jnp.sum(sums[...], axis=0)
        one, two = total[0:1], total[1:2]
    pixels = float(geo["D"] * geo["G"] * geo["R"] * geo["C"])
    return center, inv, inv * gains[layer : layer + 1, :], one * (1.0 / pixels), two * (1.0 / pixels)


def weight_term(geo, low, g, right, acc):
    rows, cols = geo["R"], geo["C"]
    parts = [low[s, g, r : r + rows] for r in range(3) for s in range(3)]
    spread = jnp.concatenate(parts, axis=-1).reshape(rows * cols, 9 * LANES)
    term = lax.dot_general(right, spread, (((0,), (0,)), ((), ())), preferred_element_type=F32)
    if g == 0:
        acc[...] = term
    else:
        acc[...] += term


def split_halves(info, acc, keep_half, send_half):
    half = 9 * LANES // 2

    def give(out):
        def act(upper):
            start = half if upper else 0
            for t in range(9):
                lo, hi = max(t * LANES, start), min((t + 1) * LANES, start + half)
                if lo < hi:
                    block = acc[:, t * LANES : (t + 1) * LANES].T
                    out[lo - start : hi - start] = block[lo - t * LANES : hi - t * LANES]
        return act

    both_ways(info[1], give(keep_half), give(send_half))


def backward_kernel(layer, geo, *refs):
    grids, rows, devices, width, cols = geo["G"], geo["R"], geo["D"], geo["CE"], geo["C"]
    heights = geo["heights"]
    refs = list(refs)
    info, gains, offsets, kernels, stats, sums, pre, low = (refs.pop(0) for _ in range(8))
    masked = keep_top = field = cot = z_in = None
    if layer == 3:
        masked, keep_top, field = refs.pop(0), refs.pop(0), refs.pop(0)
    else:
        z_in = refs.pop(0)
    if layer == 2:
        cot = refs.pop(0)
    keep, stats_below, pre_below = refs.pop(0), refs.pop(0), refs.pop(0)
    sums_out, keep_half, send_half, z_out = (refs.pop(0) for _ in range(4))
    grad_out = refs.pop(0) if layer == 2 else None
    result = refs.pop(0) if layer == 3 else None
    taps, weight, acc = refs
    lo, hi = EXT - layer, EXT + rows + layer
    keep_off = EXT - heights[layer]

    lay_weights(kernels, layer, True, weight)
    center, inv, scale, one, two = back_consts(layer, geo, stats, sums, gains)
    first_row, last_row = info[2], info[3]
    center_b, inv_b = norm_consts(stats_below, devices)
    sums_here = [jnp.zeros((8, LANES), F32)] * 4

    def prepare(g, r, slot):
        p = pre[g, pl.ds(r, 2)]
        s = sigmoid(p)
        normed = (p * s - center) * inv
        if layer == 3:
            z = masked[g, pl.ds(r - (EXT - heights[4]), 2)].astype(F32) * (1.0 / keep_rate)
        else:
            z = z_in[g, pl.ds(r, 2)]
        value = scale * (z - one - normed * two) * (s * (1.0 + p * (1.0 - s)))
        real = [jnp.where((r + k >= first_row) & (r + k < last_row), 1.0, 0.0).astype(F32) for k in range(2)]
        value = jnp.stack([value[0] * real[0], value[1] * real[1]])
        store_shifted(taps, slot, r, value, width)
        if layer == 3:
            def save():
                kept = keep_top[g, pl.ds(r - EXT, 2)].astype(F32) * (1.0 / keep_rate)
                y = (normed[:, 0:cols] * gains[layer : layer + 1, :] + offsets[layer : layer + 1, :]) * kept
                result[g, pl.ds(r - EXT, 2)] = (field[g, pl.ds(r - EXT + 1, 2)] + y).astype(LOW)

            guard((r >= EXT) & (r < EXT + rows), save)

    def convolve(g, at, count, slot):
        for k, part in enumerate(conv_pairs(taps, slot, weight, at, count, width)):
            r = at + k
            inner = EXT <= r < EXT + rows
            if layer == 2:
                part = part + cot[g, r - (EXT - heights[5])].astype(F32)
                if inner:
                    grad_out[g, r - EXT] = part[0:cols]
            z = part * (keep[g, r - keep_off].astype(F32) * (1.0 / keep_rate))
            z_out[g, r] = z
            if inner:
                z = z[0:cols]
                p = pre_below[g, r, 0:cols, :]
                s = sigmoid(p)
                sums_here[0] = sums_here[0] + fold(z)
                sums_here[1] = sums_here[1] + fold(z * (p * s - center_b))
                if layer == 1:
                    sums_here[3] = sums_here[3] + fold(z * (s * (1.0 + p * (1.0 - s))))

    def after(g, slot):
        right = taps[slot, 1, EXT : EXT + rows, 0:cols, :].reshape(rows * cols, LANES)
        sums_here[2] = sums_here[2] + fold(right.astype(F32))
        weight_term(geo, low, g, right, acc)

    pipeline(grids, lo, hi, 5, prepare, convolve, after)
    split_halves(info, acc, keep_half, send_half)
    out = [to_row(v) for v in sums_here]
    out[1] = out[1] * inv_b
    for k in range(4 if layer == 1 else 3):
        sums_out[:, k : k + 1, :] = jnp.broadcast_to(out[k][None], (devices, 1, LANES))


def first_weight_kernel(geo, *refs):
    grids, rows, width, cols = geo["G"], geo["R"], geo["CE"], geo["C"]
    info, gains, stats, sums, pre, low, z_in, sent, keep_half, send_both, dpre, acc = refs
    half = 9 * LANES // 2
    send_both[0:half] = sent[...]
    center, inv, scale, one, two = back_consts(0, geo, stats, sums, gains)
    first_row, last_row = info[2], info[3]

    for g in range(grids):
        for k in range(rows + 2):
            r = EXT - 1 + k
            p = pre[g, r]
            s = sigmoid(p)
            normed = (p * s - center) * inv
            value = scale * (z_in[g, r] - one - normed * two) * (s * (1.0 + p * (1.0 - s)))
            if k in (0, rows + 1):
                value = value * jnp.where((r >= first_row) & (r < last_row), 1.0, 0.0).astype(F32)
            dpre[g, k] = value.astype(LOW)
        weight_term(geo, low, g, dpre[g, 1 : rows + 1, 0:cols, :].reshape(rows * cols, LANES), acc)
    split_halves(info, acc, keep_half, send_both.at[half : 2 * half])


def input_grad_kernel(geo, kernels, dpre, grad, out, taps, weight):
    grids, rows, width, cols = geo["G"], geo["R"], geo["CE"], geo["C"]
    lay_weights(kernels, 0, True, weight)

    def prepare(g, r, slot):
        store_shifted(taps, slot, r, dpre[g, pl.ds(r, 2)].astype(F32), width)

    def convolve(g, at, count, slot):
        for k, part in enumerate(conv_pairs(taps, slot, weight, at, count, cols)):
            out[g, at + k - 1] = grad[g, at + k - 1] + part

    pipeline(grids, 1, rows + 1, 8, prepare, convolve, lambda g, slot: None)


def share_kernel(*refs):
    third, second, both, out = refs[4:]
    half = 9 * LANES // 2
    gots = [both[half : 2 * half], both[0:half], second[...], third[...]]
    for k in range(4):
        out[k * half : (k + 1) * half] = (refs[k][...] + gots[k]).astype(LOW)


def total_kernel(devices, got, out):
    total = jnp.sum(got[...].astype(F32), axis=0)
    out[...] = jnp.broadcast_to(total.astype(LOW)[None], out.shape)


def join_kernel(geo, info, mine, other, out):
    half = 9 * LANES // 2

    def place(low, high):
        for k in range(4):
            out[k, 0:half] = low[k].astype(F32)
            out[k, half:] = high[k].astype(F32)

    @pl.when(info[1] == 1)
    def _():
        place(mine, other)

    @pl.when(info[1] == 0)
    def _():
        place(other, mine)


def rows_kernel(geo, gains, *refs):
    stats, sums = refs[0:4], refs[4:7]
    bias_out, gain_out, offset_out = refs[7:]
    for layer in range(4):
        center, inv = norm_consts(stats[layer], geo["D"])
        if layer == 3:
            one, two = top_sums(stats[3], center, inv)
        else:
            total = jnp.sum(sums[layer][...], axis=0)
            one, two = total[0:1], total[1:2]
        offset_out[layer : layer + 1] = one
        gain_out[layer : layer + 1] = two
        if layer:
            bias_out[layer : layer + 1] = jnp.sum(sums[layer - 1][...], axis=0)[2:3]
        else:
            pixels = float(geo["D"] * geo["G"] * geo["R"] * geo["C"])
            slopes = jnp.sum(stats[0][...], axis=0)
            flat, lifted = slopes[2:3], (slopes[3:4] - center * slopes[2:3]) * inv
            bias_out[0:1] = inv * gains[0:1, :] * (total[3:4] - flat * one / pixels - lifted * two / pixels)


def call(kernel, operands, outs, scratch=(), flops=10**6, moved=10**6, scalars=1, final=(), outside=False):
    space = pl.BlockSpec(memory_space=pltpu.VMEM)
    specs = [pl.BlockSpec(memory_space=pltpu.SMEM)] * scalars
    operands = list(operands)
    for k in range(scalars, len(operands)):
        if outside:
            specs.append(pl.BlockSpec(memory_space=pltpu.HBM))
        else:
            specs.append(space)
            operands[k] = pltpu.with_memory_space_constraint(operands[k], pltpu.VMEM)
    shapes = [jax.ShapeDtypeStruct(s, d) if k in final else pltpu.VMEM(s, d) for k, (s, d) in enumerate(outs)]
    return pl.pallas_call(
        kernel,
        in_specs=specs,
        out_specs=[space] * len(outs),
        out_shape=shapes,
        scratch_shapes=[v if hasattr(v, "shape") and not isinstance(v, tuple) else pltpu.VMEM(*v) for v in scratch],
        compiler_params=pltpu.CompilerParams(vmem_limit_bytes=12 * 2**20),
        cost_estimate=pl.CostEstimate(flops=flops, bytes_accessed=moved, transcendentals=0),
    )(*operands)


def conv_scratch(geo, tall):
    return [((2, 3, tall, geo["CE"], LANES), LOW), ((12 * LANES, 2 * LANES), LOW)]


def forward_call(layer, geo, operands):
    grids, rows, rows_ext, width, devices, cols = geo["G"], geo["R"], geo["RE"], geo["CE"], geo["D"], geo["C"]
    kinds = 4 if layer in (0, 3) else 2
    outs = [((devices, kinds, LANES), F32)]
    for k in geo["members"][layer]:
        outs.append(((grids, rows + 2 * geo["heights"][k], width, LANES), LOW))
    outs.append(((grids, rows_ext, width, LANES), F32))
    outs.append(((3, grids, rows + 2, cols, LANES), LOW))
    if layer == 2:
        outs.append(((grids, rows + 2, cols, LANES), F32))
    scratch = conv_scratch(geo, rows_ext) + [((2, rows, cols, LANES), F32), ((kinds * grids, LANES), F32)]
    return call(functools.partial(forward_kernel, layer, geo), operands, outs, scratch, 2 * 10**9, 8 * 10**6)


def backward_call(layer, geo, operands):
    grids, rows, rows_ext, width, devices, cols = geo["G"], geo["R"], geo["RE"], geo["CE"], geo["D"], geo["C"]
    half = ((9 * LANES // 2, LANES), F32)
    outs = [((devices, 4 if layer == 1 else 3, LANES), F32), half, half, ((grids, rows_ext, width, LANES), F32)]
    if layer == 2:
        outs.append(((grids, rows, cols, LANES), F32))
    if layer == 3:
        outs.append(((grids, rows, cols, LANES), LOW))
    scratch = conv_scratch(geo, rows_ext) + [((LANES, 9 * LANES), F32)]
    return call(
        functools.partial(backward_kernel, layer, geo), operands, outs, scratch, 3 * 10**9, 8 * 10**6,
        final=(4,) if layer == 3 else (),
    )


def local(inputs, kernels, biases, gains, offsets, keep_masks, cotangent):
    grids, rows, cols, _ = inputs.shape
    devices = lax.axis_size("batch") * lax.axis_size("lat") * lax.axis_size("lon")
    heights = [EXT, 7, 6, 5, 4, 2]
    starts = [0]
    for k in (3, 4):
        starts.append(starts[-1] + rows + 2 * heights[k])
    geo = dict(
        G=grids, R=rows, C=cols, D=devices, RE=rows + 2 * EXT, CE=cols + 2 * EXT, heights=heights,
        starts={0: [0], 3: starts}, members=[[0], [1], [2], [3, 4, 5]],
    )
    lat, lon = lax.axis_index("lat"), lax.axis_index("lon")
    info = jnp.stack(
        [
            1 - lax.rem(lat, 2),
            1 - lax.rem(lon, 2),
            jnp.where(lat == 0, EXT, 0),
            jnp.where(lat == lax.axis_size("lat") - 1, EXT + rows, rows + 2 * EXT),
        ]
    ).astype(jnp.int32)
    kernels = kernels.reshape(4, 9, LANES, LANES)

    def block(tall, wide):
        return ((grids, tall, wide, LANES), LOW)

    x_edges = call(
        functools.partial(field_edge_kernel, geo), [info, inputs], [block(EXT, cols)] * 2,
        [pltpu.SemaphoreType.DMA((2,))], outside=True,
    )
    x_got = trade(x_edges, "lat", False)
    late = sum(heights[3:])
    outs = call(
        functools.partial(mask_edge_kernel, geo), [info, keep_masks, cotangent],
        [block(rows, cols)] * 5 + [block(2 * rows, EXT)] * 2 + [block(late, cols)] * 2,
    )
    low_masks, masked = outs[0:4], outs[4]
    soon_got = trade(outs[5:7], "lon", True)
    late_got = trade(outs[7:9], "lat", False)
    outs = call(
        functools.partial(middle_kernel, geo),
        [info, inputs, *x_got, low_masks[0], low_masks[1], *soon_got],
        [block(rows + 2 * EXT, cols)] + [block(rows + 2 * EXT, EXT)] * 2
        + [block(rows, cols + 2 * EXT)] * 2 + [block(heights[1] + heights[2], cols + 2 * EXT)] * 2,
    )
    pieces = [[outs[0], *trade(outs[1:3], "lon", True)]]
    halos = list(trade(outs[5:7], "lat", False))
    pieces += [[outs[3], *halos], [outs[4], *halos]]
    talls = [rows + 2 * h for h in heights[3:]]
    outs = call(
        functools.partial(late_kernel, geo), [info, low_masks[2], masked, cotangent, *late_got, outs[1]],
        [block(t, cols) for t in talls] + [block(sum(talls), EXT)] * 2,
    )
    pieces.append([*outs[0:3], *trade(outs[3:5], "lon", True)])
    halos += pieces[3][3:]

    pres, lows, stats, exts = [None] * 4, [None] * 4, [None] * 4, [None] * 6
    field = None
    for layer in range(4):
        operands = [info, gains, offsets, biases, kernels]
        if layer:
            operands += [stats[layer - 1], pres[layer - 1]]
        if layer == 2:
            operands.append(exts[0])
        outs = list(forward_call(layer, geo, operands + pieces[layer]))
        part = outs.pop(0)
        if layer == 0:
            (part,) = call(gate_kernel, [part] + halos, [(part.shape, F32)], scalars=0)
        stats[layer] = to_all(part)
        for k in geo["members"][layer]:
            exts[k] = outs.pop(0)
        pres[layer], lows[layer] = outs.pop(0), outs.pop(0)
        if layer == 2:
            field = outs.pop(0)

    sums = [None] * 4
    sums[3] = stats[3]
    kept, got = [None] * 4, []
    z = grad = output = None
    for layer in (3, 2, 1):
        operands = [info, gains, offsets, kernels, stats[layer], sums[layer], pres[layer], lows[layer]]
        operands += [exts[4], low_masks[3], field] if layer == 3 else [z]
        if layer == 2:
            operands.append(exts[5])
        operands += [exts[layer], stats[layer - 1], pres[layer - 1]]
        outs = backward_call(layer, geo, operands)
        sums[layer - 1] = to_all(outs[0])
        kept[layer], sent = outs[1], outs[2]
        if layer > 1:
            got.append(to_pair(sent))
        z = outs[3]
        if layer == 2:
            grad = outs[4]
        if layer == 3:
            output = outs[4]
    half = 9 * LANES // 2
    term = ((half, LANES), F32)
    kept[0], sent, dpre = call(
        functools.partial(first_weight_kernel, geo), [info, gains, stats[0], sums[0], pres[0], lows[0], z, sent],
        [term, ((2 * half, LANES), F32), block(rows + 2, cols + 2 * EXT)], [((LANES, 9 * LANES), F32)], 10**9, 8 * 10**6,
    )
    got.append(to_pair(sent))

    (shares,) = call(share_kernel, kept + got, [((4 * half, LANES), LOW)], scalars=0)
    slots = (devices // 2, 4 * half // (devices // 2), LANES)
    arrived = to_half(shares.reshape(slots), devices)
    (mine,) = call(functools.partial(total_kernel, devices), [arrived], [(slots, LOW)], scalars=0)
    mine = to_half(mine, devices).reshape(4, half, LANES)
    (kernel_grad,) = call(
        functools.partial(join_kernel, geo), [info, mine, to_pair(mine)], [((4, 9 * LANES, LANES), F32)], final=(0,)
    )
    (input_grad,) = call(
        functools.partial(input_grad_kernel, geo), [kernels, dpre, grad], [((grids, rows, cols, LANES), F32)],
        conv_scratch(geo, rows + 2), 10**9, 3 * 10**6, scalars=0, final=(0,),
    )
    small = ((4, LANES), F32)
    bias_grad, gain_grad, offset_grad = call(
        functools.partial(rows_kernel, geo), [gains] + stats + sums[:3], [small] * 3, scalars=0, final=(0, 1, 2)
    )
    return (output, input_grad, kernel_grad.reshape(4, 3, 3, LANES, LANES), bias_grad, gain_grad, offset_grad)


def solution(mesh):
    in_specs = (
        P("batch", "lat", "lon", None),
        P(),
        P(),
        P(),
        P(),
        P(None, "batch", "lat", "lon", None),
        P("batch", "lat", "lon", None),
    )
    out_specs = (P("batch", "lat", "lon", None), P("batch", "lat", "lon", None), P(), P(), P(), P())
    return jax.shard_map(local, mesh=mesh, in_specs=in_specs, out_specs=out_specs, check_vma=False)
```

time: 259 us -> 190 us (0.73)
  local copies, waits for them, and re-layouts: 38.6 us -> 4.3 us
  blocking collectives: 79.3 us -> 105 us
  Pallas kernels: 69.4 us -> 45.8 us
  waiting for transfers between devices: 32.8 us -> 14.2 us
  starting transfers between devices: 36.9 us -> 20 us
    unnamed x124 -> x18, local copies, waits for them, and re-layouts: 38.6 us -> 4.3 us
    all_to_all x4 -> x7, blocking collectives: 36 us -> 65.4 us  [to_all(): return lax.all_to_all(rows, EVERY, 0, 0)]
    pallas_call x24 -> x18, Pallas kernels: 69.4 us -> 45.8 us  [call(): pl.pallas_call(kernel, in_specs=specs, out_specs=[space] * len(outs), out...]
    all_to_all x3 -> x0, starting transfers between devices: 16.4 us -> none  [to_all(): return lax.all_to_all(rows, EVERY, 0, 0)]
    ppermute x6, waiting for transfers between devices: 18 us -> 5.71 us  [trade(): lax.ppermute(pair[1], axis, second)]
    all_to_all x3 -> x0, waiting for transfers between devices: 7.85 us -> none  [to_all(): return lax.all_to_all(rows, EVERY, 0, 0)]
    all_to_all x2, blocking collectives: 43.3 us -> 39.2 us  [to_half(): return lax.all_to_all(rows, EVERY, 0, 0, axis_index_groups=groups)]
  transfers between devices with their start and end apart: 20 -> 16, of which waited for: 5 -> 7; matrix products, arithmetic and copies ran while one was open for 1% -> 0% of each run, Pallas kernels for 17% -> 5%
where the time goes in v2:
time: 190 us
  blocking collectives  105 us (55%)
  Pallas kernels  45.8 us (24%)
  starting transfers between devices  20 us (11%)
  waiting for transfers between devices  14.2 us (7%)
  local copies, waits for them, and re-layouts  4.3 us (2%)
    all_to_all x7, blocking collectives, to_all(): return lax.all_to_all(rows, EVERY, 0, 0)  65.4 us
    pallas_call x18, Pallas kernels, call(): pl.pallas_call(kernel, in_specs=specs, out_specs=[space] * len(outs), out...  45.8 us
    all_to_all x2, blocking collectives, to_half(): return lax.all_to_all(rows, EVERY, 0, 0, axis_index_groups=groups)  39.2 us
    ppermute x6, starting transfers between devices, trade(): lax.ppermute(pair[0], axis, first)  12.7 us
    ppermute x6, waiting for transfers between devices, trade(): lax.ppermute(pair[0], axis, first)  6.54 us
    ppermute x6, waiting for transfers between devices, trade(): lax.ppermute(pair[1], axis, second)  5.71 us
    ppermute x6, starting transfers between devices, trade(): lax.ppermute(pair[1], axis, second)  4.44 us
    unnamed x18, local copies, waits for them, and re-layouts  4.3 us
  transfers between devices with their start and end apart: 16, of which 7 were waited for; matrix products, arithmetic and copies ran while one was open for 0% of the time, Pallas kernels for 5%

profile of v2, /device:TPU:1, one launch (start us, length us, event | category | flops | bytes accessed | tf_op | source)
XLA Modules:
  0.0 189.8 jit_solution(14983536047983520758)
XLA Ops:
  0.6 0.1 pad_add_fusion.info.refs_0_
  0.7 1.0 copy-done.4
  1.8 0.6 shard_map.118
  2.4 2.2 %collective-permute-start = (bf16[4,8,32,128]{3,2,1,0:T(8,128)(2,1)S(1)}, bf16[4,8,32,128]{3,2,1,0:T(8,128)(2,1)S(1)}, u32[]{:S(2)}, u32[]{:S(2)}) collective-permute-start(bf16[4,8,32,128]{3,2,1,0:T(8,128)(2,1)S(1)} %get-tuple-element.68), channel_id=1, source_target_pairs={{0,4},{4,0},{8,12},{12,8},{1,5},{5,1},{9,13},{13,9},{2,6},{6,2},{1... | collective-permute-start | bytes 786440 | tf_op jit(solution)/shard_map/ppermute | solution.py:34
  4.6 0.7 collective-permute-start.1
  5.3 0.0 copy-start.1
  5.3 2.2 %copy-done.1 = s32[4,4,16,32,128]{4,3,2,1,0:T(8,128)S(1)} copy-done((s32[4,4,16,32,128]{4,3,2,1,0:T(8,128)S(1)}, s32[4,4,16,32,128]{4,3,2,1,0:T(8,128)}, u32[]{:S(2)}) %copy-start.1) | copy-done | bytes 4194328
  7.4 1.0 copy-done.2
  8.5 1.0 shard_map.119
  9.5 0.0 copy-start.3
  9.5 1.0 collective-permute-start.2
  10.5 1.2 collective-permute-start.3
  11.7 4.1 %collective-permute-start.8 = (bf16[4,11,32,128]{3,2,1,0:T(8,128)(2,1)S(1)}, bf16[4,11,32,128]{3,2,1,0:T(8,128)(2,1)S(1)}, u32[]{:S(2)}, u32[]{:S(2)}) collective-permute-start(bf16[4,11,32,128]{3,2,1,0:T(8,128)(2,1)S(1)} %get-tuple-element.82), channel_id=1, source_target_pairs={{0,4},{4,0},{8,12},{12,8},{1,5},{5,1},{9,13},{13,9},{2,6},{6,2},{1... | collective-permute-start | bytes 1081352 | tf_op jit(solution)/shard_map/ppermute | solution.py:34
  15.9 0.0 collective-permute-done.x_first
  15.9 0.7 collective-permute-start.9
  16.5 0.0 collective-permute-done.2.m_first
  16.6 2.3 %collective-permute-done.3.m_second = bf16[4,32,8,128]{3,2,1,0:T(8,128)(2,1)S(1)} collective-permute-done((bf16[4,32,8,128]{3,2,1,0:T(8,128)(2,1)S(1)}, bf16[4,32,8,128]{3,2,1,0:T(8,128)(2,1)S(1)}, u32[]{:S(2)}, u32[]{:S(2)}) %collective-permute-start.3) | collective-permute-done | bytes 262176 | tf_op jit(solution)/shard_map/ppermute | solution.py:34
  18.8 1.0 shard_map.120
  19.8 0.0 copy-start
  19.8 0.0 copy-start.6
  19.8 0.0 copy-start.7
  19.8 0.0 copy-start.8
  19.9 1.0 collective-permute-start.5
  20.9 4.1 %collective-permute-start.6 = (bf16[4,13,48,128]{3,2,1,0:T(8,128)(2,1)S(1)}, bf16[4,13,48,128]{3,2,1,0:T(8,128)(2,1)S(1)}, u32[]{:S(2)}, u32[]{:S(2)}) collective-permute-start(bf16[4,13,48,128]{3,2,1,0:T(8,128)(2,1)S(1)} %get-tuple-element.78), channel_id=1, source_target_pairs={{0,4},{4,0},{8,12},{12,8},{1,5},{5,1},{9,13},{13,9},{2,6},{6,2},{1... | collective-permute-start | bytes 1916936 | tf_op jit(solution)/shard_map/ppermute | solution.py:34
  25.0 0.7 collective-permute-start.7
  25.7 0.0 collective-permute-done.8.first
  25.7 0.0 collective-permute-done.9.second
  25.7 0.9 shard_map.122
  26.6 1.0 collective-permute-start.10
  27.6 0.2 collective-permute-start.11
  27.8 0.2 collective-permute-done.5.refs_7_
  28.0 0.3 collective-permute-start.4
  28.3 1.3 collective-permute-done.4.refs_6_
  29.6 4.2 %shard_map.121 = (f32[32,4,128]{2,1,0:T(4,128)S(1)}, bf16[4,32,48,128]{3,2,1,0:T(8,128)(2,1)S(1)}, f32[4,32,48,128]{3,2,1,0:T(8,128)S(1)}, bf16[3,4,18,32,128]{4,3,2,1,0:T(8,128)(2,1)S(1)}) custom-call(s32[4]{0:T(128)S(1)} %pad_add_fusion.info.refs_0_, f32[4,128]{1,0:T(4,128)S(1)} %copy-done.6, f32[4,128]{1,0:T(4,128)S(1)} %copy-done.7, ...), custom_call_target="tpu_custom_call" | custom-call | flops 2000000000 | bytes 8000000 | tf_op jit(solution)/shard_map/pallas_call | solution.py:605
  33.9 5.2 %collective-permute-done.6.refs_0_.refs_8_.refs_9_ = bf16[4,13,48,128]{3,2,1,0:T(8,128)(2,1)S(1)} collective-permute-done((bf16[4,13,48,128]{3,2,1,0:T(8,128)(2,1)S(1)}, bf16[4,13,48,128]{3,2,1,0:T(8,128)(2,1)S(1)}, u32[]{:S(2)}, u32[]{:S(2)}) %collective-permute-start.6) | collective-permute-done | bytes 639008 | tf_op jit(solution)/shard_map/ppermute | solution.py:34
  39.1 0.0 collective-permute-done.7.refs_1_.refs_9_.refs_10_
  39.1 3.2 %collective-permute-done.11.refs_3_.refs_11_ = bf16[4,70,8,128]{3,2,1,0:T(8,128)(2,1)S(1)} collective-permute-done((bf16[4,70,8,128]{3,2,1,0:T(8,128)(2,1)S(1)}, bf16[4,70,8,128]{3,2,1,0:T(8,128)(2,1)S(1)}, u32[]{:S(2)}, u32[]{:S(2)}) %collective-permute-start.11) | collective-permute-done | bytes 573472 | tf_op jit(solution)/shard_map/ppermute | solution.py:34
  42.3 11.2 %all_to_all.45.refs_5_.refs_10_.refs_2_.refs_0_ = f32[32,4,128]{2,1,0:T(4,128)S(1)} all-to-all(f32[32,4,128]{2,1,0:T(4,128)S(1)} %shard_map.123), channel_id=1, replica_groups=mesh['batch'=2,'lat'=4,'lon'=4] {'batch','lat','lon'}, dimensions={0} | all-to-all | bytes 131072 | tf_op jit(solution)/shard_map/all_to_all | solution.py:38
  53.5 4.7 %shard_map.124 = (f32[32,2,128]{2,1,0:T(2,128)S(1)}, bf16[4,30,48,128]{3,2,1,0:T(8,128)(2,1)S(1)}, f32[4,32,48,128]{3,2,1,0:T(8,128)S(1)}, bf16[3,4,18,32,128]{4,3,2,1,0:T(8,128)(2,1)S(1)}) custom-call(s32[4]{0:T(128)S(1)} %pad_add_fusion.info.refs_0_, f32[4,128]{1,0:T(4,128)S(1)} %copy-done.6, f32[4,128]{1,0:T(4,128)S(1)} %copy-done.7, ...), custom_call_target="tpu_custom_call" | custom-call | flops 2000000000 | bytes 8000000 | tf_op jit(solution)/shard_map/pallas_call | solution.py:605
  58.2 8.9 %all_to_all.46.refs_5_.refs_11_.refs_4_.refs_1_ = f32[32,2,128]{2,1,0:T(2,128)S(1)} all-to-all(f32[32,2,128]{2,1,0:T(2,128)S(1)} %get-tuple-element.88), channel_id=1, replica_groups=mesh['batch'=2,'lat'=4,'lon'=4] {'batch','lat','lon'}, dimensions={0} | all-to-all | bytes 65536 | tf_op jit(solution)/shard_map/all_to_all | solution.py:38
  67.2 4.8 %shard_map.125 = (f32[32,2,128]{2,1,0:T(2,128)S(1)}, bf16[4,28,48,128]{3,2,1,0:T(8,128)(2,1)S(1)}, f32[4,32,48,128]{3,2,1,0:T(8,128)S(1)}, bf16[3,4,18,32,128]{4...) custom-call(s32[4]{0:T(128)S(1)} %pad_add_fusion.info.refs_0_, f32[4,128]{1,0:T(4,128)S(1)} %copy-done.6, ...), custom_call_target="tpu_custom_call" | custom-call | flops 2000000000 | bytes 8000000 | tf_op jit(solution)/shard_map/pallas_call | solution.py:605
  72.0 8.9 %all_to_all.47.refs_5_.refs_12_.refs_4_.refs_2_ = f32[32,2,128]{2,1,0:T(2,128)S(1)} all-to-all(f32[32,2,128]{2,1,0:T(2,128)S(1)} %get-tuple-element.92), channel_id=1, replica_groups=mesh['batch'=2,'lat'=4,'lon'=4] {'batch','lat','lon'}, dimensions={0} | all-to-all | bytes 65536 | tf_op jit(solution)/shard_map/all_to_all | solution.py:38
  80.9 4.6 %shard_map.126 = (f32[32,4,128]{2,1,0:T(4,128)S(1)}, bf16[4,26,48,128]{3,2,1,0:T(8,128)(2,1)S(1)}, bf16[4,24,48,128]{3,2,1,0:T(8,128)(2,1)S(1)}, bf16[4,20,48,12...) custom-call(s32[4]{0:T(128)S(1)} %pad_add_fusion.info.refs_0_, ...), custom_call_target="tpu_custom_call" | custom-call | flops 2000000000 | bytes 8000000 | tf_op jit(solution)/shard_map/pallas_call | solution.py:605
  85.5 9.1 %all_to_all.48.refs_4_.refs_5_.refs_3_ = f32[32,4,128]{2,1,0:T(4,128)S(1)} all-to-all(f32[32,4,128]{2,1,0:T(4,128)S(1)} %get-tuple-element.97), channel_id=1, replica_groups=mesh['batch'=2,'lat'=4,'lon'=4] {'batch','lat','lon'}, dimensions={0} | all-to-all | bytes 131072 | tf_op jit(solution)/shard_map/all_to_all | solution.py:38
  94.6 6.5 %shard_map.127 = (f32[32,3,128]{2,1,0:T(4,128)S(1)}, f32[576,128]{1,0:T(8,128)S(1)}, f32[576,128]{1,0:T(8,128)S(1)}, f32[4,32,48,128]{3,2,1,0:T(8,128)S(1)}, bf16[4,16,32,128]{3,2,1,0:T(8,128)(2,1)}) custom-call(s32[4]{0:T(128)S(1)} %pad_add_fusion.info.refs_0_, f32[4,128]{1,0:T(4,128)S(1)} %copy-done.6, f32[4,128]{1,0:T(4,128)S(1)} %copy-done.7, ...), custom_call_target="tpu_custom_call" | custom-call | flops 3000000000 | bytes 8000000 | tf_op jit(solution)/shard_map/pallas_call | solution.py:605
  101.1 9.0 %all_to_all.49.refs_5_.refs_6_ = f32[32,3,128]{2,1,0:T(4,128)S(1)} all-to-all(f32[32,3,128]{2,1,0:T(4,128)S(1)} %get-tuple-element.105), channel_id=1, replica_groups=mesh['batch'=2,'lat'=4,'lon'=4] {'batch','lat','lon'}, dimensions={0} | all-to-all | bytes 98304 | tf_op jit(solution)/shard_map/all_to_all | solution.py:38
  110.1 4.9 %shard_map.128 = (f32[32,3,128]{2,1,0:T(4,128)S(1)}, f32[576,128]{1,0:T(8,128)S(1)}, f32[576,128]{1,0:T(8,128)S(1)}, f32[4,32,48,128]{3,2,1,0:T(8,128)S(1)}, f32[4,16,32,128]{3,2,1,0:T(8,128)S(1)}) custom-call(s32[4]{0:T(128)S(1)} %pad_add_fusion.info.refs_0_, f32[4,128]{1,0:T(4,128)S(1)} %copy-done.6, f32[4,128]{1,0:T(4,128)S(1)} %copy-done.7, ...), custom_call_target="tpu_custom_call" | custom-call | flops 3000000000 | bytes 8000000 | tf_op jit(solution)/shard_map/pallas_call | solution.py:605
  115.0 9.1 %all_to_all.50.refs_5_ = f32[32,3,128]{2,1,0:T(4,128)S(1)} all-to-all(f32[32,3,128]{2,1,0:T(4,128)S(1)} %get-tuple-element.110), channel_id=1, replica_groups=mesh['batch'=2,'lat'=4,'lon'=4] {'batch','lat','lon'}, dimensions={0} | all-to-all | bytes 98304 | tf_op jit(solution)/shard_map/all_to_all | solution.py:38
  124.1 4.5 %shard_map.129 = (f32[32,4,128]{2,1,0:T(4,128)S(1)}, f32[576,128]{1,0:T(8,128)S(1)}, f32[576,128]{1,0:T(8,128)S(1)}, f32[4,32,48,128]{3,2,1,0:T(8,128)S(1)}) custom-call(s32[4]{0:T(128)S(1)} %pad_add_fusion.info.refs_0_, f32[4,128]{1,0:T(4,128)S(1)} %copy-done.6, f32[4,128]{1,0:T(4,128)S(1)} %copy-done.7, bf16[4,9,128,128]{3,2,1,0:T(8,128)(2,1)S(1)} %bitcast.14, ...), custom_call_target="tpu_custom_call" | custom-call | flops 3000000000 | bytes 8000000 | tf_op jit(solution)/shard_map/pallas_call | solution.py:605
  128.6 9.1 %all_to_all.51.refs_3_.refs_4_ = f32[32,4,128]{2,1,0:T(4,128)S(1)} all-to-all(f32[32,4,128]{2,1,0:T(4,128)S(1)} %get-tuple-element.114), channel_id=1, replica_groups=mesh['batch'=2,'lat'=4,'lon'=4] {'batch','lat','lon'}, dimensions={0} | all-to-all | bytes 131072 | tf_op jit(solution)/shard_map/all_to_all | solution.py:38
  137.7 2.6 %shard_map.130 = (f32[576,128]{1,0:T(8,128)S(1)}, f32[1152,128]{1,0:T(8,128)S(1)}, bf16[4,18,48,128]{3,2,1,0:T(8,128)(2,1)S(1)}) custom-call(s32[4]{0:T(128)S(1)} %pad_add_fusion.info.refs_0_, f32[4,128]{1,0:T(4,128)S(1)} %copy-done.6, f32[32,4,128]{2,1,0:T(4,128)S(1)} %all_to_all.45.refs_5_.refs_10_.refs_2_.refs_0_, ...), custom_call_target="tpu_custom_call" | custom-call | flops 1000000000 | bytes 8000000 | tf_op jit(solution)/shard_map/pallas_call | solution.py:605
  140.3 0.4 collective-permute-start.14
  140.8 0.1 collective-permute-start.12
  140.9 0.4 collective-permute-start.13
  141.3 1.5 collective-permute-done.12.refs_4_
  142.8 0.4 collective-permute-done.13.refs_5_
  143.3 0.1 shard_map.132
  143.4 19.4 %all_to_all.52.got = bf16[16,144,128]{2,1,0:T(8,128)(2,1)S(1)} all-to-all(bf16[16,144,128]{2,1,0:T(8,128)(2,1)S(1)} %bitcast.16), channel_id=1, replica_groups={{0,2,4,6,8,10,12,14,16,18,20,22,24,26,28,30},{1,3,5,7,9,11,13,15,17,19,..., dimensions={0} | all-to-all | bytes 1179648 | tf_op jit(solution)/shard_map/all_to_all | solution.py:43
  162.7 0.1 shard_map.133
  162.8 19.8 %all_to_all.53 = bf16[16,144,128]{2,1,0:T(8,128)(2,1)S(1)} all-to-all(bf16[16,144,128]{2,1,0:T(8,128)(2,1)S(1)} %shard_map.133), channel_id=1, replica_groups={{0,2,4,6,8,10,12,14,16,18,20,22,24,26,28,30},{1,3,5,7,9,11,13,15,17,19,..., dimensions={0} | all-to-all | bytes 1179648 | tf_op jit(solution)/shard_map/all_to_all | solution.py:43
  182.7 1.9 collective-permute-start.15
  184.6 0.7 shard_map.135
  185.3 2.4 %shard_map.131 = f32[4,16,32,128]{3,2,1,0:T(8,128)} custom-call(bf16[4,9,128,128]{3,2,1,0:T(8,128)(2,1)S(1)} %bitcast.15, bf16[4,18,48,128]{3,2,1,0:T(8,128)(2,1)S(1)} %get-tuple-element.118.dpre, f32[4,16,32,128]{3,2,1,0:T(8,128)S(1)} %get-tuple-element.119.grad), custom_call_target="tpu_custom_call" | custom-call | flops 1000000000 | bytes 3000000 | tf_op jit(solution)/shard_map/pallas_call | solution.py:605
  187.7 2.1 %shard_map.134 = f32[4,1152,128]{2,1,0:T(8,128)} custom-call(s32[4]{0:T(128)S(1)} %pad_add_fusion.info.refs_0_, bf16[4,576,128]{2,1,0:T(8,128)(2,1)S(1)} %bitcast.18, bf16[4,576,128]{2,1,0:T(8,128)(2,1)S(1)} %collective-permute-done.15.other), custom_call_target="tpu_custom_call" | custom-call | flops 1000000 | bytes 1000000 | tf_op jit(solution)/shard_map/pallas_call | solution.py:605
  (14 shorter events, 0.0 us)
Async XLA Ops:
  0.7 1.0 copy-start.4
  2.4 13.5 %collective-permute-start = (bf16[4,8,32,128]{3,2,1,0:T(8,128)(2,1)S(1)}, bf16[4,8,32,128]{3,2,1,0:T(8,128)(2,1)S(1)}, u32[]{:S(2)}, u32[]{:S(2)}) collective-permute-start(bf16[4,8,32,128]{3,2,1,0:T(8,128)(2,1)S(1)} %get-tuple-element.68), channel_id=1, source_target_pairs={{0,4},{4,0},{8,12},{12,8},{1,5},{5,1},{9,13},{13,9},{2,6},{6,2},{1... | collective-permute-start | bytes 786440 | tf_op jit(solution)/shard_map/ppermute | solution.py:34
  4.6 12.0 %collective-permute-start.1 = (bf16[4,8,32,128]{3,2,1,0:T(8,128)(2,1)S(1)}, bf16[4,8,32,128]{3,2,1,0:T(8,128)(2,1)S(1)}, u32[]{:S(2)}, u32[]{:S(2)}) collective-permute-start(bf16[4,8,32,128]{3,2,1,0:T(8,128)(2,1)S(1)} %get-tuple-element.69), channel_id=1, source_target_pairs={{4,8},{8,4},{5,9},{9,5},{6,10},{10,6},{7,11},{11,7},{20,24},{24,20... | collective-permute-start | bytes 786440 | tf_op jit(solution)/shard_map/ppermute | solution.py:34
  5.3 2.2 %copy-start.1 = (s32[4,4,16,32,128]{4,3,2,1,0:T(8,128)S(1)}, s32[4,4,16,32,128]{4,3,2,1,0:T(8,128)}, u32[]{:S(2)}) copy-start(s32[4,4,16,32,128]{4,3,2,1,0:T(8,128)} %masks.1) | copy-start | bytes 12582916
  7.4 1.0 copy-start.2
  8.5 10.4 %copy-start.5 = (bf16[4,16,32,128]{3,2,1,0:T(8,128)(2,1)S(1)}, bf16[4,16,32,128]{3,2,1,0:T(8,128)(2,1)}, u32[]{:S(2)}) copy-start(bf16[4,16,32,128]{3,2,1,0:T(8,128)(2,1)} %x.3) | copy-start | bytes 1572868
  9.5 16.2 %copy-start.3 = (bf16[4,16,32,128]{3,2,1,0:T(8,128)(2,1)S(1)}, bf16[4,16,32,128]{3,2,1,0:T(8,128)(2,1)}, u32[]{:S(2)}) copy-start(bf16[4,16,32,128]{3,2,1,0:T(8,128)(2,1)} %cot.3) | copy-start | bytes 1572868
  9.5 7.0 %collective-permute-start.2 = (bf16[4,32,8,128]{3,2,1,0:T(8,128)(2,1)S(1)}, bf16[4,32,8,128]{3,2,1,0:T(8,128)(2,1)S(1)}, u32[]{:S(2)}, u32[]{:S(2)}) collective-permute-start(bf16[4,32,8,128]{3,2,1,0:T(8,128)(2,1)S(1)} %get-tuple-element.72), channel_id=1, source_target_pairs={{0,1},{1,0},{2,3},{3,2},{4,5},{5,4},{6,7},{7,6},{8,9},{9,8},{10,11... | collective-permute-start | bytes 786440 | tf_op jit(solution)/shard_map/ppermute | solution.py:34
  10.5 8.3 %collective-permute-start.3 = (bf16[4,32,8,128]{3,2,1,0:T(8,128)(2,1)S(1)}, bf16[4,32,8,128]{3,2,1,0:T(8,128)(2,1)S(1)}, u32[]{:S(2)}, u32[]{:S(2)}) collective-permute-start(bf16[4,32,8,128]{3,2,1,0:T(8,128)(2,1)S(1)} %get-tuple-element.73), channel_id=1, source_target_pairs={{0,3},{1,2},{2,1},{3,0},{4,7},{5,6},{6,5},{7,4},{8,11},{9,10},{10,... | collective-permute-start | bytes 786440 | tf_op jit(solution)/shard_map/ppermute | solution.py:34
  11.7 13.9 %collective-permute-start.8 = (bf16[4,11,32,128]{3,2,1,0:T(8,128)(2,1)S(1)}, bf16[4,11,32,128]{3,2,1,0:T(8,128)(2,1)S(1)}, u32[]{:S(2)}, u32[]{:S(2)}) collective-permute-start(bf16[4,11,32,128]{3,2,1,0:T(8,128)(2,1)S(1)} %get-tuple-element.82), channel_id=1, source_target_pairs={{0,4},{4,0},{8,12},{12,8},{1,5},{5,1},{9,13},{13,9},{2,6},{6,2},{1... | collective-permute-start | bytes 1081352 | tf_op jit(solution)/shard_map/ppermute | solution.py:34
  15.9 9.8 %collective-permute-start.9 = (bf16[4,11,32,128]{3,2,1,0:T(8,128)(2,1)S(1)}, bf16[4,11,32,128]{3,2,1,0:T(8,128)(2,1)S(1)}, u32[]{:S(2)}, u32[]{:S(2)}) collective-permute-start(bf16[4,11,32,128]{3,2,1,0:T(8,128)(2,1)S(1)} %get-tuple-element.83), channel_id=1, source_target_pairs={{4,8},{8,4},{5,9},{9,5},{6,10},{10,6},{7,11},{11,7},{20,24},{24,20... | collective-permute-start | bytes 1081352 | tf_op jit(solution)/shard_map/ppermute | solution.py:34
  19.8 9.8 %copy-start = (bf16[4,3,3,128,128]{4,3,2,1,0:T(8,128)(2,1)S(1)}, bf16[4,3,3,128,128]{4,3,2,1,0:T(8,128)(2,1)}, u32[]{:S(2)}) copy-start(bf16[4,3,3,128,128]{4,3,2,1,0:T(8,128)(2,1)} %param.8) | copy-start | bytes 3538948
  19.8 9.8 %copy-start.6 = (f32[4,128]{1,0:T(4,128)S(1)}, f32[4,128]{1,0:T(4,128)}, u32[]{:S(2)}) copy-start(f32[4,128]{1,0:T(4,128)} %gains.1) | copy-start | bytes 6148
  19.8 9.8 %copy-start.7 = (f32[4,128]{1,0:T(4,128)S(1)}, f32[4,128]{1,0:T(4,128)}, u32[]{:S(2)}) copy-start(f32[4,128]{1,0:T(4,128)} %refs_2_.13) | copy-start | bytes 6148
  19.8 9.8 %copy-start.8 = (f32[4,128]{1,0:T(4,128)S(1)}, f32[4,128]{1,0:T(4,128)}, u32[]{:S(2)}) copy-start(f32[4,128]{1,0:T(4,128)} %refs_3_.7) | copy-start | bytes 6148
  19.9 8.2 %collective-permute-start.5 = (bf16[4,32,8,128]{3,2,1,0:T(8,128)(2,1)S(1)}, bf16[4,32,8,128]{3,2,1,0:T(8,128)(2,1)S(1)}, u32[]{:S(2)}, u32[]{:S(2)}) collective-permute-start(bf16[4,32,8,128]{3,2,1,0:T(8,128)(2,1)S(1)} %get-tuple-element.76), channel_id=1, source_target_pairs={{0,3},{1,2},{2,1},{3,0},{4,7},{5,6},{6,5},{7,4},{8,11},{9,10},{10,... | collective-permute-start | bytes 786440 | tf_op jit(solution)/shard_map/ppermute | solution.py:34
  20.9 18.2 %collective-permute-start.6 = (bf16[4,13,48,128]{3,2,1,0:T(8,128)(2,1)S(1)}, bf16[4,13,48,128]{3,2,1,0:T(8,128)(2,1)S(1)}, u32[]{:S(2)}, u32[]{:S(2)}) collective-permute-start(bf16[4,13,48,128]{3,2,1,0:T(8,128)(2,1)S(1)} %get-tuple-element.78), channel_id=1, source_target_pairs={{0,4},{4,0},{8,12},{12,8},{1,5},{5,1},{9,13},{13,9},{2,6},{6,2},{1... | collective-permute-start | bytes 1916936 | tf_op jit(solution)/shard_map/ppermute | solution.py:34
  25.0 14.1 %collective-permute-start.7 = (bf16[4,13,48,128]{3,2,1,0:T(8,128)(2,1)S(1)}, bf16[4,13,48,128]{3,2,1,0:T(8,128)(2,1)S(1)}, u32[]{:S(2)}, u32[]{:S(2)}) collective-permute-start(bf16[4,13,48,128]{3,2,1,0:T(8,128)(2,1)S(1)} %get-tuple-element.79), channel_id=1, source_target_pairs={{4,8},{8,4},{5,9},{9,5},{6,10},{10,6},{7,11},{11,7},{20,24},{24,20... | collective-permute-start | bytes 1916936 | tf_op jit(solution)/shard_map/ppermute | solution.py:34
  26.6 12.5 %collective-permute-start.10 = (bf16[4,70,8,128]{3,2,1,0:T(8,128)(2,1)S(1)}, bf16[4,70,8,128]{3,2,1,0:T(8,128)(2,1)S(1)}, u32[]{:S(2)}, u32[]{:S(2)}) collective-permute-start(bf16[4,70,8,128]{3,2,1,0:T(8,128)(2,1)S(1)} %get-tuple-element.84), channel_id=1, source_target_pairs={{0,1},{1,0},{2,3},{3,2},{4,5},{5,4},{6,7},{7,6},{8,9},{9,8},{10,11... | collective-permute-start | bytes 1720328 | tf_op jit(solution)/shard_map/ppermute | solution.py:34
  27.6 14.7 %collective-permute-start.11 = (bf16[4,70,8,128]{3,2,1,0:T(8,128)(2,1)S(1)}, bf16[4,70,8,128]{3,2,1,0:T(8,128)(2,1)S(1)}, u32[]{:S(2)}, u32[]{:S(2)}) collective-permute-start(bf16[4,70,8,128]{3,2,1,0:T(8,128)(2,1)S(1)} %get-tuple-element.85), channel_id=1, source_target_pairs={{0,3},{1,2},{2,1},{3,0},{4,7},{5,6},{6,5},{7,4},{8,11},{9,10},{10,... | collective-permute-start | bytes 1720328 | tf_op jit(solution)/shard_map/ppermute | solution.py:34
  28.0 1.6 collective-permute-start.4
  140.3 2.9 %collective-permute-start.14 = (f32[1152,128]{1,0:T(8,128)S(1)}, f32[1152,128]{1,0:T(8,128)S(1)}, u32[]{:S(2)}, u32[]{:S(2)}) collective-permute-start(f32[1152,128]{1,0:T(8,128)S(1)} %get-tuple-element.126), channel_id=1, source_target_pairs={{0,1},{1,0},{2,3},{3,2},{4,5},{5,4},{6,7},{7,6},{8,9},{9,8},{10,11... | collective-permute-start | bytes 1769480 | tf_op jit(solution)/shard_map/ppermute | solution.py:47
  140.8 2.1 %collective-permute-start.12 = (f32[576,128]{1,0:T(8,128)S(1)}, f32[576,128]{1,0:T(8,128)S(1)}, u32[]{:S(2)}, u32[]{:S(2)}) collective-permute-start(f32[576,128]{1,0:T(8,128)S(1)} %get-tuple-element.124), channel_id=1, source_target_pairs={{0,1},{1,0},{2,3},{3,2},{4,5},{5,4},{6,7},{7,6},{8,9},{9,8},{10,11... | collective-permute-start | bytes 884744 | tf_op jit(solution)/shard_map/ppermute | solution.py:47
  140.9 2.3 %collective-permute-start.13 = (f32[576,128]{1,0:T(8,128)S(1)}, f32[576,128]{1,0:T(8,128)S(1)}, u32[]{:S(2)}, u32[]{:S(2)}) collective-permute-start(f32[576,128]{1,0:T(8,128)S(1)} %get-tuple-element.125), channel_id=1, source_target_pairs={{0,1},{1,0},{2,3},{3,2},{4,5},{5,4},{6,7},{7,6},{8,9},{9,8},{10,11... | collective-permute-start | bytes 884744 | tf_op jit(solution)/shard_map/ppermute | solution.py:47
  182.7 5.0 %collective-permute-start.15 = (bf16[4,576,128]{2,1,0:T(8,128)(2,1)S(1)}, bf16[4,576,128]{2,1,0:T(8,128)(2,1)S(1)}, u32[]{:S(2)}, u32[]{:S(2)}) collective-permute-start(bf16[4,576,128]{2,1,0:T(8,128)(2,1)S(1)} %bitcast.17), channel_id=1, source_target_pairs={{0,1},{1,0},{2,3},{3,2},{4,5},{5,4},{6,7},{7,6},{8,9},{9,8},{10,11... | collective-permute-start | bytes 1769480 | tf_op jit(solution)/shard_map/ppermute | solution.py:47

commit v3 on v2

--- a/solution.py
+++ b/solution.py
@@ -49,6 +49,11 @@
 
 def sigmoid(v):
     return 0.5 * jnp.tanh(0.5 * v) + 0.5
+
+
+def silu(v):
+    half = 0.5 * v
+    return half + half * jnp.tanh(half)
 
 
 def norm_consts(stats_ref, devices):
@@ -114,12 +119,9 @@
 
 
 def pipeline(grids, lo, hi, pairs, prepare, convolve, after):
-    def step(i, carry):
+    count = (hi - lo) // 2 + 1
+    for i in range(count):
         prepare(0, lo - 1 + 2 * i, 0)
-        return carry
-
-    count = (hi - lo) // 2 + 1
-    lax.fori_loop(0, count, step, 0, unroll=4)
     parts = list(chunks(lo, hi, pairs))
     for g in range(grids):
         for j, (at, size) in enumerate(parts):
@@ -233,13 +235,13 @@
             out[g, :, 0:cols, :] = src[g]
 
 
-def field_edge_kernel(geo, info, x, first, second, sem):
+def field_edge_kernel(geo, info, x, first, second, sems):
     rows = geo["R"]
 
     def fetch(high_out, low_out):
         copies = [
-            pltpu.make_async_copy(x.at[:, rows - EXT : rows], high_out, sem.at[0]),
-            pltpu.make_async_copy(x.at[:, 0:EXT], low_out, sem.at[1]),
+            pltpu.make_async_copy(x.at[:, rows - EXT : rows], high_out, sems.at[0]),
+            pltpu.make_async_copy(x.at[:, 0:EXT], low_out, sems.at[1]),
         ]
         for c in copies:
             c.start()
@@ -255,33 +257,58 @@
         fetch(second, first)
 
 
-def mask_edge_kernel(geo, info, masks, cot, *outs):
-    grids = geo["G"]
-    lows, masked = outs[0:4], outs[4]
-    for g in range(grids):
+def mask_edge_kernel(geo, info, masks, first, second, near, sems):
+    rows, height = geo["R"], geo["heights"][1]
+    nears = [
+        pltpu.make_async_copy(masks.at[0, :, 0:height], near.at[0], sems.at[0]),
+        pltpu.make_async_copy(masks.at[0, :, rows - height : rows], near.at[1], sems.at[1]),
+    ]
+    for c in nears:
+        c.start()
+    for c in nears:
+        c.wait()
+
+    def give(out):
+        def act(low):
+            out[...] = near[0 if low else 1].astype(F32).astype(LOW)
+        return act
+
+    both_ways(info[0], give(first), give(second))
+
+
+def tall_kernel(geo, heights, info, *refs):
+    n = len(heights)
+    talls = refs[n + 2 : 2 * n + 2]
+    add_rows(geo, info, refs[:n], heights, refs[n], refs[n + 1], talls)
+    cut_cols(geo, info, talls, refs[2 * n + 2], refs[2 * n + 3])
+
+
+def mask_kernel(geo, masks, cot, *outs):
+    for g in range(geo["G"]):
         for k in range(4):
-            lows[k][g] = masks[k, g].astype(F32).astype(LOW)
-        masked[g] = (cot[g].astype(F32) * masks[3, g].astype(F32)).astype(LOW)
-    cut_cols(geo, info, lows[0:2], outs[5], outs[6])
-    cut_rows(geo, info, [lows[2], masked, cot], geo["heights"][3:], outs[7], outs[8])
-
-
-def middle_kernel(geo, info, x, x_first, x_second, mask0, mask1, m_first, m_second, *outs):
-    x_tall, x_out, wides, m_out = outs[0], outs[1:3], outs[3:5], outs[5:7]
-    add_rows(geo, info, [x], [EXT], x_first, x_second, [x_tall])
-    cut_cols(geo, info, [x_tall], *x_out)
-    add_cols(geo, info, [mask0, mask1], [0, geo["R"]], m_first, m_second, wides)
-    cut_rows(geo, info, wides, geo["heights"][1:3], *m_out)
-
-
-def late_kernel(geo, info, mask2, masked, cot, first, second, before, *outs):
+            outs[k][g] = masks[k, g].astype(F32).astype(LOW)
+        outs[4][g] = (cot[g].astype(F32) * masks[3, g].astype(F32)).astype(LOW)
+
+
+def cut_kernel(geo, info, mask1, mask2, masked, cot, before, first, second):
     del before
-    add_rows(geo, info, [mask2, masked, cot], geo["heights"][3:], first, second, outs[0:3])
-    cut_cols(geo, info, outs[0:3], *outs[3:5])
-
-
-def gate_kernel(sums, *refs):
-    refs[-1][...] = sums[...]
+    cut_rows(geo, info, [mask1, mask2, masked, cot], geo["heights"][2:], first, second)
+
+
+def late_kernel(geo, info, mask1, mask2, masked, cot, first, second, before, *outs):
+    del before
+    add_rows(geo, info, [mask1, mask2, masked, cot], geo["heights"][2:], first, second, outs[0:4])
+    cut_cols(geo, info, outs[0:1], *outs[4:6])
+
+
+def last_kernel(geo, info, tall2, tall3, tall4, before, first, second):
+    del before
+    cut_cols(geo, info, [tall2, tall3, tall4], first, second)
+
+
+def gate_kernel(sums, first, second, out):
+    del first, second
+    out[...] = sums[...]
 
 
 def forward_kernel(layer, geo, *refs):
@@ -295,6 +322,8 @@
     members = geo["members"][layer]
     sources = [refs.pop(0) for _ in members]
     got = [refs.pop(0), refs.pop(0)]
+    if layer in (1, 2):
+        refs.pop(0)
     sums_out = refs.pop(0)
     exts = [refs.pop(0) for _ in members]
     pre_out, low_out = refs.pop(0), refs.pop(0)
@@ -303,17 +332,13 @@
     lo, hi = layer + 1, geo["RE"] - 1 - layer
 
     lay_weights(kernels, layer, False, weight)
-    if layer in (0, 3):
-        add_cols(geo, info, sources, geo["starts"][layer], *got, exts)
-    else:
-        skip = 0 if layer == 1 else heights[1]
-        place = [r.at[:, skip : skip + heights[layer]] for r in got]
-        add_rows(geo, info, sources, [heights[layer]], *place, exts)
+    add_cols(geo, info, sources, geo["starts"][layer], *got, exts)
     ext = exts[0]
     if layer:
         center, inv = norm_consts(stats, devices)
-        scale = inv * gains[layer - 1 : layer, :]
-        shift = offsets[layer - 1 : layer, :]
+        scale = inv * gains[layer - 1 : layer, :] * (1.0 / keep_rate)
+        shift = offsets[layer - 1 : layer, :] * (1.0 / keep_rate) - center * scale
+        scale = 0.5 * scale
     bias = biases[layer : layer + 1, :]
     number = rows * cols
     totals = [jnp.zeros((8, LANES), F32)] * grids
@@ -323,9 +348,8 @@
             value = ext[g, pl.ds(r, 2)].astype(F32)
         else:
             p = pre_in[g, pl.ds(r, 2)]
-            act = p * sigmoid(p)
-            kept = ext[g, pl.ds(r - layer, 2)].astype(F32) * (1.0 / keep_rate)
-            value = ((act - center) * scale + shift) * kept
+            part = p * scale
+            value = (part + part * jnp.tanh(0.5 * p) + shift) * ext[g, pl.ds(r - layer, 2)].astype(F32)
             if layer == 2:
                 value = value + field[g, pl.ds(r, 2)].astype(F32)
 
@@ -340,8 +364,7 @@
             part = part + bias
             pre_out[g, at + k] = part
             if EXT <= at + k < EXT + rows:
-                inner = part[0:cols]
-                act = inner * sigmoid(inner)
+                act = silu(part[0:cols])
                 acts[slot, at + k - EXT] = act
                 totals[g] = totals[g] + fold(act)
 
@@ -363,7 +386,7 @@
             if layer == 0:
                 p = pre_out[g, EXT + k, 0:cols, :]
                 s = sigmoid(p)
-                slope = s * (1.0 + p * (1.0 - s))
+                slope = s + act * (1.0 - s)
                 first = first + fold(slope)
                 second = second + fold(slope * act)
         acc[g : g + 1] = mean
@@ -396,7 +419,16 @@
         total = jnp.sum(sums[...], axis=0)
         one, two = total[0:1], total[1:2]
     pixels = float(geo["D"] * geo["G"] * geo["R"] * geo["C"])
-    return center, inv, inv * gains[layer : layer + 1, :], one * (1.0 / pixels), two * (1.0 / pixels)
+    scale = inv * gains[layer : layer + 1, :]
+    tilt = scale * inv * two * (-1.0 / pixels)
+    flat = scale * one * (-1.0 / pixels) - center * tilt
+    return center, inv, scale * (1.0 / keep_rate), flat, tilt
+
+
+def through(p, dn, scale, flat, tilt):
+    s = sigmoid(p)
+    act = p * s
+    return (dn * scale + act * tilt + flat) * (s + act * (1.0 - s)), act
 
 
 def weight_term(geo, low, g, right, acc):
@@ -442,32 +474,36 @@
     sums_out, keep_half, send_half, z_out = (refs.pop(0) for _ in range(4))
     grad_out = refs.pop(0) if layer == 2 else None
     result = refs.pop(0) if layer == 3 else None
-    taps, weight, acc = refs
+    taps, weight, acc = refs[:3]
+    if layer == 3:
+        result_out, (result, sems) = result, refs[3:]
+        leaving = [pltpu.make_async_copy(result.at[g], result_out.at[g], sems.at[g]) for g in range(grids)]
     lo, hi = EXT - layer, EXT + rows + layer
     keep_off = EXT - heights[layer]
 
     lay_weights(kernels, layer, True, weight)
-    center, inv, scale, one, two = back_consts(layer, geo, stats, sums, gains)
+    center, inv, scale, flat, tilt = back_consts(layer, geo, stats, sums, gains)
     first_row, last_row = info[2], info[3]
     center_b, inv_b = norm_consts(stats_below, devices)
     sums_here = [jnp.zeros((8, LANES), F32)] * 4
 
+    if layer == 3:
+        lift = inv * gains[layer : layer + 1, :] * (1.0 / keep_rate)
+        base = offsets[layer : layer + 1, :] * (1.0 / keep_rate) - center * lift
+
     def prepare(g, r, slot):
-        p = pre[g, pl.ds(r, 2)]
-        s = sigmoid(p)
-        normed = (p * s - center) * inv
         if layer == 3:
-            z = masked[g, pl.ds(r - (EXT - heights[4]), 2)].astype(F32) * (1.0 / keep_rate)
+            z = masked[g, pl.ds(r - (EXT - heights[4]), 2)].astype(F32)
         else:
             z = z_in[g, pl.ds(r, 2)]
-        value = scale * (z - one - normed * two) * (s * (1.0 + p * (1.0 - s)))
-        real = [jnp.where((r + k >= first_row) & (r + k < last_row), 1.0, 0.0).astype(F32) for k in range(2)]
-        value = jnp.stack([value[0] * real[0], value[1] * real[1]])
+        value, act = through(pre[g, pl.ds(r, 2)], z, scale, flat, tilt)
+        if not (isinstance(r, int) and EXT <= r and r + 2 <= EXT + rows):
+            real = [jnp.where((r + k >= first_row) & (r + k < last_row), 1.0, 0.0).astype(F32) for k in range(2)]
+            value = jnp.stack([value[0] * real[0], value[1] * real[1]])
         store_shifted(taps, slot, r, value, width)
         if layer == 3:
             def save():
-                kept = keep_top[g, pl.ds(r - EXT, 2)].astype(F32) * (1.0 / keep_rate)
-                y = (normed[:, 0:cols] * gains[layer : layer + 1, :] + offsets[layer : layer + 1, :]) * kept
+                y = (act[:, 0:cols] * lift + base) * keep_top[g, pl.ds(r - EXT, 2)].astype(F32)
                 result[g, pl.ds(r - EXT, 2)] = (field[g, pl.ds(r - EXT + 1, 2)] + y).astype(LOW)
 
             guard((r >= EXT) & (r < EXT + rows), save)
@@ -480,18 +516,21 @@
                 part = part + cot[g, r - (EXT - heights[5])].astype(F32)
                 if inner:
                     grad_out[g, r - EXT] = part[0:cols]
-            z = part * (keep[g, r - keep_off].astype(F32) * (1.0 / keep_rate))
+            z = part * keep[g, r - keep_off].astype(F32)
             z_out[g, r] = z
             if inner:
                 z = z[0:cols]
                 p = pre_below[g, r, 0:cols, :]
                 s = sigmoid(p)
                 sums_here[0] = sums_here[0] + fold(z)
-                sums_here[1] = sums_here[1] + fold(z * (p * s - center_b))
+                act = p * s
+                sums_here[1] = sums_here[1] + fold(z * (act - center_b))
                 if layer == 1:
-                    sums_here[3] = sums_here[3] + fold(z * (s * (1.0 + p * (1.0 - s))))
+                    sums_here[3] = sums_here[3] + fold(z * (s + act * (1.0 - s)))
 
     def after(g, slot):
+        if layer == 3:
+            leaving[g].start()
         right = taps[slot, 1, EXT : EXT + rows, 0:cols, :].reshape(rows * cols, LANES)
         sums_here[2] = sums_here[2] + fold(right.astype(F32))
         weight_term(geo, low, g, right, acc)
@@ -499,9 +538,14 @@
     pipeline(grids, lo, hi, 5, prepare, convolve, after)
     split_halves(info, acc, keep_half, send_half)
     out = [to_row(v) for v in sums_here]
-    out[1] = out[1] * inv_b
+    out[0] = out[0] * (1.0 / keep_rate)
+    out[1] = out[1] * inv_b * (1.0 / keep_rate)
+    out[3] = out[3] * (1.0 / keep_rate)
     for k in range(4 if layer == 1 else 3):
         sums_out[:, k : k + 1, :] = jnp.broadcast_to(out[k][None], (devices, 1, LANES))
+    if layer == 3:
+        for c in leaving:
+            c.wait()
 
 
 def first_weight_kernel(geo, *refs):
@@ -509,16 +553,13 @@
     info, gains, stats, sums, pre, low, z_in, sent, keep_half, send_both, dpre, acc = refs
     half = 9 * LANES // 2
     send_both[0:half] = sent[...]
-    center, inv, scale, one, two = back_consts(0, geo, stats, sums, gains)
+    scale, flat, tilt = back_consts(0, geo, stats, sums, gains)[2:]
     first_row, last_row = info[2], info[3]
 
     for g in range(grids):
         for k in range(rows + 2):
             r = EXT - 1 + k
-            p = pre[g, r]
-            s = sigmoid(p)
-            normed = (p * s - center) * inv
-            value = scale * (z_in[g, r] - one - normed * two) * (s * (1.0 + p * (1.0 - s)))
+            value, _ = through(pre[g, r], z_in[g, r], scale, flat, tilt)
             if k in (0, rows + 1):
                 value = value * jnp.where((r >= first_row) & (r < last_row), 1.0, 0.0).astype(F32)
             dpre[g, k] = value.astype(LOW)
@@ -526,8 +567,10 @@
     split_halves(info, acc, keep_half, send_both.at[half : 2 * half])
 
 
-def input_grad_kernel(geo, kernels, dpre, grad, out, taps, weight):
+def input_grad_kernel(geo, kernels, dpre, grad, gains, *refs):
     grids, rows, width, cols = geo["G"], geo["R"], geo["CE"], geo["C"]
+    out, taps, weight, buffer, sems = refs[7], *refs[11:]
+    leaving = [pltpu.make_async_copy(buffer.at[g], out.at[g], sems.at[g]) for g in range(grids)]
     lay_weights(kernels, 0, True, weight)
 
     def prepare(g, r, slot):
@@ -535,9 +578,12 @@
 
     def convolve(g, at, count, slot):
         for k, part in enumerate(conv_pairs(taps, slot, weight, at, count, cols)):
-            out[g, at + k - 1] = grad[g, at + k - 1] + part
-
-    pipeline(grids, 1, rows + 1, 8, prepare, convolve, lambda g, slot: None)
+            buffer[g, at + k - 1] = grad[g, at + k - 1] + part
+
+    pipeline(grids, 1, rows + 1, 8, prepare, convolve, lambda g, slot: leaving[g].start())
+    gather_rows(geo, gains, *refs[0:7], *refs[8:11])
+    for c in leaving:
+        c.wait()
 
 
 def share_kernel(*refs):
@@ -553,13 +599,15 @@
     out[...] = jnp.broadcast_to(total.astype(LOW)[None], out.shape)
 
 
-def join_kernel(geo, info, mine, other, out):
+def join_kernel(geo, info, mine, other, out, buffer, sems):
     half = 9 * LANES // 2
+    leaving = [pltpu.make_async_copy(buffer.at[k], out.at[k], sems.at[k]) for k in range(4)]
 
     def place(low, high):
         for k in range(4):
-            out[k, 0:half] = low[k].astype(F32)
-            out[k, half:] = high[k].astype(F32)
+            buffer[k, 0:half] = low[k].astype(F32)
+            buffer[k, half:] = high[k].astype(F32)
+            leaving[k].start()
 
     @pl.when(info[1] == 1)
     def _():
@@ -569,8 +617,11 @@
     def _():
         place(other, mine)
 
-
-def rows_kernel(geo, gains, *refs):
+    for c in leaving:
+        c.wait()
+
+
+def gather_rows(geo, gains, *refs):
     stats, sums = refs[0:4], refs[4:7]
     bias_out, gain_out, offset_out = refs[7:]
     for layer in range(4):
@@ -591,21 +642,24 @@
             bias_out[0:1] = inv * gains[0:1, :] * (total[3:4] - flat * one / pixels - lifted * two / pixels)
 
 
-def call(kernel, operands, outs, scratch=(), flops=10**6, moved=10**6, scalars=1, final=(), outside=False):
+def call(kernel, operands, outs, scratch=(), flops=10**6, moved=10**6, scalars=1, final=(), small=(), outside=False):
     space = pl.BlockSpec(memory_space=pltpu.VMEM)
     specs = [pl.BlockSpec(memory_space=pltpu.SMEM)] * scalars
     operands = list(operands)
     for k in range(scalars, len(operands)):
         if outside:
             specs.append(pl.BlockSpec(memory_space=pltpu.HBM))
+            operands[k] = pltpu.with_memory_space_constraint(operands[k], pltpu.HBM)
         else:
             specs.append(space)
             operands[k] = pltpu.with_memory_space_constraint(operands[k], pltpu.VMEM)
-    shapes = [jax.ShapeDtypeStruct(s, d) if k in final else pltpu.VMEM(s, d) for k, (s, d) in enumerate(outs)]
+    plain = set(final) | set(small)
+    shapes = [jax.ShapeDtypeStruct(s, d) if k in plain else pltpu.VMEM(s, d) for k, (s, d) in enumerate(outs)]
+    places = [pl.BlockSpec(memory_space=pltpu.HBM) if k in final else space for k in range(len(outs))]
     return pl.pallas_call(
         kernel,
         in_specs=specs,
-        out_specs=[space] * len(outs),
+        out_specs=places,
         out_shape=shapes,
         scratch_shapes=[v if hasattr(v, "shape") and not isinstance(v, tuple) else pltpu.VMEM(*v) for v in scratch],
         compiler_params=pltpu.CompilerParams(vmem_limit_bytes=12 * 2**20),
@@ -640,6 +694,8 @@
     if layer == 3:
         outs.append(((grids, rows, cols, LANES), LOW))
     scratch = conv_scratch(geo, rows_ext) + [((LANES, 9 * LANES), F32)]
+    if layer == 3:
+        scratch += [((grids, rows, cols, LANES), LOW), pltpu.SemaphoreType.DMA((grids,))]
     return call(
         functools.partial(backward_kernel, layer, geo), operands, outs, scratch, 3 * 10**9, 8 * 10**6,
         final=(4,) if layer == 3 else (),
@@ -655,7 +711,7 @@
         starts.append(starts[-1] + rows + 2 * heights[k])
     geo = dict(
         G=grids, R=rows, C=cols, D=devices, RE=rows + 2 * EXT, CE=cols + 2 * EXT, heights=heights,
-        starts={0: [0], 3: starts}, members=[[0], [1], [2], [3, 4, 5]],
+        starts=[[0], [0], [0], starts], members=[[0], [1], [2], [3, 4, 5]],
     )
     lat, lon = lax.axis_index("lat"), lax.axis_index("lon")
     info = jnp.stack(
@@ -671,49 +727,65 @@
     def block(tall, wide):
         return ((grids, tall, wide, LANES), LOW)
 
-    x_edges = call(
-        functools.partial(field_edge_kernel, geo), [info, inputs], [block(EXT, cols)] * 2,
-        [pltpu.SemaphoreType.DMA((2,))], outside=True,
-    )
-    x_got = trade(x_edges, "lat", False)
-    late = sum(heights[3:])
+    x_height, soon, late = heights[0], heights[1], sum(heights[2:])
+    pair_sems = pltpu.SemaphoreType.DMA((2,))
     outs = call(
-        functools.partial(mask_edge_kernel, geo), [info, keep_masks, cotangent],
-        [block(rows, cols)] * 5 + [block(2 * rows, EXT)] * 2 + [block(late, cols)] * 2,
-    )
-    low_masks, masked = outs[0:4], outs[4]
-    soon_got = trade(outs[5:7], "lon", True)
-    late_got = trade(outs[7:9], "lat", False)
+        functools.partial(field_edge_kernel, geo), [info, inputs], [block(x_height, cols)] * 2, [pair_sems], outside=True
+    )
+    x_got = trade(outs, "lat", False)
     outs = call(
-        functools.partial(middle_kernel, geo),
-        [info, inputs, *x_got, low_masks[0], low_masks[1], *soon_got],
-        [block(rows + 2 * EXT, cols)] + [block(rows + 2 * EXT, EXT)] * 2
-        + [block(rows, cols + 2 * EXT)] * 2 + [block(heights[1] + heights[2], cols + 2 * EXT)] * 2,
+        functools.partial(mask_edge_kernel, geo), [info, keep_masks], [block(soon, cols)] * 2,
+        [((2, grids, soon, cols, LANES), jnp.int32), pair_sems], outside=True,
+    )
+    soon_got = trade(outs, "lat", False)
+    outs = call(
+        functools.partial(tall_kernel, geo, heights[:1]), [info, inputs, *x_got],
+        [block(rows + 2 * x_height, cols)] + [block(rows + 2 * x_height, EXT)] * 2,
     )
     pieces = [[outs[0], *trade(outs[1:3], "lon", True)]]
-    halos = list(trade(outs[5:7], "lat", False))
-    pieces += [[outs[3], *halos], [outs[4], *halos]]
-    talls = [rows + 2 * h for h in heights[3:]]
+    outs = call(functools.partial(mask_kernel, geo), [keep_masks, cotangent], [block(rows, cols)] * 5, scalars=0)
+    low_masks, masked = list(outs[0:4]), outs[4]
     outs = call(
-        functools.partial(late_kernel, geo), [info, low_masks[2], masked, cotangent, *late_got, outs[1]],
-        [block(t, cols) for t in talls] + [block(sum(talls), EXT)] * 2,
-    )
-    pieces.append([*outs[0:3], *trade(outs[3:5], "lon", True)])
-    halos += pieces[3][3:]
+        functools.partial(tall_kernel, geo, heights[1:2]), [info, low_masks[0], *soon_got],
+        [block(rows + 2 * soon, cols)] + [block(rows + 2 * soon, EXT)] * 2,
+    )
+    pieces.append([outs[0], *trade(outs[1:3], "lon", True)])
+    edges = call(
+        functools.partial(cut_kernel, geo), [info, low_masks[1], low_masks[2], masked, cotangent, outs[1]],
+        [block(late, cols)] * 2,
+    )
+    late_got = trade(edges, "lat", False)
+    talls = [rows + 2 * h for h in heights[2:]]
 
     pres, lows, stats, exts = [None] * 4, [None] * 4, [None] * 4, [None] * 6
-    field = None
+    field = order = None
     for layer in range(4):
         operands = [info, gains, offsets, biases, kernels]
         if layer:
             operands += [stats[layer - 1], pres[layer - 1]]
         if layer == 2:
             operands.append(exts[0])
-        outs = list(forward_call(layer, geo, operands + pieces[layer]))
+        operands += pieces[layer]
+        if layer in (1, 2):
+            operands.append(order)
+        outs = list(forward_call(layer, geo, operands))
         part = outs.pop(0)
+        if layer < 2:
+            (part,) = call(gate_kernel, [part] + pieces[layer + 1][1:], [(part.shape, F32)], scalars=0)
+        stats[layer] = to_all(part)
         if layer == 0:
-            (part,) = call(gate_kernel, [part] + halos, [(part.shape, F32)], scalars=0)
-        stats[layer] = to_all(part)
+            ends = call(
+                functools.partial(late_kernel, geo), [info] + low_masks[1:3] + [masked, cotangent, *late_got, stats[0]],
+                [block(t, cols) for t in talls] + [block(talls[0], EXT)] * 2,
+            )
+            pieces.append([ends[0], *trade(ends[4:6], "lon", True)])
+            order = ends[4]
+        if layer == 1:
+            edges = call(
+                functools.partial(last_kernel, geo), [info, *ends[1:4], stats[1]], [block(sum(talls[1:]), EXT)] * 2
+            )
+            pieces.append([*ends[1:4], *trade(edges, "lon", True)])
+            order = edges[0]
         for k in geo["members"][layer]:
             exts[k] = outs.pop(0)
         pres[layer], lows[layer] = outs.pop(0), outs.pop(0)
@@ -754,15 +826,15 @@
     (mine,) = call(functools.partial(total_kernel, devices), [arrived], [(slots, LOW)], scalars=0)
     mine = to_half(mine, devices).reshape(4, half, LANES)
     (kernel_grad,) = call(
-        functools.partial(join_kernel, geo), [info, mine, to_pair(mine)], [((4, 9 * LANES, LANES), F32)], final=(0,)
-    )
-    (input_grad,) = call(
-        functools.partial(input_grad_kernel, geo), [kernels, dpre, grad], [((grids, rows, cols, LANES), F32)],
-        conv_scratch(geo, rows + 2), 10**9, 3 * 10**6, scalars=0, final=(0,),
+        functools.partial(join_kernel, geo), [info, mine, to_pair(mine)], [((4, 9 * LANES, LANES), F32)],
+        [((4, 9 * LANES, LANES), F32), pltpu.SemaphoreType.DMA((4,))], final=(0,),
     )
     small = ((4, LANES), F32)
-    bias_grad, gain_grad, offset_grad = call(
-        functools.partial(rows_kernel, geo), [gains] + stats + sums[:3], [small] * 3, scalars=0, final=(0, 1, 2)
+    field_like = ((grids, rows, cols, LANES), F32)
+    input_grad, bias_grad, gain_grad, offset_grad = call(
+        functools.partial(input_grad_kernel, geo), [kernels, dpre, grad, gains] + stats + sums[:3],
+        [field_like] + [small] * 3, conv_scratch(geo, rows + 2) + [field_like, pltpu.SemaphoreType.DMA((grids,))],
+        10**9, 3 * 10**6, scalars=0, final=(0,), small=(1, 2, 3),
     )
     return (output, input_grad, kernel_grad.reshape(4, 3, 3, LANES, LANES), bias_grad, gain_grad, offset_grad)
 

time: 190 us -> 185 us (0.974)
  waiting for transfers between devices: 14.2 us -> 7.04 us
  local copies, waits for them, and re-layouts: 4.3 us -> 0.04 us
  starting transfers between devices: 20 us -> 22.4 us
    ppermute x6 -> x7, waiting for transfers between devices: 6.54 us -> 0.1 us  [trade(): lax.ppermute(pair[0], axis, first)]
    unnamed x18 -> x14, local copies, waits for them, and re-layouts: 4.3 us -> 0.04 us
    ppermute x6 -> x7, starting transfers between devices: 4.44 us -> 7.55 us  [trade(): lax.ppermute(pair[1], axis, second)]
    pallas_call x18 -> x22, Pallas kernels: 45.8 us -> 47.4 us  [call(): pl.pallas_call(kernel, in_specs=specs, out_specs=places, out_shape=shapes...]
    ppermute x6 -> x7, waiting for transfers between devices: 5.71 us -> 4.97 us  [trade(): lax.ppermute(pair[1], axis, second)]
    ppermute x6 -> x7, starting transfers between devices: 12.7 us -> 12 us  [trade(): lax.ppermute(pair[0], axis, first)]
  transfers between devices with their start and end apart: 16 -> 18, of which waited for: 7 -> 5; matrix products, arithmetic and copies ran while one was open for 0% -> 0% of each run, Pallas kernels for 5% -> 11%
where the time goes in v3:
time: 185 us; the launch traced here: 184 us
  blocking collectives  106 us (57%)
  Pallas kernels  47.4 us (26%)
  starting transfers between devices  22.4 us (12%)
  waiting for transfers between devices  7.04 us (4%)
    all_to_all x7, blocking collectives, to_all(): return lax.all_to_all(rows, EVERY, 0, 0)  67.1 us
    pallas_call x22, Pallas kernels, call(): pl.pallas_call(kernel, in_specs=specs, out_specs=places, out_shape=shapes...  47.4 us
    all_to_all x2, blocking collectives, to_half(): return lax.all_to_all(rows, EVERY, 0, 0, axis_index_groups=groups)  39.2 us
    ppermute x7, starting transfers between devices, trade(): lax.ppermute(pair[0], axis, first)  12 us
    ppermute x7, starting transfers between devices, trade(): lax.ppermute(pair[1], axis, second)  7.55 us
    ppermute x7, waiting for transfers between devices, trade(): lax.ppermute(pair[1], axis, second)  4.97 us
  transfers between devices with their start and end apart: 18, of which 5 were waited for; matrix products, arithmetic and copies ran while one was open for 0% of the time, Pallas kernels for 11%

profile of v3, /device:TPU:1, one launch (start us, length us, event | category | flops | bytes accessed | tf_op | source)
XLA Modules:
  0.0 184.3 jit_solution(6816231228377157833)
XLA Ops:
  0.6 0.1 pad_add_fusion.info.refs_0_
  0.7 1.6 shard_map.118
  2.3 2.2 %collective-permute-start = (bf16[4,8,32,128]{3,2,1,0:T(8,128)(2,1)S(1)}, bf16[4,8,32,128]{3,2,1,0:T(8,128)(2,1)S(1)}, u32[]{:S(2)}, u32[]{:S(2)}) collective-permute-start(bf16[4,8,32,128]{3,2,1,0:T(8,128)(2,1)S(1)} %get-tuple-element.71), channel_id=1, source_target_pairs={{0,4},{4,0},{8,12},{12,8},{1,5},{5,1},{9,13},{13,9},{2,6},{6,2},{1... | collective-permute-start | bytes 786440 | tf_op jit(solution)/shard_map/ppermute | solution.py:34
  4.5 0.8 collective-permute-start.1
  5.3 2.0 %shard_map.122 = (bf16[4,7,32,128]{3,2,1,0:T(8,128)(2,1)S(1)}, bf16[4,7,32,128]{3,2,1,0:T(8,128)(2,1)S(1)}) custom-call(s32[4]{0:T(128)S(1)} %pad_add_fusion.info.refs_0_, s32[4,4,16,32,128]{4,3,2,1,0:T(8,128)} %masks.3), custom_call_target="tpu_custom_call" | custom-call | flops 1000000 | bytes 1000000 | tf_op jit(solution)/shard_map/pallas_call | solution.py:659
  7.3 3.8 %collective-permute-start.4 = (bf16[4,7,32,128]{3,2,1,0:T(8,128)(2,1)S(1)}, bf16[4,7,32,128]{3,2,1,0:T(8,128)(2,1)S(1)}, u32[]{:S(2)}, u32[]{:S(2)}) collective-permute-start(bf16[4,7,32,128]{3,2,1,0:T(8,128)(2,1)S(1)} %get-tuple-element.78), channel_id=1, source_target_pairs={{0,4},{4,0},{8,12},{12,8},{1,5},{5,1},{9,13},{13,9},{2,6},{6,2},{1... | collective-permute-start | bytes 688136 | tf_op jit(solution)/shard_map/ppermute | solution.py:34
  11.1 0.7 collective-permute-start.5
  11.8 0.0 collective-permute-done.refs_1_
  11.8 0.0 collective-permute-done.1.refs_2_
  11.8 0.7 shard_map.119
  12.5 1.6 collective-permute-start.2
  14.1 1.2 collective-permute-start.3
  15.3 0.3 shard_map.121
  15.7 0.0 copy-start
  15.7 0.0 copy-start.4
  15.7 0.0 copy-start.5
  15.7 0.0 copy-start.6
  15.7 0.1 collective-permute-done.4.refs_1_
  15.8 0.0 collective-permute-done.5.refs_2_
  15.8 0.7 shard_map.123
  16.5 0.6 shard_map.125
  17.2 4.2 %collective-permute-start.8 = (bf16[4,17,32,128]{3,2,1,0:T(8,128)(2,1)S(1)}, bf16[4,17,32,128]{3,2,1,0:T(8,128)(2,1)S(1)}, u32[]{:S(2)}, u32[]{:S(2)}) collective-permute-start(bf16[4,17,32,128]{3,2,1,0:T(8,128)(2,1)S(1)} %get-tuple-element.87), channel_id=1, source_target_pairs={{0,4},{4,0},{8,12},{12,8},{1,5},{5,1},{9,13},{13,9},{2,6},{6,2},{1... | collective-permute-start | bytes 1671176 | tf_op jit(solution)/shard_map/ppermute | solution.py:34
  21.4 0.7 collective-permute-start.9
  22.0 3.1 %collective-permute-start.7 = (bf16[4,30,8,128]{3,2,1,0:T(8,128)(2,1)S(1)}, bf16[4,30,8,128]{3,2,1,0:T(8,128)(2,1)S(1)}, u32[]{:S(2)}, u32[]{:S(2)}) collective-permute-start(bf16[4,30,8,128]{3,2,1,0:T(8,128)(2,1)S(1)} %get-tuple-element.81), channel_id=1, source_target_pairs={{0,3},{1,2},{2,1},{3,0},{4,7},{5,6},{6,5},{7,4},{8,11},{9,10},{10,... | collective-permute-start | bytes 737288 | tf_op jit(solution)/shard_map/ppermute | solution.py:34
  25.2 0.0 collective-permute-start.6
  25.2 0.0 collective-permute-done.3.refs_7_
  25.2 4.3 %shard_map.120 = (f32[32,4,128]{2,1,0:T(4,128)S(1)}, bf16[4,32,48,128]{3,2,1,0:T(8,128)(2,1)S(1)}, f32[4,32,48,128]{3,2,1,0:T(8,128)S(1)}, bf16[3,4,18,32,128]{4,3,2,1,0:T(8,128)(2,1)S(1)}) custom-call(s32[4]{0:T(128)S(1)} %pad_add_fusion.info.refs_0_, f32[4,128]{1,0:T(4,128)S(1)} %copy-done.4, f32[4,128]{1,0:T(4,128)S(1)} %copy-done.5, ...), custom_call_target="tpu_custom_call" | custom-call | flops 2000000000 | bytes 8000000 | tf_op jit(solution)/shard_map/pallas_call | solution.py:659
  29.5 2.4 %collective-permute-done.7.second.refs_9_ = bf16[4,30,8,128]{3,2,1,0:T(8,128)(2,1)S(1)} collective-permute-done((bf16[4,30,8,128]{3,2,1,0:T(8,128)(2,1)S(1)}, bf16[4,30,8,128]{3,2,1,0:T(8,128)(2,1)S(1)}, u32[]{:S(2)}, u32[]{:S(2)}) %collective-permute-start.7) | collective-permute-done | bytes 245792 | tf_op jit(solution)/shard_map/ppermute | solution.py:34
  31.9 0.0 collective-permute-done.6.first.refs_8_
  31.9 11.4 %all_to_all.45.before.refs_5_.refs_10_.refs_2_.refs_0_ = f32[32,4,128]{2,1,0:T(4,128)S(1)} all-to-all(f32[32,4,128]{2,1,0:T(4,128)S(1)} %shard_map.124), channel_id=1, replica_groups=mesh['batch'=2,'lat'=4,'lon'=4] {'batch','lat','lon'}, dimensions={0} | all-to-all | bytes 131072 | tf_op jit(solution)/shard_map/all_to_all | solution.py:38
  43.3 0.8 shard_map.126
  44.1 0.5 collective-permute-start.11
  44.6 0.1 collective-permute-start.10
  44.8 4.5 %shard_map.127 = (f32[32,2,128]{2,1,0:T(2,128)S(1)}, bf16[4,30,48,128]{3,2,1,0:T(8,128)(2,1)S(1)}, f32[4,32,48,128]{3,2,1,0:T(8,128)S(1)}, bf16[3,4,18,32,128]{4,3,2,1,0:T(8,128)(2,1)S(1)}) custom-call(s32[4]{0:T(128)S(1)} %pad_add_fusion.info.refs_0_, f32[4,128]{1,0:T(4,128)S(1)} %copy-done.4, f32[4,128]{1,0:T(4,128)S(1)} %copy-done.5, ...), custom_call_target="tpu_custom_call" | custom-call | flops 2000000000 | bytes 8000000 | tf_op jit(solution)/shard_map/pallas_call | solution.py:659
  49.3 2.6 %collective-permute-done.11.second.refs_10_ = bf16[4,28,8,128]{3,2,1,0:T(8,128)(2,1)S(1)} collective-permute-done((bf16[4,28,8,128]{3,2,1,0:T(8,128)(2,1)S(1)}, bf16[4,28,8,128]{3,2,1,0:T(8,128)(2,1)S(1)}, u32[]{:S(2)}, u32[]{:S(2)}) %collective-permute-start.11) | collective-permute-done | bytes 229408 | tf_op jit(solution)/shard_map/ppermute | solution.py:34
  51.8 0.0 collective-permute-done.10.first.refs_9_
  51.8 8.9 %all_to_all.46.before.refs_5_.refs_11_.refs_4_.refs_1_ = f32[32,2,128]{2,1,0:T(2,128)S(1)} all-to-all(f32[32,2,128]{2,1,0:T(2,128)S(1)} %shard_map.128), channel_id=1, replica_groups=mesh['batch'=2,'lat'=4,'lon'=4] {'batch','lat','lon'}, dimensions={0} | all-to-all | bytes 65536 | tf_op jit(solution)/shard_map/all_to_all | solution.py:38
  60.7 0.7 shard_map.129
  61.5 0.6 collective-permute-start.13
  62.1 0.1 collective-permute-start.12
  62.2 4.6 %shard_map.130 = (f32[32,2,128]{2,1,0:T(2,128)S(1)}, bf16[4,28,48,128]{3,2,1,0:T(8,128)(2,1)S(1)}, f32[4,32,48,128]{3,2,1,0:T(8,128)S(1)}, bf16[3,4,18,32,128]{4...) custom-call(s32[4]{0:T(128)S(1)} %pad_add_fusion.info.refs_0_, f32[4,128]{1,0:T(4,128)S(1)} %copy-done.4, ...), custom_call_target="tpu_custom_call" | custom-call | flops 2000000000 | bytes 8000000 | tf_op jit(solution)/shard_map/pallas_call | solution.py:659
  66.8 10.4 %all_to_all.47.refs_5_.refs_12_.refs_4_.refs_2_ = f32[32,2,128]{2,1,0:T(2,128)S(1)} all-to-all(f32[32,2,128]{2,1,0:T(2,128)S(1)} %get-tuple-element.99), channel_id=1, replica_groups=mesh['batch'=2,'lat'=4,'lon'=4] {'batch','lat','lon'}, dimensions={0} | all-to-all | bytes 65536 | tf_op jit(solution)/shard_map/all_to_all | solution.py:38
  77.2 4.4 %shard_map.131 = (f32[32,4,128]{2,1,0:T(4,128)S(1)}, bf16[4,26,48,128]{3,2,1,0:T(8,128)(2,1)S(1)}, bf16[4,24,48,128]{3,2,1,0:T(8,128)(2,1)S(1)}, bf16[4,20,48,12...) custom-call(s32[4]{0:T(128)S(1)} %pad_add_fusion.info.refs_0_, ...), custom_call_target="tpu_custom_call" | custom-call | flops 2000000000 | bytes 8000000 | tf_op jit(solution)/shard_map/pallas_call | solution.py:659
  81.5 9.1 %all_to_all.48.refs_4_.refs_5_.refs_3_ = f32[32,4,128]{2,1,0:T(4,128)S(1)} all-to-all(f32[32,4,128]{2,1,0:T(4,128)S(1)} %get-tuple-element.102), channel_id=1, replica_groups=mesh['batch'=2,'lat'=4,'lon'=4] {'batch','lat','lon'}, dimensions={0} | all-to-all | bytes 131072 | tf_op jit(solution)/shard_map/all_to_all | solution.py:38
  90.6 5.8 %shard_map.132 = (f32[32,3,128]{2,1,0:T(4,128)S(1)}, f32[576,128]{1,0:T(8,128)S(1)}, f32[576,128]{1,0:T(8,128)S(1)}, f32[4,32,48,128]{3,2,1,0:T(8,128)S(1)}, bf16[4,16,32,128]{3,2,1,0:T(8,128)(2,1)}) custom-call(s32[4]{0:T(128)S(1)} %pad_add_fusion.info.refs_0_, f32[4,128]{1,0:T(4,128)S(1)} %copy-done.4, f32[4,128]{1,0:T(4,128)S(1)} %copy-done.5, ...), custom_call_target="tpu_custom_call" | custom-call | flops 3000000000 | bytes 8000000 | tf_op jit(solution)/shard_map/pallas_call | solution.py:659
  96.5 9.1 %all_to_all.49.refs_5_.refs_6_ = f32[32,3,128]{2,1,0:T(4,128)S(1)} all-to-all(f32[32,3,128]{2,1,0:T(4,128)S(1)} %get-tuple-element.110), channel_id=1, replica_groups=mesh['batch'=2,'lat'=4,'lon'=4] {'batch','lat','lon'}, dimensions={0} | all-to-all | bytes 98304 | tf_op jit(solution)/shard_map/all_to_all | solution.py:38
  105.6 4.7 %shard_map.133 = (f32[32,3,128]{2,1,0:T(4,128)S(1)}, f32[576,128]{1,0:T(8,128)S(1)}, f32[576,128]{1,0:T(8,128)S(1)}, f32[4,32,48,128]{3,2,1,0:T(8,128)S(1)}, f32[4,16,32,128]{3,2,1,0:T(8,128)S(1)}) custom-call(s32[4]{0:T(128)S(1)} %pad_add_fusion.info.refs_0_, f32[4,128]{1,0:T(4,128)S(1)} %copy-done.4, f32[4,128]{1,0:T(4,128)S(1)} %copy-done.5, ...), custom_call_target="tpu_custom_call" | custom-call | flops 3000000000 | bytes 8000000 | tf_op jit(solution)/shard_map/pallas_call | solution.py:659
  110.2 9.1 %all_to_all.50.refs_5_ = f32[32,3,128]{2,1,0:T(4,128)S(1)} all-to-all(f32[32,3,128]{2,1,0:T(4,128)S(1)} %get-tuple-element.115), channel_id=1, replica_groups=mesh['batch'=2,'lat'=4,'lon'=4] {'batch','lat','lon'}, dimensions={0} | all-to-all | bytes 98304 | tf_op jit(solution)/shard_map/all_to_all | solution.py:38
  119.3 4.3 %shard_map.134 = (f32[32,4,128]{2,1,0:T(4,128)S(1)}, f32[576,128]{1,0:T(8,128)S(1)}, f32[576,128]{1,0:T(8,128)S(1)}, f32[4,32,48,128]{3,2,1,0:T(8,128)S(1)}) custom-call(s32[4]{0:T(128)S(1)} %pad_add_fusion.info.refs_0_, f32[4,128]{1,0:T(4,128)S(1)} %copy-done.4, f32[4,128]{1,0:T(4,128)S(1)} %copy-done.5, bf16[4,9,128,128]{3,2,1,0:T(8,128)(2,1)S(1)} %bitcast.14, ...), custom_call_target="tpu_custom_call" | custom-call | flops 3000000000 | bytes 8000000 | tf_op jit(solution)/shard_map/pallas_call | solution.py:659
  123.7 9.1 %all_to_all.51.refs_3_.refs_4_ = f32[32,4,128]{2,1,0:T(4,128)S(1)} all-to-all(f32[32,4,128]{2,1,0:T(4,128)S(1)} %get-tuple-element.119), channel_id=1, replica_groups=mesh['batch'=2,'lat'=4,'lon'=4] {'batch','lat','lon'}, dimensions={0} | all-to-all | bytes 131072 | tf_op jit(solution)/shard_map/all_to_all | solution.py:38
  132.8 2.3 %shard_map.135 = (f32[576,128]{1,0:T(8,128)S(1)}, f32[1152,128]{1,0:T(8,128)S(1)}, bf16[4,18,48,128]{3,2,1,0:T(8,128)(2,1)S(1)}) custom-call(s32[4]{0:T(128)S(1)} %pad_add_fusion.info.refs_0_, f32[4,128]{1,0:T(4,128)S(1)} %copy-done.4, f32[32,4,128]{2,1,0:T(4,128)S(1)} %all_to_all.45.before.refs_5_.refs_10_.refs_2_.refs_0_, ...), custom_call_target="tpu_custom_call" | custom-call | flops 1000000000 | bytes 8000000 | tf_op jit(solution)/shard_map/pallas_call | solution.py:659
  135.1 0.4 collective-permute-start.16
  135.5 0.1 collective-permute-start.14
  135.7 0.4 collective-permute-start.15
  136.0 1.5 collective-permute-done.14.refs_4_
  137.6 0.4 collective-permute-done.15.refs_5_
  138.0 0.0 collective-permute-done.16.refs_6_
  138.0 0.1 shard_map.137
  138.1 19.4 %all_to_all.52.got = bf16[16,144,128]{2,1,0:T(8,128)(2,1)S(1)} all-to-all(bf16[16,144,128]{2,1,0:T(8,128)(2,1)S(1)} %bitcast.16), channel_id=1, replica_groups={{0,2,4,6,8,10,12,14,16,18,20,22,24,26,28,30},{1,3,5,7,9,11,13,15,17,19,..., dimensions={0} | all-to-all | bytes 1179648 | tf_op jit(solution)/shard_map/all_to_all | solution.py:43
  157.5 0.1 shard_map.138
  157.6 19.8 %all_to_all.53 = bf16[16,144,128]{2,1,0:T(8,128)(2,1)S(1)} all-to-all(bf16[16,144,128]{2,1,0:T(8,128)(2,1)S(1)} %shard_map.138), channel_id=1, replica_groups={{0,2,4,6,8,10,12,14,16,18,20,22,24,26,28,30},{1,3,5,7,9,11,13,15,17,19,..., dimensions={0} | all-to-all | bytes 1179648 | tf_op jit(solution)/shard_map/all_to_all | solution.py:43
  177.4 1.9 %collective-permute-start.17 = (bf16[4,576,128]{2,1,0:T(8,128)(2,1)S(1)}, bf16[4,576,128]{2,1,0:T(8,128)(2,1)S(1)}, u32[]{:S(2)}, u32[]{:S(2)}) collective-permute-start(bf16[4,576,128]{2,1,0:T(8,128)(2,1)S(1)} %bitcast.17), channel_id=1, source_target_pairs={{0,1},{1,0},{2,3},{3,2},{4,5},{5,4},{6,7},{7,6},{8,9},{9,8},{10,11... | collective-permute-start | bytes 1769480 | tf_op jit(solution)/shard_map/ppermute | solution.py:47
  179.3 2.8 %shard_map.136 = (f32[4,16,32,128]{3,2,1,0:T(8,128)}, f32[4,128]{1,0:T(4,128)}, f32[4,128]{1,0:T(4,128)}, f32[4,128]{1,0:T(4,128)}) custom-call(bf16[4,9,128,128]{3,2,1,0:T(8,128)(2,1)S(1)} %bitcast.15, bf16[4,18,48,128]{3,2,1,0:T(8,128)(2,1)S(1)} %get-tuple-element.123.dpre, f32[4,16,32,128]{3,2,1,0:T(8,128)S(1)} %get-tuple-element.124.grad, ...), custom_call_target="tpu_custom_call" | custom-call | flops 1000000000 | bytes 3000000 | tf_op jit(solution)/shard_map/pallas_call | solution.py:659
  182.1 2.0 %shard_map.139 = f32[4,1152,128]{2,1,0:T(8,128)} custom-call(s32[4]{0:T(128)S(1)} %pad_add_fusion.info.refs_0_, bf16[4,576,128]{2,1,0:T(8,128)(2,1)S(1)} %bitcast.18, bf16[4,576,128]{2,1,0:T(8,128)(2,1)S(1)} %collective-permute-done.17.other), custom_call_target="tpu_custom_call" | custom-call | flops 1000000 | bytes 1000000 | tf_op jit(solution)/shard_map/pallas_call | solution.py:659
  (18 shorter events, 0.0 us)
Async XLA Ops:
  2.3 9.5 %collective-permute-start = (bf16[4,8,32,128]{3,2,1,0:T(8,128)(2,1)S(1)}, bf16[4,8,32,128]{3,2,1,0:T(8,128)(2,1)S(1)}, u32[]{:S(2)}, u32[]{:S(2)}) collective-permute-start(bf16[4,8,32,128]{3,2,1,0:T(8,128)(2,1)S(1)} %get-tuple-element.71), channel_id=1, source_target_pairs={{0,4},{4,0},{8,12},{12,8},{1,5},{5,1},{9,13},{13,9},{2,6},{6,2},{1... | collective-permute-start | bytes 786440 | tf_op jit(solution)/shard_map/ppermute | solution.py:34
  4.5 7.3 %copy-start.3 = (bf16[4,16,32,128]{3,2,1,0:T(8,128)(2,1)S(1)}, bf16[4,16,32,128]{3,2,1,0:T(8,128)(2,1)}, u32[]{:S(2)}) copy-start(bf16[4,16,32,128]{3,2,1,0:T(8,128)(2,1)} %refs_0_.1) | copy-start | bytes 1572868
  4.5 10.8 %copy-start.1 = (s32[4,4,16,32,128]{4,3,2,1,0:T(8,128)S(1)}, s32[4,4,16,32,128]{4,3,2,1,0:T(8,128)}, u32[]{:S(2)}) copy-start(s32[4,4,16,32,128]{4,3,2,1,0:T(8,128)} %masks.3) | copy-start | bytes 12582916
  4.5 10.8 %copy-start.2 = (bf16[4,16,32,128]{3,2,1,0:T(8,128)(2,1)S(1)}, bf16[4,16,32,128]{3,2,1,0:T(8,128)(2,1)}, u32[]{:S(2)}) copy-start(bf16[4,16,32,128]{3,2,1,0:T(8,128)(2,1)} %cot.5) | copy-start | bytes 1572868
  4.5 7.3 %collective-permute-start.1 = (bf16[4,8,32,128]{3,2,1,0:T(8,128)(2,1)S(1)}, bf16[4,8,32,128]{3,2,1,0:T(8,128)(2,1)S(1)}, u32[]{:S(2)}, u32[]{:S(2)}) collective-permute-start(bf16[4,8,32,128]{3,2,1,0:T(8,128)(2,1)S(1)} %get-tuple-element.72), channel_id=1, source_target_pairs={{4,8},{8,4},{5,9},{9,5},{6,10},{10,6},{7,11},{11,7},{20,24},{24,20... | collective-permute-start | bytes 786440 | tf_op jit(solution)/shard_map/ppermute | solution.py:34
  7.3 8.5 %collective-permute-start.4 = (bf16[4,7,32,128]{3,2,1,0:T(8,128)(2,1)S(1)}, bf16[4,7,32,128]{3,2,1,0:T(8,128)(2,1)S(1)}, u32[]{:S(2)}, u32[]{:S(2)}) collective-permute-start(bf16[4,7,32,128]{3,2,1,0:T(8,128)(2,1)S(1)} %get-tuple-element.78), channel_id=1, source_target_pairs={{0,4},{4,0},{8,12},{12,8},{1,5},{5,1},{9,13},{13,9},{2,6},{6,2},{1... | collective-permute-start | bytes 688136 | tf_op jit(solution)/shard_map/ppermute | solution.py:34
  11.1 4.7 %collective-permute-start.5 = (bf16[4,7,32,128]{3,2,1,0:T(8,128)(2,1)S(1)}, bf16[4,7,32,128]{3,2,1,0:T(8,128)(2,1)S(1)}, u32[]{:S(2)}, u32[]{:S(2)}) collective-permute-start(bf16[4,7,32,128]{3,2,1,0:T(8,128)(2,1)S(1)} %get-tuple-element.79), channel_id=1, source_target_pairs={{4,8},{8,4},{5,9},{9,5},{6,10},{10,6},{7,11},{11,7},{20,24},{24,20... | collective-permute-start | bytes 688136 | tf_op jit(solution)/shard_map/ppermute | solution.py:34
  12.5 12.6 %collective-permute-start.2 = (bf16[4,32,8,128]{3,2,1,0:T(8,128)(2,1)S(1)}, bf16[4,32,8,128]{3,2,1,0:T(8,128)(2,1)S(1)}, u32[]{:S(2)}, u32[]{:S(2)}) collective-permute-start(bf16[4,32,8,128]{3,2,1,0:T(8,128)(2,1)S(1)} %get-tuple-element.74), channel_id=1, source_target_pairs={{0,1},{1,0},{2,3},{3,2},{4,5},{5,4},{6,7},{7,6},{8,9},{9,8},{10,11... | collective-permute-start | bytes 786440 | tf_op jit(solution)/shard_map/ppermute | solution.py:34
  14.1 11.0 %collective-permute-start.3 = (bf16[4,32,8,128]{3,2,1,0:T(8,128)(2,1)S(1)}, bf16[4,32,8,128]{3,2,1,0:T(8,128)(2,1)S(1)}, u32[]{:S(2)}, u32[]{:S(2)}) collective-permute-start(bf16[4,32,8,128]{3,2,1,0:T(8,128)(2,1)S(1)} %get-tuple-element.75), channel_id=1, source_target_pairs={{0,3},{1,2},{2,1},{3,0},{4,7},{5,6},{6,5},{7,4},{8,11},{9,10},{10,... | collective-permute-start | bytes 786440 | tf_op jit(solution)/shard_map/ppermute | solution.py:34
  15.7 9.5 %copy-start = (bf16[4,3,3,128,128]{4,3,2,1,0:T(8,128)(2,1)S(1)}, bf16[4,3,3,128,128]{4,3,2,1,0:T(8,128)(2,1)}, u32[]{:S(2)}) copy-start(bf16[4,3,3,128,128]{4,3,2,1,0:T(8,128)(2,1)} %param.8) | copy-start | bytes 3538948
  15.7 9.5 %copy-start.4 = (f32[4,128]{1,0:T(4,128)S(1)}, f32[4,128]{1,0:T(4,128)}, u32[]{:S(2)}) copy-start(f32[4,128]{1,0:T(4,128)} %gains.1) | copy-start | bytes 6148
  15.7 9.5 %copy-start.5 = (f32[4,128]{1,0:T(4,128)S(1)}, f32[4,128]{1,0:T(4,128)}, u32[]{:S(2)}) copy-start(f32[4,128]{1,0:T(4,128)} %refs_2_.13) | copy-start | bytes 6148
  15.7 9.5 %copy-start.6 = (f32[4,128]{1,0:T(4,128)S(1)}, f32[4,128]{1,0:T(4,128)}, u32[]{:S(2)}) copy-start(f32[4,128]{1,0:T(4,128)} %refs_3_.7) | copy-start | bytes 6148
  17.2 26.1 %collective-permute-start.8 = (bf16[4,17,32,128]{3,2,1,0:T(8,128)(2,1)S(1)}, bf16[4,17,32,128]{3,2,1,0:T(8,128)(2,1)S(1)}, u32[]{:S(2)}, u32[]{:S(2)}) collective-permute-start(bf16[4,17,32,128]{3,2,1,0:T(8,128)(2,1)S(1)} %get-tuple-element.87), channel_id=1, source_target_pairs={{0,4},{4,0},{8,12},{12,8},{1,5},{5,1},{9,13},{13,9},{2,6},{6,2},{1... | collective-permute-start | bytes 1671176 | tf_op jit(solution)/shard_map/ppermute | solution.py:34
  21.4 21.9 %collective-permute-start.9 = (bf16[4,17,32,128]{3,2,1,0:T(8,128)(2,1)S(1)}, bf16[4,17,32,128]{3,2,1,0:T(8,128)(2,1)S(1)}, u32[]{:S(2)}, u32[]{:S(2)}) collective-permute-start(bf16[4,17,32,128]{3,2,1,0:T(8,128)(2,1)S(1)} %get-tuple-element.88), channel_id=1, source_target_pairs={{4,8},{8,4},{5,9},{9,5},{6,10},{10,6},{7,11},{11,7},{20,24},{24,20... | collective-permute-start | bytes 1671176 | tf_op jit(solution)/shard_map/ppermute | solution.py:34
  22.0 9.8 %collective-permute-start.7 = (bf16[4,30,8,128]{3,2,1,0:T(8,128)(2,1)S(1)}, bf16[4,30,8,128]{3,2,1,0:T(8,128)(2,1)S(1)}, u32[]{:S(2)}, u32[]{:S(2)}) collective-permute-start(bf16[4,30,8,128]{3,2,1,0:T(8,128)(2,1)S(1)} %get-tuple-element.81), channel_id=1, source_target_pairs={{0,3},{1,2},{2,1},{3,0},{4,7},{5,6},{6,5},{7,4},{8,11},{9,10},{10,... | collective-permute-start | bytes 737288 | tf_op jit(solution)/shard_map/ppermute | solution.py:34
  25.2 6.7 %collective-permute-start.6 = (bf16[4,30,8,128]{3,2,1,0:T(8,128)(2,1)S(1)}, bf16[4,30,8,128]{3,2,1,0:T(8,128)(2,1)S(1)}, u32[]{:S(2)}, u32[]{:S(2)}) collective-permute-start(bf16[4,30,8,128]{3,2,1,0:T(8,128)(2,1)S(1)} %get-tuple-element.80.before), channel_id=1, source_target_pairs={{0,1},{1,0},{2,3},{3,2},{4,5},{5,4},{6,7},{7,6},{8,9},{9,8},{10,11... | collective-permute-start | bytes 737288 | tf_op jit(solution)/shard_map/ppermute | solution.py:34
  44.1 7.7 %collective-permute-start.11 = (bf16[4,28,8,128]{3,2,1,0:T(8,128)(2,1)S(1)}, bf16[4,28,8,128]{3,2,1,0:T(8,128)(2,1)S(1)}, u32[]{:S(2)}, u32[]{:S(2)}) collective-permute-start(bf16[4,28,8,128]{3,2,1,0:T(8,128)(2,1)S(1)} %get-tuple-element.91), channel_id=1, source_target_pairs={{0,3},{1,2},{2,1},{3,0},{4,7},{5,6},{6,5},{7,4},{8,11},{9,10},{10,... | collective-permute-start | bytes 688136 | tf_op jit(solution)/shard_map/ppermute | solution.py:34
  44.6 7.2 %collective-permute-start.10 = (bf16[4,28,8,128]{3,2,1,0:T(8,128)(2,1)S(1)}, bf16[4,28,8,128]{3,2,1,0:T(8,128)(2,1)S(1)}, u32[]{:S(2)}, u32[]{:S(2)}) collective-permute-start(bf16[4,28,8,128]{3,2,1,0:T(8,128)(2,1)S(1)} %get-tuple-element.89.refs_10_), channel_id=1, source_target_pairs={{0,1},{1,0},{2,3},{3,2},{4,5},{5,4},{6,7},{7,6},{8,9},{9,8},{10,11... | collective-permute-start | bytes 688136 | tf_op jit(solution)/shard_map/ppermute | solution.py:34
  61.5 15.7 %collective-permute-start.13 = (bf16[4,70,8,128]{3,2,1,0:T(8,128)(2,1)S(1)}, bf16[4,70,8,128]{3,2,1,0:T(8,128)(2,1)S(1)}, u32[]{:S(2)}, u32[]{:S(2)}) collective-permute-start(bf16[4,70,8,128]{3,2,1,0:T(8,128)(2,1)S(1)} %get-tuple-element.101), channel_id=1, source_target_pairs={{0,3},{1,2},{2,1},{3,0},{4,7},{5,6},{6,5},{7,4},{8,11},{9,10},{10,... | collective-permute-start | bytes 1720328 | tf_op jit(solution)/shard_map/ppermute | solution.py:34
  62.1 15.1 %collective-permute-start.12 = (bf16[4,70,8,128]{3,2,1,0:T(8,128)(2,1)S(1)}, bf16[4,70,8,128]{3,2,1,0:T(8,128)(2,1)S(1)}, u32[]{:S(2)}, u32[]{:S(2)}) collective-permute-start(bf16[4,70,8,128]{3,2,1,0:T(8,128)(2,1)S(1)} %get-tuple-element.98.refs_11_), channel_id=1, source_target_pairs={{0,1},{1,0},{2,3},{3,2},{4,5},{5,4},{6,7},{7,6},{8,9},{9,8},{10,11... | collective-permute-start | bytes 1720328 | tf_op jit(solution)/shard_map/ppermute | solution.py:34
  135.1 2.9 %collective-permute-start.16 = (f32[1152,128]{1,0:T(8,128)S(1)}, f32[1152,128]{1,0:T(8,128)S(1)}, u32[]{:S(2)}, u32[]{:S(2)}) collective-permute-start(f32[1152,128]{1,0:T(8,128)S(1)} %get-tuple-element.132), channel_id=1, source_target_pairs={{0,1},{1,0},{2,3},{3,2},{4,5},{5,4},{6,7},{7,6},{8,9},{9,8},{10,11... | collective-permute-start | bytes 1769480 | tf_op jit(solution)/shard_map/ppermute | solution.py:47
  135.5 2.1 %collective-permute-start.14 = (f32[576,128]{1,0:T(8,128)S(1)}, f32[576,128]{1,0:T(8,128)S(1)}, u32[]{:S(2)}, u32[]{:S(2)}) collective-permute-start(f32[576,128]{1,0:T(8,128)S(1)} %get-tuple-element.130), channel_id=1, source_target_pairs={{0,1},{1,0},{2,3},{3,2},{4,5},{5,4},{6,7},{7,6},{8,9},{9,8},{10,11... | collective-permute-start | bytes 884744 | tf_op jit(solution)/shard_map/ppermute | solution.py:47
  135.7 2.3 %collective-permute-start.15 = (f32[576,128]{1,0:T(8,128)S(1)}, f32[576,128]{1,0:T(8,128)S(1)}, u32[]{:S(2)}, u32[]{:S(2)}) collective-permute-start(f32[576,128]{1,0:T(8,128)S(1)} %get-tuple-element.131), channel_id=1, source_target_pairs={{0,1},{1,0},{2,3},{3,2},{4,5},{5,4},{6,7},{7,6},{8,9},{9,8},{10,11... | collective-permute-start | bytes 884744 | tf_op jit(solution)/shard_map/ppermute | solution.py:47
  177.4 4.7 %collective-permute-start.17 = (bf16[4,576,128]{2,1,0:T(8,128)(2,1)S(1)}, bf16[4,576,128]{2,1,0:T(8,128)(2,1)S(1)}, u32[]{:S(2)}, u32[]{:S(2)}) collective-permute-start(bf16[4,576,128]{2,1,0:T(8,128)(2,1)S(1)} %bitcast.17), channel_id=1, source_target_pairs={{0,1},{1,0},{2,3},{3,2},{4,5},{5,4},{6,7},{7,6},{8,9},{9,8},{10,11... | collective-permute-start | bytes 1769480 | tf_op jit(solution)/shard_map/ppermute | solution.py:47

commit v4 on v3

--- a/solution.py
+++ b/solution.py
@@ -76,9 +76,15 @@
     return pltpu.roll(value, 1, 1), value, pltpu.roll(value, width - 1, 1)
 
 
-def store_shifted(taps, slot, row, value, width):
+def store_shifted(taps, slot, row, value, width, inner=None):
     for s, part in enumerate(shifted(value, width)):
-        taps[slot, s, pl.ds(row, 2)] = part.astype(LOW)
+        part = part.astype(LOW)
+        taps[slot, s, pl.ds(row, 2)] = part
+        if inner is not None:
+            for k in range(2):
+                at = row + k - (EXT - 1)
+                if 0 <= at < inner.shape[2]:
+                    inner[s, slot, at] = part[k, 0 : inner.shape[3]]
 
 
 def lay_weights(kernel_ref, layer, back, out):
@@ -96,40 +102,97 @@
             out[at + 3 * LANES : at + 4 * LANES, LANES : 2 * LANES] = block
 
 
-def conv_pairs(taps, slot, weight_ref, row, pairs, cols):
-    parts = []
-    for t in range(4):
-        for s in range(3):
-            parts.append(jnp.stack([taps[slot, s, row - 1 + t + 2 * k, 0:cols, :] for k in range(pairs)]))
-    left = jnp.concatenate(parts, axis=-1).reshape(pairs * cols, 12 * LANES)
-    both = jnp.dot(left, weight_ref[...], preferred_element_type=F32)
+def even_parts(lo, hi, most):
+    pairs = (hi - lo) // 2
+    count = -(-pairs // most)
     out = []
-    for k in range(pairs):
-        for h in range(2):
-            out.append(both[k * cols : (k + 1) * cols, h * LANES : (h + 1) * LANES])
+    for k in range(count):
+        start, stop = pairs * k // count, pairs * (k + 1) // count
+        out.append((lo + 2 * start, stop - start))
     return out
 
 
-def chunks(lo, hi, pairs):
-    at = lo
-    while at < hi:
-        count = min(pairs, (hi - at) // 2)
-        yield at, count
-        at += 2 * count
-
-
-def pipeline(grids, lo, hi, pairs, prepare, convolve, after):
-    count = (hi - lo) // 2 + 1
-    for i in range(count):
-        prepare(0, lo - 1 + 2 * i, 0)
-    parts = list(chunks(lo, hi, pairs))
-    for g in range(grids):
-        for j, (at, size) in enumerate(parts):
-            if g + 1 < grids:
-                for i in range(count * j // len(parts), count * (j + 1) // len(parts)):
-                    prepare(g + 1, lo - 1 + 2 * i, (g + 1) % 2)
-            convolve(g, at, size, g % 2)
-        after(g, g % 2)
+def pipeline(grids, lo, hi, taps, weight, cols, prepare, emit, after, finish, extra=None, take=None, extra_totals=()):
+    parts = even_parts(lo, hi, 5)
+    count = len(parts)
+
+    def body(*refs):
+        totals, more = refs[: 2 * count], refs[2 * count :]
+        staged = [0, 0]
+
+        def push(unit, tile):
+            staged[unit] = 1 - staged[unit]
+            pltpu.matmul_push_rhs(tile, staged[unit], unit)
+            return staged[unit]
+
+        def operand(g, part, k):
+            start, size = parts[part]
+            halves = []
+            for unit in (2 * k, 2 * k + 1):
+                t, s = divmod(unit, 3)
+                halves.append(jnp.concatenate([taps[g, s, start - 1 + t + 2 * n, 0:cols, :] for n in range(size)], axis=0))
+            return jnp.concatenate(halves, axis=-1)
+
+        def product(first, unit, part, k):
+            def act():
+                at = push(unit, weight[k * 2 * LANES : (k + 1) * 2 * LANES, :])
+                pltpu.matmul_acc_lhs(totals[unit * count + part], operand(first + unit, part, k), load_staged_rhs=at)
+            return act
+
+        def collect(first, part):
+            def act():
+                start, size = parts[part]
+                for unit in range(2):
+                    both = pltpu.matmul_pop(totals[unit * count + part])
+                    for n in range(size):
+                        for h in range(2):
+                            emit(first + unit, start + 2 * n + h, both[n * cols : (n + 1) * cols, h * LANES : (h + 1) * LANES])
+            return act
+
+        def rows_before(part):
+            start, size = parts[part]
+            return start + 2 * size + 1
+
+        def ready(first, start, stop):
+            return [functools.partial(prepare, first + unit, r) for r in range(start, stop, 2) for unit in range(2)]
+
+        for task in ready(0, lo - 1, rows_before(0)):
+            task()
+        waiting = []
+
+        def run(steps, tasks):
+            done = 0
+            for n, step in enumerate(steps):
+                step()
+                if n == 3:
+                    while waiting:
+                        waiting.pop(0)()
+                while done < len(tasks) * (n + 1) // len(steps):
+                    tasks[done]()
+                    done += 1
+
+        for first in range(0, grids, 2):
+            last = first + 2 >= grids
+            ahead = [] if last else ready(first + 2, lo - 1, hi + 1)
+            if extra and last:
+                run(extra(first, push, more), [])
+                ahead = take(more)
+            for part in range(count):
+                tasks = []
+                if first == 0 and part + 1 < count:
+                    tasks += ready(0, rows_before(part), rows_before(part + 1))
+                tasks += ahead[len(ahead) * part // count : len(ahead) * (part + 1) // count]
+                run([product(first, unit, part, k) for k in range(6) for unit in range(2)], tasks)
+                waiting.append(collect(first, part))
+            waiting += [functools.partial(after, first + unit) for unit in range(2)]
+            if extra and not last:
+                run(extra(first, push, more), [])
+        while waiting:
+            waiting.pop(0)()
+        finish()
+
+    totals = [pltpu.ACC(unit)((size * cols, 2 * LANES), F32) for unit in range(2) for _, size in parts]
+    pl.run_scoped(body, *totals, *extra_totals)
 
 
 def guard(condition, act):
@@ -138,6 +201,10 @@
             act()
     else:
         pl.when(condition)(act)
+
+
+def gather(sums, k, value):
+    sums[k] = value if sums[k] is None else sums[k] + value
 
 
 def fold(value):
@@ -218,21 +285,21 @@
             out[g, h : h + rows] = src[g]
 
 
-def add_cols(geo, info, sources, starts, got_first, got_second, outs):
-    cols = geo["C"]
-
+def add_sides(geo, info, starts, got_first, got_second, outs):
     def place(low, high):
-        for src, out, at in zip(sources, outs, starts):
-            total = src.shape[1]
+        for out, at in zip(outs, starts):
+            total = out.shape[1]
             for g in range(geo["G"]):
                 right = high[g, at : at + total].astype(F32)
                 left = low[g, at : at + total].astype(F32)
-                out[g, :, cols:, :] = jnp.concatenate([right, left], axis=1).astype(LOW)
+                out[g] = jnp.concatenate([right, left], axis=1).astype(LOW)
 
     whichever(info[1], place, got_first, got_second)
-    for src, out in zip(sources, outs):
-        for g in range(geo["G"]):
-            out[g, :, 0:cols, :] = src[g]
+
+
+def across(pair, g, rows):
+    parts = [ref[g, rows].astype(F32) for ref in pair]
+    return jnp.concatenate(parts, axis=parts[0].ndim - 2)
 
 
 def field_edge_kernel(geo, info, x, first, second, sems):
@@ -295,6 +362,13 @@
     cut_rows(geo, info, [mask1, mask2, masked, cot], geo["heights"][2:], first, second)
 
 
+def weights_kernel(kernels, before, *outs):
+    del before
+    for layer in range(4):
+        lay_weights(kernels, layer, False, outs[layer])
+        lay_weights(kernels, layer, True, outs[4 + layer])
+
+
 def late_kernel(geo, info, mask1, mask2, masked, cot, first, second, before, *outs):
     del before
     add_rows(geo, info, [mask1, mask2, masked, cot], geo["heights"][2:], first, second, outs[0:4])
@@ -315,25 +389,24 @@
     grids, rows, devices, width, cols = geo["G"], geo["R"], geo["D"], geo["CE"], geo["C"]
     heights = geo["heights"]
     refs = list(refs)
-    info, gains, offsets, biases, kernels = (refs.pop(0) for _ in range(5))
+    info, gains, offsets, biases, weight = (refs.pop(0) for _ in range(5))
     if layer:
         stats, pre_in = refs.pop(0), refs.pop(0)
-    field = refs.pop(0) if layer == 2 else None
+    field = [refs.pop(0), refs.pop(0)] if layer == 2 else None
     members = geo["members"][layer]
     sources = [refs.pop(0) for _ in members]
     got = [refs.pop(0), refs.pop(0)]
     if layer in (1, 2):
         refs.pop(0)
     sums_out = refs.pop(0)
-    exts = [refs.pop(0) for _ in members]
+    side_outs = [refs.pop(0) for _ in members]
     pre_out, low_out = refs.pop(0), refs.pop(0)
     field_out = refs.pop(0) if layer == 2 else None
-    taps, weight, acts, acc = refs
+    taps, acts, acc = refs
     lo, hi = layer + 1, geo["RE"] - 1 - layer
 
-    lay_weights(kernels, layer, False, weight)
-    add_cols(geo, info, sources, geo["starts"][layer], *got, exts)
-    ext = exts[0]
+    add_sides(geo, info, geo["starts"][layer], *got, side_outs)
+    ext = [sources[0], side_outs[0]]
     if layer:
         center, inv = norm_consts(stats, devices)
         scale = inv * gains[layer - 1 : layer, :] * (1.0 / keep_rate)
@@ -341,46 +414,43 @@
         scale = 0.5 * scale
     bias = biases[layer : layer + 1, :]
     number = rows * cols
-    totals = [jnp.zeros((8, LANES), F32)] * grids
-
-    def prepare(g, r, slot):
+    totals = [None] * grids
+
+    def prepare(g, r):
         if layer == 0:
-            value = ext[g, pl.ds(r, 2)].astype(F32)
+            value = across(ext, g, pl.ds(r, 2))
         else:
             p = pre_in[g, pl.ds(r, 2)]
             part = p * scale
-            value = (part + part * jnp.tanh(0.5 * p) + shift) * ext[g, pl.ds(r - layer, 2)].astype(F32)
+            value = (part + part * jnp.tanh(0.5 * p) + shift) * across(ext, g, pl.ds(r - layer, 2))
             if layer == 2:
-                value = value + field[g, pl.ds(r, 2)].astype(F32)
+                value = value + across(field, g, pl.ds(r, 2))
 
                 def save():
                     field_out[g, pl.ds(r - (EXT - 1), 2)] = value[:, 0:cols, :]
 
                 guard((r >= EXT - 1) & (r < EXT + rows), save)
-        store_shifted(taps, slot, r, value, width)
-
-    def convolve(g, at, count, slot):
-        for k, part in enumerate(conv_pairs(taps, slot, weight, at, count, width)):
-            part = part + bias
-            pre_out[g, at + k] = part
-            if EXT <= at + k < EXT + rows:
-                act = silu(part[0:cols])
-                acts[slot, at + k - EXT] = act
-                totals[g] = totals[g] + fold(act)
-
-    def after(g, slot):
-        for s in range(3):
-            low_out[s, g] = taps[slot, s, EXT - 1 : EXT + 1 + rows, 0:cols, :]
+        store_shifted(taps, g, r, value, width, low_out)
+
+    def emit(g, r, part):
+        part = part + bias
+        pre_out[g, r] = part
+        if EXT <= r < EXT + rows:
+            act = silu(part[0:cols])
+            acts[g, r - EXT] = act
+            gather(totals, g, fold(act))
+
+    def after(g):
         mean = to_row(totals[g]) * (1.0 / number)
         square = jnp.zeros((8, LANES), F32)
         first = jnp.zeros((8, LANES), F32)
         second = jnp.zeros((8, LANES), F32)
         for k in range(rows):
-            act = acts[slot, k]
+            act = acts[g, k]
             apart = act - mean
             square = square + fold(jnp.square(apart))
             if layer == 3:
-                z = exts[1][g, heights[4] + k, 0:cols, :].astype(F32)
+                z = sources[1][g, heights[4] + k].astype(F32)
                 first = first + fold(z)
                 second = second + fold(z * apart)
             if layer == 0:
@@ -395,20 +465,22 @@
             acc[2 * grids + g : 2 * grids + g + 1] = to_row(first)
             acc[3 * grids + g : 3 * grids + g + 1] = to_row(second)
 
-    pipeline(grids, lo, hi, 5, prepare, convolve, after)
-    means = acc[0:grids]
-    middle = jnp.mean(means, axis=0, keepdims=True)
-    away = means - middle
-    spread = jnp.mean(acc[grids : 2 * grids] + jnp.square(away), axis=0, keepdims=True)
-    out = [middle, spread]
-    if layer == 3:
-        ones = acc[2 * grids : 3 * grids]
-        out.append(to_row(ones) * (1.0 / keep_rate))
-        out.append(to_row(acc[3 * grids : 4 * grids] + away * ones) * (1.0 / keep_rate))
-    if layer == 0:
-        out += [to_row(acc[2 * grids : 3 * grids]), to_row(acc[3 * grids : 4 * grids])]
-    for k, row in enumerate(out):
-        sums_out[:, k : k + 1, :] = jnp.broadcast_to(row[None], (devices, 1, LANES))
+    def finish():
+        means = acc[0:grids]
+        middle = jnp.mean(means, axis=0, keepdims=True)
+        away = means - middle
+        spread = jnp.mean(acc[grids : 2 * grids] + jnp.square(away), axis=0, keepdims=True)
+        out = [middle, spread]
+        if layer == 3:
+            ones = acc[2 * grids : 3 * grids]
+            out.append(to_row(ones) * (1.0 / keep_rate))
+            out.append(to_row(acc[3 * grids : 4 * grids] + away * ones) * (1.0 / keep_rate))
+        if layer == 0:
+            out += [to_row(acc[2 * grids : 3 * grids]), to_row(acc[3 * grids : 4 * grids])]
+        for k, row in enumerate(out):
+            sums_out[:, k : k + 1, :] = jnp.broadcast_to(row[None], (devices, 1, LANES))
+
+    pipeline(grids, lo, hi, taps, weight, width, prepare, emit, after, finish)
 
 
 def back_consts(layer, geo, stats, sums, gains):
@@ -462,45 +534,45 @@
     grids, rows, devices, width, cols = geo["G"], geo["R"], geo["D"], geo["CE"], geo["C"]
     heights = geo["heights"]
     refs = list(refs)
-    info, gains, offsets, kernels, stats, sums, pre, low = (refs.pop(0) for _ in range(8))
+    info, gains, offsets, weight, stats, sums, pre, low = (refs.pop(0) for _ in range(8))
     masked = keep_top = field = cot = z_in = None
     if layer == 3:
-        masked, keep_top, field = refs.pop(0), refs.pop(0), refs.pop(0)
+        masked, keep_top, field = [refs.pop(0), refs.pop(0)], refs.pop(0), refs.pop(0)
     else:
         z_in = refs.pop(0)
     if layer == 2:
-        cot = refs.pop(0)
-    keep, stats_below, pre_below = refs.pop(0), refs.pop(0), refs.pop(0)
+        cot = [refs.pop(0), refs.pop(0)]
+    keep = [refs.pop(0), refs.pop(0)]
+    stats_below, pre_below = refs.pop(0), refs.pop(0)
     sums_out, keep_half, send_half, z_out = (refs.pop(0) for _ in range(4))
     grad_out = refs.pop(0) if layer == 2 else None
     result = refs.pop(0) if layer == 3 else None
-    taps, weight, acc = refs[:3]
+    taps, term = refs[:2]
     if layer == 3:
-        result_out, (result, sems) = result, refs[3:]
+        result_out, (result, sems) = result, refs[2:]
         leaving = [pltpu.make_async_copy(result.at[g], result_out.at[g], sems.at[g]) for g in range(grids)]
     lo, hi = EXT - layer, EXT + rows + layer
     keep_off = EXT - heights[layer]
 
-    lay_weights(kernels, layer, True, weight)
     center, inv, scale, flat, tilt = back_consts(layer, geo, stats, sums, gains)
     first_row, last_row = info[2], info[3]
     center_b, inv_b = norm_consts(stats_below, devices)
-    sums_here = [jnp.zeros((8, LANES), F32)] * 4
+    sums_here = [None] * 4
 
     if layer == 3:
         lift = inv * gains[layer : layer + 1, :] * (1.0 / keep_rate)
         base = offsets[layer : layer + 1, :] * (1.0 / keep_rate) - center * lift
 
-    def prepare(g, r, slot):
+    def prepare(g, r):
         if layer == 3:
-            z = masked[g, pl.ds(r - (EXT - heights[4]), 2)].astype(F32)
+            z = across(masked, g, pl.ds(r - (EXT - heights[4]), 2))
         else:
             z = z_in[g, pl.ds(r, 2)]
         value, act = through(pre[g, pl.ds(r, 2)], z, scale, flat, tilt)
         if not (isinstance(r, int) and EXT <= r and r + 2 <= EXT + rows):
             real = [jnp.where((r + k >= first_row) & (r + k < last_row), 1.0, 0.0).astype(F32) for k in range(2)]
             value = jnp.stack([value[0] * real[0], value[1] * real[1]])
-        store_shifted(taps, slot, r, value, width)
+        store_shifted(taps, g, r, value, width)
         if layer == 3:
             def save():
                 y = (act[:, 0:cols] * lift + base) * keep_top[g, pl.ds(r - EXT, 2)].astype(F32)
@@ -508,44 +580,80 @@
 
             guard((r >= EXT) & (r < EXT + rows), save)
 
-    def convolve(g, at, count, slot):
-        for k, part in enumerate(conv_pairs(taps, slot, weight, at, count, width)):
-            r = at + k
-            inner = EXT <= r < EXT + rows
-            if layer == 2:
-                part = part + cot[g, r - (EXT - heights[5])].astype(F32)
-                if inner:
-                    grad_out[g, r - EXT] = part[0:cols]
-            z = part * keep[g, r - keep_off].astype(F32)
-            z_out[g, r] = z
+    def emit(g, r, part):
+        inner = EXT <= r < EXT + rows
+        if layer == 2:
+            part = part + across(cot, g, r - (EXT - heights[5]))
             if inner:
-                z = z[0:cols]
-                p = pre_below[g, r, 0:cols, :]
-                s = sigmoid(p)
-                sums_here[0] = sums_here[0] + fold(z)
-                act = p * s
-                sums_here[1] = sums_here[1] + fold(z * (act - center_b))
-                if layer == 1:
-                    sums_here[3] = sums_here[3] + fold(z * (s + act * (1.0 - s)))
-
-    def after(g, slot):
+                grad_out[g, r - EXT] = part[0:cols]
+        z = part * across(keep, g, r - keep_off)
+        z_out[g, r] = z
+        if inner:
+            z = z[0:cols]
+            p = pre_below[g, r, 0:cols, :]
+            s = sigmoid(p)
+            act = p * s
+            gather(sums_here, 0, fold(z))
+            gather(sums_here, 1, fold(z * (act - center_b)))
+            if layer == 1:
+                gather(sums_here, 3, fold(z * (s + act * (1.0 - s))))
+
+    def inside(g):
+        return taps[g, 1, EXT : EXT + rows, 0:cols, :].reshape(rows * cols, LANES)
+
+    def after(g):
         if layer == 3:
             leaving[g].start()
-        right = taps[slot, 1, EXT : EXT + rows, 0:cols, :].reshape(rows * cols, LANES)
-        sums_here[2] = sums_here[2] + fold(right.astype(F32))
-        weight_term(geo, low, g, right, acc)
-
-    pipeline(grids, lo, hi, 5, prepare, convolve, after)
-    split_halves(info, acc, keep_half, send_half)
-    out = [to_row(v) for v in sums_here]
-    out[0] = out[0] * (1.0 / keep_rate)
-    out[1] = out[1] * inv_b * (1.0 / keep_rate)
-    out[3] = out[3] * (1.0 / keep_rate)
-    for k in range(4 if layer == 1 else 3):
-        sums_out[:, k : k + 1, :] = jnp.broadcast_to(out[k][None], (devices, 1, LANES))
-    if layer == 3:
-        for c in leaving:
-            c.wait()
+        gather(sums_here, 2, fold(inside(g).astype(F32)))
+
+    def weight_steps(first, push, totals):
+        depth = 2 * LANES // cols
+        steps = []
+        for g in (first, first + 1):
+            for at in range(0, rows, depth):
+                turned = []
+
+                def act(n, g=g, at=at, turned=turned):
+                    if not turned:
+                        block = taps[g, 1, EXT + at : EXT + at + depth, 0:cols, :].reshape(2 * LANES, LANES)
+                        turned.append(block.T)
+                    halves = []
+                    for tap in (2 * n, 2 * n + 1):
+                        r, s = divmod(min(tap, 8), 3)
+                        halves.append(low[s, g, at + r : at + r + depth].reshape(2 * LANES, LANES))
+                    staged = push(n % 2, jnp.concatenate(halves, axis=-1))
+                    pltpu.matmul_acc_lhs(totals[n], turned[0], load_staged_rhs=staged)
+
+                steps += [functools.partial(act, n) for n in range(5)]
+        return steps
+
+    def take_term(totals):
+        def act(n):
+            both = pltpu.matmul_pop(totals[n])
+            for tap in range(2 * n, min(2 * n + 2, 9)):
+                at = (tap - 2 * n) * LANES
+                term[tap * LANES : (tap + 1) * LANES] = both[:, at : at + LANES].T
+
+        return [functools.partial(act, n) for n in range(5)]
+
+    def finish():
+        half = 9 * LANES // 2
+        start = pl.multiple_of((1 - info[1]) * half, 8)
+        keep_half[...] = term[pl.ds(start, half)]
+        send_half[...] = term[pl.ds(pl.multiple_of(half - start, 8), half)]
+        out = [to_row(sums_here[k]) for k in range(4 if layer == 1 else 3)]
+        out[0] = out[0] * (1.0 / keep_rate)
+        out[1] = out[1] * inv_b * (1.0 / keep_rate)
+        if layer == 1:
+            out[3] = out[3] * (1.0 / keep_rate)
+        for k, row in enumerate(out):
+            sums_out[:, k : k + 1, :] = jnp.broadcast_to(row[None], (devices, 1, LANES))
+        if layer == 3:
+            for c in leaving:
+                c.wait()
+
+    totals = [pltpu.ACC(n % 2)((LANES, 2 * LANES), F32) for n in range(5)]
+    pipeline(grids, lo, hi, taps, weight, width, prepare, emit, after, finish, weight_steps, take_term, totals)
 
 
 def first_weight_kernel(geo, *refs):
@@ -567,20 +675,17 @@
     split_halves(info, acc, keep_half, send_both.at[half : 2 * half])
 
 
-def input_grad_kernel(geo, kernels, dpre, grad, gains, *refs):
+def input_grad_kernel(geo, weight, dpre, grad, gains, *refs):
     grids, rows, width, cols = geo["G"], geo["R"], geo["CE"], geo["C"]
-    out, taps, weight, buffer, sems = refs[7], *refs[11:]
+    out, taps, buffer, sems = refs[7], *refs[11:]
     leaving = [pltpu.make_async_copy(buffer.at[g], out.at[g], sems.at[g]) for g in range(grids)]
-    lay_weights(kernels, 0, True, weight)
-
-    def prepare(g, r, slot):
-        store_shifted(taps, slot, r, dpre[g, pl.ds(r, 2)].astype(F32), width)
-
-    def convolve(g, at, count, slot):
-        for k, part in enumerate(conv_pairs(taps, slot, weight, at, count, cols)):
-            buffer[g, at + k - 1] = grad[g, at + k - 1] + part
-
-    pipeline(grids, 1, rows + 1, 8, prepare, convolve, lambda g, slot: leaving[g].start())
+    def prepare(g, r):
+        store_shifted(taps, g, r, dpre[g, pl.ds(r, 2)].astype(F32), width)
+
+    def emit(g, r, part):
+        buffer[g, r - 1] = grad[g, r - 1] + part
+
+    pipeline(grids, 1, rows + 1, taps, weight, cols, prepare, emit, lambda g: leaving[g].start(), lambda: None)
     gather_rows(geo, gains, *refs[0:7], *refs[8:11])
     for c in leaving:
         c.wait()
@@ -662,13 +767,13 @@
         out_specs=places,
         out_shape=shapes,
         scratch_shapes=[v if hasattr(v, "shape") and not isinstance(v, tuple) else pltpu.VMEM(*v) for v in scratch],
-        compiler_params=pltpu.CompilerParams(vmem_limit_bytes=12 * 2**20),
+        compiler_params=pltpu.CompilerParams(vmem_limit_bytes=10 * 2**20),
         cost_estimate=pl.CostEstimate(flops=flops, bytes_accessed=moved, transcendentals=0),
     )(*operands)
 
 
 def conv_scratch(geo, tall):
-    return [((2, 3, tall, geo["CE"], LANES), LOW), ((12 * LANES, 2 * LANES), LOW)]
+    return [((geo["G"], 3, tall, geo["CE"], LANES), LOW)]
 
 
 def forward_call(layer, geo, operands):
@@ -676,12 +781,12 @@
     kinds = 4 if layer in (0, 3) else 2
     outs = [((devices, kinds, LANES), F32)]
     for k in geo["members"][layer]:
-        outs.append(((grids, rows + 2 * geo["heights"][k], width, LANES), LOW))
+        outs.append(((grids, rows + 2 * geo["heights"][k], 2 * EXT, LANES), LOW))
     outs.append(((grids, rows_ext, width, LANES), F32))
     outs.append(((3, grids, rows + 2, cols, LANES), LOW))
     if layer == 2:
         outs.append(((grids, rows + 2, cols, LANES), F32))
-    scratch = conv_scratch(geo, rows_ext) + [((2, rows, cols, LANES), F32), ((kinds * grids, LANES), F32)]
+    scratch = conv_scratch(geo, rows_ext) + [((grids, rows, cols, LANES), F32), ((kinds * grids, LANES), F32)]
     return call(functools.partial(forward_kernel, layer, geo), operands, outs, scratch, 2 * 10**9, 8 * 10**6)
 
 
@@ -693,7 +798,7 @@
         outs.append(((grids, rows, cols, LANES), F32))
     if layer == 3:
         outs.append(((grids, rows, cols, LANES), LOW))
-    scratch = conv_scratch(geo, rows_ext) + [((LANES, 9 * LANES), F32)]
+    scratch = conv_scratch(geo, rows_ext) + [((9 * LANES, LANES), F32)]
     if layer == 3:
         scratch += [((grids, rows, cols, LANES), LOW), pltpu.SemaphoreType.DMA((grids,))]
     return call(
@@ -738,6 +843,7 @@
         [((2, grids, soon, cols, LANES), jnp.int32), pair_sems], outside=True,
     )
     soon_got = trade(outs, "lat", False)
+    weights = call(weights_kernel, [kernels, outs[0]], [((12 * LANES, 2 * LANES), LOW)] * 8, scalars=0)
     outs = call(
         functools.partial(tall_kernel, geo, heights[:1]), [info, inputs, *x_got],
         [block(rows + 2 * x_height, cols)] + [block(rows + 2 * x_height, EXT)] * 2,
@@ -760,11 +866,11 @@
     pres, lows, stats, exts = [None] * 4, [None] * 4, [None] * 4, [None] * 6
     field = order = None
     for layer in range(4):
-        operands = [info, gains, offsets, biases, kernels]
+        operands = [info, gains, offsets, biases, weights[layer]]
         if layer:
             operands += [stats[layer - 1], pres[layer - 1]]
         if layer == 2:
-            operands.append(exts[0])
+            operands += exts[0]
         operands += pieces[layer]
         if layer in (1, 2):
             operands.append(order)
@@ -786,8 +892,8 @@
             )
             pieces.append([*ends[1:4], *trade(edges, "lon", True)])
             order = edges[0]
-        for k in geo["members"][layer]:
-            exts[k] = outs.pop(0)
+        for n, k in enumerate(geo["members"][layer]):
+            exts[k] = [pieces[layer][n], outs.pop(0)]
         pres[layer], lows[layer] = outs.pop(0), outs.pop(0)
         if layer == 2:
             field = outs.pop(0)
@@ -797,11 +903,11 @@
     kept, got = [None] * 4, []
     z = grad = output = None
     for layer in (3, 2, 1):
-        operands = [info, gains, offsets, kernels, stats[layer], sums[layer], pres[layer], lows[layer]]
-        operands += [exts[4], low_masks[3], field] if layer == 3 else [z]
+        operands = [info, gains, offsets, weights[4 + layer], stats[layer], sums[layer], pres[layer], lows[layer]]
+        operands += [*exts[4], low_masks[3], field] if layer == 3 else [z]
         if layer == 2:
-            operands.append(exts[5])
-        operands += [exts[layer], stats[layer - 1], pres[layer - 1]]
+            operands += exts[5]
+        operands += [*exts[layer], stats[layer - 1], pres[layer - 1]]
         outs = backward_call(layer, geo, operands)
         sums[layer - 1] = to_all(outs[0])
         kept[layer], sent = outs[1], outs[2]
@@ -832,7 +938,7 @@
     small = ((4, LANES), F32)
     field_like = ((grids, rows, cols, LANES), F32)
     input_grad, bias_grad, gain_grad, offset_grad = call(
-        functools.partial(input_grad_kernel, geo), [kernels, dpre, grad, gains] + stats + sums[:3],
+        functools.partial(input_grad_kernel, geo), [weights[4], dpre, grad, gains] + stats + sums[:3],
         [field_like] + [small] * 3, conv_scratch(geo, rows + 2) + [field_like, pltpu.SemaphoreType.DMA((grids,))],
         10**9, 3 * 10**6, scalars=0, final=(0,), small=(1, 2, 3),
     )

time: 185 us -> 182 us (0.984)
  Pallas kernels: 47.4 us -> 43.5 us
    pallas_call x22 -> x23, Pallas kernels: 47.4 us -> 43.5 us  [call(): pl.pallas_call(kernel, in_specs=specs, out_specs=places, out_shape=shapes...]
where the time goes in v4:
time: 182 us; the launch traced here: 181 us
  blocking collectives  107 us (59%)
  Pallas kernels  43.5 us (24%)
  starting transfers between devices  21.6 us (12%)
  waiting for transfers between devices  7.93 us (4%)
    all_to_all x7, blocking collectives, to_all(): return lax.all_to_all(rows, EVERY, 0, 0)  67.9 us
    pallas_call x23, Pallas kernels, call(): pl.pallas_call(kernel, in_specs=specs, out_specs=places, out_shape=shapes...  43.5 us
    all_to_all x2, blocking collectives, to_half(): return lax.all_to_all(rows, EVERY, 0, 0, axis_index_groups=groups)  39.2 us
    ppermute x7, starting transfers between devices, trade(): lax.ppermute(pair[0], axis, first)  11.2 us
    ppermute x7, starting transfers between devices, trade(): lax.ppermute(pair[1], axis, second)  7.49 us
    ppermute x7, waiting for transfers between devices, trade(): lax.ppermute(pair[1], axis, second)  5.17 us
  transfers between devices with their start and end apart: 18, of which 5 were waited for; matrix products, arithmetic and copies ran while one was open for 0% of the time, Pallas kernels for 11%

profile of v4, /device:TPU:1, one launch (start us, length us, event | category | flops | bytes accessed | tf_op | source)
XLA Modules:
  0.0 181.4 jit_solution(9668250667652147669)
XLA Ops:
  0.6 0.0 copy-start.2
  0.7 0.0 copy-start
  0.7 0.1 pad_add_fusion.info.refs_0_
  0.8 1.9 %shard_map.120 = (bf16[4,8,32,128]{3,2,1,0:T(8,128)(2,1)S(1)}, bf16[4,8,32,128]{3,2,1,0:T(8,128)(2,1)S(1)}) custom-call(s32[4]{0:T(128)S(1)} %pad_add_fusion.info.refs_0_, bf16[4,16,32,128]{3,2,1,0:T(8,128)(2,1)} %refs_0_.1), custom_call_target="tpu_custom_call" | custom-call | flops 1000000 | bytes 1000000 | tf_op jit(solution)/shard_map/pallas_call | solution.py:764
  2.7 2.2 %collective-permute-start = (bf16[4,8,32,128]{3,2,1,0:T(8,128)(2,1)S(1)}, bf16[4,8,32,128]{3,2,1,0:T(8,128)(2,1)S(1)}, u32[]{:S(2)}, u32[]{:S(2)}) collective-permute-start(bf16[4,8,32,128]{3,2,1,0:T(8,128)(2,1)S(1)} %get-tuple-element.85), channel_id=1, source_target_pairs={{0,4},{4,0},{8,12},{12,8},{1,5},{5,1},{9,13},{13,9},{2,6},{6,2},{1... | collective-permute-start | bytes 786440 | tf_op jit(solution)/shard_map/ppermute | solution.py:34
  4.9 0.7 collective-permute-start.1
  5.5 1.8 shard_map.118
  7.3 0.7 collective-permute-start.5
  8.0 5.1 %collective-permute-start.4 = (bf16[4,7,32,128]{3,2,1,0:T(8,128)(2,1)S(1)}, bf16[4,7,32,128]{3,2,1,0:T(8,128)(2,1)S(1)}, u32[]{:S(2)}, u32[]{:S(2)}) collective-permute-start(bf16[4,7,32,128]{3,2,1,0:T(8,128)(2,1)S(1)} %get-tuple-element.79.before), channel_id=1, source_target_pairs={{0,4},{4,0},{8,12},{12,8},{1,5},{5,1},{9,13},{13,9},{2,6},{6,2},{1... | collective-permute-start | bytes 688136 | tf_op jit(solution)/shard_map/ppermute | solution.py:34
  13.1 0.0 collective-permute-done.refs_1_
  13.1 0.7 shard_map.121
  13.9 1.6 collective-permute-start.2
  15.5 1.2 collective-permute-start.3
  16.7 0.3 shard_map.123
  17.0 0.0 copy-start.4
  17.0 0.0 copy-start.5
  17.0 0.0 copy-start.6
  17.0 0.0 collective-permute-done.5.refs_2_
  17.1 0.8 collective-permute-done.4.refs_1_
  17.8 0.7 shard_map.124
  18.5 0.6 shard_map.126
  19.2 2.1 %collective-permute-start.8 = (bf16[4,17,32,128]{3,2,1,0:T(8,128)(2,1)S(1)}, bf16[4,17,32,128]{3,2,1,0:T(8,128)(2,1)S(1)}, u32[]{:S(2)}, u32[]{:S(2)}) collective-permute-start(bf16[4,17,32,128]{3,2,1,0:T(8,128)(2,1)S(1)} %get-tuple-element.100), channel_id=1, source_target_pairs={{0,4},{4,0},{8,12},{12,8},{1,5},{5,1},{9,13},{13,9},{2,6},{6,2},{1... | collective-permute-start | bytes 1671176 | tf_op jit(solution)/shard_map/ppermute | solution.py:34
  21.3 0.7 collective-permute-start.9
  21.9 3.2 %collective-permute-start.7 = (bf16[4,30,8,128]{3,2,1,0:T(8,128)(2,1)S(1)}, bf16[4,30,8,128]{3,2,1,0:T(8,128)(2,1)S(1)}, u32[]{:S(2)}, u32[]{:S(2)}) collective-permute-start(bf16[4,30,8,128]{3,2,1,0:T(8,128)(2,1)S(1)} %get-tuple-element.94), channel_id=1, source_target_pairs={{0,3},{1,2},{2,1},{3,0},{4,7},{5,6},{6,5},{7,4},{8,11},{9,10},{10,... | collective-permute-start | bytes 737288 | tf_op jit(solution)/shard_map/ppermute | solution.py:34
  25.1 0.0 collective-permute-done.2.refs_6_
  25.1 0.0 collective-permute-start.6
  25.1 0.9 shard_map.119
  26.0 3.9 %shard_map.122 = (f32[32,4,128]{2,1,0:T(4,128)S(1)}, bf16[4,32,16,128]{3,2,1,0:T(8,128)(2,1)S(1)}, f32[4,32,48,128]{3,2,1,0:T(8,128)S(1)}, bf16[3,4,18,32,128]{4,3,2,1,0:T(8,128)(2,1)S(1)}) custom-call(s32[4]{0:T(128)S(1)} %pad_add_fusion.info.refs_0_, f32[4,128]{1,0:T(4,128)S(1)} %copy-done.4, f32[4,128]{1,0:T(4,128)S(1)} %copy-done.5, ...), custom_call_target="tpu_custom_call" | custom-call | flops 2000000000 | bytes 8000000 | tf_op jit(solution)/shard_map/pallas_call | solution.py:764
  30.0 1.9 %collective-permute-done.7.second.refs_9_ = bf16[4,30,8,128]{3,2,1,0:T(8,128)(2,1)S(1)} collective-permute-done((bf16[4,30,8,128]{3,2,1,0:T(8,128)(2,1)S(1)}, bf16[4,30,8,128]{3,2,1,0:T(8,128)(2,1)S(1)}, u32[]{:S(2)}, u32[]{:S(2)}) %collective-permute-start.7) | collective-permute-done | bytes 245792 | tf_op jit(solution)/shard_map/ppermute | solution.py:34
  31.9 11.5 %all_to_all.45.before.refs_5_.refs_11_.refs_2_.refs_0_ = f32[32,4,128]{2,1,0:T(4,128)S(1)} all-to-all(f32[32,4,128]{2,1,0:T(4,128)S(1)} %shard_map.125), channel_id=1, replica_groups=mesh['batch'=2,'lat'=4,'lon'=4] {'batch','lat','lon'}, dimensions={0} | all-to-all | bytes 131072 | tf_op jit(solution)/shard_map/all_to_all | solution.py:38
  43.4 0.0 collective-permute-done.8.first
  43.4 0.0 collective-permute-done.9.second
  43.4 0.8 shard_map.127
  44.2 0.5 collective-permute-start.11
  44.7 0.1 collective-permute-start.10
  44.9 3.7 %shard_map.128 = (f32[32,2,128]{2,1,0:T(2,128)S(1)}, bf16[4,30,16,128]{3,2,1,0:T(8,128)(2,1)S(1)}, f32[4,32,48,128]{3,2,1,0:T(8,128)S(1)}, bf16[3,4,18,32,128]{4,3,2,1,0:T(8,128)(2,1)S(1)}) custom-call(s32[4]{0:T(128)S(1)} %pad_add_fusion.info.refs_0_, f32[4,128]{1,0:T(4,128)S(1)} %copy-done.4, f32[4,128]{1,0:T(4,128)S(1)} %copy-done.5, ...), custom_call_target="tpu_custom_call" | custom-call | flops 2000000000 | bytes 8000000 | tf_op jit(solution)/shard_map/pallas_call | solution.py:764
  48.6 3.3 %collective-permute-done.11.second.refs_11_ = bf16[4,28,8,128]{3,2,1,0:T(8,128)(2,1)S(1)} collective-permute-done((bf16[4,28,8,128]{3,2,1,0:T(8,128)(2,1)S(1)}, bf16[4,28,8,128]{3,2,1,0:T(8,128)(2,1)S(1)}, u32[]{:S(2)}, u32[]{:S(2)}) %collective-permute-start.11) | collective-permute-done | bytes 229408 | tf_op jit(solution)/shard_map/ppermute | solution.py:34
  51.9 8.9 %all_to_all.46.before.refs_5_.refs_13_.refs_4_.refs_1_ = f32[32,2,128]{2,1,0:T(2,128)S(1)} all-to-all(f32[32,2,128]{2,1,0:T(2,128)S(1)} %shard_map.129), channel_id=1, replica_groups=mesh['batch'=2,'lat'=4,'lon'=4] {'batch','lat','lon'}, dimensions={0} | all-to-all | bytes 65536 | tf_op jit(solution)/shard_map/all_to_all | solution.py:38
  60.8 0.7 shard_map.130
  61.6 0.6 collective-permute-start.13
  62.2 0.1 collective-permute-start.12
  62.3 3.9 %shard_map.131 = (f32[32,2,128]{2,1,0:T(2,128)S(1)}, bf16[4,28,16,128]{3,2,1,0:T(8,128)(2,1)S(1)}, f32[4,32,48,128]{3,2,1,0:T(8,128)S(1)}, bf16[3,4,18,32,128]{4...) custom-call(s32[4]{0:T(128)S(1)} %pad_add_fusion.info.refs_0_, f32[4,128]{1,0:T(4,128)S(1)} %copy-done.4, ...), custom_call_target="tpu_custom_call" | custom-call | flops 2000000000 | bytes 8000000 | tf_op jit(solution)/shard_map/pallas_call | solution.py:764
  66.2 11.1 %all_to_all.47.refs_5_.refs_14_.refs_4_.refs_2_ = f32[32,2,128]{2,1,0:T(2,128)S(1)} all-to-all(f32[32,2,128]{2,1,0:T(2,128)S(1)} %get-tuple-element.112), channel_id=1, replica_groups=mesh['batch'=2,'lat'=4,'lon'=4] {'batch','lat','lon'}, dimensions={0} | all-to-all | bytes 65536 | tf_op jit(solution)/shard_map/all_to_all | solution.py:38
  77.3 3.5 %shard_map.132 = (f32[32,4,128]{2,1,0:T(4,128)S(1)}, bf16[4,26,16,128]{3,2,1,0:T(8,128)(2,1)S(1)}, bf16[4,24,16,128]{3,2,1,0:T(8,128)(2,1)S(1)}, bf16[4,20,16,12...) custom-call(s32[4]{0:T(128)S(1)} %pad_add_fusion.info.refs_0_, ...), custom_call_target="tpu_custom_call" | custom-call | flops 2000000000 | bytes 8000000 | tf_op jit(solution)/shard_map/pallas_call | solution.py:764
  80.8 9.1 %all_to_all.48.refs_4_.refs_5_.refs_3_ = f32[32,4,128]{2,1,0:T(4,128)S(1)} all-to-all(f32[32,4,128]{2,1,0:T(4,128)S(1)} %get-tuple-element.115), channel_id=1, replica_groups=mesh['batch'=2,'lat'=4,'lon'=4] {'batch','lat','lon'}, dimensions={0} | all-to-all | bytes 131072 | tf_op jit(solution)/shard_map/all_to_all | solution.py:38
  89.9 5.0 %shard_map.133 = (f32[32,3,128]{2,1,0:T(4,128)S(1)}, f32[576,128]{1,0:T(8,128)S(1)}, f32[576,128]{1,0:T(8,128)S(1)}, f32[4,32,48,128]{3,2,1,0:T(8,128)S(1)}, bf16[4,16,32,128]{3,2,1,0:T(8,128)(2,1)}) custom-call(s32[4]{0:T(128)S(1)} %pad_add_fusion.info.refs_0_, f32[4,128]{1,0:T(4,128)S(1)} %copy-done.4, f32[4,128]{1,0:T(4,128)S(1)} %copy-done.5, ...), custom_call_target="tpu_custom_call" | custom-call | flops 3000000000 | bytes 8000000 | tf_op jit(solution)/shard_map/pallas_call | solution.py:764
  94.9 9.1 %all_to_all.49.refs_5_.refs_6_ = f32[32,3,128]{2,1,0:T(4,128)S(1)} all-to-all(f32[32,3,128]{2,1,0:T(4,128)S(1)} %get-tuple-element.126), channel_id=1, replica_groups=mesh['batch'=2,'lat'=4,'lon'=4] {'batch','lat','lon'}, dimensions={0} | all-to-all | bytes 98304 | tf_op jit(solution)/shard_map/all_to_all | solution.py:38
  104.0 4.0 %shard_map.134 = (f32[32,3,128]{2,1,0:T(4,128)S(1)}, f32[576,128]{1,0:T(8,128)S(1)}, f32[576,128]{1,0:T(8,128)S(1)}, f32[4,32,48,128]{3,2,1,0:T(8,128)S(1)}, f32[4,16,32,128]{3,2,1,0:T(8,128)S(1)}) custom-call(s32[4]{0:T(128)S(1)} %pad_add_fusion.info.refs_0_, f32[4,128]{1,0:T(4,128)S(1)} %copy-done.4, f32[4,128]{1,0:T(4,128)S(1)} %copy-done.5, ...), custom_call_target="tpu_custom_call" | custom-call | flops 3000000000 | bytes 8000000 | tf_op jit(solution)/shard_map/pallas_call | solution.py:764
  108.0 9.1 %all_to_all.50.refs_5_ = f32[32,3,128]{2,1,0:T(4,128)S(1)} all-to-all(f32[32,3,128]{2,1,0:T(4,128)S(1)} %get-tuple-element.131), channel_id=1, replica_groups=mesh['batch'=2,'lat'=4,'lon'=4] {'batch','lat','lon'}, dimensions={0} | all-to-all | bytes 98304 | tf_op jit(solution)/shard_map/all_to_all | solution.py:38
  117.1 3.8 %shard_map.135 = (f32[32,4,128]{2,1,0:T(4,128)S(1)}, f32[576,128]{1,0:T(8,128)S(1)}, f32[576,128]{1,0:T(8,128)S(1)}, f32[4,32,48,128]{3,2,1,0:T(8,128)S(1)}) custom-call(s32[4]{0:T(128)S(1)} %pad_add_fusion.info.refs_0_, f32[4,128]{1,0:T(4,128)S(1)} %copy-done.4, f32[4,128]{1,0:T(4,128)S(1)} %copy-done.5, bf16[1536,256]{1,0:T(8,128)(2,1)S(1)} %get-tuple-element.124.refs_3_, ...), custom_call_target="tpu_custom_call" | custom-call | flops 3000000000 | bytes 8000000 | tf_op jit(solution)/shard_map/pallas_call | solution.py:764
  120.9 9.1 %all_to_all.51.refs_3_.refs_4_ = f32[32,4,128]{2,1,0:T(4,128)S(1)} all-to-all(f32[32,4,128]{2,1,0:T(4,128)S(1)} %get-tuple-element.135), channel_id=1, replica_groups=mesh['batch'=2,'lat'=4,'lon'=4] {'batch','lat','lon'}, dimensions={0} | all-to-all | bytes 131072 | tf_op jit(solution)/shard_map/all_to_all | solution.py:38
  130.0 2.3 %shard_map.136 = (f32[576,128]{1,0:T(8,128)S(1)}, f32[1152,128]{1,0:T(8,128)S(1)}, bf16[4,18,48,128]{3,2,1,0:T(8,128)(2,1)S(1)}) custom-call(s32[4]{0:T(128)S(1)} %pad_add_fusion.info.refs_0_, f32[4,128]{1,0:T(4,128)S(1)} %copy-done.4, f32[32,4,128]{2,1,0:T(4,128)S(1)} %all_to_all.45.before.refs_5_.refs_11_.refs_2_.refs_0_, ...), custom_call_target="tpu_custom_call" | custom-call | flops 1000000000 | bytes 8000000 | tf_op jit(solution)/shard_map/pallas_call | solution.py:764
  132.4 0.5 collective-permute-start.16
  132.8 0.1 collective-permute-start.14
  132.9 0.4 collective-permute-start.15
  133.3 1.5 collective-permute-done.14.refs_4_
  134.9 0.4 collective-permute-done.15.refs_5_
  135.3 0.1 shard_map.138
  135.4 19.4 %all_to_all.52.got = bf16[16,144,128]{2,1,0:T(8,128)(2,1)S(1)} all-to-all(bf16[16,144,128]{2,1,0:T(8,128)(2,1)S(1)} %bitcast.8), channel_id=1, replica_groups={{0,2,4,6,8,10,12,14,16,18,20,22,24,26,28,30},{1,3,5,7,9,11,13,15,17,19,..., dimensions={0} | all-to-all | bytes 1179648 | tf_op jit(solution)/shard_map/all_to_all | solution.py:43
  154.8 0.1 shard_map.139
  154.9 19.8 %all_to_all.53 = bf16[16,144,128]{2,1,0:T(8,128)(2,1)S(1)} all-to-all(bf16[16,144,128]{2,1,0:T(8,128)(2,1)S(1)} %shard_map.139), channel_id=1, replica_groups={{0,2,4,6,8,10,12,14,16,18,20,22,24,26,28,30},{1,3,5,7,9,11,13,15,17,19,..., dimensions={0} | all-to-all | bytes 1179648 | tf_op jit(solution)/shard_map/all_to_all | solution.py:43
  174.7 1.9 %collective-permute-start.17 = (bf16[4,576,128]{2,1,0:T(8,128)(2,1)S(1)}, bf16[4,576,128]{2,1,0:T(8,128)(2,1)S(1)}, u32[]{:S(2)}, u32[]{:S(2)}) collective-permute-start(bf16[4,576,128]{2,1,0:T(8,128)(2,1)S(1)} %bitcast.9), channel_id=1, source_target_pairs={{0,1},{1,0},{2,3},{3,2},{4,5},{5,4},{6,7},{7,6},{8,9},{9,8},{10,11... | collective-permute-start | bytes 1769480 | tf_op jit(solution)/shard_map/ppermute | solution.py:47
  176.6 2.6 %shard_map.137 = (f32[4,16,32,128]{3,2,1,0:T(8,128)}, f32[4,128]{1,0:T(4,128)}, f32[4,128]{1,0:T(4,128)}, f32[4,128]{1,0:T(4,128)}) custom-call(bf16[1536,256]{1,0:T(8,128)(2,1)S(1)} %get-tuple-element.123.weight, bf16[4,18,48,128]{3,2,1,0:T(8,128)(2,1)S(1)} %get-tuple-element.139.dpre, f32[4,16,32,128]{3,2,1,0:T(8,128)S(1)} %get-tuple-element.140.grad, ...), custom_call_target="tpu_custom_call" | custom-call | flops 1000000000 | bytes 3000000 | tf_op jit(solution)/shard_map/pallas_call | solution.py:764
  179.2 2.0 %shard_map.140 = f32[4,1152,128]{2,1,0:T(8,128)} custom-call(s32[4]{0:T(128)S(1)} %pad_add_fusion.info.refs_0_, bf16[4,576,128]{2,1,0:T(8,128)(2,1)S(1)} %bitcast.10, bf16[4,576,128]{2,1,0:T(8,128)(2,1)S(1)} %collective-permute-done.17.other), custom_call_target="tpu_custom_call" | custom-call | flops 1000000 | bytes 1000000 | tf_op jit(solution)/shard_map/pallas_call | solution.py:764
  (19 shorter events, 0.0 us)
Async XLA Ops:
  0.6 12.5 %copy-start.2 = (bf16[4,16,32,128]{3,2,1,0:T(8,128)(2,1)S(1)}, bf16[4,16,32,128]{3,2,1,0:T(8,128)(2,1)}, u32[]{:S(2)}) copy-start(bf16[4,16,32,128]{3,2,1,0:T(8,128)(2,1)} %refs_0_.1) | copy-start | bytes 1572868
  0.6 16.0 %copy-start.1 = (bf16[4,16,32,128]{3,2,1,0:T(8,128)(2,1)S(1)}, bf16[4,16,32,128]{3,2,1,0:T(8,128)(2,1)}, u32[]{:S(2)}) copy-start(bf16[4,16,32,128]{3,2,1,0:T(8,128)(2,1)} %cot.5) | copy-start | bytes 1572868
  0.7 16.0 %copy-start = (s32[4,4,16,32,128]{4,3,2,1,0:T(8,128)S(1)}, s32[4,4,16,32,128]{4,3,2,1,0:T(8,128)}, u32[]{:S(2)}) copy-start(s32[4,4,16,32,128]{4,3,2,1,0:T(8,128)} %masks.3) | copy-start | bytes 12582916
  2.7 10.5 %collective-permute-start = (bf16[4,8,32,128]{3,2,1,0:T(8,128)(2,1)S(1)}, bf16[4,8,32,128]{3,2,1,0:T(8,128)(2,1)S(1)}, u32[]{:S(2)}, u32[]{:S(2)}) collective-permute-start(bf16[4,8,32,128]{3,2,1,0:T(8,128)(2,1)S(1)} %get-tuple-element.85), channel_id=1, source_target_pairs={{0,4},{4,0},{8,12},{12,8},{1,5},{5,1},{9,13},{13,9},{2,6},{6,2},{1... | collective-permute-start | bytes 786440 | tf_op jit(solution)/shard_map/ppermute | solution.py:34
  4.9 8.3 %collective-permute-start.1 = (bf16[4,8,32,128]{3,2,1,0:T(8,128)(2,1)S(1)}, bf16[4,8,32,128]{3,2,1,0:T(8,128)(2,1)S(1)}, u32[]{:S(2)}, u32[]{:S(2)}) collective-permute-start(bf16[4,8,32,128]{3,2,1,0:T(8,128)(2,1)S(1)} %get-tuple-element.86), channel_id=1, source_target_pairs={{4,8},{8,4},{5,9},{9,5},{6,10},{10,6},{7,11},{11,7},{20,24},{24,20... | collective-permute-start | bytes 786440 | tf_op jit(solution)/shard_map/ppermute | solution.py:34
  7.3 9.7 %collective-permute-start.5 = (bf16[4,7,32,128]{3,2,1,0:T(8,128)(2,1)S(1)}, bf16[4,7,32,128]{3,2,1,0:T(8,128)(2,1)S(1)}, u32[]{:S(2)}, u32[]{:S(2)}) collective-permute-start(bf16[4,7,32,128]{3,2,1,0:T(8,128)(2,1)S(1)} %get-tuple-element.92), channel_id=1, source_target_pairs={{4,8},{8,4},{5,9},{9,5},{6,10},{10,6},{7,11},{11,7},{20,24},{24,20... | collective-permute-start | bytes 688136 | tf_op jit(solution)/shard_map/ppermute | solution.py:34
  8.0 9.8 %collective-permute-start.4 = (bf16[4,7,32,128]{3,2,1,0:T(8,128)(2,1)S(1)}, bf16[4,7,32,128]{3,2,1,0:T(8,128)(2,1)S(1)}, u32[]{:S(2)}, u32[]{:S(2)}) collective-permute-start(bf16[4,7,32,128]{3,2,1,0:T(8,128)(2,1)S(1)} %get-tuple-element.79.before), channel_id=1, source_target_pairs={{0,4},{4,0},{8,12},{12,8},{1,5},{5,1},{9,13},{13,9},{2,6},{6,2},{1... | collective-permute-start | bytes 688136 | tf_op jit(solution)/shard_map/ppermute | solution.py:34
  13.9 11.2 %collective-permute-start.2 = (bf16[4,32,8,128]{3,2,1,0:T(8,128)(2,1)S(1)}, bf16[4,32,8,128]{3,2,1,0:T(8,128)(2,1)S(1)}, u32[]{:S(2)}, u32[]{:S(2)}) collective-permute-start(bf16[4,32,8,128]{3,2,1,0:T(8,128)(2,1)S(1)} %get-tuple-element.88), channel_id=1, source_target_pairs={{0,1},{1,0},{2,3},{3,2},{4,5},{5,4},{6,7},{7,6},{8,9},{9,8},{10,11... | collective-permute-start | bytes 786440 | tf_op jit(solution)/shard_map/ppermute | solution.py:34
  15.5 9.7 %copy-start.3 = (bf16[4,3,3,128,128]{4,3,2,1,0:T(8,128)(2,1)S(1)}, bf16[4,3,3,128,128]{4,3,2,1,0:T(8,128)(2,1)}, u32[]{:S(2)}) copy-start(bf16[4,3,3,128,128]{4,3,2,1,0:T(8,128)(2,1)} %param.8) | copy-start | bytes 3538948
  15.5 10.6 %collective-permute-start.3 = (bf16[4,32,8,128]{3,2,1,0:T(8,128)(2,1)S(1)}, bf16[4,32,8,128]{3,2,1,0:T(8,128)(2,1)S(1)}, u32[]{:S(2)}, u32[]{:S(2)}) collective-permute-start(bf16[4,32,8,128]{3,2,1,0:T(8,128)(2,1)S(1)} %get-tuple-element.89), channel_id=1, source_target_pairs={{0,3},{1,2},{2,1},{3,0},{4,7},{5,6},{6,5},{7,4},{8,11},{9,10},{10,... | collective-permute-start | bytes 786440 | tf_op jit(solution)/shard_map/ppermute | solution.py:34
  17.0 9.0 %copy-start.4 = (f32[4,128]{1,0:T(4,128)S(1)}, f32[4,128]{1,0:T(4,128)}, u32[]{:S(2)}) copy-start(f32[4,128]{1,0:T(4,128)} %gains.1) | copy-start | bytes 6148
  17.0 9.0 %copy-start.5 = (f32[4,128]{1,0:T(4,128)S(1)}, f32[4,128]{1,0:T(4,128)}, u32[]{:S(2)}) copy-start(f32[4,128]{1,0:T(4,128)} %refs_2_.13) | copy-start | bytes 6148
  17.0 9.0 %copy-start.6 = (f32[4,128]{1,0:T(4,128)S(1)}, f32[4,128]{1,0:T(4,128)}, u32[]{:S(2)}) copy-start(f32[4,128]{1,0:T(4,128)} %refs_3_.7) | copy-start | bytes 6148
  19.2 24.2 %collective-permute-start.8 = (bf16[4,17,32,128]{3,2,1,0:T(8,128)(2,1)S(1)}, bf16[4,17,32,128]{3,2,1,0:T(8,128)(2,1)S(1)}, u32[]{:S(2)}, u32[]{:S(2)}) collective-permute-start(bf16[4,17,32,128]{3,2,1,0:T(8,128)(2,1)S(1)} %get-tuple-element.100), channel_id=1, source_target_pairs={{0,4},{4,0},{8,12},{12,8},{1,5},{5,1},{9,13},{13,9},{2,6},{6,2},{1... | collective-permute-start | bytes 1671176 | tf_op jit(solution)/shard_map/ppermute | solution.py:34
  21.3 22.1 %collective-permute-start.9 = (bf16[4,17,32,128]{3,2,1,0:T(8,128)(2,1)S(1)}, bf16[4,17,32,128]{3,2,1,0:T(8,128)(2,1)S(1)}, u32[]{:S(2)}, u32[]{:S(2)}) collective-permute-start(bf16[4,17,32,128]{3,2,1,0:T(8,128)(2,1)S(1)} %get-tuple-element.101), channel_id=1, source_target_pairs={{4,8},{8,4},{5,9},{9,5},{6,10},{10,6},{7,11},{11,7},{20,24},{24,20... | collective-permute-start | bytes 1671176 | tf_op jit(solution)/shard_map/ppermute | solution.py:34
  21.9 9.9 %collective-permute-start.7 = (bf16[4,30,8,128]{3,2,1,0:T(8,128)(2,1)S(1)}, bf16[4,30,8,128]{3,2,1,0:T(8,128)(2,1)S(1)}, u32[]{:S(2)}, u32[]{:S(2)}) collective-permute-start(bf16[4,30,8,128]{3,2,1,0:T(8,128)(2,1)S(1)} %get-tuple-element.94), channel_id=1, source_target_pairs={{0,3},{1,2},{2,1},{3,0},{4,7},{5,6},{6,5},{7,4},{8,11},{9,10},{10,... | collective-permute-start | bytes 737288 | tf_op jit(solution)/shard_map/ppermute | solution.py:34
  25.1 6.7 %collective-permute-start.6 = (bf16[4,30,8,128]{3,2,1,0:T(8,128)(2,1)S(1)}, bf16[4,30,8,128]{3,2,1,0:T(8,128)(2,1)S(1)}, u32[]{:S(2)}, u32[]{:S(2)}) collective-permute-start(bf16[4,30,8,128]{3,2,1,0:T(8,128)(2,1)S(1)} %get-tuple-element.93.before), channel_id=1, source_target_pairs={{0,1},{1,0},{2,3},{3,2},{4,5},{5,4},{6,7},{7,6},{8,9},{9,8},{10,11... | collective-permute-start | bytes 737288 | tf_op jit(solution)/shard_map/ppermute | solution.py:34
  44.2 7.7 %collective-permute-start.11 = (bf16[4,28,8,128]{3,2,1,0:T(8,128)(2,1)S(1)}, bf16[4,28,8,128]{3,2,1,0:T(8,128)(2,1)S(1)}, u32[]{:S(2)}, u32[]{:S(2)}) collective-permute-start(bf16[4,28,8,128]{3,2,1,0:T(8,128)(2,1)S(1)} %get-tuple-element.104), channel_id=1, source_target_pairs={{0,3},{1,2},{2,1},{3,0},{4,7},{5,6},{6,5},{7,4},{8,11},{9,10},{10,... | collective-permute-start | bytes 688136 | tf_op jit(solution)/shard_map/ppermute | solution.py:34
  44.7 7.2 %collective-permute-start.10 = (bf16[4,28,8,128]{3,2,1,0:T(8,128)(2,1)S(1)}, bf16[4,28,8,128]{3,2,1,0:T(8,128)(2,1)S(1)}, u32[]{:S(2)}, u32[]{:S(2)}) collective-permute-start(bf16[4,28,8,128]{3,2,1,0:T(8,128)(2,1)S(1)} %get-tuple-element.102.refs_10_), channel_id=1, source_target_pairs={{0,1},{1,0},{2,3},{3,2},{4,5},{5,4},{6,7},{7,6},{8,9},{9,8},{10,11... | collective-permute-start | bytes 688136 | tf_op jit(solution)/shard_map/ppermute | solution.py:34
  61.6 15.7 %collective-permute-start.13 = (bf16[4,70,8,128]{3,2,1,0:T(8,128)(2,1)S(1)}, bf16[4,70,8,128]{3,2,1,0:T(8,128)(2,1)S(1)}, u32[]{:S(2)}, u32[]{:S(2)}) collective-permute-start(bf16[4,70,8,128]{3,2,1,0:T(8,128)(2,1)S(1)} %get-tuple-element.114), channel_id=1, source_target_pairs={{0,3},{1,2},{2,1},{3,0},{4,7},{5,6},{6,5},{7,4},{8,11},{9,10},{10,... | collective-permute-start | bytes 1720328 | tf_op jit(solution)/shard_map/ppermute | solution.py:34
  62.2 15.1 %collective-permute-start.12 = (bf16[4,70,8,128]{3,2,1,0:T(8,128)(2,1)S(1)}, bf16[4,70,8,128]{3,2,1,0:T(8,128)(2,1)S(1)}, u32[]{:S(2)}, u32[]{:S(2)}) collective-permute-start(bf16[4,70,8,128]{3,2,1,0:T(8,128)(2,1)S(1)} %get-tuple-element.111.refs_12_), channel_id=1, source_target_pairs={{0,1},{1,0},{2,3},{3,2},{4,5},{5,4},{6,7},{7,6},{8,9},{9,8},{10,11... | collective-permute-start | bytes 1720328 | tf_op jit(solution)/shard_map/ppermute | solution.py:34
  132.4 2.9 %collective-permute-start.16 = (f32[1152,128]{1,0:T(8,128)S(1)}, f32[1152,128]{1,0:T(8,128)S(1)}, u32[]{:S(2)}, u32[]{:S(2)}) collective-permute-start(f32[1152,128]{1,0:T(8,128)S(1)} %get-tuple-element.148), channel_id=1, source_target_pairs={{0,1},{1,0},{2,3},{3,2},{4,5},{5,4},{6,7},{7,6},{8,9},{9,8},{10,11... | collective-permute-start | bytes 1769480 | tf_op jit(solution)/shard_map/ppermute | solution.py:47
  132.8 2.1 %collective-permute-start.14 = (f32[576,128]{1,0:T(8,128)S(1)}, f32[576,128]{1,0:T(8,128)S(1)}, u32[]{:S(2)}, u32[]{:S(2)}) collective-permute-start(f32[576,128]{1,0:T(8,128)S(1)} %get-tuple-element.146), channel_id=1, source_target_pairs={{0,1},{1,0},{2,3},{3,2},{4,5},{5,4},{6,7},{7,6},{8,9},{9,8},{10,11... | collective-permute-start | bytes 884744 | tf_op jit(solution)/shard_map/ppermute | solution.py:47
  132.9 2.4 %collective-permute-start.15 = (f32[576,128]{1,0:T(8,128)S(1)}, f32[576,128]{1,0:T(8,128)S(1)}, u32[]{:S(2)}, u32[]{:S(2)}) collective-permute-start(f32[576,128]{1,0:T(8,128)S(1)} %get-tuple-element.147), channel_id=1, source_target_pairs={{0,1},{1,0},{2,3},{3,2},{4,5},{5,4},{6,7},{7,6},{8,9},{9,8},{10,11... | collective-permute-start | bytes 884744 | tf_op jit(solution)/shard_map/ppermute | solution.py:47
  174.7 4.5 %collective-permute-start.17 = (bf16[4,576,128]{2,1,0:T(8,128)(2,1)S(1)}, bf16[4,576,128]{2,1,0:T(8,128)(2,1)S(1)}, u32[]{:S(2)}, u32[]{:S(2)}) collective-permute-start(bf16[4,576,128]{2,1,0:T(8,128)(2,1)S(1)} %bitcast.9), channel_id=1, source_target_pairs={{0,1},{1,0},{2,3},{3,2},{4,5},{5,4},{6,7},{7,6},{8,9},{9,8},{10,11... | collective-permute-start | bytes 1769480 | tf_op jit(solution)/shard_map/ppermute | solution.py:47

commit v5 on v4

--- a/solution.py
+++ b/solution.py
@@ -287,11 +287,13 @@
 
 def add_sides(geo, info, starts, got_first, got_second, outs):
     def place(low, high):
-        for out, at in zip(outs, starts):
+        for n, (out, at) in enumerate(zip(outs, starts)):
             total = out.shape[1]
             for g in range(geo["G"]):
                 right = high[g, at : at + total].astype(F32)
                 left = low[g, at : at + total].astype(F32)
+                if n == 2:
+                    right, left = pltpu.roll(right, EXT // 2, 1), pltpu.roll(left, EXT // 2, 1)
                 out[g] = jnp.concatenate([right, left], axis=1).astype(LOW)
 
     whichever(info[1], place, got_first, got_second)
@@ -362,11 +364,10 @@
     cut_rows(geo, info, [mask1, mask2, masked, cot], geo["heights"][2:], first, second)
 
 
-def weights_kernel(kernels, before, *outs):
+def weights_kernel(which, kernels, before, *outs):
     del before
-    for layer in range(4):
-        lay_weights(kernels, layer, False, outs[layer])
-        lay_weights(kernels, layer, True, outs[4 + layer])
+    for (layer, back), out in zip(which, outs):
+        lay_weights(kernels, layer, back, out)
 
 
 def late_kernel(geo, info, mask1, mask2, masked, cot, first, second, before, *outs):
@@ -377,12 +378,27 @@
 
 def last_kernel(geo, info, tall2, tall3, tall4, before, first, second):
     del before
-    cut_cols(geo, info, [tall2, tall3, tall4], first, second)
-
-
-def gate_kernel(sums, first, second, out):
-    del first, second
-    out[...] = sums[...]
+    cols, above, shared = geo["C"], tall2.shape[1], tall4.shape[1]
+    extra = (tall3.shape[1] - shared) // 2
+    cut_cols(geo, info, [tall2], first, second)
+
+    def give(out):
+        def act(low):
+            at = pl.ds(0, EXT) if low else pl.ds(cols - EXT, EXT)
+            place = lax.broadcasted_iota(jnp.int32, (shared, EXT, LANES), 1)
+            near = place < EXT // 2 if low else place >= EXT // 2
+            for g in range(geo["G"]):
+                out[g, above : above + tall3.shape[1]] = tall3[g, :, at]
+                mine = tall3[g, extra : extra + shared, at].astype(F32)
+                other = pltpu.roll(tall4[g, :, at].astype(F32), EXT // 2, 1)
+                out[g, above + extra : above + extra + shared] = jnp.where(near, mine, other).astype(LOW)
+        return act
+
+    both_ways(info[1], give(first), give(second))
+
+
+def gate_kernel(sums, *refs):
+    refs[-1][...] = sums[...]
 
 
 def forward_kernel(layer, geo, *refs):
@@ -677,7 +693,8 @@
 
 def input_grad_kernel(geo, weight, dpre, grad, gains, *refs):
     grids, rows, width, cols = geo["G"], geo["R"], geo["CE"], geo["C"]
-    out, taps, buffer, sems = refs[7], *refs[11:]
+    out, taps, buffer, sems = refs[7], *refs[12:]
+    refs[11][...] = jnp.zeros((4, LANES), F32)
     leaving = [pltpu.make_async_copy(buffer.at[g], out.at[g], sems.at[g]) for g in range(grids)]
     def prepare(g, r):
         store_shifted(taps, g, r, dpre[g, pl.ds(r, 2)].astype(F32), width)
@@ -692,7 +709,7 @@
 
 
 def share_kernel(*refs):
-    third, second, both, out = refs[4:]
+    third, second, both, _, out = refs[4:]
     half = 9 * LANES // 2
     gots = [both[half : 2 * half], both[0:half], second[...], third[...]]
     for k in range(4):
@@ -704,24 +721,15 @@
     out[...] = jnp.broadcast_to(total.astype(LOW)[None], out.shape)
 
 
-def join_kernel(geo, info, mine, other, out, buffer, sems):
+def join_kernel(geo, other, info, block, *refs):
+    out, buffer, sems = refs[-3:]
     half = 9 * LANES // 2
-    leaving = [pltpu.make_async_copy(buffer.at[k], out.at[k], sems.at[k]) for k in range(4)]
-
-    def place(low, high):
-        for k in range(4):
-            buffer[k, 0:half] = low[k].astype(F32)
-            buffer[k, half:] = high[k].astype(F32)
-            leaving[k].start()
-
-    @pl.when(info[1] == 1)
-    def _():
-        place(mine, other)
-
-    @pl.when(info[1] == 0)
-    def _():
-        place(other, mine)
-
+    upper = info[1] if other else 1 - info[1]
+    start = pl.multiple_of(upper * half, 8)
+    leaving = [pltpu.make_async_copy(buffer.at[k], out.at[k, pl.ds(start, half)], sems.at[k]) for k in range(4)]
+    for k in range(4):
+        buffer[k] = block[k].astype(F32)
+        leaving[k].start()
     for c in leaving:
         c.wait()
 
@@ -747,12 +755,12 @@
             bias_out[0:1] = inv * gains[0:1, :] * (total[3:4] - flat * one / pixels - lifted * two / pixels)
 
 
-def call(kernel, operands, outs, scratch=(), flops=10**6, moved=10**6, scalars=1, final=(), small=(), outside=False):
+def call(kernel, operands, outs, scratch=(), flops=10**6, moved=10**6, scalars=1, final=(), small=(), outside=False, onto=None):
     space = pl.BlockSpec(memory_space=pltpu.VMEM)
     specs = [pl.BlockSpec(memory_space=pltpu.SMEM)] * scalars
     operands = list(operands)
     for k in range(scalars, len(operands)):
-        if outside:
+        if outside or k == onto:
             specs.append(pl.BlockSpec(memory_space=pltpu.HBM))
             operands[k] = pltpu.with_memory_space_constraint(operands[k], pltpu.HBM)
         else:
@@ -765,6 +773,7 @@
         kernel,
         in_specs=specs,
         out_specs=places,
+        input_output_aliases={} if onto is None else {onto: 0},
         out_shape=shapes,
         scratch_shapes=[v if hasattr(v, "shape") and not isinstance(v, tuple) else pltpu.VMEM(*v) for v in scratch],
         compiler_params=pltpu.CompilerParams(vmem_limit_bytes=10 * 2**20),
@@ -811,9 +820,8 @@
     grids, rows, cols, _ = inputs.shape
     devices = lax.axis_size("batch") * lax.axis_size("lat") * lax.axis_size("lon")
     heights = [EXT, 7, 6, 5, 4, 2]
-    starts = [0]
-    for k in (3, 4):
-        starts.append(starts[-1] + rows + 2 * heights[k])
+    above = rows + 2 * heights[3]
+    starts = [0, above, above + heights[4] - heights[5]]
     geo = dict(
         G=grids, R=rows, C=cols, D=devices, RE=rows + 2 * EXT, CE=cols + 2 * EXT, heights=heights,
         starts=[[0], [0], [0], starts], members=[[0], [1], [2], [3, 4, 5]],
@@ -843,7 +851,12 @@
         [((2, grids, soon, cols, LANES), jnp.int32), pair_sems], outside=True,
     )
     soon_got = trade(outs, "lat", False)
-    weights = call(weights_kernel, [kernels, outs[0]], [((12 * LANES, 2 * LANES), LOW)] * 8, scalars=0)
+
+    def weights_for(which, before):
+        outs = [((12 * LANES, 2 * LANES), LOW)] * len(which)
+        return list(call(functools.partial(weights_kernel, which), [kernels, before], outs, scalars=0))
+
+    weights = weights_for([(0, False), (1, False)], outs[0])
     outs = call(
         functools.partial(tall_kernel, geo, heights[:1]), [info, inputs, *x_got],
         [block(rows + 2 * x_height, cols)] + [block(rows + 2 * x_height, EXT)] * 2,
@@ -877,7 +890,11 @@
         outs = list(forward_call(layer, geo, operands))
         part = outs.pop(0)
         if layer < 2:
-            (part,) = call(gate_kernel, [part] + pieces[layer + 1][1:], [(part.shape, F32)], scalars=0)
+            beside = []
+            if layer == 0:
+                weights += weights_for([(2, False), (3, False), (0, True), (1, True), (2, True), (3, True)], part)
+                beside = weights[2:]
+            (part,) = call(gate_kernel, [part] + pieces[layer + 1][1:] + beside, [(part.shape, F32)], scalars=0)
         stats[layer] = to_all(part)
         if layer == 0:
             ends = call(
@@ -888,7 +905,7 @@
             order = ends[4]
         if layer == 1:
             edges = call(
-                functools.partial(last_kernel, geo), [info, *ends[1:4], stats[1]], [block(sum(talls[1:]), EXT)] * 2
+                functools.partial(last_kernel, geo), [info, *ends[1:4], stats[1]], [block(talls[1] + talls[2], EXT)] * 2
             )
             pieces.append([*ends[1:4], *trade(edges, "lon", True)])
             order = edges[0]
@@ -926,21 +943,25 @@
     )
     got.append(to_pair(sent))
 
-    (shares,) = call(share_kernel, kept + got, [((4 * half, LANES), LOW)], scalars=0)
+    small = ((4, LANES), F32)
+    field_like = ((grids, rows, cols, LANES), F32)
+    input_grad, bias_grad, gain_grad, offset_grad, order = call(
+        functools.partial(input_grad_kernel, geo), [weights[4], dpre, grad, gains] + stats + sums[:3],
+        [field_like] + [small] * 4, conv_scratch(geo, rows + 2) + [field_like, pltpu.SemaphoreType.DMA((grids,))],
+        10**9, 3 * 10**6, scalars=0, final=(0,), small=(1, 2, 3),
+    )
+
+    (shares,) = call(share_kernel, kept + got + [order], [((4 * half, LANES), LOW)], scalars=0)
     slots = (devices // 2, 4 * half // (devices // 2), LANES)
     arrived = to_half(shares.reshape(slots), devices)
     (mine,) = call(functools.partial(total_kernel, devices), [arrived], [(slots, LOW)], scalars=0)
     mine = to_half(mine, devices).reshape(4, half, LANES)
+    other = to_pair(mine)
+    whole = [((4, 9 * LANES, LANES), F32)]
+    scratch = [((4, half, LANES), F32), pltpu.SemaphoreType.DMA((4,))]
+    (kernel_grad,) = call(functools.partial(join_kernel, geo, False), [info, mine], whole, scratch, final=(0,))
     (kernel_grad,) = call(
-        functools.partial(join_kernel, geo), [info, mine, to_pair(mine)], [((4, 9 * LANES, LANES), F32)],
-        [((4, 9 * LANES, LANES), F32), pltpu.SemaphoreType.DMA((4,))], final=(0,),
-    )
-    small = ((4, LANES), F32)
-    field_like = ((grids, rows, cols, LANES), F32)
-    input_grad, bias_grad, gain_grad, offset_grad = call(
-        functools.partial(input_grad_kernel, geo), [weights[4], dpre, grad, gains] + stats + sums[:3],
-        [field_like] + [small] * 3, conv_scratch(geo, rows + 2) + [field_like, pltpu.SemaphoreType.DMA((grids,))],
-        10**9, 3 * 10**6, scalars=0, final=(0,), small=(1, 2, 3),
+        functools.partial(join_kernel, geo, True), [info, other, kernel_grad], whole, scratch, final=(0,), onto=2
     )
     return (output, input_grad, kernel_grad.reshape(4, 3, 3, LANES, LANES), bias_grad, gain_grad, offset_grad)
 

time: 182 us -> 179 us (0.984)
  blocking collectives: 107 us -> 105 us
    all_to_all x7, blocking collectives: 67.9 us -> 65.9 us  [to_all(): return lax.all_to_all(rows, EVERY, 0, 0)]
    ppermute x4, waiting for transfers between devices: 1.97 us -> 0.03 us  [to_pair(): return lax.ppermute(block, 'lon', partners('lon', True)[0])]
    pallas_call x23 -> x25, Pallas kernels: 43.5 us -> 44.5 us  [call(): pl.pallas_call(kernel, in_specs=specs, out_specs=places, input_output_ali...]
  transfers between devices with their start and end apart: 18 -> 18, of which waited for: 5 -> 3; matrix products, arithmetic and copies ran while one was open for 0% -> 0% of each run, Pallas kernels for 11% -> 11%
where the time goes in v5:
time: 179 us
  blocking collectives  105 us (59%)
  Pallas kernels  44.5 us (25%)
  starting transfers between devices  21.6 us (12%)
  waiting for transfers between devices  6.16 us (3%)
    all_to_all x7, blocking collectives, to_all(): return lax.all_to_all(rows, EVERY, 0, 0)  65.9 us
    pallas_call x25, Pallas kernels, call(): pl.pallas_call(kernel, in_specs=specs, out_specs=places, input_output_ali...  44.5 us
    all_to_all x2, blocking collectives, to_half(): return lax.all_to_all(rows, EVERY, 0, 0, axis_index_groups=groups)  39.2 us
    ppermute x7, starting transfers between devices, trade(): lax.ppermute(pair[0], axis, first)  11.2 us
    ppermute x7, starting transfers between devices, trade(): lax.ppermute(pair[1], axis, second)  7.49 us
    ppermute x7, waiting for transfers between devices, trade(): lax.ppermute(pair[1], axis, second)  5.34 us
  transfers between devices with their start and end apart: 18, of which 3 were waited for; matrix products, arithmetic and copies ran while one was open for 0% of the time, Pallas kernels for 11%

profile of v5, /device:TPU:1, one launch (start us, length us, event | category | flops | bytes accessed | tf_op | source)
XLA Modules:
  0.0 178.6 jit_solution(14856184143053774689)
XLA Ops:
  0.6 0.0 copy-start.3
  0.7 0.0 copy-start
  0.7 0.1 pad_add_fusion.info.refs_0_
  0.8 1.9 %shard_map.120 = (bf16[4,8,32,128]{3,2,1,0:T(8,128)(2,1)S(1)}, bf16[4,8,32,128]{3,2,1,0:T(8,128)(2,1)S(1)}) custom-call(s32[4]{0:T(128)S(1)} %pad_add_fusion.info.refs_0_, bf16[4,16,32,128]{3,2,1,0:T(8,128)(2,1)} %refs_0_.1), custom_call_target="tpu_custom_call" | custom-call | flops 1000000 | bytes 1000000 | tf_op jit(solution)/shard_map/pallas_call | solution.py:772
  2.7 2.2 %collective-permute-start = (bf16[4,8,32,128]{3,2,1,0:T(8,128)(2,1)S(1)}, bf16[4,8,32,128]{3,2,1,0:T(8,128)(2,1)S(1)}, u32[]{:S(2)}, u32[]{:S(2)}) collective-permute-start(bf16[4,8,32,128]{3,2,1,0:T(8,128)(2,1)S(1)} %get-tuple-element.82), channel_id=1, source_target_pairs={{0,4},{4,0},{8,12},{12,8},{1,5},{5,1},{9,13},{13,9},{2,6},{6,2},{1... | collective-permute-start | bytes 786440 | tf_op jit(solution)/shard_map/ppermute | solution.py:34
  4.9 0.7 collective-permute-start.1
  5.5 1.8 shard_map.118
  7.3 0.7 collective-permute-start.5
  8.0 5.1 %collective-permute-start.4 = (bf16[4,7,32,128]{3,2,1,0:T(8,128)(2,1)S(1)}, bf16[4,7,32,128]{3,2,1,0:T(8,128)(2,1)S(1)}, u32[]{:S(2)}, u32[]{:S(2)}) collective-permute-start(bf16[4,7,32,128]{3,2,1,0:T(8,128)(2,1)S(1)} %get-tuple-element.80.before), channel_id=1, source_target_pairs={{0,4},{4,0},{8,12},{12,8},{1,5},{5,1},{9,13},{13,9},{2,6},{6,2},{1... | collective-permute-start | bytes 688136 | tf_op jit(solution)/shard_map/ppermute | solution.py:34
  13.1 0.0 collective-permute-done.refs_1_
  13.1 0.0 collective-permute-done.1.refs_2_
  13.1 0.7 shard_map.121
  13.9 1.6 collective-permute-start.2
  15.5 1.2 collective-permute-start.3
  16.7 0.3 shard_map.124
  17.0 0.0 copy-start.4
  17.0 0.0 copy-start.5
  17.0 0.0 copy-start.6
  17.0 0.0 collective-permute-done.5.refs_2_
  17.1 0.8 collective-permute-done.4.refs_1_
  17.8 0.7 shard_map.125
  18.5 0.6 shard_map.127
  19.2 2.1 %collective-permute-start.8 = (bf16[4,17,32,128]{3,2,1,0:T(8,128)(2,1)S(1)}, bf16[4,17,32,128]{3,2,1,0:T(8,128)(2,1)S(1)}, u32[]{:S(2)}, u32[]{:S(2)}) collective-permute-start(bf16[4,17,32,128]{3,2,1,0:T(8,128)(2,1)S(1)} %get-tuple-element.104), channel_id=1, source_target_pairs={{0,4},{4,0},{8,12},{12,8},{1,5},{5,1},{9,13},{13,9},{2,6},{6,2},{1... | collective-permute-start | bytes 1671176 | tf_op jit(solution)/shard_map/ppermute | solution.py:34
  21.3 0.7 collective-permute-start.9
  21.9 3.2 %collective-permute-start.7 = (bf16[4,30,8,128]{3,2,1,0:T(8,128)(2,1)S(1)}, bf16[4,30,8,128]{3,2,1,0:T(8,128)(2,1)S(1)}, u32[]{:S(2)}, u32[]{:S(2)}) collective-permute-start(bf16[4,30,8,128]{3,2,1,0:T(8,128)(2,1)S(1)} %get-tuple-element.95), channel_id=1, source_target_pairs={{0,3},{1,2},{2,1},{3,0},{4,7},{5,6},{6,5},{7,4},{8,11},{9,10},{10,... | collective-permute-start | bytes 737288 | tf_op jit(solution)/shard_map/ppermute | solution.py:34
  25.1 0.2 shard_map.119
  25.4 3.8 %shard_map.122 = (f32[32,4,128]{2,1,0:T(4,128)S(1)}, bf16[4,32,16,128]{3,2,1,0:T(8,128)(2,1)S(1)}, f32[4,32,48,128]{3,2,1,0:T(8,128)S(1)}, bf16[3,4,18,32,128]{4,3,2,1,0:T(8,128)(2,1)S(1)}) custom-call(s32[4]{0:T(128)S(1)} %pad_add_fusion.info.refs_0_, f32[4,128]{1,0:T(4,128)S(1)} %copy-done.4, f32[4,128]{1,0:T(4,128)S(1)} %copy-done.5, ...), custom_call_target="tpu_custom_call" | custom-call | flops 2000000000 | bytes 8000000 | tf_op jit(solution)/shard_map/pallas_call | solution.py:772
  29.2 0.7 shard_map.123
  29.9 1.9 %collective-permute-done.7.refs_1_.refs_9_ = bf16[4,30,8,128]{3,2,1,0:T(8,128)(2,1)S(1)} collective-permute-done((bf16[4,30,8,128]{3,2,1,0:T(8,128)(2,1)S(1)}, bf16[4,30,8,128]{3,2,1,0:T(8,128)(2,1)S(1)}, u32[]{:S(2)}, u32[]{:S(2)}) %collective-permute-start.7) | collective-permute-done | bytes 245792 | tf_op jit(solution)/shard_map/ppermute | solution.py:34
  31.8 0.0 collective-permute-done.6.refs_0_.refs_8_
  31.9 11.5 %all_to_all.45.before.refs_5_.refs_11_.refs_2_.refs_0_ = f32[32,4,128]{2,1,0:T(4,128)S(1)} all-to-all(f32[32,4,128]{2,1,0:T(4,128)S(1)} %shard_map.126), channel_id=1, replica_groups=mesh['batch'=2,'lat'=4,'lon'=4] {'batch','lat','lon'}, dimensions={0} | all-to-all | bytes 131072 | tf_op jit(solution)/shard_map/all_to_all | solution.py:38
  43.4 0.8 shard_map.128
  44.2 0.5 collective-permute-start.11
  44.7 0.1 collective-permute-start.10
  44.9 3.7 %shard_map.129 = (f32[32,2,128]{2,1,0:T(2,128)S(1)}, bf16[4,30,16,128]{3,2,1,0:T(8,128)(2,1)S(1)}, f32[4,32,48,128]{3,2,1,0:T(8,128)S(1)}, bf16[3,4,18,32,128]{4,3,2,1,0:T(8,128)(2,1)S(1)}) custom-call(s32[4]{0:T(128)S(1)} %pad_add_fusion.info.refs_0_, f32[4,128]{1,0:T(4,128)S(1)} %copy-done.4, f32[4,128]{1,0:T(4,128)S(1)} %copy-done.5, ...), custom_call_target="tpu_custom_call" | custom-call | flops 2000000000 | bytes 8000000 | tf_op jit(solution)/shard_map/pallas_call | solution.py:772
  48.5 3.4 %collective-permute-done.11.refs_1_.refs_11_ = bf16[4,28,8,128]{3,2,1,0:T(8,128)(2,1)S(1)} collective-permute-done((bf16[4,28,8,128]{3,2,1,0:T(8,128)(2,1)S(1)}, bf16[4,28,8,128]{3,2,1,0:T(8,128)(2,1)S(1)}, u32[]{:S(2)}, u32[]{:S(2)}) %collective-permute-start.11) | collective-permute-done | bytes 229408 | tf_op jit(solution)/shard_map/ppermute | solution.py:34
  51.9 0.0 collective-permute-done.10.refs_0_.refs_10_
  51.9 8.9 %all_to_all.46.before.refs_5_.refs_13_.refs_4_.refs_1_ = f32[32,2,128]{2,1,0:T(2,128)S(1)} all-to-all(f32[32,2,128]{2,1,0:T(2,128)S(1)} %shard_map.130), channel_id=1, replica_groups=mesh['batch'=2,'lat'=4,'lon'=4] {'batch','lat','lon'}, dimensions={0} | all-to-all | bytes 65536 | tf_op jit(solution)/shard_map/all_to_all | solution.py:38
  60.8 0.8 shard_map.131
  61.6 0.6 collective-permute-start.13
  62.2 0.1 collective-permute-start.12
  62.3 3.8 %shard_map.132 = (f32[32,2,128]{2,1,0:T(2,128)S(1)}, bf16[4,28,16,128]{3,2,1,0:T(8,128)(2,1)S(1)}, f32[4,32,48,128]{3,2,1,0:T(8,128)S(1)}, bf16[3,4,18,32,128]{4...) custom-call(s32[4]{0:T(128)S(1)} %pad_add_fusion.info.refs_0_, f32[4,128]{1,0:T(4,128)S(1)} %copy-done.4, ...), custom_call_target="tpu_custom_call" | custom-call | flops 2000000000 | bytes 8000000 | tf_op jit(solution)/shard_map/pallas_call | solution.py:772
  66.1 9.0 %all_to_all.47.refs_5_.refs_14_.refs_4_.refs_2_ = f32[32,2,128]{2,1,0:T(2,128)S(1)} all-to-all(f32[32,2,128]{2,1,0:T(2,128)S(1)} %get-tuple-element.116), channel_id=1, replica_groups=mesh['batch'=2,'lat'=4,'lon'=4] {'batch','lat','lon'}, dimensions={0} | all-to-all | bytes 65536 | tf_op jit(solution)/shard_map/all_to_all | solution.py:38
  75.1 3.5 %shard_map.133 = (f32[32,4,128]{2,1,0:T(4,128)S(1)}, bf16[4,26,16,128]{3,2,1,0:T(8,128)(2,1)S(1)}, bf16[4,24,16,128]{3,2,1,0:T(8,128)(2,1)S(1)}, bf16[4,20,16,12...) custom-call(s32[4]{0:T(128)S(1)} %pad_add_fusion.info.refs_0_, ...), custom_call_target="tpu_custom_call" | custom-call | flops 2000000000 | bytes 8000000 | tf_op jit(solution)/shard_map/pallas_call | solution.py:772
  78.7 9.1 %all_to_all.48.refs_4_.refs_5_.refs_3_ = f32[32,4,128]{2,1,0:T(4,128)S(1)} all-to-all(f32[32,4,128]{2,1,0:T(4,128)S(1)} %get-tuple-element.119), channel_id=1, replica_groups=mesh['batch'=2,'lat'=4,'lon'=4] {'batch','lat','lon'}, dimensions={0} | all-to-all | bytes 131072 | tf_op jit(solution)/shard_map/all_to_all | solution.py:38
  87.8 4.9 %shard_map.134 = (f32[32,3,128]{2,1,0:T(4,128)S(1)}, f32[576,128]{1,0:T(8,128)S(1)}, f32[576,128]{1,0:T(8,128)S(1)}, f32[4,32,48,128]{3,2,1,0:T(8,128)S(1)}, bf16[4,16,32,128]{3,2,1,0:T(8,128)(2,1)}) custom-call(s32[4]{0:T(128)S(1)} %pad_add_fusion.info.refs_0_, f32[4,128]{1,0:T(4,128)S(1)} %copy-done.4, f32[4,128]{1,0:T(4,128)S(1)} %copy-done.5, ...), custom_call_target="tpu_custom_call" | custom-call | flops 3000000000 | bytes 8000000 | tf_op jit(solution)/shard_map/pallas_call | solution.py:772
  92.7 9.1 %all_to_all.49.refs_5_.refs_6_ = f32[32,3,128]{2,1,0:T(4,128)S(1)} all-to-all(f32[32,3,128]{2,1,0:T(4,128)S(1)} %get-tuple-element.127), channel_id=1, replica_groups=mesh['batch'=2,'lat'=4,'lon'=4] {'batch','lat','lon'}, dimensions={0} | all-to-all | bytes 98304 | tf_op jit(solution)/shard_map/all_to_all | solution.py:38
  101.8 4.0 %shard_map.135 = (f32[32,3,128]{2,1,0:T(4,128)S(1)}, f32[576,128]{1,0:T(8,128)S(1)}, f32[576,128]{1,0:T(8,128)S(1)}, f32[4,32,48,128]{3,2,1,0:T(8,128)S(1)}, f32[4,16,32,128]{3,2,1,0:T(8,128)S(1)}) custom-call(s32[4]{0:T(128)S(1)} %pad_add_fusion.info.refs_0_, f32[4,128]{1,0:T(4,128)S(1)} %copy-done.4, f32[4,128]{1,0:T(4,128)S(1)} %copy-done.5, ...), custom_call_target="tpu_custom_call" | custom-call | flops 3000000000 | bytes 8000000 | tf_op jit(solution)/shard_map/pallas_call | solution.py:772
  105.8 9.1 %all_to_all.50.refs_5_ = f32[32,3,128]{2,1,0:T(4,128)S(1)} all-to-all(f32[32,3,128]{2,1,0:T(4,128)S(1)} %get-tuple-element.132), channel_id=1, replica_groups=mesh['batch'=2,'lat'=4,'lon'=4] {'batch','lat','lon'}, dimensions={0} | all-to-all | bytes 98304 | tf_op jit(solution)/shard_map/all_to_all | solution.py:38
  114.9 3.8 %shard_map.136 = (f32[32,4,128]{2,1,0:T(4,128)S(1)}, f32[576,128]{1,0:T(8,128)S(1)}, f32[576,128]{1,0:T(8,128)S(1)}, f32[4,32,48,128]{3,2,1,0:T(8,128)S(1)}) custom-call(s32[4]{0:T(128)S(1)} %pad_add_fusion.info.refs_0_, f32[4,128]{1,0:T(4,128)S(1)} %copy-done.4, f32[4,128]{1,0:T(4,128)S(1)} %copy-done.5, ...), custom_call_target="tpu_custom_call" | custom-call | flops 3000000000 | bytes 8000000 | tf_op jit(solution)/shard_map/pallas_call | solution.py:772
  118.8 9.1 %all_to_all.51.refs_3_.refs_4_ = f32[32,4,128]{2,1,0:T(4,128)S(1)} all-to-all(f32[32,4,128]{2,1,0:T(4,128)S(1)} %get-tuple-element.136), channel_id=1, replica_groups=mesh['batch'=2,'lat'=4,'lon'=4] {'batch','lat','lon'}, dimensions={0} | all-to-all | bytes 131072 | tf_op jit(solution)/shard_map/all_to_all | solution.py:38
  127.9 2.3 %shard_map.137 = (f32[576,128]{1,0:T(8,128)S(1)}, f32[1152,128]{1,0:T(8,128)S(1)}, bf16[4,18,48,128]{3,2,1,0:T(8,128)(2,1)S(1)}) custom-call(s32[4]{0:T(128)S(1)} %pad_add_fusion.info.refs_0_, f32[4,128]{1,0:T(4,128)S(1)} %copy-done.4, f32[32,4,128]{2,1,0:T(4,128)S(1)} %all_to_all.45.before.refs_5_.refs_11_.refs_2_.refs_0_, ...), custom_call_target="tpu_custom_call" | custom-call | flops 1000000000 | bytes 8000000 | tf_op jit(solution)/shard_map/pallas_call | solution.py:772
  130.2 0.4 collective-permute-start.16
  130.6 0.1 collective-permute-start.14
  130.8 0.4 collective-permute-start.15
  131.1 2.6 %shard_map.138 = (f32[4,16,32,128]{3,2,1,0:T(8,128)}, f32[4,128]{1,0:T(4,128)}, f32[4,128]{1,0:T(4,128)}, f32[4,128]{1,0:T(4,128)}, f32[4,128]{1,0:T(4,128)S(1)}) custom-call(bf16[1536,256]{1,0:T(8,128)(2,1)S(1)} %get-tuple-element.96.refs_4_.weight, bf16[4,18,48,128]{3,2,1,0:T(8,128)(2,1)S(1)} %get-tuple-element.140.dpre, ...), custom_call_target="tpu_custom_call" | custom-call | flops 1000000000 | bytes 3000000 | tf_op jit(solution)/shard_map/pallas_call | solution.py:772
  133.8 0.2 shard_map.139
  134.0 19.6 %all_to_all.52.got = bf16[16,144,128]{2,1,0:T(8,128)(2,1)S(1)} all-to-all(bf16[16,144,128]{2,1,0:T(8,128)(2,1)S(1)} %bitcast.10), channel_id=1, replica_groups={{0,2,4,6,8,10,12,14,16,18,20,22,24,26,28,30},{1,3,5,7,9,11,13,15,17,19,..., dimensions={0} | all-to-all | bytes 1179648 | tf_op jit(solution)/shard_map/all_to_all | solution.py:43
  153.6 0.1 shard_map.140
  153.7 19.6 %all_to_all.53 = bf16[16,144,128]{2,1,0:T(8,128)(2,1)S(1)} all-to-all(bf16[16,144,128]{2,1,0:T(8,128)(2,1)S(1)} %shard_map.140), channel_id=1, replica_groups={{0,2,4,6,8,10,12,14,16,18,20,22,24,26,28,30},{1,3,5,7,9,11,13,15,17,19,..., dimensions={0} | all-to-all | bytes 1179648 | tf_op jit(solution)/shard_map/all_to_all | solution.py:43
  173.3 1.9 %collective-permute-start.17 = (bf16[4,576,128]{2,1,0:T(8,128)(2,1)S(1)}, bf16[4,576,128]{2,1,0:T(8,128)(2,1)S(1)}, u32[]{:S(2)}, u32[]{:S(2)}) collective-permute-start(bf16[4,576,128]{2,1,0:T(8,128)(2,1)S(1)} %bitcast.11), channel_id=1, source_target_pairs={{0,1},{1,0},{2,3},{3,2},{4,5},{5,4},{6,7},{7,6},{8,9},{9,8},{10,11... | collective-permute-start | bytes 1769480 | tf_op jit(solution)/shard_map/ppermute | solution.py:47
  175.2 1.6 shard_map.141.refs_0_
  176.8 0.0 collective-permute-done.17.block
  176.9 1.6 shard_map.142
  (21 shorter events, 0.1 us)
Async XLA Ops:
  0.6 12.5 %copy-start.3 = (bf16[4,16,32,128]{3,2,1,0:T(8,128)(2,1)S(1)}, bf16[4,16,32,128]{3,2,1,0:T(8,128)(2,1)}, u32[]{:S(2)}) copy-start(bf16[4,16,32,128]{3,2,1,0:T(8,128)(2,1)} %refs_0_.1) | copy-start | bytes 1572868
  0.6 16.0 %copy-start.1 = (bf16[4,16,32,128]{3,2,1,0:T(8,128)(2,1)S(1)}, bf16[4,16,32,128]{3,2,1,0:T(8,128)(2,1)}, u32[]{:S(2)}) copy-start(bf16[4,16,32,128]{3,2,1,0:T(8,128)(2,1)} %cot.5) | copy-start | bytes 1572868
  0.7 16.0 %copy-start = (s32[4,4,16,32,128]{4,3,2,1,0:T(8,128)S(1)}, s32[4,4,16,32,128]{4,3,2,1,0:T(8,128)}, u32[]{:S(2)}) copy-start(s32[4,4,16,32,128]{4,3,2,1,0:T(8,128)} %masks.3) | copy-start | bytes 12582916
  2.7 10.5 %collective-permute-start = (bf16[4,8,32,128]{3,2,1,0:T(8,128)(2,1)S(1)}, bf16[4,8,32,128]{3,2,1,0:T(8,128)(2,1)S(1)}, u32[]{:S(2)}, u32[]{:S(2)}) collective-permute-start(bf16[4,8,32,128]{3,2,1,0:T(8,128)(2,1)S(1)} %get-tuple-element.82), channel_id=1, source_target_pairs={{0,4},{4,0},{8,12},{12,8},{1,5},{5,1},{9,13},{13,9},{2,6},{6,2},{1... | collective-permute-start | bytes 786440 | tf_op jit(solution)/shard_map/ppermute | solution.py:34
  4.9 8.3 %collective-permute-start.1 = (bf16[4,8,32,128]{3,2,1,0:T(8,128)(2,1)S(1)}, bf16[4,8,32,128]{3,2,1,0:T(8,128)(2,1)S(1)}, u32[]{:S(2)}, u32[]{:S(2)}) collective-permute-start(bf16[4,8,32,128]{3,2,1,0:T(8,128)(2,1)S(1)} %get-tuple-element.83), channel_id=1, source_target_pairs={{4,8},{8,4},{5,9},{9,5},{6,10},{10,6},{7,11},{11,7},{20,24},{24,20... | collective-permute-start | bytes 786440 | tf_op jit(solution)/shard_map/ppermute | solution.py:34
  7.3 9.7 %collective-permute-start.5 = (bf16[4,7,32,128]{3,2,1,0:T(8,128)(2,1)S(1)}, bf16[4,7,32,128]{3,2,1,0:T(8,128)(2,1)S(1)}, u32[]{:S(2)}, u32[]{:S(2)}) collective-permute-start(bf16[4,7,32,128]{3,2,1,0:T(8,128)(2,1)S(1)} %get-tuple-element.93), channel_id=1, source_target_pairs={{4,8},{8,4},{5,9},{9,5},{6,10},{10,6},{7,11},{11,7},{20,24},{24,20... | collective-permute-start | bytes 688136 | tf_op jit(solution)/shard_map/ppermute | solution.py:34
  8.0 9.8 %collective-permute-start.4 = (bf16[4,7,32,128]{3,2,1,0:T(8,128)(2,1)S(1)}, bf16[4,7,32,128]{3,2,1,0:T(8,128)(2,1)S(1)}, u32[]{:S(2)}, u32[]{:S(2)}) collective-permute-start(bf16[4,7,32,128]{3,2,1,0:T(8,128)(2,1)S(1)} %get-tuple-element.80.before), channel_id=1, source_target_pairs={{0,4},{4,0},{8,12},{12,8},{1,5},{5,1},{9,13},{13,9},{2,6},{6,2},{1... | collective-permute-start | bytes 688136 | tf_op jit(solution)/shard_map/ppermute | solution.py:34
  13.9 11.2 %collective-permute-start.2 = (bf16[4,32,8,128]{3,2,1,0:T(8,128)(2,1)S(1)}, bf16[4,32,8,128]{3,2,1,0:T(8,128)(2,1)S(1)}, u32[]{:S(2)}, u32[]{:S(2)}) collective-permute-start(bf16[4,32,8,128]{3,2,1,0:T(8,128)(2,1)S(1)} %get-tuple-element.85), channel_id=1, source_target_pairs={{0,1},{1,0},{2,3},{3,2},{4,5},{5,4},{6,7},{7,6},{8,9},{9,8},{10,11... | collective-permute-start | bytes 786440 | tf_op jit(solution)/shard_map/ppermute | solution.py:34
  15.5 9.7 %copy-start.2 = (bf16[4,3,3,128,128]{4,3,2,1,0:T(8,128)(2,1)S(1)}, bf16[4,3,3,128,128]{4,3,2,1,0:T(8,128)(2,1)}, u32[]{:S(2)}) copy-start(bf16[4,3,3,128,128]{4,3,2,1,0:T(8,128)(2,1)} %param.8) | copy-start | bytes 3538948
  15.5 9.9 %collective-permute-start.3 = (bf16[4,32,8,128]{3,2,1,0:T(8,128)(2,1)S(1)}, bf16[4,32,8,128]{3,2,1,0:T(8,128)(2,1)S(1)}, u32[]{:S(2)}, u32[]{:S(2)}) collective-permute-start(bf16[4,32,8,128]{3,2,1,0:T(8,128)(2,1)S(1)} %get-tuple-element.86), channel_id=1, source_target_pairs={{0,3},{1,2},{2,1},{3,0},{4,7},{5,6},{6,5},{7,4},{8,11},{9,10},{10,... | collective-permute-start | bytes 786440 | tf_op jit(solution)/shard_map/ppermute | solution.py:34
  17.0 8.3 %copy-start.4 = (f32[4,128]{1,0:T(4,128)S(1)}, f32[4,128]{1,0:T(4,128)}, u32[]{:S(2)}) copy-start(f32[4,128]{1,0:T(4,128)} %gains.1) | copy-start | bytes 6148
  17.0 8.3 %copy-start.5 = (f32[4,128]{1,0:T(4,128)S(1)}, f32[4,128]{1,0:T(4,128)}, u32[]{:S(2)}) copy-start(f32[4,128]{1,0:T(4,128)} %refs_2_.13) | copy-start | bytes 6148
  17.0 8.3 %copy-start.6 = (f32[4,128]{1,0:T(4,128)S(1)}, f32[4,128]{1,0:T(4,128)}, u32[]{:S(2)}) copy-start(f32[4,128]{1,0:T(4,128)} %refs_3_.7) | copy-start | bytes 6148
  19.2 24.2 %collective-permute-start.8 = (bf16[4,17,32,128]{3,2,1,0:T(8,128)(2,1)S(1)}, bf16[4,17,32,128]{3,2,1,0:T(8,128)(2,1)S(1)}, u32[]{:S(2)}, u32[]{:S(2)}) collective-permute-start(bf16[4,17,32,128]{3,2,1,0:T(8,128)(2,1)S(1)} %get-tuple-element.104), channel_id=1, source_target_pairs={{0,4},{4,0},{8,12},{12,8},{1,5},{5,1},{9,13},{13,9},{2,6},{6,2},{1... | collective-permute-start | bytes 1671176 | tf_op jit(solution)/shard_map/ppermute | solution.py:34
  21.3 22.1 %collective-permute-start.9 = (bf16[4,17,32,128]{3,2,1,0:T(8,128)(2,1)S(1)}, bf16[4,17,32,128]{3,2,1,0:T(8,128)(2,1)S(1)}, u32[]{:S(2)}, u32[]{:S(2)}) collective-permute-start(bf16[4,17,32,128]{3,2,1,0:T(8,128)(2,1)S(1)} %get-tuple-element.105), channel_id=1, source_target_pairs={{4,8},{8,4},{5,9},{9,5},{6,10},{10,6},{7,11},{11,7},{20,24},{24,20... | collective-permute-start | bytes 1671176 | tf_op jit(solution)/shard_map/ppermute | solution.py:34
  21.9 9.9 %collective-permute-start.7 = (bf16[4,30,8,128]{3,2,1,0:T(8,128)(2,1)S(1)}, bf16[4,30,8,128]{3,2,1,0:T(8,128)(2,1)S(1)}, u32[]{:S(2)}, u32[]{:S(2)}) collective-permute-start(bf16[4,30,8,128]{3,2,1,0:T(8,128)(2,1)S(1)} %get-tuple-element.95), channel_id=1, source_target_pairs={{0,3},{1,2},{2,1},{3,0},{4,7},{5,6},{6,5},{7,4},{8,11},{9,10},{10,... | collective-permute-start | bytes 737288 | tf_op jit(solution)/shard_map/ppermute | solution.py:34
  25.1 6.7 %collective-permute-start.6 = (bf16[4,30,8,128]{3,2,1,0:T(8,128)(2,1)S(1)}, bf16[4,30,8,128]{3,2,1,0:T(8,128)(2,1)S(1)}, u32[]{:S(2)}, u32[]{:S(2)}) collective-permute-start(bf16[4,30,8,128]{3,2,1,0:T(8,128)(2,1)S(1)} %get-tuple-element.94.before), channel_id=1, source_target_pairs={{0,1},{1,0},{2,3},{3,2},{4,5},{5,4},{6,7},{7,6},{8,9},{9,8},{10,11... | collective-permute-start | bytes 737288 | tf_op jit(solution)/shard_map/ppermute | solution.py:34
  44.2 7.7 %collective-permute-start.11 = (bf16[4,28,8,128]{3,2,1,0:T(8,128)(2,1)S(1)}, bf16[4,28,8,128]{3,2,1,0:T(8,128)(2,1)S(1)}, u32[]{:S(2)}, u32[]{:S(2)}) collective-permute-start(bf16[4,28,8,128]{3,2,1,0:T(8,128)(2,1)S(1)} %get-tuple-element.108), channel_id=1, source_target_pairs={{0,3},{1,2},{2,1},{3,0},{4,7},{5,6},{6,5},{7,4},{8,11},{9,10},{10,... | collective-permute-start | bytes 688136 | tf_op jit(solution)/shard_map/ppermute | solution.py:34
  44.7 7.2 %collective-permute-start.10 = (bf16[4,28,8,128]{3,2,1,0:T(8,128)(2,1)S(1)}, bf16[4,28,8,128]{3,2,1,0:T(8,128)(2,1)S(1)}, u32[]{:S(2)}, u32[]{:S(2)}) collective-permute-start(bf16[4,28,8,128]{3,2,1,0:T(8,128)(2,1)S(1)} %get-tuple-element.106.refs_10_), channel_id=1, source_target_pairs={{0,1},{1,0},{2,3},{3,2},{4,5},{5,4},{6,7},{7,6},{8,9},{9,8},{10,11... | collective-permute-start | bytes 688136 | tf_op jit(solution)/shard_map/ppermute | solution.py:34
  61.6 13.5 %collective-permute-start.13 = (bf16[4,50,8,128]{3,2,1,0:T(8,128)(2,1)S(1)}, bf16[4,50,8,128]{3,2,1,0:T(8,128)(2,1)S(1)}, u32[]{:S(2)}, u32[]{:S(2)}) collective-permute-start(bf16[4,50,8,128]{3,2,1,0:T(8,128)(2,1)S(1)} %get-tuple-element.118), channel_id=1, source_target_pairs={{0,3},{1,2},{2,1},{3,0},{4,7},{5,6},{6,5},{7,4},{8,11},{9,10},{10,... | collective-permute-start | bytes 1228808 | tf_op jit(solution)/shard_map/ppermute | solution.py:34
  62.2 12.9 %collective-permute-start.12 = (bf16[4,50,8,128]{3,2,1,0:T(8,128)(2,1)S(1)}, bf16[4,50,8,128]{3,2,1,0:T(8,128)(2,1)S(1)}, u32[]{:S(2)}, u32[]{:S(2)}) collective-permute-start(bf16[4,50,8,128]{3,2,1,0:T(8,128)(2,1)S(1)} %get-tuple-element.115.refs_12_), channel_id=1, source_target_pairs={{0,1},{1,0},{2,3},{3,2},{4,5},{5,4},{6,7},{7,6},{8,9},{9,8},{10,11... | collective-permute-start | bytes 1228808 | tf_op jit(solution)/shard_map/ppermute | solution.py:34
  130.2 3.6 %collective-permute-start.16 = (f32[1152,128]{1,0:T(8,128)S(1)}, f32[1152,128]{1,0:T(8,128)S(1)}, u32[]{:S(2)}, u32[]{:S(2)}) collective-permute-start(f32[1152,128]{1,0:T(8,128)S(1)} %get-tuple-element.149), channel_id=1, source_target_pairs={{0,1},{1,0},{2,3},{3,2},{4,5},{5,4},{6,7},{7,6},{8,9},{9,8},{10,11... | collective-permute-start | bytes 1769480 | tf_op jit(solution)/shard_map/ppermute | solution.py:47
  130.6 3.1 %collective-permute-start.14 = (f32[576,128]{1,0:T(8,128)S(1)}, f32[576,128]{1,0:T(8,128)S(1)}, u32[]{:S(2)}, u32[]{:S(2)}) collective-permute-start(f32[576,128]{1,0:T(8,128)S(1)} %get-tuple-element.147), channel_id=1, source_target_pairs={{0,1},{1,0},{2,3},{3,2},{4,5},{5,4},{6,7},{7,6},{8,9},{9,8},{10,11... | collective-permute-start | bytes 884744 | tf_op jit(solution)/shard_map/ppermute | solution.py:47
  130.8 3.0 %collective-permute-start.15 = (f32[576,128]{1,0:T(8,128)S(1)}, f32[576,128]{1,0:T(8,128)S(1)}, u32[]{:S(2)}, u32[]{:S(2)}) collective-permute-start(f32[576,128]{1,0:T(8,128)S(1)} %get-tuple-element.148), channel_id=1, source_target_pairs={{0,1},{1,0},{2,3},{3,2},{4,5},{5,4},{6,7},{7,6},{8,9},{9,8},{10,11... | collective-permute-start | bytes 884744 | tf_op jit(solution)/shard_map/ppermute | solution.py:47
  173.3 3.6 %collective-permute-start.17 = (bf16[4,576,128]{2,1,0:T(8,128)(2,1)S(1)}, bf16[4,576,128]{2,1,0:T(8,128)(2,1)S(1)}, u32[]{:S(2)}, u32[]{:S(2)}) collective-permute-start(bf16[4,576,128]{2,1,0:T(8,128)(2,1)S(1)} %bitcast.11), channel_id=1, source_target_pairs={{0,1},{1,0},{2,3},{3,2},{4,5},{5,4},{6,7},{7,6},{8,9},{9,8},{10,11... | collective-permute-start | bytes 1769480 | tf_op jit(solution)/shard_map/ppermute | solution.py:47

commit v6 on v5

--- a/solution.py
+++ b/solution.py
@@ -112,18 +112,24 @@
     return out
 
 
+def pusher():
+    staged = [0, 0]
+
+    def push(unit, tile):
+        staged[unit] = 1 - staged[unit]
+        pltpu.matmul_push_rhs(tile, staged[unit], unit)
+        return staged[unit]
+
+    return push
+
+
 def pipeline(grids, lo, hi, taps, weight, cols, prepare, emit, after, finish, extra=None, take=None, extra_totals=()):
     parts = even_parts(lo, hi, 5)
     count = len(parts)
 
     def body(*refs):
         totals, more = refs[: 2 * count], refs[2 * count :]
-        staged = [0, 0]
-
-        def push(unit, tile):
-            staged[unit] = 1 - staged[unit]
-            pltpu.matmul_push_rhs(tile, staged[unit], unit)
-            return staged[unit]
+        push = pusher()
 
         def operand(g, part, k):
             start, size = parts[part]
@@ -519,31 +525,47 @@
     return (dn * scale + act * tilt + flat) * (s + act * (1.0 - s)), act
 
 
-def weight_term(geo, low, g, right, acc):
+def weight_totals():
+    return [pltpu.ACC(n % 2)((LANES, 2 * LANES), F32) for n in range(5)]
+
+
+def weight_steps(geo, low, inside, first, push, totals):
     rows, cols = geo["R"], geo["C"]
-    parts = [low[s, g, r : r + rows] for r in range(3) for s in range(3)]
-    spread = jnp.concatenate(parts, axis=-1).reshape(rows * cols, 9 * LANES)
-    term = lax.dot_general(right, spread, (((0,), (0,)), ((), ())), preferred_element_type=F32)
-    if g == 0:
-        acc[...] = term
-    else:
-        acc[...] += term
-
-
-def split_halves(info, acc, keep_half, send_half):
+    depth = 2 * LANES // cols
+    steps = []
+    for g in (first, first + 1):
+        for at in range(0, rows, depth):
+            turned = []
+
+            def act(n, g=g, at=at, turned=turned):
+                if not turned:
+                    turned.append(inside(g, at, depth).reshape(2 * LANES, LANES).T)
+                halves = []
+                for tap in (2 * n, 2 * n + 1):
+                    r, s = divmod(min(tap, 8), 3)
+                    halves.append(low[s, g, at + r : at + r + depth].reshape(2 * LANES, LANES))
+                staged = push(n % 2, jnp.concatenate(halves, axis=-1))
+                pltpu.matmul_acc_lhs(totals[n], turned[0], load_staged_rhs=staged)
+
+            steps += [functools.partial(act, n) for n in range(5)]
+    return steps
+
+
+def take_term(term, totals):
+    def act(n):
+        both = pltpu.matmul_pop(totals[n])
+        for tap in range(2 * n, min(2 * n + 2, 9)):
+            at = (tap - 2 * n) * LANES
+            term[tap * LANES : (tap + 1) * LANES] = both[:, at : at + LANES].T
+
+    return [functools.partial(act, n) for n in range(5)]
+
+
+def split_halves(info, term, keep_half, send_half):
     half = 9 * LANES // 2
-
-    def give(out):
-        def act(upper):
-            start = half if upper else 0
-            for t in range(9):
-                lo, hi = max(t * LANES, start), min((t + 1) * LANES, start + half)
-                if lo < hi:
-                    block = acc[:, t * LANES : (t + 1) * LANES].T
-                    out[lo - start : hi - start] = block[lo - t * LANES : hi - t * LANES]
-        return act
-
-    both_ways(info[1], give(keep_half), give(send_half))
+    start = pl.multiple_of((1 - info[1]) * half, 8)
+    keep_half[...] = term[pl.ds(start, half)]
+    send_half[...] = term[pl.ds(pl.multiple_of(half - start, 8), half)]
 
 
 def backward_kernel(layer, geo, *refs):
@@ -614,49 +636,16 @@
             if layer == 1:
                 gather(sums_here, 3, fold(z * (s + act * (1.0 - s))))
 
-    def inside(g):
-        return taps[g, 1, EXT : EXT + rows, 0:cols, :].reshape(rows * cols, LANES)
+    def inside(g, at, depth):
+        return taps[g, 1, EXT + at : EXT + at + depth, 0:cols, :]
 
     def after(g):
         if layer == 3:
             leaving[g].start()
-        gather(sums_here, 2, fold(inside(g).astype(F32)))
-
-    def weight_steps(first, push, totals):
-        depth = 2 * LANES // cols
-        steps = []
-        for g in (first, first + 1):
-            for at in range(0, rows, depth):
-                turned = []
-
-                def act(n, g=g, at=at, turned=turned):
-                    if not turned:
-                        block = taps[g, 1, EXT + at : EXT + at + depth, 0:cols, :].reshape(2 * LANES, LANES)
-                        turned.append(block.T)
-                    halves = []
-                    for tap in (2 * n, 2 * n + 1):
-                        r, s = divmod(min(tap, 8), 3)
-                        halves.append(low[s, g, at + r : at + r + depth].reshape(2 * LANES, LANES))
-                    staged = push(n % 2, jnp.concatenate(halves, axis=-1))
-                    pltpu.matmul_acc_lhs(totals[n], turned[0], load_staged_rhs=staged)
-
-                steps += [functools.partial(act, n) for n in range(5)]
-        return steps
-
-    def take_term(totals):
-        def act(n):
-            both = pltpu.matmul_pop(totals[n])
-            for tap in range(2 * n, min(2 * n + 2, 9)):
-                at = (tap - 2 * n) * LANES
-                term[tap * LANES : (tap + 1) * LANES] = both[:, at : at + LANES].T
-
-        return [functools.partial(act, n) for n in range(5)]
+        gather(sums_here, 2, fold(inside(g, 0, rows).astype(F32)))
 
     def finish():
-        half = 9 * LANES // 2
-        start = pl.multiple_of((1 - info[1]) * half, 8)
-        keep_half[...] = term[pl.ds(start, half)]
-        send_half[...] = term[pl.ds(pl.multiple_of(half - start, 8), half)]
+        split_halves(info, term, keep_half, send_half)
         out = [to_row(sums_here[k]) for k in range(4 if layer == 1 else 3)]
         out[0] = out[0] * (1.0 / keep_rate)
         out[1] = out[1] * inv_b * (1.0 / keep_rate)
@@ -668,44 +657,66 @@
             for c in leaving:
                 c.wait()
 
-    totals = [pltpu.ACC(n % 2)((LANES, 2 * LANES), F32) for n in range(5)]
-    pipeline(grids, lo, hi, taps, weight, width, prepare, emit, after, finish, weight_steps, take_term, totals)
+    steps = functools.partial(weight_steps, geo, low, inside)
+    take = functools.partial(take_term, term)
+    pipeline(grids, lo, hi, taps, weight, width, prepare, emit, after, finish, steps, take, weight_totals())
 
 
 def first_weight_kernel(geo, *refs):
-    grids, rows, width, cols = geo["G"], geo["R"], geo["CE"], geo["C"]
-    info, gains, stats, sums, pre, low, z_in, sent, keep_half, send_both, dpre, acc = refs
+    grids, rows, cols = geo["G"], geo["R"], geo["C"]
+    info, gains, stats, sums, pre, low, z_in, sent, keep_half, send_both, dpre, term = refs
     half = 9 * LANES // 2
     send_both[0:half] = sent[...]
     scale, flat, tilt = back_consts(0, geo, stats, sums, gains)[2:]
     first_row, last_row = info[2], info[3]
 
-    for g in range(grids):
-        for k in range(rows + 2):
-            r = EXT - 1 + k
-            value, _ = through(pre[g, r], z_in[g, r], scale, flat, tilt)
-            if k in (0, rows + 1):
-                value = value * jnp.where((r >= first_row) & (r < last_row), 1.0, 0.0).astype(F32)
-            dpre[g, k] = value.astype(LOW)
-        weight_term(geo, low, g, dpre[g, 1 : rows + 1, 0:cols, :].reshape(rows * cols, LANES), acc)
-    split_halves(info, acc, keep_half, send_both.at[half : 2 * half])
+    def prepare(g, k):
+        r = EXT - 1 + k
+        value, _ = through(pre[g, r], z_in[g, r], scale, flat, tilt)
+        if k in (0, rows + 1):
+            value = value * jnp.where((r >= first_row) & (r < last_row), 1.0, 0.0).astype(F32)
+        dpre[g, k] = value.astype(LOW)
+
+    def ready(first):
+        return [functools.partial(prepare, first + unit, k) for k in range(rows + 2) for unit in range(2)]
+
+    def inside(g, at, depth):
+        return dpre[g, 1 + at : 1 + at + depth, 0:cols, :]
+
+    def body(*totals):
+        push = pusher()
+        for task in ready(0):
+            task()
+        for first in range(0, grids, 2):
+            tasks = ready(first + 2) if first + 2 < grids else []
+            steps = weight_steps(geo, low, inside, first, push, totals)
+            done = 0
+            for n, step in enumerate(steps):
+                step()
+                while done < len(tasks) * (n + 1) // len(steps):
+                    tasks[done]()
+                    done += 1
+        for task in take_term(term, totals):
+            task()
+        split_halves(info, term, keep_half, send_both.at[half : 2 * half])
+
+    pl.run_scoped(body, *weight_totals())
 
 
 def input_grad_kernel(geo, weight, dpre, grad, gains, *refs):
+    out, taps = refs[7], refs[11]
     grids, rows, width, cols = geo["G"], geo["R"], geo["CE"], geo["C"]
-    out, taps, buffer, sems = refs[7], *refs[12:]
-    refs[11][...] = jnp.zeros((4, LANES), F32)
-    leaving = [pltpu.make_async_copy(buffer.at[g], out.at[g], sems.at[g]) for g in range(grids)]
+
     def prepare(g, r):
         store_shifted(taps, g, r, dpre[g, pl.ds(r, 2)].astype(F32), width)
 
     def emit(g, r, part):
-        buffer[g, r - 1] = grad[g, r - 1] + part
-
-    pipeline(grids, 1, rows + 1, taps, weight, cols, prepare, emit, lambda g: leaving[g].start(), lambda: None)
-    gather_rows(geo, gains, *refs[0:7], *refs[8:11])
-    for c in leaving:
-        c.wait()
+        out[g, r - 1] = grad[g, r - 1] + part
+
+    def finish():
+        gather_rows(geo, gains, *refs[0:7], *refs[8:11])
+
+    pipeline(grids, 1, rows + 1, taps, weight, cols, prepare, emit, lambda g: None, finish)
 
 
 def share_kernel(*refs):
@@ -721,16 +732,26 @@
     out[...] = jnp.broadcast_to(total.astype(LOW)[None], out.shape)
 
 
-def join_kernel(geo, other, info, block, *refs):
-    out, buffer, sems = refs[-3:]
+def write_half(upper, block, out, buffer, sems):
     half = 9 * LANES // 2
-    upper = info[1] if other else 1 - info[1]
     start = pl.multiple_of(upper * half, 8)
     leaving = [pltpu.make_async_copy(buffer.at[k], out.at[k, pl.ds(start, half)], sems.at[k]) for k in range(4)]
     for k in range(4):
         buffer[k] = block[k].astype(F32)
         leaving[k].start()
+    return leaving
+
+
+def own_half_kernel(info, block, grad, out, grad_out, buffer, sems, grad_sem):
+    leaving = write_half(1 - info[1], block, out, buffer, sems)
+    leaving.append(pltpu.make_async_copy(grad, grad_out, grad_sem.at[0]))
+    leaving[-1].start()
     for c in leaving:
+        c.wait()
+
+
+def other_half_kernel(info, block, _, out, buffer, sems):
+    for c in write_half(info[1], block, out, buffer, sems):
         c.wait()
 
 
@@ -939,30 +960,29 @@
     term = ((half, LANES), F32)
     kept[0], sent, dpre = call(
         functools.partial(first_weight_kernel, geo), [info, gains, stats[0], sums[0], pres[0], lows[0], z, sent],
-        [term, ((2 * half, LANES), F32), block(rows + 2, cols + 2 * EXT)], [((LANES, 9 * LANES), F32)], 10**9, 8 * 10**6,
+        [term, ((2 * half, LANES), F32), block(rows + 2, cols + 2 * EXT)], [((9 * LANES, LANES), F32)], 10**9, 8 * 10**6,
     )
     got.append(to_pair(sent))
 
     small = ((4, LANES), F32)
     field_like = ((grids, rows, cols, LANES), F32)
-    input_grad, bias_grad, gain_grad, offset_grad, order = call(
+    input_grad, bias_grad, gain_grad, offset_grad = call(
         functools.partial(input_grad_kernel, geo), [weights[4], dpre, grad, gains] + stats + sums[:3],
-        [field_like] + [small] * 4, conv_scratch(geo, rows + 2) + [field_like, pltpu.SemaphoreType.DMA((grids,))],
-        10**9, 3 * 10**6, scalars=0, final=(0,), small=(1, 2, 3),
+        [field_like] + [small] * 3, conv_scratch(geo, rows + 2), 10**9, 3 * 10**6, scalars=0, small=(1, 2, 3),
     )
 
-    (shares,) = call(share_kernel, kept + got + [order], [((4 * half, LANES), LOW)], scalars=0)
+    (shares,) = call(share_kernel, kept + got + [input_grad], [((4 * half, LANES), LOW)], scalars=0)
     slots = (devices // 2, 4 * half // (devices // 2), LANES)
     arrived = to_half(shares.reshape(slots), devices)
     (mine,) = call(functools.partial(total_kernel, devices), [arrived], [(slots, LOW)], scalars=0)
     mine = to_half(mine, devices).reshape(4, half, LANES)
     other = to_pair(mine)
-    whole = [((4, 9 * LANES, LANES), F32)]
+    whole = ((4, 9 * LANES, LANES), F32)
     scratch = [((4, half, LANES), F32), pltpu.SemaphoreType.DMA((4,))]
-    (kernel_grad,) = call(functools.partial(join_kernel, geo, False), [info, mine], whole, scratch, final=(0,))
-    (kernel_grad,) = call(
-        functools.partial(join_kernel, geo, True), [info, other, kernel_grad], whole, scratch, final=(0,), onto=2
+    kernel_grad, input_grad = call(
+        own_half_kernel, [info, mine, input_grad], [whole, field_like], scratch + [pltpu.SemaphoreType.DMA((1,))], final=(0, 1)
     )
+    (kernel_grad,) = call(other_half_kernel, [info, other, kernel_grad], [whole], scratch, final=(0,), onto=2)
     return (output, input_grad, kernel_grad.reshape(4, 3, 3, LANES, LANES), bias_grad, gain_grad, offset_grad)
 
 

time: 179 us -> 178 us (level)
  transfers between devices with their start and end apart: 18 -> 18, of which waited for: 3 -> 4; matrix products, arithmetic and copies ran while one was open for 0% -> 0% of each run, Pallas kernels for 11% -> 11%
where the time goes in v6:
time: 178 us
  blocking collectives  105 us (59%)
  Pallas kernels  43.9 us (25%)
  starting transfers between devices  21.6 us (12%)
  waiting for transfers between devices  6.18 us (3%)
    all_to_all x7, blocking collectives, to_all(): return lax.all_to_all(rows, EVERY, 0, 0)  65.9 us
    pallas_call x25, Pallas kernels, call(): pl.pallas_call(kernel, in_specs=specs, out_specs=places, input_output_ali...  43.9 us
    all_to_all x2, blocking collectives, to_half(): return lax.all_to_all(rows, EVERY, 0, 0, axis_index_groups=groups)  39.2 us
    ppermute x7, starting transfers between devices, trade(): lax.ppermute(pair[0], axis, first)  11.2 us
    ppermute x7, starting transfers between devices, trade(): lax.ppermute(pair[1], axis, second)  7.49 us
    ppermute x7, waiting for transfers between devices, trade(): lax.ppermute(pair[1], axis, second)  5.24 us
  transfers between devices with their start and end apart: 18, of which 4 were waited for; matrix products, arithmetic and copies ran while one was open for 0% of the time, Pallas kernels for 11%

profile of v6, /device:TPU:1, one launch (start us, length us, event | category | flops | bytes accessed | tf_op | source)
XLA Modules:
  0.0 178.0 jit_solution(7279122042250571576)
XLA Ops:
  0.6 0.0 copy-start.3
  0.7 0.0 copy-start
  0.7 0.1 pad_add_fusion.info.refs_0_
  0.8 1.9 %shard_map.120 = (bf16[4,8,32,128]{3,2,1,0:T(8,128)(2,1)S(1)}, bf16[4,8,32,128]{3,2,1,0:T(8,128)(2,1)S(1)}) custom-call(s32[4]{0:T(128)S(1)} %pad_add_fusion.info.refs_0_, bf16[4,16,32,128]{3,2,1,0:T(8,128)(2,1)} %refs_0_.1), custom_call_target="tpu_custom_call" | custom-call | flops 1000000 | bytes 1000000 | tf_op jit(solution)/shard_map/pallas_call | solution.py:793
  2.7 2.2 %collective-permute-start = (bf16[4,8,32,128]{3,2,1,0:T(8,128)(2,1)S(1)}, bf16[4,8,32,128]{3,2,1,0:T(8,128)(2,1)S(1)}, u32[]{:S(2)}, u32[]{:S(2)}) collective-permute-start(bf16[4,8,32,128]{3,2,1,0:T(8,128)(2,1)S(1)} %get-tuple-element.83), channel_id=1, source_target_pairs={{0,4},{4,0},{8,12},{12,8},{1,5},{5,1},{9,13},{13,9},{2,6},{6,2},{1... | collective-permute-start | bytes 786440 | tf_op jit(solution)/shard_map/ppermute | solution.py:34
  4.9 0.7 collective-permute-start.1
  5.5 1.8 shard_map.118
  7.3 0.7 collective-permute-start.5
  8.0 5.1 %collective-permute-start.4 = (bf16[4,7,32,128]{3,2,1,0:T(8,128)(2,1)S(1)}, bf16[4,7,32,128]{3,2,1,0:T(8,128)(2,1)S(1)}, u32[]{:S(2)}, u32[]{:S(2)}) collective-permute-start(bf16[4,7,32,128]{3,2,1,0:T(8,128)(2,1)S(1)} %get-tuple-element.81.before), channel_id=1, source_target_pairs={{0,4},{4,0},{8,12},{12,8},{1,5},{5,1},{9,13},{13,9},{2,6},{6,2},{1... | collective-permute-start | bytes 688136 | tf_op jit(solution)/shard_map/ppermute | solution.py:34
  13.1 0.0 collective-permute-done.refs_1_
  13.1 0.7 shard_map.121
  13.9 1.6 collective-permute-start.2
  15.5 1.2 collective-permute-start.3
  16.7 0.3 shard_map.124
  17.0 0.0 copy-start.4
  17.0 0.0 copy-start.5
  17.0 0.0 copy-start.6
  17.0 0.0 collective-permute-done.5.refs_2_
  17.1 0.8 collective-permute-done.4.refs_1_
  17.8 0.7 shard_map.125
  18.5 0.6 shard_map.127
  19.2 2.1 %collective-permute-start.8 = (bf16[4,17,32,128]{3,2,1,0:T(8,128)(2,1)S(1)}, bf16[4,17,32,128]{3,2,1,0:T(8,128)(2,1)S(1)}, u32[]{:S(2)}, u32[]{:S(2)}) collective-permute-start(bf16[4,17,32,128]{3,2,1,0:T(8,128)(2,1)S(1)} %get-tuple-element.105), channel_id=1, source_target_pairs={{0,4},{4,0},{8,12},{12,8},{1,5},{5,1},{9,13},{13,9},{2,6},{6,2},{1... | collective-permute-start | bytes 1671176 | tf_op jit(solution)/shard_map/ppermute | solution.py:34
  21.3 0.7 collective-permute-start.9
  21.9 3.2 %collective-permute-start.7 = (bf16[4,30,8,128]{3,2,1,0:T(8,128)(2,1)S(1)}, bf16[4,30,8,128]{3,2,1,0:T(8,128)(2,1)S(1)}, u32[]{:S(2)}, u32[]{:S(2)}) collective-permute-start(bf16[4,30,8,128]{3,2,1,0:T(8,128)(2,1)S(1)} %get-tuple-element.96), channel_id=1, source_target_pairs={{0,3},{1,2},{2,1},{3,0},{4,7},{5,6},{6,5},{7,4},{8,11},{9,10},{10,... | collective-permute-start | bytes 737288 | tf_op jit(solution)/shard_map/ppermute | solution.py:34
  25.1 0.0 collective-permute-done.2.refs_6_
  25.1 0.0 collective-permute-start.6
  25.1 0.2 shard_map.119
  25.4 3.8 %shard_map.122 = (f32[32,4,128]{2,1,0:T(4,128)S(1)}, bf16[4,32,16,128]{3,2,1,0:T(8,128)(2,1)S(1)}, f32[4,32,48,128]{3,2,1,0:T(8,128)S(1)}, bf16[3,4,18,32,128]{4,3,2,1,0:T(8,128)(2,1)S(1)}) custom-call(s32[4]{0:T(128)S(1)} %pad_add_fusion.info.refs_0_, f32[4,128]{1,0:T(4,128)S(1)} %copy-done.4, f32[4,128]{1,0:T(4,128)S(1)} %copy-done.5, ...), custom_call_target="tpu_custom_call" | custom-call | flops 2000000000 | bytes 8000000 | tf_op jit(solution)/shard_map/pallas_call | solution.py:793
  29.2 0.7 shard_map.123
  29.9 1.9 %collective-permute-done.7.refs_1_.refs_9_ = bf16[4,30,8,128]{3,2,1,0:T(8,128)(2,1)S(1)} collective-permute-done((bf16[4,30,8,128]{3,2,1,0:T(8,128)(2,1)S(1)}, bf16[4,30,8,128]{3,2,1,0:T(8,128)(2,1)S(1)}, u32[]{:S(2)}, u32[]{:S(2)}) %collective-permute-start.7) | collective-permute-done | bytes 245792 | tf_op jit(solution)/shard_map/ppermute | solution.py:34
  31.9 11.5 %all_to_all.45.before.refs_5_.refs_11_.refs_2_.refs_0_ = f32[32,4,128]{2,1,0:T(4,128)S(1)} all-to-all(f32[32,4,128]{2,1,0:T(4,128)S(1)} %shard_map.126), channel_id=1, replica_groups=mesh['batch'=2,'lat'=4,'lon'=4] {'batch','lat','lon'}, dimensions={0} | all-to-all | bytes 131072 | tf_op jit(solution)/shard_map/all_to_all | solution.py:38
  43.4 0.0 collective-permute-done.8.first
  43.4 0.8 shard_map.128
  44.2 0.5 collective-permute-start.11
  44.7 0.1 collective-permute-start.10
  44.9 3.8 %shard_map.129 = (f32[32,2,128]{2,1,0:T(2,128)S(1)}, bf16[4,30,16,128]{3,2,1,0:T(8,128)(2,1)S(1)}, f32[4,32,48,128]{3,2,1,0:T(8,128)S(1)}, bf16[3,4,18,32,128]{4,3,2,1,0:T(8,128)(2,1)S(1)}) custom-call(s32[4]{0:T(128)S(1)} %pad_add_fusion.info.refs_0_, f32[4,128]{1,0:T(4,128)S(1)} %copy-done.4, f32[4,128]{1,0:T(4,128)S(1)} %copy-done.5, ...), custom_call_target="tpu_custom_call" | custom-call | flops 2000000000 | bytes 8000000 | tf_op jit(solution)/shard_map/pallas_call | solution.py:793
  48.6 3.3 %collective-permute-done.11.refs_1_.refs_11_ = bf16[4,28,8,128]{3,2,1,0:T(8,128)(2,1)S(1)} collective-permute-done((bf16[4,28,8,128]{3,2,1,0:T(8,128)(2,1)S(1)}, bf16[4,28,8,128]{3,2,1,0:T(8,128)(2,1)S(1)}, u32[]{:S(2)}, u32[]{:S(2)}) %collective-permute-start.11) | collective-permute-done | bytes 229408 | tf_op jit(solution)/shard_map/ppermute | solution.py:34
  51.9 8.9 %all_to_all.46.before.refs_5_.refs_13_.refs_4_.refs_1_ = f32[32,2,128]{2,1,0:T(2,128)S(1)} all-to-all(f32[32,2,128]{2,1,0:T(2,128)S(1)} %shard_map.130), channel_id=1, replica_groups=mesh['batch'=2,'lat'=4,'lon'=4] {'batch','lat','lon'}, dimensions={0} | all-to-all | bytes 65536 | tf_op jit(solution)/shard_map/all_to_all | solution.py:38
  60.8 0.8 shard_map.131
  61.6 0.6 collective-permute-start.13
  62.2 0.1 collective-permute-start.12
  62.3 3.8 %shard_map.132 = (f32[32,2,128]{2,1,0:T(2,128)S(1)}, bf16[4,28,16,128]{3,2,1,0:T(8,128)(2,1)S(1)}, f32[4,32,48,128]{3,2,1,0:T(8,128)S(1)}, bf16[3,4,18,32,128]{4...) custom-call(s32[4]{0:T(128)S(1)} %pad_add_fusion.info.refs_0_, f32[4,128]{1,0:T(4,128)S(1)} %copy-done.4, ...), custom_call_target="tpu_custom_call" | custom-call | flops 2000000000 | bytes 8000000 | tf_op jit(solution)/shard_map/pallas_call | solution.py:793
  66.1 9.0 %all_to_all.47.refs_5_.refs_14_.refs_4_.refs_2_ = f32[32,2,128]{2,1,0:T(2,128)S(1)} all-to-all(f32[32,2,128]{2,1,0:T(2,128)S(1)} %get-tuple-element.117), channel_id=1, replica_groups=mesh['batch'=2,'lat'=4,'lon'=4] {'batch','lat','lon'}, dimensions={0} | all-to-all | bytes 65536 | tf_op jit(solution)/shard_map/all_to_all | solution.py:38
  75.2 3.5 %shard_map.133 = (f32[32,4,128]{2,1,0:T(4,128)S(1)}, bf16[4,26,16,128]{3,2,1,0:T(8,128)(2,1)S(1)}, bf16[4,24,16,128]{3,2,1,0:T(8,128)(2,1)S(1)}, bf16[4,20,16,12...) custom-call(s32[4]{0:T(128)S(1)} %pad_add_fusion.info.refs_0_, ...), custom_call_target="tpu_custom_call" | custom-call | flops 2000000000 | bytes 8000000 | tf_op jit(solution)/shard_map/pallas_call | solution.py:793
  78.7 9.1 %all_to_all.48.refs_4_.refs_5_.refs_3_ = f32[32,4,128]{2,1,0:T(4,128)S(1)} all-to-all(f32[32,4,128]{2,1,0:T(4,128)S(1)} %get-tuple-element.120), channel_id=1, replica_groups=mesh['batch'=2,'lat'=4,'lon'=4] {'batch','lat','lon'}, dimensions={0} | all-to-all | bytes 131072 | tf_op jit(solution)/shard_map/all_to_all | solution.py:38
  87.8 5.0 %shard_map.134 = (f32[32,3,128]{2,1,0:T(4,128)S(1)}, f32[576,128]{1,0:T(8,128)S(1)}, f32[576,128]{1,0:T(8,128)S(1)}, f32[4,32,48,128]{3,2,1,0:T(8,128)S(1)}, bf16[4,16,32,128]{3,2,1,0:T(8,128)(2,1)}) custom-call(s32[4]{0:T(128)S(1)} %pad_add_fusion.info.refs_0_, f32[4,128]{1,0:T(4,128)S(1)} %copy-done.4, f32[4,128]{1,0:T(4,128)S(1)} %copy-done.5, ...), custom_call_target="tpu_custom_call" | custom-call | flops 3000000000 | bytes 8000000 | tf_op jit(solution)/shard_map/pallas_call | solution.py:793
  92.7 9.1 %all_to_all.49.refs_5_.refs_6_ = f32[32,3,128]{2,1,0:T(4,128)S(1)} all-to-all(f32[32,3,128]{2,1,0:T(4,128)S(1)} %get-tuple-element.128), channel_id=1, replica_groups=mesh['batch'=2,'lat'=4,'lon'=4] {'batch','lat','lon'}, dimensions={0} | all-to-all | bytes 98304 | tf_op jit(solution)/shard_map/all_to_all | solution.py:38
  101.8 4.0 %shard_map.135 = (f32[32,3,128]{2,1,0:T(4,128)S(1)}, f32[576,128]{1,0:T(8,128)S(1)}, f32[576,128]{1,0:T(8,128)S(1)}, f32[4,32,48,128]{3,2,1,0:T(8,128)S(1)}, f32[4,16,32,128]{3,2,1,0:T(8,128)S(1)}) custom-call(s32[4]{0:T(128)S(1)} %pad_add_fusion.info.refs_0_, f32[4,128]{1,0:T(4,128)S(1)} %copy-done.4, f32[4,128]{1,0:T(4,128)S(1)} %copy-done.5, ...), custom_call_target="tpu_custom_call" | custom-call | flops 3000000000 | bytes 8000000 | tf_op jit(solution)/shard_map/pallas_call | solution.py:793
  105.9 9.1 %all_to_all.50.refs_5_ = f32[32,3,128]{2,1,0:T(4,128)S(1)} all-to-all(f32[32,3,128]{2,1,0:T(4,128)S(1)} %get-tuple-element.133), channel_id=1, replica_groups=mesh['batch'=2,'lat'=4,'lon'=4] {'batch','lat','lon'}, dimensions={0} | all-to-all | bytes 98304 | tf_op jit(solution)/shard_map/all_to_all | solution.py:38
  115.0 3.8 %shard_map.136 = (f32[32,4,128]{2,1,0:T(4,128)S(1)}, f32[576,128]{1,0:T(8,128)S(1)}, f32[576,128]{1,0:T(8,128)S(1)}, f32[4,32,48,128]{3,2,1,0:T(8,128)S(1)}) custom-call(s32[4]{0:T(128)S(1)} %pad_add_fusion.info.refs_0_, f32[4,128]{1,0:T(4,128)S(1)} %copy-done.4, f32[4,128]{1,0:T(4,128)S(1)} %copy-done.5, ...), custom_call_target="tpu_custom_call" | custom-call | flops 3000000000 | bytes 8000000 | tf_op jit(solution)/shard_map/pallas_call | solution.py:793
  118.8 9.1 %all_to_all.51.refs_3_.refs_4_ = f32[32,4,128]{2,1,0:T(4,128)S(1)} all-to-all(f32[32,4,128]{2,1,0:T(4,128)S(1)} %get-tuple-element.137), channel_id=1, replica_groups=mesh['batch'=2,'lat'=4,'lon'=4] {'batch','lat','lon'}, dimensions={0} | all-to-all | bytes 131072 | tf_op jit(solution)/shard_map/all_to_all | solution.py:38
  127.9 2.1 %shard_map.137 = (f32[576,128]{1,0:T(8,128)S(1)}, f32[1152,128]{1,0:T(8,128)S(1)}, bf16[4,18,48,128]{3,2,1,0:T(8,128)(2,1)S(1)}) custom-call(s32[4]{0:T(128)S(1)} %pad_add_fusion.info.refs_0_, f32[4,128]{1,0:T(4,128)S(1)} %copy-done.4, f32[32,4,128]{2,1,0:T(4,128)S(1)} %all_to_all.45.before.refs_5_.refs_11_.refs_2_.refs_0_, ...), custom_call_target="tpu_custom_call" | custom-call | flops 1000000000 | bytes 8000000 | tf_op jit(solution)/shard_map/pallas_call | solution.py:793
  130.0 0.5 collective-permute-start.16
  130.5 0.1 collective-permute-start.14
  130.6 0.4 collective-permute-start.15
  131.0 1.8 %shard_map.138 = (f32[4,16,32,128]{3,2,1,0:T(8,128)S(1)}, f32[4,128]{1,0:T(4,128)}, f32[4,128]{1,0:T(4,128)}, f32[4,128]{1,0:T(4,128)}) custom-call(bf16[1536,256]{1,0:T(8,128)(2,1)S(1)} %get-tuple-element.97.refs_4_.weight, bf16[4,18,48,128]{3,2,1,0:T(8,128)(2,1)S(1)} %get-tuple-element.148.dpre, f32[4,16,32,128]{3,2,1,0:T(8,128)S(1)} %get-tuple-element.149.grad, ...), custom_call_target="tpu_custom_call" | custom-call | flops 1000000000 | bytes 3000000 | tf_op jit(solution)/shard_map/pallas_call | solution.py:793
  132.8 0.1 collective-permute-done.15.refs_5_
  132.9 0.2 shard_map.139
  133.1 19.4 %all_to_all.52.got = bf16[16,144,128]{2,1,0:T(8,128)(2,1)S(1)} all-to-all(bf16[16,144,128]{2,1,0:T(8,128)(2,1)S(1)} %bitcast.12), channel_id=1, replica_groups={{0,2,4,6,8,10,12,14,16,18,20,22,24,26,28,30},{1,3,5,7,9,11,13,15,17,19,..., dimensions={0} | all-to-all | bytes 1179648 | tf_op jit(solution)/shard_map/all_to_all | solution.py:43
  152.5 0.1 shard_map.140
  152.6 19.8 %all_to_all.53 = bf16[16,144,128]{2,1,0:T(8,128)(2,1)S(1)} all-to-all(bf16[16,144,128]{2,1,0:T(8,128)(2,1)S(1)} %shard_map.140), channel_id=1, replica_groups={{0,2,4,6,8,10,12,14,16,18,20,22,24,26,28,30},{1,3,5,7,9,11,13,15,17,19,..., dimensions={0} | all-to-all | bytes 1179648 | tf_op jit(solution)/shard_map/all_to_all | solution.py:43
  172.4 1.9 %collective-permute-start.17 = (bf16[4,576,128]{2,1,0:T(8,128)(2,1)S(1)}, bf16[4,576,128]{2,1,0:T(8,128)(2,1)S(1)}, u32[]{:S(2)}, u32[]{:S(2)}) collective-permute-start(bf16[4,576,128]{2,1,0:T(8,128)(2,1)S(1)} %bitcast.10), channel_id=1, source_target_pairs={{0,1},{1,0},{2,3},{3,2},{4,5},{5,4},{6,7},{7,6},{8,9},{9,8},{10,11... | collective-permute-start | bytes 1769480 | tf_op jit(solution)/shard_map/ppermute | solution.py:47
  174.3 1.9 %shard_map.141 = (f32[4,1152,128]{2,1,0:T(8,128)}, f32[4,16,32,128]{3,2,1,0:T(8,128)}) custom-call(s32[4]{0:T(128)S(1)} %pad_add_fusion.info.refs_0_, bf16[4,576,128]{2,1,0:T(8,128)(2,1)S(1)} %bitcast.11, f32[4,16,32,128]{3,2,1,0:T(8,128)S(1)} %get-tuple-element.150.refs_7_.grad), custom_call_target="tpu_custom_call" | custom-call | flops 1000000 | bytes 1000000 | tf_op jit(solution)/shard_map/pallas_call | solution.py:793
  176.2 1.6 shard_map.142
  (21 shorter events, 0.1 us)
Async XLA Ops:
  0.6 12.5 %copy-start.3 = (bf16[4,16,32,128]{3,2,1,0:T(8,128)(2,1)S(1)}, bf16[4,16,32,128]{3,2,1,0:T(8,128)(2,1)}, u32[]{:S(2)}) copy-start(bf16[4,16,32,128]{3,2,1,0:T(8,128)(2,1)} %refs_0_.1) | copy-start | bytes 1572868
  0.6 16.0 %copy-start.1 = (bf16[4,16,32,128]{3,2,1,0:T(8,128)(2,1)S(1)}, bf16[4,16,32,128]{3,2,1,0:T(8,128)(2,1)}, u32[]{:S(2)}) copy-start(bf16[4,16,32,128]{3,2,1,0:T(8,128)(2,1)} %cot.5) | copy-start | bytes 1572868
  0.7 16.0 %copy-start = (s32[4,4,16,32,128]{4,3,2,1,0:T(8,128)S(1)}, s32[4,4,16,32,128]{4,3,2,1,0:T(8,128)}, u32[]{:S(2)}) copy-start(s32[4,4,16,32,128]{4,3,2,1,0:T(8,128)} %masks.3) | copy-start | bytes 12582916
  2.7 10.5 %collective-permute-start = (bf16[4,8,32,128]{3,2,1,0:T(8,128)(2,1)S(1)}, bf16[4,8,32,128]{3,2,1,0:T(8,128)(2,1)S(1)}, u32[]{:S(2)}, u32[]{:S(2)}) collective-permute-start(bf16[4,8,32,128]{3,2,1,0:T(8,128)(2,1)S(1)} %get-tuple-element.83), channel_id=1, source_target_pairs={{0,4},{4,0},{8,12},{12,8},{1,5},{5,1},{9,13},{13,9},{2,6},{6,2},{1... | collective-permute-start | bytes 786440 | tf_op jit(solution)/shard_map/ppermute | solution.py:34
  4.9 8.3 %collective-permute-start.1 = (bf16[4,8,32,128]{3,2,1,0:T(8,128)(2,1)S(1)}, bf16[4,8,32,128]{3,2,1,0:T(8,128)(2,1)S(1)}, u32[]{:S(2)}, u32[]{:S(2)}) collective-permute-start(bf16[4,8,32,128]{3,2,1,0:T(8,128)(2,1)S(1)} %get-tuple-element.84), channel_id=1, source_target_pairs={{4,8},{8,4},{5,9},{9,5},{6,10},{10,6},{7,11},{11,7},{20,24},{24,20... | collective-permute-start | bytes 786440 | tf_op jit(solution)/shard_map/ppermute | solution.py:34
  7.3 9.7 %collective-permute-start.5 = (bf16[4,7,32,128]{3,2,1,0:T(8,128)(2,1)S(1)}, bf16[4,7,32,128]{3,2,1,0:T(8,128)(2,1)S(1)}, u32[]{:S(2)}, u32[]{:S(2)}) collective-permute-start(bf16[4,7,32,128]{3,2,1,0:T(8,128)(2,1)S(1)} %get-tuple-element.94), channel_id=1, source_target_pairs={{4,8},{8,4},{5,9},{9,5},{6,10},{10,6},{7,11},{11,7},{20,24},{24,20... | collective-permute-start | bytes 688136 | tf_op jit(solution)/shard_map/ppermute | solution.py:34
  8.0 9.8 %collective-permute-start.4 = (bf16[4,7,32,128]{3,2,1,0:T(8,128)(2,1)S(1)}, bf16[4,7,32,128]{3,2,1,0:T(8,128)(2,1)S(1)}, u32[]{:S(2)}, u32[]{:S(2)}) collective-permute-start(bf16[4,7,32,128]{3,2,1,0:T(8,128)(2,1)S(1)} %get-tuple-element.81.before), channel_id=1, source_target_pairs={{0,4},{4,0},{8,12},{12,8},{1,5},{5,1},{9,13},{13,9},{2,6},{6,2},{1... | collective-permute-start | bytes 688136 | tf_op jit(solution)/shard_map/ppermute | solution.py:34
  13.9 11.2 %collective-permute-start.2 = (bf16[4,32,8,128]{3,2,1,0:T(8,128)(2,1)S(1)}, bf16[4,32,8,128]{3,2,1,0:T(8,128)(2,1)S(1)}, u32[]{:S(2)}, u32[]{:S(2)}) collective-permute-start(bf16[4,32,8,128]{3,2,1,0:T(8,128)(2,1)S(1)} %get-tuple-element.86), channel_id=1, source_target_pairs={{0,1},{1,0},{2,3},{3,2},{4,5},{5,4},{6,7},{7,6},{8,9},{9,8},{10,11... | collective-permute-start | bytes 786440 | tf_op jit(solution)/shard_map/ppermute | solution.py:34
  15.5 9.7 %copy-start.2 = (bf16[4,3,3,128,128]{4,3,2,1,0:T(8,128)(2,1)S(1)}, bf16[4,3,3,128,128]{4,3,2,1,0:T(8,128)(2,1)}, u32[]{:S(2)}) copy-start(bf16[4,3,3,128,128]{4,3,2,1,0:T(8,128)(2,1)} %param.8) | copy-start | bytes 3538948
  15.5 9.9 %collective-permute-start.3 = (bf16[4,32,8,128]{3,2,1,0:T(8,128)(2,1)S(1)}, bf16[4,32,8,128]{3,2,1,0:T(8,128)(2,1)S(1)}, u32[]{:S(2)}, u32[]{:S(2)}) collective-permute-start(bf16[4,32,8,128]{3,2,1,0:T(8,128)(2,1)S(1)} %get-tuple-element.87), channel_id=1, source_target_pairs={{0,3},{1,2},{2,1},{3,0},{4,7},{5,6},{6,5},{7,4},{8,11},{9,10},{10,... | collective-permute-start | bytes 786440 | tf_op jit(solution)/shard_map/ppermute | solution.py:34
  17.0 8.3 %copy-start.4 = (f32[4,128]{1,0:T(4,128)S(1)}, f32[4,128]{1,0:T(4,128)}, u32[]{:S(2)}) copy-start(f32[4,128]{1,0:T(4,128)} %gains.1) | copy-start | bytes 6148
  17.0 8.3 %copy-start.5 = (f32[4,128]{1,0:T(4,128)S(1)}, f32[4,128]{1,0:T(4,128)}, u32[]{:S(2)}) copy-start(f32[4,128]{1,0:T(4,128)} %refs_2_.13) | copy-start | bytes 6148
  17.0 8.3 %copy-start.6 = (f32[4,128]{1,0:T(4,128)S(1)}, f32[4,128]{1,0:T(4,128)}, u32[]{:S(2)}) copy-start(f32[4,128]{1,0:T(4,128)} %refs_3_.7) | copy-start | bytes 6148
  19.2 24.2 %collective-permute-start.8 = (bf16[4,17,32,128]{3,2,1,0:T(8,128)(2,1)S(1)}, bf16[4,17,32,128]{3,2,1,0:T(8,128)(2,1)S(1)}, u32[]{:S(2)}, u32[]{:S(2)}) collective-permute-start(bf16[4,17,32,128]{3,2,1,0:T(8,128)(2,1)S(1)} %get-tuple-element.105), channel_id=1, source_target_pairs={{0,4},{4,0},{8,12},{12,8},{1,5},{5,1},{9,13},{13,9},{2,6},{6,2},{1... | collective-permute-start | bytes 1671176 | tf_op jit(solution)/shard_map/ppermute | solution.py:34
  21.3 22.1 %collective-permute-start.9 = (bf16[4,17,32,128]{3,2,1,0:T(8,128)(2,1)S(1)}, bf16[4,17,32,128]{3,2,1,0:T(8,128)(2,1)S(1)}, u32[]{:S(2)}, u32[]{:S(2)}) collective-permute-start(bf16[4,17,32,128]{3,2,1,0:T(8,128)(2,1)S(1)} %get-tuple-element.106), channel_id=1, source_target_pairs={{4,8},{8,4},{5,9},{9,5},{6,10},{10,6},{7,11},{11,7},{20,24},{24,20... | collective-permute-start | bytes 1671176 | tf_op jit(solution)/shard_map/ppermute | solution.py:34
  21.9 9.9 %collective-permute-start.7 = (bf16[4,30,8,128]{3,2,1,0:T(8,128)(2,1)S(1)}, bf16[4,30,8,128]{3,2,1,0:T(8,128)(2,1)S(1)}, u32[]{:S(2)}, u32[]{:S(2)}) collective-permute-start(bf16[4,30,8,128]{3,2,1,0:T(8,128)(2,1)S(1)} %get-tuple-element.96), channel_id=1, source_target_pairs={{0,3},{1,2},{2,1},{3,0},{4,7},{5,6},{6,5},{7,4},{8,11},{9,10},{10,... | collective-permute-start | bytes 737288 | tf_op jit(solution)/shard_map/ppermute | solution.py:34
  25.1 6.7 %collective-permute-start.6 = (bf16[4,30,8,128]{3,2,1,0:T(8,128)(2,1)S(1)}, bf16[4,30,8,128]{3,2,1,0:T(8,128)(2,1)S(1)}, u32[]{:S(2)}, u32[]{:S(2)}) collective-permute-start(bf16[4,30,8,128]{3,2,1,0:T(8,128)(2,1)S(1)} %get-tuple-element.95.before), channel_id=1, source_target_pairs={{0,1},{1,0},{2,3},{3,2},{4,5},{5,4},{6,7},{7,6},{8,9},{9,8},{10,11... | collective-permute-start | bytes 737288 | tf_op jit(solution)/shard_map/ppermute | solution.py:34
  44.2 7.7 %collective-permute-start.11 = (bf16[4,28,8,128]{3,2,1,0:T(8,128)(2,1)S(1)}, bf16[4,28,8,128]{3,2,1,0:T(8,128)(2,1)S(1)}, u32[]{:S(2)}, u32[]{:S(2)}) collective-permute-start(bf16[4,28,8,128]{3,2,1,0:T(8,128)(2,1)S(1)} %get-tuple-element.109), channel_id=1, source_target_pairs={{0,3},{1,2},{2,1},{3,0},{4,7},{5,6},{6,5},{7,4},{8,11},{9,10},{10,... | collective-permute-start | bytes 688136 | tf_op jit(solution)/shard_map/ppermute | solution.py:34
  44.7 7.2 %collective-permute-start.10 = (bf16[4,28,8,128]{3,2,1,0:T(8,128)(2,1)S(1)}, bf16[4,28,8,128]{3,2,1,0:T(8,128)(2,1)S(1)}, u32[]{:S(2)}, u32[]{:S(2)}) collective-permute-start(bf16[4,28,8,128]{3,2,1,0:T(8,128)(2,1)S(1)} %get-tuple-element.107.refs_10_), channel_id=1, source_target_pairs={{0,1},{1,0},{2,3},{3,2},{4,5},{5,4},{6,7},{7,6},{8,9},{9,8},{10,11... | collective-permute-start | bytes 688136 | tf_op jit(solution)/shard_map/ppermute | solution.py:34
  61.6 13.5 %collective-permute-start.13 = (bf16[4,50,8,128]{3,2,1,0:T(8,128)(2,1)S(1)}, bf16[4,50,8,128]{3,2,1,0:T(8,128)(2,1)S(1)}, u32[]{:S(2)}, u32[]{:S(2)}) collective-permute-start(bf16[4,50,8,128]{3,2,1,0:T(8,128)(2,1)S(1)} %get-tuple-element.119), channel_id=1, source_target_pairs={{0,3},{1,2},{2,1},{3,0},{4,7},{5,6},{6,5},{7,4},{8,11},{9,10},{10,... | collective-permute-start | bytes 1228808 | tf_op jit(solution)/shard_map/ppermute | solution.py:34
  62.2 13.0 %collective-permute-start.12 = (bf16[4,50,8,128]{3,2,1,0:T(8,128)(2,1)S(1)}, bf16[4,50,8,128]{3,2,1,0:T(8,128)(2,1)S(1)}, u32[]{:S(2)}, u32[]{:S(2)}) collective-permute-start(bf16[4,50,8,128]{3,2,1,0:T(8,128)(2,1)S(1)} %get-tuple-element.116.refs_12_), channel_id=1, source_target_pairs={{0,1},{1,0},{2,3},{3,2},{4,5},{5,4},{6,7},{7,6},{8,9},{9,8},{10,11... | collective-permute-start | bytes 1228808 | tf_op jit(solution)/shard_map/ppermute | solution.py:34
  130.0 2.9 %collective-permute-start.16 = (f32[1152,128]{1,0:T(8,128)S(1)}, f32[1152,128]{1,0:T(8,128)S(1)}, u32[]{:S(2)}, u32[]{:S(2)}) collective-permute-start(f32[1152,128]{1,0:T(8,128)S(1)} %get-tuple-element.147), channel_id=1, source_target_pairs={{0,1},{1,0},{2,3},{3,2},{4,5},{5,4},{6,7},{7,6},{8,9},{9,8},{10,11... | collective-permute-start | bytes 1769480 | tf_op jit(solution)/shard_map/ppermute | solution.py:47
  130.5 2.3 %collective-permute-start.14 = (f32[576,128]{1,0:T(8,128)S(1)}, f32[576,128]{1,0:T(8,128)S(1)}, u32[]{:S(2)}, u32[]{:S(2)}) collective-permute-start(f32[576,128]{1,0:T(8,128)S(1)} %get-tuple-element.145), channel_id=1, source_target_pairs={{0,1},{1,0},{2,3},{3,2},{4,5},{5,4},{6,7},{7,6},{8,9},{9,8},{10,11... | collective-permute-start | bytes 884744 | tf_op jit(solution)/shard_map/ppermute | solution.py:47
  130.6 2.4 %collective-permute-start.15 = (f32[576,128]{1,0:T(8,128)S(1)}, f32[576,128]{1,0:T(8,128)S(1)}, u32[]{:S(2)}, u32[]{:S(2)}) collective-permute-start(f32[576,128]{1,0:T(8,128)S(1)} %get-tuple-element.146), channel_id=1, source_target_pairs={{0,1},{1,0},{2,3},{3,2},{4,5},{5,4},{6,7},{7,6},{8,9},{9,8},{10,11... | collective-permute-start | bytes 884744 | tf_op jit(solution)/shard_map/ppermute | solution.py:47
  172.4 3.8 %collective-permute-start.17 = (bf16[4,576,128]{2,1,0:T(8,128)(2,1)S(1)}, bf16[4,576,128]{2,1,0:T(8,128)(2,1)S(1)}, u32[]{:S(2)}, u32[]{:S(2)}) collective-permute-start(bf16[4,576,128]{2,1,0:T(8,128)(2,1)S(1)} %bitcast.10), channel_id=1, source_target_pairs={{0,1},{1,0},{2,3},{3,2},{4,5},{5,4},{6,7},{7,6},{8,9},{9,8},{10,11... | collective-permute-start | bytes 1769480 | tf_op jit(solution)/shard_map/ppermute | solution.py:47

commit v7 on v6

--- a/solution.py
+++ b/solution.py
@@ -124,7 +124,7 @@
 
 
 def pipeline(grids, lo, hi, taps, weight, cols, prepare, emit, after, finish, extra=None, take=None, extra_totals=()):
-    parts = even_parts(lo, hi, 5)
+    parts = even_parts(lo, hi, 4)
     count = len(parts)
 
     def body(*refs):
@@ -274,11 +274,11 @@
     both_ways(info[1], give(first), give(second))
 
 
-def add_rows(geo, info, sources, heights, got_first, got_second, outs):
+def add_rows(geo, info, sources, heights, got_first, got_second, outs, start=0):
     grids, rows = geo["G"], geo["R"]
 
     def place(low, high):
-        at = 0
+        at = start
         for out, h in zip(outs, heights):
             for g in range(grids):
                 out[g, 0:h] = low[g, at : at + h]
@@ -376,10 +376,11 @@
         lay_weights(kernels, layer, back, out)
 
 
-def late_kernel(geo, info, mask1, mask2, masked, cot, first, second, before, *outs):
-    del before
-    add_rows(geo, info, [mask1, mask2, masked, cot], geo["heights"][2:], first, second, outs[0:4])
-    cut_cols(geo, info, outs[0:1], *outs[4:6])
+def late_kernel(geo, heights, info, *refs):
+    n = len(heights)
+    add_rows(geo, info, refs[:n], heights, refs[n], refs[n + 1], refs[n + 3 : 2 * n + 3], 0 if n == 1 else geo["heights"][2])
+    if len(refs) > 2 * n + 3:
+        cut_cols(geo, info, refs[n + 3 : n + 4], *refs[2 * n + 3 :])
 
 
 def last_kernel(geo, info, tall2, tall3, tall4, before, first, second):
@@ -898,7 +899,7 @@
     talls = [rows + 2 * h for h in heights[2:]]
 
     pres, lows, stats, exts = [None] * 4, [None] * 4, [None] * 4, [None] * 6
-    field = order = None
+    field = order = last = None
     for layer in range(4):
         operands = [info, gains, offsets, biases, weights[layer]]
         if layer:
@@ -915,20 +916,25 @@
             if layer == 0:
                 weights += weights_for([(2, False), (3, False), (0, True), (1, True), (2, True), (3, True)], part)
                 beside = weights[2:]
-            (part,) = call(gate_kernel, [part] + pieces[layer + 1][1:] + beside, [(part.shape, F32)], scalars=0)
+            else:
+                beside = last = call(
+                    functools.partial(late_kernel, geo, heights[3:]),
+                    [info, low_masks[2], masked, cotangent, *late_got, part], [block(t, cols) for t in talls[1:]],
+                )
+            (part,) = call(gate_kernel, [part, *pieces[layer + 1][1:], *beside], [(part.shape, F32)], scalars=0)
         stats[layer] = to_all(part)
         if layer == 0:
             ends = call(
-                functools.partial(late_kernel, geo), [info] + low_masks[1:3] + [masked, cotangent, *late_got, stats[0]],
-                [block(t, cols) for t in talls] + [block(talls[0], EXT)] * 2,
+                functools.partial(late_kernel, geo, heights[2:3]), [info, low_masks[1], *late_got, stats[0]],
+                [block(talls[0], cols)] + [block(talls[0], EXT)] * 2,
             )
-            pieces.append([ends[0], *trade(ends[4:6], "lon", True)])
-            order = ends[4]
+            pieces.append([ends[0], *trade(ends[1:3], "lon", True)])
+            order = ends[1]
         if layer == 1:
             edges = call(
-                functools.partial(last_kernel, geo), [info, *ends[1:4], stats[1]], [block(talls[1] + talls[2], EXT)] * 2
+                functools.partial(last_kernel, geo), [info, *last, stats[1]], [block(talls[1] + talls[2], EXT)] * 2
             )
-            pieces.append([*ends[1:4], *trade(edges, "lon", True)])
+            pieces.append([*last, *trade(edges, "lon", True)])
             order = edges[0]
         for n, k in enumerate(geo["members"][layer]):
             exts[k] = [pieces[layer][n], outs.pop(0)]

time: 178 us -> 178 us (level)
    pallas_call x25 -> x26, Pallas kernels: 43.9 us -> 43.8 us  [call(): pl.pallas_call(kernel, in_specs=specs, out_specs=places, input_output_ali...]
  transfers between devices with their start and end apart: 18 -> 18, of which waited for: 4 -> 4; matrix products, arithmetic and copies ran while one was open for 0% -> 0% of each run, Pallas kernels for 11% -> 12%
where the time goes in v7:
time: 178 us; the launch traced here: 177 us
  blocking collectives  105 us (59%)
  Pallas kernels  43.8 us (25%)
  starting transfers between devices  21.6 us (12%)
  waiting for transfers between devices  5.68 us (3%)
    all_to_all x7, blocking collectives, to_all(): return lax.all_to_all(rows, EVERY, 0, 0)  65.9 us
    pallas_call x26, Pallas kernels, call(): pl.pallas_call(kernel, in_specs=specs, out_specs=places, input_output_ali...  43.8 us
    all_to_all x2, blocking collectives, to_half(): return lax.all_to_all(rows, EVERY, 0, 0, axis_index_groups=groups)  39.2 us
    ppermute x7, starting transfers between devices, trade(): lax.ppermute(pair[0], axis, first)  11.2 us
    ppermute x7, starting transfers between devices, trade(): lax.ppermute(pair[1], axis, second)  7.49 us
    ppermute x7, waiting for transfers between devices, trade(): lax.ppermute(pair[1], axis, second)  4.71 us
  transfers between devices with their start and end apart: 18, of which 4 were waited for; matrix products, arithmetic and copies ran while one was open for 0% of the time, Pallas kernels for 12%

profile of v7, /device:TPU:1, one launch (start us, length us, event | category | flops | bytes accessed | tf_op | source)
XLA Modules:
  0.0 177.4 jit_solution(10699499063833820710)
XLA Ops:
  0.6 0.0 copy-start.3
  0.7 0.0 copy-start
  0.7 0.1 pad_add_fusion.info.refs_0_
  0.8 1.9 %shard_map.120 = (bf16[4,8,32,128]{3,2,1,0:T(8,128)(2,1)S(1)}, bf16[4,8,32,128]{3,2,1,0:T(8,128)(2,1)S(1)}) custom-call(s32[4]{0:T(128)S(1)} %pad_add_fusion.info.refs_0_, bf16[4,16,32,128]{3,2,1,0:T(8,128)(2,1)} %refs_0_.1), custom_call_target="tpu_custom_call" | custom-call | flops 1000000 | bytes 1000000 | tf_op jit(solution)/shard_map/pallas_call | solution.py:794
  2.7 2.2 %collective-permute-start = (bf16[4,8,32,128]{3,2,1,0:T(8,128)(2,1)S(1)}, bf16[4,8,32,128]{3,2,1,0:T(8,128)(2,1)S(1)}, u32[]{:S(2)}, u32[]{:S(2)}) collective-permute-start(bf16[4,8,32,128]{3,2,1,0:T(8,128)(2,1)S(1)} %get-tuple-element.83), channel_id=1, source_target_pairs={{0,4},{4,0},{8,12},{12,8},{1,5},{5,1},{9,13},{13,9},{2,6},{6,2},{1... | collective-permute-start | bytes 786440 | tf_op jit(solution)/shard_map/ppermute | solution.py:34
  4.9 0.7 collective-permute-start.1
  5.5 1.8 shard_map.118
  7.3 0.7 collective-permute-start.5
  8.0 5.1 %collective-permute-start.4 = (bf16[4,7,32,128]{3,2,1,0:T(8,128)(2,1)S(1)}, bf16[4,7,32,128]{3,2,1,0:T(8,128)(2,1)S(1)}, u32[]{:S(2)}, u32[]{:S(2)}) collective-permute-start(bf16[4,7,32,128]{3,2,1,0:T(8,128)(2,1)S(1)} %get-tuple-element.81.before), channel_id=1, source_target_pairs={{0,4},{4,0},{8,12},{12,8},{1,5},{5,1},{9,13},{13,9},{2,6},{6,2},{1... | collective-permute-start | bytes 688136 | tf_op jit(solution)/shard_map/ppermute | solution.py:34
  13.1 0.0 collective-permute-done.refs_1_
  13.1 0.7 shard_map.121
  13.9 1.6 collective-permute-start.2
  15.5 1.2 collective-permute-start.3
  16.7 0.3 shard_map.124
  17.0 0.0 copy-start.4
  17.0 0.0 copy-start.5
  17.0 0.0 copy-start.6
  17.0 0.0 collective-permute-done.5.refs_2_
  17.1 0.8 collective-permute-done.4.refs_1_
  17.8 0.7 shard_map.125
  18.5 0.6 shard_map.127
  19.2 2.1 %collective-permute-start.8 = (bf16[4,17,32,128]{3,2,1,0:T(8,128)(2,1)S(1)}, bf16[4,17,32,128]{3,2,1,0:T(8,128)(2,1)S(1)}, u32[]{:S(2)}, u32[]{:S(2)}) collective-permute-start(bf16[4,17,32,128]{3,2,1,0:T(8,128)(2,1)S(1)} %get-tuple-element.105), channel_id=1, source_target_pairs={{0,4},{4,0},{8,12},{12,8},{1,5},{5,1},{9,13},{13,9},{2,6},{6,2},{1... | collective-permute-start | bytes 1671176 | tf_op jit(solution)/shard_map/ppermute | solution.py:34
  21.3 0.7 collective-permute-start.9
  21.9 3.2 %collective-permute-start.7 = (bf16[4,30,8,128]{3,2,1,0:T(8,128)(2,1)S(1)}, bf16[4,30,8,128]{3,2,1,0:T(8,128)(2,1)S(1)}, u32[]{:S(2)}, u32[]{:S(2)}) collective-permute-start(bf16[4,30,8,128]{3,2,1,0:T(8,128)(2,1)S(1)} %get-tuple-element.96), channel_id=1, source_target_pairs={{0,3},{1,2},{2,1},{3,0},{4,7},{5,6},{6,5},{7,4},{8,11},{9,10},{10,... | collective-permute-start | bytes 737288 | tf_op jit(solution)/shard_map/ppermute | solution.py:34
  25.1 0.0 collective-permute-done.2.refs_6_
  25.1 0.0 collective-permute-start.6
  25.1 0.2 shard_map.119
  25.4 4.0 %shard_map.122 = (f32[32,4,128]{2,1,0:T(4,128)S(1)}, bf16[4,32,16,128]{3,2,1,0:T(8,128)(2,1)S(1)}, f32[4,32,48,128]{3,2,1,0:T(8,128)S(1)}, bf16[3,4,18,32,128]{4,3,2,1,0:T(8,128)(2,1)S(1)}) custom-call(s32[4]{0:T(128)S(1)} %pad_add_fusion.info.refs_0_, f32[4,128]{1,0:T(4,128)S(1)} %copy-done.4, f32[4,128]{1,0:T(4,128)S(1)} %copy-done.5, ...), custom_call_target="tpu_custom_call" | custom-call | flops 2000000000 | bytes 8000000 | tf_op jit(solution)/shard_map/pallas_call | solution.py:794
  29.3 0.7 shard_map.123
  30.0 1.8 %collective-permute-done.7.refs_1_.refs_9_ = bf16[4,30,8,128]{3,2,1,0:T(8,128)(2,1)S(1)} collective-permute-done((bf16[4,30,8,128]{3,2,1,0:T(8,128)(2,1)S(1)}, bf16[4,30,8,128]{3,2,1,0:T(8,128)(2,1)S(1)}, u32[]{:S(2)}, u32[]{:S(2)}) %collective-permute-start.7) | collective-permute-done | bytes 245792 | tf_op jit(solution)/shard_map/ppermute | solution.py:34
  31.9 11.5 %all_to_all.45.refs_3_.refs_5_.refs_11_.refs_2_.refs_0_ = f32[32,4,128]{2,1,0:T(4,128)S(1)} all-to-all(f32[32,4,128]{2,1,0:T(4,128)S(1)} %shard_map.126), channel_id=1, replica_groups=mesh['batch'=2,'lat'=4,'lon'=4] {'batch','lat','lon'}, dimensions={0} | all-to-all | bytes 131072 | tf_op jit(solution)/shard_map/all_to_all | solution.py:38
  43.4 0.7 shard_map.128
  44.1 0.5 collective-permute-start.11
  44.6 0.1 collective-permute-start.10
  44.7 3.4 %shard_map.129 = (f32[32,2,128]{2,1,0:T(2,128)S(1)}, bf16[4,30,16,128]{3,2,1,0:T(8,128)(2,1)S(1)}, f32[4,32,48,128]{3,2,1,0:T(8,128)S(1)}, bf16[3,4,18,32,128]{4,3,2,1,0:T(8,128)(2,1)S(1)}) custom-call(s32[4]{0:T(128)S(1)} %pad_add_fusion.info.refs_0_, f32[4,128]{1,0:T(4,128)S(1)} %copy-done.4, f32[4,128]{1,0:T(4,128)S(1)} %copy-done.5, ...), custom_call_target="tpu_custom_call" | custom-call | flops 2000000000 | bytes 8000000 | tf_op jit(solution)/shard_map/pallas_call | solution.py:794
  48.2 0.7 shard_map.130
  48.9 2.9 %collective-permute-done.11.refs_1_.refs_11_ = bf16[4,28,8,128]{3,2,1,0:T(8,128)(2,1)S(1)} collective-permute-done((bf16[4,28,8,128]{3,2,1,0:T(8,128)(2,1)S(1)}, bf16[4,28,8,128]{3,2,1,0:T(8,128)(2,1)S(1)}, u32[]{:S(2)}, u32[]{:S(2)}) %collective-permute-start.11) | collective-permute-done | bytes 229408 | tf_op jit(solution)/shard_map/ppermute | solution.py:34
  51.8 8.9 %all_to_all.46.before.refs_5_.refs_13_.refs_4_.refs_1_ = f32[32,2,128]{2,1,0:T(2,128)S(1)} all-to-all(f32[32,2,128]{2,1,0:T(2,128)S(1)} %shard_map.131), channel_id=1, replica_groups=mesh['batch'=2,'lat'=4,'lon'=4] {'batch','lat','lon'}, dimensions={0} | all-to-all | bytes 65536 | tf_op jit(solution)/shard_map/all_to_all | solution.py:38
  60.7 0.8 shard_map.132
  61.5 0.6 collective-permute-start.13
  62.0 0.1 collective-permute-start.12
  62.2 3.6 %shard_map.133 = (f32[32,2,128]{2,1,0:T(2,128)S(1)}, bf16[4,28,16,128]{3,2,1,0:T(8,128)(2,1)S(1)}, f32[4,32,48,128]{3,2,1,0:T(8,128)S(1)}, bf16[3,4,18,32,128]{4...) custom-call(s32[4]{0:T(128)S(1)} %pad_add_fusion.info.refs_0_, f32[4,128]{1,0:T(4,128)S(1)} %copy-done.4, ...), custom_call_target="tpu_custom_call" | custom-call | flops 2000000000 | bytes 8000000 | tf_op jit(solution)/shard_map/pallas_call | solution.py:794
  65.8 9.0 %all_to_all.47.refs_5_.refs_14_.refs_4_.refs_2_ = f32[32,2,128]{2,1,0:T(2,128)S(1)} all-to-all(f32[32,2,128]{2,1,0:T(2,128)S(1)} %get-tuple-element.117), channel_id=1, replica_groups=mesh['batch'=2,'lat'=4,'lon'=4] {'batch','lat','lon'}, dimensions={0} | all-to-all | bytes 65536 | tf_op jit(solution)/shard_map/all_to_all | solution.py:38
  74.8 3.5 %shard_map.134 = (f32[32,4,128]{2,1,0:T(4,128)S(1)}, bf16[4,26,16,128]{3,2,1,0:T(8,128)(2,1)S(1)}, bf16[4,24,16,128]{3,2,1,0:T(8,128)(2,1)S(1)}, bf16[4,20,16,12...) custom-call(s32[4]{0:T(128)S(1)} %pad_add_fusion.info.refs_0_, ...), custom_call_target="tpu_custom_call" | custom-call | flops 2000000000 | bytes 8000000 | tf_op jit(solution)/shard_map/pallas_call | solution.py:794
  78.3 9.1 %all_to_all.48.refs_4_.refs_5_.refs_3_ = f32[32,4,128]{2,1,0:T(4,128)S(1)} all-to-all(f32[32,4,128]{2,1,0:T(4,128)S(1)} %get-tuple-element.120), channel_id=1, replica_groups=mesh['batch'=2,'lat'=4,'lon'=4] {'batch','lat','lon'}, dimensions={0} | all-to-all | bytes 131072 | tf_op jit(solution)/shard_map/all_to_all | solution.py:38
  87.4 5.0 %shard_map.135 = (f32[32,3,128]{2,1,0:T(4,128)S(1)}, f32[576,128]{1,0:T(8,128)S(1)}, f32[576,128]{1,0:T(8,128)S(1)}, f32[4,32,48,128]{3,2,1,0:T(8,128)S(1)}, bf16[4,16,32,128]{3,2,1,0:T(8,128)(2,1)}) custom-call(s32[4]{0:T(128)S(1)} %pad_add_fusion.info.refs_0_, f32[4,128]{1,0:T(4,128)S(1)} %copy-done.4, f32[4,128]{1,0:T(4,128)S(1)} %copy-done.5, ...), custom_call_target="tpu_custom_call" | custom-call | flops 3000000000 | bytes 8000000 | tf_op jit(solution)/shard_map/pallas_call | solution.py:794
  92.4 9.1 %all_to_all.49.refs_5_.refs_6_ = f32[32,3,128]{2,1,0:T(4,128)S(1)} all-to-all(f32[32,3,128]{2,1,0:T(4,128)S(1)} %get-tuple-element.128), channel_id=1, replica_groups=mesh['batch'=2,'lat'=4,'lon'=4] {'batch','lat','lon'}, dimensions={0} | all-to-all | bytes 98304 | tf_op jit(solution)/shard_map/all_to_all | solution.py:38
  101.5 3.9 %shard_map.136 = (f32[32,3,128]{2,1,0:T(4,128)S(1)}, f32[576,128]{1,0:T(8,128)S(1)}, f32[576,128]{1,0:T(8,128)S(1)}, f32[4,32,48,128]{3,2,1,0:T(8,128)S(1)}, f32[4,16,32,128]{3,2,1,0:T(8,128)S(1)}) custom-call(s32[4]{0:T(128)S(1)} %pad_add_fusion.info.refs_0_, f32[4,128]{1,0:T(4,128)S(1)} %copy-done.4, f32[4,128]{1,0:T(4,128)S(1)} %copy-done.5, ...), custom_call_target="tpu_custom_call" | custom-call | flops 3000000000 | bytes 8000000 | tf_op jit(solution)/shard_map/pallas_call | solution.py:794
  105.4 9.1 %all_to_all.50.refs_5_ = f32[32,3,128]{2,1,0:T(4,128)S(1)} all-to-all(f32[32,3,128]{2,1,0:T(4,128)S(1)} %get-tuple-element.133), channel_id=1, replica_groups=mesh['batch'=2,'lat'=4,'lon'=4] {'batch','lat','lon'}, dimensions={0} | all-to-all | bytes 98304 | tf_op jit(solution)/shard_map/all_to_all | solution.py:38
  114.5 3.7 %shard_map.137 = (f32[32,4,128]{2,1,0:T(4,128)S(1)}, f32[576,128]{1,0:T(8,128)S(1)}, f32[576,128]{1,0:T(8,128)S(1)}, f32[4,32,48,128]{3,2,1,0:T(8,128)S(1)}) custom-call(s32[4]{0:T(128)S(1)} %pad_add_fusion.info.refs_0_, f32[4,128]{1,0:T(4,128)S(1)} %copy-done.4, f32[4,128]{1,0:T(4,128)S(1)} %copy-done.5, ...), custom_call_target="tpu_custom_call" | custom-call | flops 3000000000 | bytes 8000000 | tf_op jit(solution)/shard_map/pallas_call | solution.py:794
  118.2 9.1 %all_to_all.51.refs_3_.refs_4_ = f32[32,4,128]{2,1,0:T(4,128)S(1)} all-to-all(f32[32,4,128]{2,1,0:T(4,128)S(1)} %get-tuple-element.137), channel_id=1, replica_groups=mesh['batch'=2,'lat'=4,'lon'=4] {'batch','lat','lon'}, dimensions={0} | all-to-all | bytes 131072 | tf_op jit(solution)/shard_map/all_to_all | solution.py:38
  127.3 2.1 %shard_map.138 = (f32[576,128]{1,0:T(8,128)S(1)}, f32[1152,128]{1,0:T(8,128)S(1)}, bf16[4,18,48,128]{3,2,1,0:T(8,128)(2,1)S(1)}) custom-call(s32[4]{0:T(128)S(1)} %pad_add_fusion.info.refs_0_, f32[4,128]{1,0:T(4,128)S(1)} %copy-done.4, f32[32,4,128]{2,1,0:T(4,128)S(1)} %all_to_all.45.refs_3_.refs_5_.refs_11_.refs_2_.refs_0_, ...), custom_call_target="tpu_custom_call" | custom-call | flops 1000000000 | bytes 8000000 | tf_op jit(solution)/shard_map/pallas_call | solution.py:794
  129.4 0.5 collective-permute-start.16
  129.9 0.1 collective-permute-start.14
  130.0 0.4 collective-permute-start.15
  130.4 1.8 %shard_map.139 = (f32[4,16,32,128]{3,2,1,0:T(8,128)S(1)}, f32[4,128]{1,0:T(4,128)}, f32[4,128]{1,0:T(4,128)}, f32[4,128]{1,0:T(4,128)}) custom-call(bf16[1536,256]{1,0:T(8,128)(2,1)S(1)} %get-tuple-element.97.refs_4_.weight, bf16[4,18,48,128]{3,2,1,0:T(8,128)(2,1)S(1)} %get-tuple-element.148.dpre, f32[4,16,32,128]{3,2,1,0:T(8,128)S(1)} %get-tuple-element.149.grad, ...), custom_call_target="tpu_custom_call" | custom-call | flops 1000000000 | bytes 3000000 | tf_op jit(solution)/shard_map/pallas_call | solution.py:794
  132.2 0.2 collective-permute-done.15.refs_5_
  132.4 0.1 shard_map.140
  132.5 19.4 %all_to_all.52.got = bf16[16,144,128]{2,1,0:T(8,128)(2,1)S(1)} all-to-all(bf16[16,144,128]{2,1,0:T(8,128)(2,1)S(1)} %bitcast.12), channel_id=1, replica_groups={{0,2,4,6,8,10,12,14,16,18,20,22,24,26,28,30},{1,3,5,7,9,11,13,15,17,19,..., dimensions={0} | all-to-all | bytes 1179648 | tf_op jit(solution)/shard_map/all_to_all | solution.py:43
  151.9 0.1 shard_map.141
  152.0 19.8 %all_to_all.53 = bf16[16,144,128]{2,1,0:T(8,128)(2,1)S(1)} all-to-all(bf16[16,144,128]{2,1,0:T(8,128)(2,1)S(1)} %shard_map.141), channel_id=1, replica_groups={{0,2,4,6,8,10,12,14,16,18,20,22,24,26,28,30},{1,3,5,7,9,11,13,15,17,19,..., dimensions={0} | all-to-all | bytes 1179648 | tf_op jit(solution)/shard_map/all_to_all | solution.py:43
  171.8 1.9 %collective-permute-start.17 = (bf16[4,576,128]{2,1,0:T(8,128)(2,1)S(1)}, bf16[4,576,128]{2,1,0:T(8,128)(2,1)S(1)}, u32[]{:S(2)}, u32[]{:S(2)}) collective-permute-start(bf16[4,576,128]{2,1,0:T(8,128)(2,1)S(1)} %bitcast.10), channel_id=1, source_target_pairs={{0,1},{1,0},{2,3},{3,2},{4,5},{5,4},{6,7},{7,6},{8,9},{9,8},{10,11... | collective-permute-start | bytes 1769480 | tf_op jit(solution)/shard_map/ppermute | solution.py:47
  173.7 1.9 %shard_map.142 = (f32[4,1152,128]{2,1,0:T(8,128)}, f32[4,16,32,128]{3,2,1,0:T(8,128)}) custom-call(s32[4]{0:T(128)S(1)} %pad_add_fusion.info.refs_0_, bf16[4,576,128]{2,1,0:T(8,128)(2,1)S(1)} %bitcast.11, f32[4,16,32,128]{3,2,1,0:T(8,128)S(1)} %get-tuple-element.150.refs_7_.grad), custom_call_target="tpu_custom_call" | custom-call | flops 1000000 | bytes 1000000 | tf_op jit(solution)/shard_map/pallas_call | solution.py:794
  175.6 1.6 shard_map.143
  (22 shorter events, 0.1 us)
Async XLA Ops:
  0.6 12.5 %copy-start.3 = (bf16[4,16,32,128]{3,2,1,0:T(8,128)(2,1)S(1)}, bf16[4,16,32,128]{3,2,1,0:T(8,128)(2,1)}, u32[]{:S(2)}) copy-start(bf16[4,16,32,128]{3,2,1,0:T(8,128)(2,1)} %refs_0_.1) | copy-start | bytes 1572868
  0.6 16.0 %copy-start.1 = (bf16[4,16,32,128]{3,2,1,0:T(8,128)(2,1)S(1)}, bf16[4,16,32,128]{3,2,1,0:T(8,128)(2,1)}, u32[]{:S(2)}) copy-start(bf16[4,16,32,128]{3,2,1,0:T(8,128)(2,1)} %refs_2_.10) | copy-start | bytes 1572868
  0.7 16.0 %copy-start = (s32[4,4,16,32,128]{4,3,2,1,0:T(8,128)S(1)}, s32[4,4,16,32,128]{4,3,2,1,0:T(8,128)}, u32[]{:S(2)}) copy-start(s32[4,4,16,32,128]{4,3,2,1,0:T(8,128)} %masks.3) | copy-start | bytes 12582916
  2.7 10.5 %collective-permute-start = (bf16[4,8,32,128]{3,2,1,0:T(8,128)(2,1)S(1)}, bf16[4,8,32,128]{3,2,1,0:T(8,128)(2,1)S(1)}, u32[]{:S(2)}, u32[]{:S(2)}) collective-permute-start(bf16[4,8,32,128]{3,2,1,0:T(8,128)(2,1)S(1)} %get-tuple-element.83), channel_id=1, source_target_pairs={{0,4},{4,0},{8,12},{12,8},{1,5},{5,1},{9,13},{13,9},{2,6},{6,2},{1... | collective-permute-start | bytes 786440 | tf_op jit(solution)/shard_map/ppermute | solution.py:34
  4.9 8.3 %collective-permute-start.1 = (bf16[4,8,32,128]{3,2,1,0:T(8,128)(2,1)S(1)}, bf16[4,8,32,128]{3,2,1,0:T(8,128)(2,1)S(1)}, u32[]{:S(2)}, u32[]{:S(2)}) collective-permute-start(bf16[4,8,32,128]{3,2,1,0:T(8,128)(2,1)S(1)} %get-tuple-element.84), channel_id=1, source_target_pairs={{4,8},{8,4},{5,9},{9,5},{6,10},{10,6},{7,11},{11,7},{20,24},{24,20... | collective-permute-start | bytes 786440 | tf_op jit(solution)/shard_map/ppermute | solution.py:34
  7.3 9.7 %collective-permute-start.5 = (bf16[4,7,32,128]{3,2,1,0:T(8,128)(2,1)S(1)}, bf16[4,7,32,128]{3,2,1,0:T(8,128)(2,1)S(1)}, u32[]{:S(2)}, u32[]{:S(2)}) collective-permute-start(bf16[4,7,32,128]{3,2,1,0:T(8,128)(2,1)S(1)} %get-tuple-element.94), channel_id=1, source_target_pairs={{4,8},{8,4},{5,9},{9,5},{6,10},{10,6},{7,11},{11,7},{20,24},{24,20... | collective-permute-start | bytes 688136 | tf_op jit(solution)/shard_map/ppermute | solution.py:34
  8.0 9.8 %collective-permute-start.4 = (bf16[4,7,32,128]{3,2,1,0:T(8,128)(2,1)S(1)}, bf16[4,7,32,128]{3,2,1,0:T(8,128)(2,1)S(1)}, u32[]{:S(2)}, u32[]{:S(2)}) collective-permute-start(bf16[4,7,32,128]{3,2,1,0:T(8,128)(2,1)S(1)} %get-tuple-element.81.before), channel_id=1, source_target_pairs={{0,4},{4,0},{8,12},{12,8},{1,5},{5,1},{9,13},{13,9},{2,6},{6,2},{1... | collective-permute-start | bytes 688136 | tf_op jit(solution)/shard_map/ppermute | solution.py:34
  13.9 11.2 %collective-permute-start.2 = (bf16[4,32,8,128]{3,2,1,0:T(8,128)(2,1)S(1)}, bf16[4,32,8,128]{3,2,1,0:T(8,128)(2,1)S(1)}, u32[]{:S(2)}, u32[]{:S(2)}) collective-permute-start(bf16[4,32,8,128]{3,2,1,0:T(8,128)(2,1)S(1)} %get-tuple-element.86), channel_id=1, source_target_pairs={{0,1},{1,0},{2,3},{3,2},{4,5},{5,4},{6,7},{7,6},{8,9},{9,8},{10,11... | collective-permute-start | bytes 786440 | tf_op jit(solution)/shard_map/ppermute | solution.py:34
  15.5 9.7 %copy-start.2 = (bf16[4,3,3,128,128]{4,3,2,1,0:T(8,128)(2,1)S(1)}, bf16[4,3,3,128,128]{4,3,2,1,0:T(8,128)(2,1)}, u32[]{:S(2)}) copy-start(bf16[4,3,3,128,128]{4,3,2,1,0:T(8,128)(2,1)} %param.8) | copy-start | bytes 3538948
  15.5 9.9 %collective-permute-start.3 = (bf16[4,32,8,128]{3,2,1,0:T(8,128)(2,1)S(1)}, bf16[4,32,8,128]{3,2,1,0:T(8,128)(2,1)S(1)}, u32[]{:S(2)}, u32[]{:S(2)}) collective-permute-start(bf16[4,32,8,128]{3,2,1,0:T(8,128)(2,1)S(1)} %get-tuple-element.87), channel_id=1, source_target_pairs={{0,3},{1,2},{2,1},{3,0},{4,7},{5,6},{6,5},{7,4},{8,11},{9,10},{10,... | collective-permute-start | bytes 786440 | tf_op jit(solution)/shard_map/ppermute | solution.py:34
  17.0 8.3 %copy-start.4 = (f32[4,128]{1,0:T(4,128)S(1)}, f32[4,128]{1,0:T(4,128)}, u32[]{:S(2)}) copy-start(f32[4,128]{1,0:T(4,128)} %gains.1) | copy-start | bytes 6148
  17.0 8.3 %copy-start.5 = (f32[4,128]{1,0:T(4,128)S(1)}, f32[4,128]{1,0:T(4,128)}, u32[]{:S(2)}) copy-start(f32[4,128]{1,0:T(4,128)} %refs_2_.15) | copy-start | bytes 6148
  17.0 8.3 %copy-start.6 = (f32[4,128]{1,0:T(4,128)S(1)}, f32[4,128]{1,0:T(4,128)}, u32[]{:S(2)}) copy-start(f32[4,128]{1,0:T(4,128)} %refs_3_.7) | copy-start | bytes 6148
  19.2 24.2 %collective-permute-start.8 = (bf16[4,17,32,128]{3,2,1,0:T(8,128)(2,1)S(1)}, bf16[4,17,32,128]{3,2,1,0:T(8,128)(2,1)S(1)}, u32[]{:S(2)}, u32[]{:S(2)}) collective-permute-start(bf16[4,17,32,128]{3,2,1,0:T(8,128)(2,1)S(1)} %get-tuple-element.105), channel_id=1, source_target_pairs={{0,4},{4,0},{8,12},{12,8},{1,5},{5,1},{9,13},{13,9},{2,6},{6,2},{1... | collective-permute-start | bytes 1671176 | tf_op jit(solution)/shard_map/ppermute | solution.py:34
  21.3 22.1 %collective-permute-start.9 = (bf16[4,17,32,128]{3,2,1,0:T(8,128)(2,1)S(1)}, bf16[4,17,32,128]{3,2,1,0:T(8,128)(2,1)S(1)}, u32[]{:S(2)}, u32[]{:S(2)}) collective-permute-start(bf16[4,17,32,128]{3,2,1,0:T(8,128)(2,1)S(1)} %get-tuple-element.106), channel_id=1, source_target_pairs={{4,8},{8,4},{5,9},{9,5},{6,10},{10,6},{7,11},{11,7},{20,24},{24,20... | collective-permute-start | bytes 1671176 | tf_op jit(solution)/shard_map/ppermute | solution.py:34
  21.9 9.9 %collective-permute-start.7 = (bf16[4,30,8,128]{3,2,1,0:T(8,128)(2,1)S(1)}, bf16[4,30,8,128]{3,2,1,0:T(8,128)(2,1)S(1)}, u32[]{:S(2)}, u32[]{:S(2)}) collective-permute-start(bf16[4,30,8,128]{3,2,1,0:T(8,128)(2,1)S(1)} %get-tuple-element.96), channel_id=1, source_target_pairs={{0,3},{1,2},{2,1},{3,0},{4,7},{5,6},{6,5},{7,4},{8,11},{9,10},{10,... | collective-permute-start | bytes 737288 | tf_op jit(solution)/shard_map/ppermute | solution.py:34
  25.1 6.7 %collective-permute-start.6 = (bf16[4,30,8,128]{3,2,1,0:T(8,128)(2,1)S(1)}, bf16[4,30,8,128]{3,2,1,0:T(8,128)(2,1)S(1)}, u32[]{:S(2)}, u32[]{:S(2)}) collective-permute-start(bf16[4,30,8,128]{3,2,1,0:T(8,128)(2,1)S(1)} %get-tuple-element.95.before), channel_id=1, source_target_pairs={{0,1},{1,0},{2,3},{3,2},{4,5},{5,4},{6,7},{7,6},{8,9},{9,8},{10,11... | collective-permute-start | bytes 737288 | tf_op jit(solution)/shard_map/ppermute | solution.py:34
  44.1 7.7 %collective-permute-start.11 = (bf16[4,28,8,128]{3,2,1,0:T(8,128)(2,1)S(1)}, bf16[4,28,8,128]{3,2,1,0:T(8,128)(2,1)S(1)}, u32[]{:S(2)}, u32[]{:S(2)}) collective-permute-start(bf16[4,28,8,128]{3,2,1,0:T(8,128)(2,1)S(1)} %get-tuple-element.109), channel_id=1, source_target_pairs={{0,3},{1,2},{2,1},{3,0},{4,7},{5,6},{6,5},{7,4},{8,11},{9,10},{10,... | collective-permute-start | bytes 688136 | tf_op jit(solution)/shard_map/ppermute | solution.py:34
  44.6 7.2 %collective-permute-start.10 = (bf16[4,28,8,128]{3,2,1,0:T(8,128)(2,1)S(1)}, bf16[4,28,8,128]{3,2,1,0:T(8,128)(2,1)S(1)}, u32[]{:S(2)}, u32[]{:S(2)}) collective-permute-start(bf16[4,28,8,128]{3,2,1,0:T(8,128)(2,1)S(1)} %get-tuple-element.107.refs_10_), channel_id=1, source_target_pairs={{0,1},{1,0},{2,3},{3,2},{4,5},{5,4},{6,7},{7,6},{8,9},{9,8},{10,11... | collective-permute-start | bytes 688136 | tf_op jit(solution)/shard_map/ppermute | solution.py:34
  61.5 13.3 %collective-permute-start.13 = (bf16[4,50,8,128]{3,2,1,0:T(8,128)(2,1)S(1)}, bf16[4,50,8,128]{3,2,1,0:T(8,128)(2,1)S(1)}, u32[]{:S(2)}, u32[]{:S(2)}) collective-permute-start(bf16[4,50,8,128]{3,2,1,0:T(8,128)(2,1)S(1)} %get-tuple-element.119), channel_id=1, source_target_pairs={{0,3},{1,2},{2,1},{3,0},{4,7},{5,6},{6,5},{7,4},{8,11},{9,10},{10,... | collective-permute-start | bytes 1228808 | tf_op jit(solution)/shard_map/ppermute | solution.py:34
  62.0 12.7 %collective-permute-start.12 = (bf16[4,50,8,128]{3,2,1,0:T(8,128)(2,1)S(1)}, bf16[4,50,8,128]{3,2,1,0:T(8,128)(2,1)S(1)}, u32[]{:S(2)}, u32[]{:S(2)}) collective-permute-start(bf16[4,50,8,128]{3,2,1,0:T(8,128)(2,1)S(1)} %get-tuple-element.116.refs_12_), channel_id=1, source_target_pairs={{0,1},{1,0},{2,3},{3,2},{4,5},{5,4},{6,7},{7,6},{8,9},{9,8},{10,11... | collective-permute-start | bytes 1228808 | tf_op jit(solution)/shard_map/ppermute | solution.py:34
  129.4 2.9 %collective-permute-start.16 = (f32[1152,128]{1,0:T(8,128)S(1)}, f32[1152,128]{1,0:T(8,128)S(1)}, u32[]{:S(2)}, u32[]{:S(2)}) collective-permute-start(f32[1152,128]{1,0:T(8,128)S(1)} %get-tuple-element.147), channel_id=1, source_target_pairs={{0,1},{1,0},{2,3},{3,2},{4,5},{5,4},{6,7},{7,6},{8,9},{9,8},{10,11... | collective-permute-start | bytes 1769480 | tf_op jit(solution)/shard_map/ppermute | solution.py:47
  129.9 2.3 %collective-permute-start.14 = (f32[576,128]{1,0:T(8,128)S(1)}, f32[576,128]{1,0:T(8,128)S(1)}, u32[]{:S(2)}, u32[]{:S(2)}) collective-permute-start(f32[576,128]{1,0:T(8,128)S(1)} %get-tuple-element.145), channel_id=1, source_target_pairs={{0,1},{1,0},{2,3},{3,2},{4,5},{5,4},{6,7},{7,6},{8,9},{9,8},{10,11... | collective-permute-start | bytes 884744 | tf_op jit(solution)/shard_map/ppermute | solution.py:47
  130.0 2.4 %collective-permute-start.15 = (f32[576,128]{1,0:T(8,128)S(1)}, f32[576,128]{1,0:T(8,128)S(1)}, u32[]{:S(2)}, u32[]{:S(2)}) collective-permute-start(f32[576,128]{1,0:T(8,128)S(1)} %get-tuple-element.146), channel_id=1, source_target_pairs={{0,1},{1,0},{2,3},{3,2},{4,5},{5,4},{6,7},{7,6},{8,9},{9,8},{10,11... | collective-permute-start | bytes 884744 | tf_op jit(solution)/shard_map/ppermute | solution.py:47
  171.8 3.8 %collective-permute-start.17 = (bf16[4,576,128]{2,1,0:T(8,128)(2,1)S(1)}, bf16[4,576,128]{2,1,0:T(8,128)(2,1)S(1)}, u32[]{:S(2)}, u32[]{:S(2)}) collective-permute-start(bf16[4,576,128]{2,1,0:T(8,128)(2,1)S(1)} %bitcast.10), channel_id=1, source_target_pairs={{0,1},{1,0},{2,3},{3,2},{4,5},{5,4},{6,7},{7,6},{8,9},{9,8},{10,11... | collective-permute-start | bytes 1769480 | tf_op jit(solution)/shard_map/ppermute | solution.py:47
